TPU v7x, 32 devices: a whole 2x2x4 slice. The times are simulated.
32 devices in a mesh: blk: 8 (over z, x), col: 4 (over y, core).
Axes of the slice: x: 2, y: 2, z: 4, core: 2. Of those that a mesh axis runs over, the one named last changes fastest.
Arguments:
- frames: bfloat16 [4, 2048, 440], P(None, ('blk', 'col')), may hold values from -6 to 6
- labels: int32 [4, 2048], P(None, ('blk', 'col')), may hold values from 0 to 9303
- mask: int32 [4, 2048], P(None, ('blk', 'col')), may hold values from 0 to 1, as said below
- w_input: float32 [440, 2048], P(None, 'col'), may hold values from -0.25 to 0.25
- w_hidden: float32 [2048, 2048], P('blk', 'col'), may hold values from -0.125 to 0.125
- w_output: float32 [2048, 9304], P('blk', 'col'), may hold values from -0.25 to 0.25
- biases: float32 [4, 3350], P('col'), may hold values from -1 to 1
- mom_input: float32 [440, 2048], P(None, 'col'), may hold values from -2.0343273e-06 to 2.0343273e-06
- mom_hidden: float32 [2048, 2048], P('blk', 'col'), may hold values from -2.0343273e-06 to 2.0343273e-06
- out_first: float32 [2048, 9304], P('blk', 'col'), may hold values from -2.0343273e-06 to 2.0343273e-06
- out_second: float32 [2048, 9304], P('blk', 'col'), may hold values from 8.2769756e-15 to 3.3107902e-14
- bias_first: float32 [4, 3350], P('col'), may hold values from -2.0343274e-05 to 2.0343274e-05
- bias_second: float32 [4, 3350], P('col'), may hold values from 8.2769756e-13 to 3.3107902e-12
- res_input: bfloat16 [8, 440, 2048], P('blk', None, 'col'), may hold values from -6.055832e-05 to 6.055832e-05
- res_hidden: bfloat16 [8, 2048, 2048], P('blk', None, 'col'), may hold values from -6.055832e-05 to 6.055832e-05
- res_output: bfloat16 [8, 2048, 9304], P('blk', None, 'col'), may hold values from -6.055832e-05 to 6.055832e-05
Outputs:
- loss_sum: float32 [], replicated
- clip_norm: float32 [], replicated
- new_input: float32 [440, 2048], P(None, 'col')
- new_hidden: float32 [2048, 2048], P('blk', 'col')
- new_output: float32 [2048, 9304], P('blk', 'col')
- new_biases: float32 [4, 3350], P('col')
- next_mom_input: float32 [440, 2048], P(None, 'col')
- next_mom_hidden: float32 [2048, 2048], P('blk', 'col')
- next_out_first: float32 [2048, 9304], P('blk', 'col')
- next_out_second: float32 [2048, 9304], P('blk', 'col')
- next_bias_first: float32 [4, 3350], P('col')
- next_bias_second: float32 [4, 3350], P('col')
- next_res_input: float32 [8, 440, 2048], P('blk', None, 'col')
- next_res_hidden: float32 [8, 2048, 2048], P('blk', None, 'col')
- next_res_output: float32 [8, 2048, 9304], P('blk', None, 'col')
Inputs may be any that keep to these rules, and one draw needn't show every extreme that they name: `mask`: each device's slots in a micro-batch hold live frames from the first slot on, with scattered dead slots among them.
All inputs are finite; a program needn't handle non-finite values. Where the computation divides by a largest or mean magnitude, that divisor is 1e-20 or more.
Results may differ from a plain program's by a relative error of at most 0.002.
The roundings to bfloat16 on the way count: a program that leaves them out, or rounds other values in their place, can miss the bound.
Values may be sent and summed in bfloat16 or wider, within the bound.
A program may use at most 320 MiB of HBM per device.

v0:
```python
import math

import jax
import jax.numpy as jnp
from jax import lax
from jax.sharding import PartitionSpec as P

NS = 5
STEP = 5


NS_A = 3.4445
NS_B = -4.775
NS_C = 2.0315
CLIP = 0.002
LR_MUON = 0.1
WD_MUON = 0.01
LR_ADAM = 0.03
WD_ADAM = 0.1


def matmul(left_side, right_side):
    return jnp.dot(left_side, right_side, preferred_element_type=jnp.float32)


def inner_rows(left_side, right_side):
    return lax.dot_general(
        left_side, right_side, (((0,), (0,)), ((), ())), preferred_element_type=jnp.float32
    )


def outer_cols(left_side, right_side):
    return lax.dot_general(
        left_side, right_side, (((1,), (1,)), ((), ())), preferred_element_type=jnp.float32
    )


def precise(left_side, right_side):
    return jnp.dot(
        left_side, right_side, precision=lax.Precision.HIGHEST, preferred_element_type=jnp.float32
    )


def spread_cols(values):
    return lax.all_gather(values, "col", axis=1, tiled=True)


def reduce_cols(values):
    return lax.psum_scatter(values, "col", scatter_dimension=1, tiled=True)


def collect_rows(values):
    return lax.all_gather(values, "blk", axis=0, tiled=True)


def squash(gradient, resid):
    value = gradient + resid.astype(jnp.float32)
    scale = jnp.mean(jnp.abs(value), axis=0, keepdims=True) + 1e-12
    signed = scale * jnp.tanh(2.0 * value / scale)
    return (signed, value - signed)


def adam_step(weight, gradient, first, second):
    first = 0.5 * first + 0.5 * gradient
    second = 0.95 * second + 0.05 * gradient * gradient
    update = first / (1.0 - 0.5**STEP) / (jnp.sqrt(second / (1.0 - 0.95**STEP)) + 1e-08)
    return (weight - LR_ADAM * (update + WD_ADAM * weight), first, second)


def body(
    frames,
    labels,
    mask,
    w_input,
    w_hidden,
    w_output,
    biases,
    mom_input,
    mom_hidden,
    out_first,
    out_second,
    bias_first,
    bias_second,
    res_input,
    res_hidden,
    res_output,
):
    ncol = lax.axis_size("col")
    nblk = lax.axis_size("blk")
    col_index = lax.axis_index("col")
    hcol = w_input.shape[1]
    scol = w_output.shape[1]
    micro = frames.shape[0]
    slot_count = frames.shape[1] * micro * nblk * ncol
    bias_row = biases[0]
    b_one = bias_row[:hcol]
    b_two = bias_row[hcol : 2 * hcol]
    b_out = bias_row[2 * hcol :]
    low_input = w_input.astype(jnp.bfloat16)
    row_tags = jnp.where(mask > 0, labels, -1)
    grad_input = jnp.zeros(w_input.shape, jnp.float32)
    grad_hidden = jnp.zeros((w_hidden.shape[0] * nblk, hcol), jnp.float32)
    grad_output = jnp.zeros((w_output.shape[0] * nblk, scol), jnp.float32)
    grad_bias = jnp.zeros(bias_row.shape, jnp.float32)
    loss_local = jnp.zeros((), jnp.float32)
    for micro_step in range(micro):
        low_hidden, low_output = (
            lax.all_gather(w_hidden.astype(jnp.bfloat16), "blk", axis=0, tiled=True),
            lax.all_gather(w_output.astype(jnp.bfloat16), "blk", axis=0, tiled=True),
        )
        inputs = lax.all_gather(frames[micro_step], "col", axis=0, tiled=True)
        tags_group = lax.all_gather(row_tags[micro_step], "col", axis=0, tiled=True)
        sig_one = jax.nn.sigmoid(matmul(inputs, low_input) + b_one)
        h_one = spread_cols(sig_one.astype(jnp.bfloat16))
        sig_two = jax.nn.sigmoid(matmul(h_one, low_hidden) + b_two)
        h_two = spread_cols(sig_two.astype(jnp.bfloat16))
        logits = matmul(h_two, low_output) + b_out
        row_top = lax.pmax(jnp.max(logits, axis=1), "col")
        exponent = jnp.exp(logits - row_top[:, None])
        target_hit = jnp.arange(scol)[None, :] == (tags_group - col_index * scol)[:, None]
        row_total, picked = lax.psum(
            (jnp.sum(exponent, axis=1), jnp.sum(jnp.where(target_hit, logits, 0.0), axis=1)), "col"
        )
        live_rows = tags_group >= 0
        loss_local = loss_local + jnp.sum(
            jnp.where(live_rows, row_top + jnp.log(row_total) - picked, 0.0)
        )
        probs = exponent / row_total[:, None]
        d_logits = (
            jnp.where(live_rows[:, None], probs - target_hit.astype(jnp.float32), 0.0) / slot_count
        ).astype(jnp.bfloat16)
        grad_output = grad_output + inner_rows(h_two, d_logits)
        d_h_two = reduce_cols(outer_cols(d_logits, low_output))
        d_z_two = (d_h_two * sig_two * (1.0 - sig_two)).astype(jnp.bfloat16)
        grad_hidden = grad_hidden + inner_rows(h_one, d_z_two)
        d_h_one = reduce_cols(outer_cols(d_z_two, low_hidden))
        d_z_one = (d_h_one * sig_one * (1.0 - sig_one)).astype(jnp.bfloat16)
        grad_input = grad_input + inner_rows(inputs, d_z_one)
        grad_bias = grad_bias + jnp.concatenate(
            [
                jnp.sum(d_z_one.astype(jnp.float32), axis=0),
                jnp.sum(d_z_two.astype(jnp.float32), axis=0),
                jnp.sum(d_logits.astype(jnp.float32), axis=0),
            ]
        )
    q_input, next_res_input = squash(grad_input, res_input[0])
    q_hidden, next_res_hidden = squash(grad_hidden, res_hidden[0])
    q_output, next_res_output = squash(grad_output, res_output[0])
    red_hidden, red_output = (
        lax.psum_scatter(q_hidden, "blk", scatter_dimension=0, tiled=True),
        lax.psum_scatter(q_output, "blk", scatter_dimension=0, tiled=True),
    )
    red_input, red_bias, loss_sum = lax.psum((q_input, grad_bias, loss_local), "blk")
    share_blk = 1.0 / nblk
    grad_square = (
        share_blk * (jnp.sum(red_input * red_input) + jnp.sum(red_bias * red_bias))
        + jnp.sum(red_hidden * red_hidden)
        + jnp.sum(red_output * red_output)
    )
    clip_norm = jnp.sqrt(lax.psum(grad_square, ("blk", "col")))
    factor = jnp.minimum(1.0, CLIP / clip_norm)
    next_mom_input = 0.5 * mom_input + factor * red_input
    next_mom_hidden = 0.5 * mom_hidden + factor * red_hidden
    square_input, square_hidden = lax.psum(
        (
            share_blk * jnp.sum(next_mom_input * next_mom_input),
            jnp.sum(next_mom_hidden * next_mom_hidden),
        ),
        ("blk", "col"),
    )
    iter_input = next_mom_input / (jnp.sqrt(square_input) + 1e-07)
    iter_hidden = next_mom_hidden / (jnp.sqrt(square_hidden) + 1e-07)
    for turn_index in range(NS):
        rows_hidden = collect_rows(iter_hidden)
        gram_input, gram_hidden = lax.psum(
            (precise(iter_input, iter_input.T), precise(iter_hidden, rows_hidden.T)), "col"
        )
        image_input = precise(gram_input, iter_input)
        image_hidden = precise(gram_hidden, rows_hidden)
        iter_input = (
            NS_A * iter_input + NS_B * image_input + NS_C * precise(gram_input, image_input)
        )
        iter_hidden = (
            NS_A * iter_hidden
            + NS_B * image_hidden
            + NS_C * precise(gram_hidden, collect_rows(image_hidden))
        )
    muon_scale = LR_MUON * 0.2 * math.sqrt(hcol * ncol)
    new_input = w_input * (1.0 - LR_MUON * WD_MUON) - muon_scale * iter_input
    new_hidden = w_hidden * (1.0 - LR_MUON * WD_MUON) - muon_scale * iter_hidden
    new_output, next_out_first, next_out_second = adam_step(
        w_output, factor * red_output, out_first, out_second
    )
    new_biases, next_bias_first, next_bias_second = adam_step(
        biases, factor * red_bias[None, :], bias_first, bias_second
    )
    return (
        loss_sum,
        clip_norm,
        new_input,
        new_hidden,
        new_output,
        new_biases,
        next_mom_input,
        next_mom_hidden,
        next_out_first,
        next_out_second,
        next_bias_first,
        next_bias_second,
        next_res_input[None],
        next_res_hidden[None],
        next_res_output[None],
    )


def solution(mesh):
    in_specs = (
        P(None, ("blk", "col"), None),
        P(None, ("blk", "col")),
        P(None, ("blk", "col")),
        P(None, "col"),
        P("blk", "col"),
        P("blk", "col"),
        P("col", None),
        P(None, "col"),
        P("blk", "col"),
        P("blk", "col"),
        P("blk", "col"),
        P("col", None),
        P("col", None),
        P("blk", None, "col"),
        P("blk", None, "col"),
        P("blk", None, "col"),
    )
    out_specs = (
        P(),
        P(),
        P(None, "col"),
        P("blk", "col"),
        P("blk", "col"),
        P("col", None),
        P(None, "col"),
        P("blk", "col"),
        P("blk", "col"),
        P("blk", "col"),
        P("col", None),
        P("col", None),
        P("blk", None, "col"),
        P("blk", None, "col"),
        P("blk", None, "col"),
    )
    return jax.shard_map(body, mesh=mesh, in_specs=in_specs, out_specs=out_specs, check_vma=False)
```

profile of v0, /device:TPU:0, one launch (start us, length us, event | category | flops | bytes accessed | tf_op | source)
XLA Modules:
  0.0 2421.3 jit_solution(11607842968091804272)
XLA Ops:
  45.1 45.3 %all-gather.31.cloned.1.call-done = bf16[2048,512]{1,0:T(8,128)(2,1)} async-done(((bf16[256,512]{1,0:T(8,128)(2,1)}), bf16[2048,512]{1,0:T(8,128)(2,1)}) %all-gather.31.cloned.1.call-update) | async-done | bytes 2097168 | tf_op jit(solution)/shard_map/all_gather | solution.py:108
  164.0 142.0 %all-gather.35.cloned.1.call-done = bf16[2048,2326]{0,1:T(8,128)(2,1)} async-done(((bf16[256,2326]{0,1:T(8,128)(2,1)}), bf16[2048,2326]{0,1:T(8,128)(2,1)}) %all-gather.35.cloned.1.call-update) | async-done | bytes 9527312 | tf_op jit(solution)/shard_map/all_gather | solution.py:109
  570.4 32.6 %reduce-scatter.13.cloned.1.call-done = f32[256,512]{1,0:T(8,128)} async-done(((f32[256,2048]{1,0:T(8,128)}), f32[256,512]{1,0:T(8,128)}) %reduce-scatter.13.cloned.1.call-update) | async-done | bytes 524304 | tf_op jit(solution)/shard_map/reduce_scatter | solution.py:49
  604.9 32.5 %reduce-scatter.17.cloned.1.call-done = f32[256,512]{1,0:T(8,128)} async-done(((f32[256,2048]{1,0:T(8,128)}), f32[256,512]{1,0:T(8,128)}) %reduce-scatter.17.cloned.1.call-update) | async-done | bytes 524304 | tf_op jit(solution)/shard_map/reduce_scatter | solution.py:49
  746.9 39.0 %all-reduce.6 = (f32[]{:T(128)}, f32[3350]{0:T(1024)S(1)}) all-reduce(f32[]{:T(128)S(6)} %add.419, f32[3350]{0:T(1024)S(1)} %fusion.63), channel_id=1, replica_groups=mesh['blk'=8,'col'=4] {'blk'}, use_global_device_ids=true, to_apply=%region_28.29 | all-reduce | flops 3351 | bytes 26808 | tf_op jit(solution)/shard_map/psum | solution.py:153
  789.9 54.0 %reduce-scatter.27.cloned.1.call-done = f32[256,512]{1,0:T(8,128)} async-done(((f32[2048,512]{1,0:T(8,128)}), f32[256,512]{1,0:T(8,128)}) %reduce-scatter.27.cloned.1.call-update) | async-done | bytes 524304 | tf_op jit(solution)/shard_map/reduce_scatter | solution.py:150
  846.3 317.0 %reduce-scatter.29.cloned.1.call-done = f32[256,2326]{0,1:T(8,128)} async-done(((f32[2048,2326]{0,1:T(8,128)}), f32[256,2326]{0,1:T(8,128)}) %reduce-scatter.29.cloned.1.call-update) | async-done | bytes 2381840 | tf_op jit(solution)/shard_map/reduce_scatter | solution.py:151
  1166.9 39.4 %psum.179 = f32[]{:T(128)} all-reduce(f32[]{:T(128)S(6)} %add.442), channel_id=1, replica_groups=mesh['blk'=8,'col'=4] {'blk','col'}, use_global_device_ids=true, to_apply=%region_60.61 | all-reduce | flops 1 | bytes 8 | tf_op jit(solution)/shard_map/psum | solution.py:160
  1210.4 40.2 %all-reduce.5 = (f32[]{:T(128)}, f32[]{:T(128)}) all-reduce(f32[]{:T(128)S(6)} %mul.380, f32[]{:T(128)} %get-tuple-element.74), channel_id=1, replica_groups=mesh['blk'=8,'col'=4] {'blk','col'}, use_global_device_ids=true, to_apply=%region_62.63 | all-reduce | flops 2 | bytes 16 | tf_op jit(solution)/shard_map/psum | solution.py:164
  1255.5 70.4 %all-gather.49.cloned.1.call-done = f32[2048,512]{1,0:T(8,128)} async-done(((f32[256,512]{1,0:T(8,128)}), f32[2048,512]{1,0:T(8,128)}) %all-gather.49.cloned.1.call-update) | async-done | bytes 4194320 | tf_op jit(solution)/shard_map/all_gather | solution.py:53
  1333.1 64.8 %all-reduce.31.cloned.1.call-done = (f32[440,440]{1,0:T(8,128)}, f32[256,2048]{1,0:T(8,128)}) async-done(((f32[440,440]{1,0:T(8,128)}, f32[256,2048]{1,0:T(8,128)}), (f32[440,440]{1,0:T(8,128)}, f32[256,2048]{1,0:T(8,128)})) %all-reduce.31.cloned.1.call-update) | async-done | bytes 2871568 | tf_op jit(solution)/shard_map/psum | solution.py:175
  1405.8 73.1 %all-gather.51.cloned.1.call-done = f32[2048,512]{1,0:T(8,128)} async-done(((f32[256,512]{1,0:T(8,128)}), f32[2048,512]{1,0:T(8,128)}) %all-gather.51.cloned.1.call-update) | async-done | bytes 4194320 | tf_op jit(solution)/shard_map/all_gather | solution.py:53
  1492.9 64.6 %all-gather.53.cloned.1.call-done = f32[2048,512]{1,0:T(8,128)} async-done(((f32[256,512]{1,0:T(8,128)}), f32[2048,512]{1,0:T(8,128)}) %all-gather.53.cloned.1.call-update) | async-done | bytes 4194320 | tf_op jit(solution)/shard_map/all_gather | solution.py:53
  1564.9 64.6 %all-reduce.29.cloned.1.call-done = (f32[440,440]{1,0:T(8,128)}, f32[256,2048]{1,0:T(8,128)}) async-done(((f32[440,440]{1,0:T(8,128)}, f32[256,2048]{1,0:T(8,128)}), (f32[440,440]{1,0:T(8,128)}, f32[256,2048]{1,0:T(8,128)})) %all-reduce.29.cloned.1.call-update) | async-done | bytes 2871568 | tf_op jit(solution)/shard_map/psum | solution.py:175
  1636.9 73.5 %all-gather.55.cloned.1.call-done = f32[2048,512]{1,0:T(8,128)} async-done(((f32[256,512]{1,0:T(8,128)}), f32[2048,512]{1,0:T(8,128)}) %all-gather.55.cloned.1.call-update) | async-done | bytes 4194320 | tf_op jit(solution)/shard_map/all_gather | solution.py:53
  1724.0 65.7 %all-gather.57.cloned.1.call-done = f32[2048,512]{1,0:T(8,128)} async-done(((f32[256,512]{1,0:T(8,128)}), f32[2048,512]{1,0:T(8,128)}) %all-gather.57.cloned.1.call-update) | async-done | bytes 4194320 | tf_op jit(solution)/shard_map/all_gather | solution.py:53
  1796.9 64.8 %all-reduce.27.cloned.1.call-done = (f32[440,440]{1,0:T(8,128)}, f32[256,2048]{1,0:T(8,128)}) async-done(((f32[440,440]{1,0:T(8,128)}, f32[256,2048]{1,0:T(8,128)}), (f32[440,440]{1,0:T(8,128)}, f32[256,2048]{1,0:T(8,128)})) %all-reduce.27.cloned.1.call-update) | async-done | bytes 2871568 | tf_op jit(solution)/shard_map/psum | solution.py:175
  1869.6 73.1 %all-gather.59.cloned.1.call-done = f32[2048,512]{1,0:T(8,128)} async-done(((f32[256,512]{1,0:T(8,128)}), f32[2048,512]{1,0:T(8,128)}) %all-gather.59.cloned.1.call-update) | async-done | bytes 4194320 | tf_op jit(solution)/shard_map/all_gather | solution.py:53
  1956.7 64.7 %all-gather.61.cloned.1.call-done = f32[2048,512]{1,0:T(8,128)} async-done(((f32[256,512]{1,0:T(8,128)}), f32[2048,512]{1,0:T(8,128)}) %all-gather.61.cloned.1.call-update) | async-done | bytes 4194320 | tf_op jit(solution)/shard_map/all_gather | solution.py:53
  2028.7 64.6 %all-reduce.25.cloned.1.call-done = (f32[440,440]{1,0:T(8,128)}, f32[256,2048]{1,0:T(8,128)}) async-done(((f32[440,440]{1,0:T(8,128)}, f32[256,2048]{1,0:T(8,128)}), (f32[440,440]{1,0:T(8,128)}, f32[256,2048]{1,0:T(8,128)})) %all-reduce.25.cloned.1.call-update) | async-done | bytes 2871568 | tf_op jit(solution)/shard_map/psum | solution.py:175
  2100.7 73.5 %all-gather.63.cloned.1.call-done = f32[2048,512]{1,0:T(8,128)} async-done(((f32[256,512]{1,0:T(8,128)}), f32[2048,512]{1,0:T(8,128)}) %all-gather.63.cloned.1.call-update) | async-done | bytes 4194320 | tf_op jit(solution)/shard_map/all_gather | solution.py:53
  2187.8 65.7 %all-gather.65.cloned.1.call-done = f32[2048,512]{1,0:T(8,128)} async-done(((f32[256,512]{1,0:T(8,128)}), f32[2048,512]{1,0:T(8,128)}) %all-gather.65.cloned.1.call-update) | async-done | bytes 4194320 | tf_op jit(solution)/shard_map/all_gather | solution.py:53
  2260.7 64.8 %all-reduce.23.cloned.1.call-done = (f32[440,440]{1,0:T(8,128)}, f32[256,2048]{1,0:T(8,128)}) async-done(((f32[440,440]{1,0:T(8,128)}, f32[256,2048]{1,0:T(8,128)}), (f32[440,440]{1,0:T(8,128)}, f32[256,2048]{1,0:T(8,128)})) %all-reduce.23.cloned.1.call-update) | async-done | bytes 2871568 | tf_op jit(solution)/shard_map/psum | solution.py:175
  2332.9 35.3 %copy.31 = f32[1,2048,2326]{1,0,2:T(1,128)} copy(f32[1,2048,2326]{1,2,0:T(8,128)} %get-tuple-element.110) | data formatting | bytes 38109184
  (354 shorter events, 671.2 us)
Async XLA Ops:
  94.0 212.1 %all-gather.35.cloned.1.call-start = ((), (), s32[]{:S(2)}) async-start(), calls=%async_computation.13 | async-start | bytes 10727424 | tf_op jit(solution)/shard_map/all_gather | solution.py:109
  97.0 226.1 %all-gather.43.cloned.1.call-start = ((), (), s32[]{:S(2)}) async-start(), calls=%async_computation.17 | async-start | bytes 1310720 | tf_op jit(solution)/shard_map/all_gather | solution.py:45
  110.7 231.4 %all-gather.39.cloned.1.call-start = ((), (), s32[]{:S(2)}) async-start(), calls=%async_computation.15 | async-start | bytes 1310720 | tf_op jit(solution)/shard_map/all_gather | solution.py:45
  129.4 231.4 %all-gather.33.cloned.1.call-start = ((), (), s32[]{:S(2)}) async-start(), calls=%async_computation.12 | async-start | bytes 1310720 | tf_op jit(solution)/shard_map/all_gather | solution.py:45
  148.2 287.9 %reduce-scatter.19.cloned.1.call-start = ((), (), s32[]{:S(2)}) async-start(), calls=%async_computation.24 | async-start | bytes 2621440 | tf_op jit(solution)/shard_map/reduce_scatter | solution.py:49
  439.5 163.5 %reduce-scatter.13.cloned.1.call-start = ((), (), s32[]{:S(2)}) async-start(), calls=%async_computation.21 | async-start | bytes 2621440 | tf_op jit(solution)/shard_map/reduce_scatter | solution.py:49
  469.6 167.8 %reduce-scatter.17.cloned.1.call-start = ((), (), s32[]{:S(2)}) async-start(), calls=%async_computation.23 | async-start | bytes 2621440 | tf_op jit(solution)/shard_map/reduce_scatter | solution.py:49
  504.2 167.8 %reduce-scatter.25.cloned.1.call-start = ((), (), s32[]{:S(2)}) async-start(), calls=%async_computation.27 | async-start | bytes 2621440 | tf_op jit(solution)/shard_map/reduce_scatter | solution.py:49
  538.8 247.7 %all-reduce.21.cloned.1.call-start = ((), (), s32[]{:S(2)}) async-start(), calls=%async_computation.28 | async-start | bytes 1802240 | tf_op jit(solution)/shard_map/psum | solution.py:153
  676.2 167.6 %reduce-scatter.27.cloned.1.call-start = ((), (), s32[]{:S(2)}) async-start(), calls=%async_computation.29 | async-start | bytes 4718592 | tf_op jit(solution)/shard_map/reduce_scatter | solution.py:150
  683.4 480.0 %reduce-scatter.29.cloned.1.call-start = ((), (), s32[]{:S(2)}) async-start(), calls=%async_computation.30 | async-start | bytes 21454848 | tf_op jit(solution)/shard_map/reduce_scatter | solution.py:151
  744.2 581.7 %all-gather.49.cloned.1.call-start = ((), (), s32[]{:S(2)}) async-start(), calls=%async_computation.31 | async-start | bytes 4718592 | tf_op jit(solution)/shard_map/all_gather | solution.py:53
  1252.2 145.7 %all-reduce.31.cloned.1.call-start = ((), (), s32[]{:S(2)}) async-start(), calls=%async_computation.45 | async-start | bytes 5996544 | tf_op jit(solution)/shard_map/psum | solution.py:175
  1333.0 145.9 %all-gather.51.cloned.1.call-start = ((), (), s32[]{:S(2)}) async-start(), calls=%async_computation.32 | async-start | bytes 4718592 | tf_op jit(solution)/shard_map/all_gather | solution.py:53
  1405.3 152.2 %all-gather.53.cloned.1.call-start = ((), (), s32[]{:S(2)}) async-start(), calls=%async_computation.33 | async-start | bytes 4718592 | tf_op jit(solution)/shard_map/all_gather | solution.py:53
  1485.7 143.8 %all-reduce.29.cloned.1.call-start = ((), (), s32[]{:S(2)}) async-start(), calls=%async_computation.44 | async-start | bytes 5996544 | tf_op jit(solution)/shard_map/psum | solution.py:175
  1564.7 145.7 %all-gather.55.cloned.1.call-start = ((), (), s32[]{:S(2)}) async-start(), calls=%async_computation.34 | async-start | bytes 4718592 | tf_op jit(solution)/shard_map/all_gather | solution.py:53
  1636.9 152.8 %all-gather.57.cloned.1.call-start = ((), (), s32[]{:S(2)}) async-start(), calls=%async_computation.35 | async-start | bytes 4718592 | tf_op jit(solution)/shard_map/all_gather | solution.py:53
  1796.8 145.9 %all-gather.59.cloned.1.call-start = ((), (), s32[]{:S(2)}) async-start(), calls=%async_computation.36 | async-start | bytes 4718592 | tf_op jit(solution)/shard_map/all_gather | solution.py:53
  1869.1 152.2 %all-gather.61.cloned.1.call-start = ((), (), s32[]{:S(2)}) async-start(), calls=%async_computation.37 | async-start | bytes 4718592 | tf_op jit(solution)/shard_map/all_gather | solution.py:53
  1949.5 143.8 %all-reduce.25.cloned.1.call-start = ((), (), s32[]{:S(2)}) async-start(), calls=%async_computation.42 | async-start | bytes 5996544 | tf_op jit(solution)/shard_map/psum | solution.py:175
  2028.5 145.7 %all-gather.63.cloned.1.call-start = ((), (), s32[]{:S(2)}) async-start(), calls=%async_computation.38 | async-start | bytes 4718592 | tf_op jit(solution)/shard_map/all_gather | solution.py:53
  2100.7 152.8 %all-gather.65.cloned.1.call-start = ((), (), s32[]{:S(2)}) async-start(), calls=%async_computation.39 | async-start | bytes 4718592 | tf_op jit(solution)/shard_map/all_gather | solution.py:53
  2260.6 145.7 %all-gather.67.cloned.1.call-start = ((), (), s32[]{:S(2)}) async-start(), calls=%async_computation.40 | async-start | bytes 4718592 | tf_op jit(solution)/shard_map/all_gather | solution.py:53
  (83 other events, 4186.3 us)
Sparse Core Ops, SparseCore 0:
  41.0 49.2 all-gather.30
  166.6 139.3 all-gather.34
  397.5 32.7 reduce-scatter.18
  433.4 31.4 reduce-scatter.10
  502.5 31.4 reduce-scatter.22
  640.5 31.4 reduce-scatter.24
  676.4 76.2 all-reduce.20
  756.7 87.1 reduce-scatter.26
  848.3 315.0 reduce-scatter.28
  1252.3 73.5 all-gather.48
  1333.1 64.6 all-reduce.30
  1405.4 73.3 all-gather.50
  1485.8 71.6 all-gather.52
  1564.8 64.6 all-reduce.28
  1637.0 73.3 all-gather.54
  1718.0 71.6 all-gather.56
  1797.0 64.6 all-reduce.26
  1869.2 73.3 all-gather.58
  1949.6 71.6 all-gather.60
  2028.6 64.6 all-reduce.24
  2100.8 73.3 all-gather.62
  2181.8 71.6 all-gather.64
  2260.8 64.6 all-reduce.22
  2332.9 73.3 all-gather.66
  (12 shorter events, 258.1 us)
where the time goes:
time: 2430 us; the launch traced here: 2420 us
  waiting for transfers between devices  1800 us (74%)
  matrix products  294 us (12%)
  blocking collectives  161 us (7%)
  other arithmetic  85.7 us (4%)
  local copies, waits for them, and re-layouts  50 us (2%)
  between operations  25.1 us (1%)
    all_gather x10, waiting for transfers between devices, collect_rows(): return lax.all_gather(values, 'blk', axis=0, tiled=True)  652 us
    psum x5, waiting for transfers between devices, body(): lax.psum((precise(iter_input, iter_input.T), precise(iter_hidden, rows_hi...  324 us
    reduce_scatter x1, waiting for transfers between devices, body(): lax.psum_scatter(q_output, 'blk', scatter_dimension=0, tiled=True)  317 us
    reduce_scatter x8, waiting for transfers between devices, reduce_cols(): return lax.psum_scatter(values, 'col', scatter_dimension=1, tiled=True)  181 us
    all_gather x1, waiting for transfers between devices, body(): lax.all_gather(w_output.astype(jnp.bfloat16), 'blk', axis=0, tiled=True)  142 us
    dot_general x30, matrix products, precise(): jnp.dot(left_side, right_side, precision=lax.Precision.HIGHEST, preferred...  141 us
    all_gather x8, waiting for transfers between devices, spread_cols(): return lax.all_gather(values, 'col', axis=1, tiled=True)  86.1 us
    dot_general x12, matrix products, inner_rows(): lax.dot_general(left_side, right_side, (((0,), (0,)), ((), ())), preferre...  67.7 us
  transfers between devices with their start and end apart: 36, of which 33 were waited for; matrix products, arithmetic and copies ran while one was open for 11% of the time, Pallas kernels for 0%

commit v1 on v0

--- a/solution.py
+++ b/solution.py
@@ -1,8 +1,11 @@
+import functools
 import math
 
 import jax
 import jax.numpy as jnp
 from jax import lax
+from jax.experimental import pallas as pl
+from jax.experimental.pallas import tpu as pltpu
 from jax.sharding import PartitionSpec as P
 
 NS = 5
@@ -18,6 +21,14 @@
 LR_ADAM = 0.03
 WD_ADAM = 0.1
 
+MESH = pl.DeviceIdType.MESH
+F32 = jnp.float32
+BF16 = jnp.bfloat16
+I16 = jnp.int16
+LN2 = math.log(2.0)
+TOP_CODE = 32700.0
+LEVELS = 64.0
+
 
 def matmul(left_side, right_side):
     return jnp.dot(left_side, right_side, preferred_element_type=jnp.float32)
@@ -67,7 +78,323 @@
     return (weight - LR_ADAM * (update + WD_ADAM * weight), first, second)
 
 
-def body(
+def halves(values):
+    top = values.astype(BF16)
+    return top, (values - top.astype(F32)).astype(BF16)
+
+
+def dot_nn(left_side, right_side):
+    return lax.dot_general(
+        left_side, right_side, (((1,), (0,)), ((), ())), preferred_element_type=F32
+    )
+
+
+def dot_nt(left_side, right_side):
+    return lax.dot_general(
+        left_side, right_side, (((1,), (1,)), ((), ())), preferred_element_type=F32
+    )
+
+
+DIM_BITS = (2, 4, 8)
+ORDERS = ((0, 1, 2), (1, 2, 0), (2, 0, 1))
+PIECE = 48
+
+
+def span_of(dims):
+    slots = [0]
+    for dim in dims:
+        slots = slots + [slot | DIM_BITS[dim] for slot in slots]
+    return slots
+
+
+def stage_sends(stage):
+    moves = []
+    for piece, order in enumerate(ORDERS):
+        for slot in span_of(order[:stage]):
+            moves.append((piece, slot, order[stage]))
+    return sorted(moves, key=lambda move: (move[1] | DIM_BITS[move[2]], move[0]))
+
+
+def muon_kernel(
+    xt_ref,
+    xin_ref,
+    hid_ref,
+    inp_ref,
+    codes,
+    tops,
+    lows,
+    scales,
+    xs,
+    us,
+    vs,
+    lhs,
+    xin,
+    xin_top,
+    xin_low,
+    gram,
+    back,
+    send_sems,
+    core_sems,
+    recv_sems,
+    back_send,
+    back_recv,
+):
+    blk = lax.axis_index("blk")
+    col = lax.axis_index("col")
+    rows, wide = xs.shape
+    other_core = {"col": col + 1 - 2 * (col % 2)}
+    dims = (
+        {"blk": blk + 1 - 2 * (blk % 2)},
+        {"col": (col + 2) % 4},
+        {"blk": blk + 2 - 4 * ((blk // 2) % 2)},
+    )
+    diagonal = {"blk": 4 * (blk // 4) + 3 - blk % 4}
+    barrier = pltpu.get_barrier_semaphore()
+    for target in (other_core, *dims, diagonal):
+        pl.semaphore_signal(barrier, inc=1, device_id=target, device_id_type=MESH)
+
+    xs[...] = xt_ref[...]
+    xin[...] = xin_ref[...]
+    for turn in range(2):
+        codes[turn, 0, rows:, :] = jnp.zeros((codes.shape[2] - rows, wide), I16)
+    eye = lax.broadcasted_iota(jnp.int32, (rows, rows), 0) == lax.broadcasted_iota(
+        jnp.int32, (rows, rows), 1
+    )
+    pl.semaphore_wait(barrier, 5)
+
+    stages = [stage_sends(stage) for stage in range(3)]
+    numbers = {move: number for number, move in enumerate(sum(stages, []))}
+
+    def part(turn, slot, piece):
+        return codes.at[turn, slot, pl.ds(piece * PIECE, PIECE), :]
+
+    def send(turn, move):
+        piece, slot, dim = move
+        return pltpu.make_async_remote_copy(
+            src_ref=part(turn, slot, piece),
+            dst_ref=part(turn, slot | DIM_BITS[dim], piece),
+            send_sem=send_sems.at[numbers[move]],
+            recv_sem=recv_sems.at[turn, slot | DIM_BITS[dim], piece],
+            device_id=dims[dim],
+            device_id_type=MESH,
+        )
+
+    def to_core(turn, slot, piece):
+        return pltpu.make_async_remote_copy(
+            src_ref=part(turn, slot, piece),
+            dst_ref=part(turn, slot + 1, piece),
+            send_sem=core_sems.at[slot // 2, piece],
+            recv_sem=recv_sems.at[turn, slot + 1, piece],
+            device_id=other_core,
+            device_id_type=MESH,
+        )
+
+    def arrived(turn, slot, piece):
+        pltpu.make_async_remote_copy(
+            src_ref=part(turn, slot, piece),
+            dst_ref=part(turn, slot, piece),
+            send_sem=core_sems.at[0, 0],
+            recv_sem=recv_sems.at[turn, slot, piece],
+            device_id=other_core,
+            device_id_type=MESH,
+        ).wait_recv()
+
+    def forward(turn, slot, piece):
+        arrived(turn, slot, piece)
+        to_core(turn, slot, piece).start()
+
+    def landed(stage):
+        return [(slot | DIM_BITS[dim], piece) for piece, slot, dim in stages[stage]]
+
+    def unpack(turn, pair):
+        for core in range(2):
+            whole = codes[turn, 2 * pair + core, 0:rows, :].astype(jnp.int32).astype(F32)
+            top, low = halves(whole)
+            tops[pair, core * rows : (core + 1) * rows, :] = top
+            lows[pair, core * rows : (core + 1) * rows, :] = low
+            step = codes[turn, 2 * pair + core, rows : rows + 16, 0:rows].astype(jnp.int32)
+            size = jnp.exp(step.astype(F32)[0:8, :] * (LN2 / LEVELS)) * (1.0 / TOP_CODE)
+            scales[pair, :, core * rows : (core + 1) * rows] = size * size
+
+    def apply_pair(pair, out):
+        both = dot_nt(lhs[...], tops[pair])
+        inner = both[:rows] + both[rows:] + dot_nt(lhs[0:rows, :], lows[pair])
+        inner = inner * scales[pair, 0:1, :]
+        top, low = halves(inner)
+        stack = jnp.concatenate([top, low], axis=0)
+        cut = 512
+        for start in range(0, wide, cut):
+            lanes = slice(start, start + cut)
+            both = dot_nn(stack, tops[pair, :, lanes])
+            out[:, lanes] += both[:rows] + both[rows:] + dot_nn(top, lows[pair, :, lanes])
+
+    def set_lhs(values):
+        top, low = halves(values)
+        lhs[0:rows, :] = top
+        lhs[rows:, :] = low
+
+    def input_gram():
+        top, low = halves(xin[...])
+        xin_top[...] = top
+        xin_low[...] = low
+        gram[...] = (
+            dot_nt(xin_top[...], xin_top[...])
+            + dot_nt(xin_low[...], xin_top[...])
+            + dot_nt(xin_top[...], xin_low[...])
+        )
+
+    def input_step():
+        size = gram.shape[0]
+        top, low = halves(gram[...])
+        square = dot_nn(top, top) + dot_nn(low, top) + dot_nn(top, low)
+        same = lax.broadcasted_iota(jnp.int32, (size, size), 0) == lax.broadcasted_iota(
+            jnp.int32, (size, size), 1
+        )
+        poly = NS_B * gram[...] + NS_C * square + jnp.where(same, NS_A, 0.0)
+        top, low = halves(poly)
+        cut = 512
+        for start in range(0, wide, cut):
+            lanes = slice(start, start + cut)
+            xin[:, lanes] = (
+                dot_nn(top, xin_top[:, lanes])
+                + dot_nn(low, xin_top[:, lanes])
+                + dot_nn(top, xin_low[:, lanes])
+            )
+
+    def iteration(number, carry):
+        turn = number % 2
+        values = xs[...]
+        largest = jnp.maximum(jnp.max(jnp.abs(values), axis=1, keepdims=True), 1e-30)
+        step = jnp.ceil(jnp.log(largest) * (LEVELS / LN2))
+        codes[turn, 0, 0:rows, :] = (
+            jnp.round(values * (TOP_CODE / jnp.exp(step * (LN2 / LEVELS))))
+            .astype(jnp.int32)
+            .astype(I16)
+        )
+        lane_step = jnp.sum(jnp.where(eye, step, 0.0), axis=0, keepdims=True)
+        codes[turn, 0, rows : rows + 16, 0:rows] = jnp.broadcast_to(
+            lane_step.astype(jnp.int32), (16, rows)
+        ).astype(I16)
+        for move in stages[0]:
+            send(turn, move).start()
+        for piece in range(3):
+            to_core(turn, 0, piece).start()
+        set_lhs(values)
+        us[...] = jnp.zeros_like(us)
+        vs[...] = jnp.zeros_like(vs)
+
+        def first_pass(pair, carry):
+            @pl.when(pair == 1)
+            def _():
+                for slot, piece in landed(0):
+                    forward(turn, slot, piece)
+                for move in stages[1]:
+                    send(turn, move).start()
+                input_gram()
+                for slot, piece in landed(1):
+                    forward(turn, slot, piece)
+                for move in stages[2]:
+                    send(turn, move).start()
+                input_step()
+
+            for slot_pair in range(1, 8):
+                mine = [(slot, piece) for slot, piece in landed(2) if slot == 2 * slot_pair]
+
+                @pl.when(pair == max(slot_pair - 1, 1))
+                def _(mine=mine):
+                    for slot, piece in mine:
+                        forward(turn, slot, piece)
+
+            for piece in range(3):
+                arrived(turn, 2 * pair + 1, piece)
+            unpack(turn, pair)
+            apply_pair(pair, us)
+            return carry
+
+        lax.fori_loop(0, 8, first_pass, 0)
+        set_lhs(us[...])
+
+        def second_pass(pair, carry):
+            apply_pair(pair, vs)
+            return carry
+
+        lax.fori_loop(0, 8, second_pass, 0)
+        xs[...] = NS_A * xs[...] + NS_B * us[...] + NS_C * vs[...]
+        for stage in stages:
+            for move in stage:
+                send(turn, move).wait_send()
+        for pair in range(8):
+            for piece in range(3):
+                to_core(turn, 2 * pair, piece).wait_send()
+        return carry
+
+    lax.fori_loop(0, NS, iteration, 0)
+
+    place = blk % 4
+    height = back.shape[2]
+    copies = []
+    for rel, target in ((1, dims[0]), (2, dims[2]), (3, diagonal)):
+        copies.append(
+            pltpu.make_async_remote_copy(
+                src_ref=xs.at[:, pl.ds(pl.multiple_of(target["blk"] * height, height), height)],
+                dst_ref=back.at[place],
+                send_sem=back_send.at[rel - 1],
+                recv_sem=back_recv.at[rel - 1],
+                device_id=target,
+                device_id_type=MESH,
+            )
+        )
+        copies[-1].start()
+    hid_ref[place] = xs[:, pl.ds(pl.multiple_of(blk * height, height), height)]
+    part_wide = inp_ref.shape[1]
+    inp_ref[...] = xin[:, pl.ds(pl.multiple_of(col * part_wide, part_wide), part_wide)]
+    for copy in copies:
+        copy.wait_recv()
+    for target in (dims[0], dims[2], diagonal):
+        other = target["blk"] % 4
+        hid_ref[other] = back[other]
+    for copy in copies:
+        copy.wait_send()
+
+
+def muon(xt, xin, height, part_wide):
+    rows, wide = xt.shape
+    deep = xin.shape[0]
+    return pl.pallas_call(
+        muon_kernel,
+        out_shape=(
+            jax.ShapeDtypeStruct((4, rows, height), F32),
+            jax.ShapeDtypeStruct((deep, part_wide), F32),
+        ),
+        in_specs=[pl.BlockSpec(memory_space=pltpu.VMEM)] * 2,
+        out_specs=(pl.BlockSpec(memory_space=pltpu.VMEM), pl.BlockSpec(memory_space=pltpu.VMEM)),
+        scratch_shapes=[
+            pltpu.VMEM((2, 16, 3 * PIECE, wide), I16),
+            pltpu.VMEM((8, 2 * rows, wide), BF16),
+            pltpu.VMEM((8, 2 * rows, wide), BF16),
+            pltpu.VMEM((8, 8, 2 * rows), F32),
+            pltpu.VMEM((rows, wide), F32),
+            pltpu.VMEM((rows, wide), F32),
+            pltpu.VMEM((rows, wide), F32),
+            pltpu.VMEM((2 * rows, wide), BF16),
+            pltpu.VMEM((deep, wide), F32),
+            pltpu.VMEM((deep, wide), BF16),
+            pltpu.VMEM((deep, wide), BF16),
+            pltpu.VMEM((deep, deep), F32),
+            pltpu.VMEM((4, rows, height), F32),
+            pltpu.SemaphoreType.DMA((21,)),
+            pltpu.SemaphoreType.DMA((8, 3)),
+            pltpu.SemaphoreType.DMA((2, 16, 3)),
+            pltpu.SemaphoreType.DMA((3,)),
+            pltpu.SemaphoreType.DMA((3,)),
+        ],
+        compiler_params=pltpu.CompilerParams(
+            collective_id=0, has_side_effects=True, vmem_limit_bytes=60 * 1024 * 1024
+        ),
+    )(xt, xin)
+
+
+def plain_body(
     frames,
     labels,
     mask,
@@ -213,6 +540,137 @@
     )
 
 
+def fast_body(
+    frames,
+    labels,
+    mask,
+    w_input,
+    w_hidden,
+    w_output,
+    biases,
+    mom_input,
+    mom_hidden,
+    out_first,
+    out_second,
+    bias_first,
+    bias_second,
+    res_input,
+    res_hidden,
+    res_output,
+):
+    ncol = lax.axis_size("col")
+    nblk = lax.axis_size("blk")
+    col_index = lax.axis_index("col")
+    blk_index = lax.axis_index("blk")
+    hcol = w_input.shape[1]
+    scol = w_output.shape[1]
+    micro = frames.shape[0]
+    slot_count = frames.shape[1] * micro * nblk * ncol
+    bias_row = biases[0]
+    b_one = bias_row[:hcol]
+    b_two = bias_row[hcol : 2 * hcol]
+    b_out = bias_row[2 * hcol :]
+    low_input = w_input.astype(jnp.bfloat16)
+    own_tags = jnp.where(mask > 0, labels, -1).reshape(-1)
+    own_inputs = frames.reshape(-1, frames.shape[2])
+    inputs = lax.all_gather(own_inputs, "col", axis=0, tiled=True)
+    tags_group = lax.all_gather(own_tags, "col", axis=0, tiled=True)
+    low_hidden = collect_rows(w_hidden.astype(jnp.bfloat16))
+    low_output = collect_rows(w_output.astype(jnp.bfloat16))
+    sig_one = jax.nn.sigmoid(matmul(inputs, low_input) + b_one)
+    h_one = spread_cols(sig_one.astype(jnp.bfloat16))
+    sig_two = jax.nn.sigmoid(matmul(h_one, low_hidden) + b_two)
+    h_two = spread_cols(sig_two.astype(jnp.bfloat16))
+    logits = matmul(h_two, low_output) + b_out
+    row_top = lax.pmax(jnp.max(logits, axis=1), "col")
+    exponent = jnp.exp(logits - row_top[:, None])
+    target_hit = jnp.arange(scol)[None, :] == (tags_group - col_index * scol)[:, None]
+    row_total, picked = lax.psum(
+        (jnp.sum(exponent, axis=1), jnp.sum(jnp.where(target_hit, logits, 0.0), axis=1)), "col"
+    )
+    live_rows = tags_group >= 0
+    loss_local = jnp.sum(jnp.where(live_rows, row_top + jnp.log(row_total) - picked, 0.0))
+    probs = exponent / row_total[:, None]
+    d_logits = (
+        jnp.where(live_rows[:, None], probs - target_hit.astype(jnp.float32), 0.0) / slot_count
+    ).astype(jnp.bfloat16)
+    grad_output = inner_rows(h_two, d_logits)
+    d_h_two = reduce_cols(outer_cols(d_logits, low_output))
+    d_z_two = (d_h_two * sig_two * (1.0 - sig_two)).astype(jnp.bfloat16)
+    grad_hidden = inner_rows(h_one, d_z_two)
+    d_h_one = reduce_cols(outer_cols(d_z_two, low_hidden))
+    d_z_one = (d_h_one * sig_one * (1.0 - sig_one)).astype(jnp.bfloat16)
+    grad_input = inner_rows(inputs, d_z_one)
+    grad_bias = jnp.concatenate(
+        [
+            jnp.sum(d_z_one.astype(jnp.float32), axis=0),
+            jnp.sum(d_z_two.astype(jnp.float32), axis=0),
+            jnp.sum(d_logits.astype(jnp.float32), axis=0),
+        ]
+    )
+    q_input, next_res_input = squash(grad_input, res_input[0])
+    q_hidden, next_res_hidden = squash(grad_hidden, res_hidden[0])
+    q_output, next_res_output = squash(grad_output, res_output[0])
+    red_hidden, red_output = (
+        lax.psum_scatter(q_hidden, "blk", scatter_dimension=0, tiled=True),
+        lax.psum_scatter(q_output, "blk", scatter_dimension=0, tiled=True),
+    )
+    red_input, red_bias, loss_sum = lax.psum((q_input, grad_bias, loss_local), "blk")
+    share_blk = 1.0 / nblk
+    grad_square = (
+        share_blk * (jnp.sum(red_input * red_input) + jnp.sum(red_bias * red_bias))
+        + jnp.sum(red_hidden * red_hidden)
+        + jnp.sum(red_output * red_output)
+    )
+    clip_norm = jnp.sqrt(lax.psum(grad_square, ("blk", "col")))
+    factor = jnp.minimum(1.0, CLIP / clip_norm)
+    next_mom_input = 0.5 * mom_input + factor * red_input
+    next_mom_hidden = 0.5 * mom_hidden + factor * red_hidden
+    square_input, square_hidden = lax.psum(
+        (
+            share_blk * jnp.sum(next_mom_input * next_mom_input),
+            jnp.sum(next_mom_hidden * next_mom_hidden),
+        ),
+        ("blk", "col"),
+    )
+    iter_input = next_mom_input / (jnp.sqrt(square_input) + 1e-07)
+    iter_hidden = next_mom_hidden / (jnp.sqrt(square_hidden) + 1e-07)
+    tall = collect_rows(iter_hidden)
+    piece = hcol // 4
+    mine = lax.dynamic_slice_in_dim(tall, (blk_index % 4) * piece, piece, axis=1).T
+    deep = w_input.shape[0]
+    padded = 512
+    whole_input = spread_cols(jnp.pad(iter_input, ((0, padded - deep), (0, 0))))
+    done_hidden, done_input = muon(mine, whole_input, w_hidden.shape[0], hcol)
+    done_hidden = done_hidden.reshape(hcol, w_hidden.shape[0]).T
+    muon_scale = LR_MUON * 0.2 * math.sqrt(hcol * ncol)
+    new_input = w_input * (1.0 - LR_MUON * WD_MUON) - muon_scale * done_input[:deep]
+    new_hidden = w_hidden * (1.0 - LR_MUON * WD_MUON) - muon_scale * done_hidden
+    new_output, next_out_first, next_out_second = adam_step(
+        w_output, factor * red_output, out_first, out_second
+    )
+    new_biases, next_bias_first, next_bias_second = adam_step(
+        biases, factor * red_bias[None, :], bias_first, bias_second
+    )
+    return (
+        loss_sum,
+        clip_norm,
+        new_input,
+        new_hidden,
+        new_output,
+        new_biases,
+        next_mom_input,
+        next_mom_hidden,
+        next_out_first,
+        next_out_second,
+        next_bias_first,
+        next_bias_second,
+        next_res_input[None],
+        next_res_hidden[None],
+        next_res_output[None],
+    )
+
+
 def solution(mesh):
     in_specs = (
         P(None, ("blk", "col"), None),
@@ -249,4 +707,6 @@
         P("blk", None, "col"),
         P("blk", None, "col"),
     )
+    cubes = mesh.shape["blk"] == 8 and mesh.shape["col"] == 4
+    body = fast_body if cubes else plain_body
     return jax.shard_map(body, mesh=mesh, in_specs=in_specs, out_specs=out_specs, check_vma=False)

time: 2430 us -> 1510 us (0.62)
  waiting for transfers between devices: 1800 us -> 824 us
  Pallas kernels: 0 us -> 304 us
  matrix products: 294 us -> 76.3 us
    all_gather x10 -> x3, waiting for transfers between devices: 652 us -> 201 us  [collect_rows(): return lax.all_gather(values, 'blk', axis=0, tiled=True)]
    pallas_call x0 -> x1, Pallas kernels: none -> 304 us  [muon(): pl.pallas_call(muon_kernel, out_shape=(jax.ShapeDtypeStruct((4, rows, hei...]
    psum x6 -> x1, waiting for transfers between devices: 324 us -> 41.2 us  [fast_body(): lax.psum((q_input, grad_bias, loss_local), 'blk')]
    all_gather x2 -> x0, waiting for transfers between devices: 187 us -> none  [the longest x1 142 us: body(): lax.all_gather(w_output.astype(jnp.bfloat16), 'blk', axis=0, tiled=True)]
    dot_general x30 -> x0, matrix products: 141 us -> none  [precise(): jnp.dot(left_side, right_side, precision=lax.Precision.HIGHEST, preferred...]
    reduce_scatter x8 -> x2, waiting for transfers between devices: 181 us -> 106 us  [reduce_cols(): return lax.psum_scatter(values, 'col', scatter_dimension=1, tiled=True)]
    dot_general x12 -> x3, matrix products: 67.7 us -> 26.7 us  [inner_rows(): lax.dot_general(left_side, right_side, (((0,), (0,)), ((), ())), preferre...]
    all_gather x8 -> x3, waiting for transfers between devices: 86.1 us -> 95.3 us  [spread_cols(): return lax.all_gather(values, 'col', axis=1, tiled=True)]
  transfers between devices with their start and end apart: 36 -> 11, of which waited for: 33 -> 11; matrix products, arithmetic and copies ran while one was open for 11% -> 8% of each run, Pallas kernels for 0% -> 0%
where the time goes in v1:
time: 1510 us; the launch traced here: 1500 us
  waiting for transfers between devices  824 us (55%)
  Pallas kernels  304 us (20%)
  blocking collectives  146 us (10%)
  other arithmetic  77.3 us (5%)
  matrix products  76.3 us (5%)
  local copies, waits for them, and re-layouts  54 us (4%)
  between operations  21.1 us (1%)
    reduce_scatter x1, waiting for transfers between devices, fast_body(): lax.psum_scatter(q_output, 'blk', scatter_dimension=0, tiled=True)  315 us
    pallas_call x1, Pallas kernels, muon(): pl.pallas_call(muon_kernel, out_shape=(jax.ShapeDtypeStruct((4, rows, hei...  304 us
    all_gather x3, waiting for transfers between devices, collect_rows(): return lax.all_gather(values, 'blk', axis=0, tiled=True)  201 us
    reduce_scatter x2, waiting for transfers between devices, reduce_cols(): return lax.psum_scatter(values, 'col', scatter_dimension=1, tiled=True)  106 us
    all_gather x3, waiting for transfers between devices, spread_cols(): return lax.all_gather(values, 'col', axis=1, tiled=True)  95.3 us
    reduce_scatter x1, waiting for transfers between devices, fast_body(): lax.psum_scatter(q_hidden, 'blk', scatter_dimension=0, tiled=True)  65.9 us
    unnamed x34, local copies, waits for them, and re-layouts  49.6 us
    psum x1, waiting for transfers between devices, fast_body(): lax.psum((q_input, grad_bias, loss_local), 'blk')  41.2 us
  transfers between devices with their start and end apart: 11, of which 11 were waited for; matrix products, arithmetic and copies ran while one was open for 8% of the time, Pallas kernels for 0%

profile of v1, /device:TPU:0, one launch (start us, length us, event | category | flops | bytes accessed | tf_op | source)
XLA Modules:
  0.0 1503.5 jit_solution(16042174369950914050)
XLA Ops:
  9.8 11.7 all_gather.25
  25.8 37.0 %all-gather.10.cloned.1.call-done = bf16[2048,512]{1,0:T(8,128)(2,1)} async-done(((bf16[256,512]{1,0:T(8,128)(2,1)}), bf16[2048,512]{1,0:T(8,128)(2,1)}) %all-gather.10.cloned.1.call-update) | async-done | bytes 2097168 | tf_op jit(solution)/shard_map/all_gather | solution.py:64
  62.7 35.1 %all-gather.8.cloned.1.call-done = bf16[1024,2048]{1,0:T(8,128)(2,1)} async-done(((bf16[1024,512]{1,0:T(8,128)(2,1)}), bf16[1024,2048]{1,0:T(8,128)(2,1)}) %all-gather.8.cloned.1.call-update) | async-done | bytes 4194320 | tf_op jit(solution)/shard_map/all_gather | solution.py:56
  97.9 7.3 fusion.7
  111.7 28.1 %all-gather.12.cloned.1.call-done = bf16[1024,2048]{1,0:T(8,128)(2,1)} async-done(((bf16[1024,512]{1,0:T(8,128)(2,1)}), bf16[1024,2048]{1,0:T(8,128)(2,1)}) %all-gather.12.cloned.1.call-update) | async-done | bytes 4194320 | tf_op jit(solution)/shard_map/all_gather | solution.py:56
  139.8 141.9 %all-gather.14.cloned.1.call-done = bf16[2048,2326]{0,1:T(8,128)(2,1)} async-done(((bf16[256,2326]{0,1:T(8,128)(2,1)}), bf16[2048,2326]{0,1:T(8,128)(2,1)}) %all-gather.14.cloned.1.call-update) | async-done | bytes 9527312 | tf_op jit(solution)/shard_map/all_gather | solution.py:64
  281.7 16.3 %add_reduce_fusion = (f32[1024]{0:T(1024)S(1)}, f32[1024,2326]{0,1:T(8,128)}) fusion(f32[2326]{0:T(1024)S(1)} %slice_reduce_fusion, bf16[1024,2048]{1,0:T(8,128)(2,1)} %all-gather.12.cloned.1.call-done, bf16[2048,2326]{0,1:T(8,128)(2,1)} %all-gather.14.cloned.1.call-done), kind=kOutput, calls=%fused_computation.10 | convolution fusion | flops 9760713728 | bytes 23262296 | tf_op jit(solution)/shard_map/dot_general | solution.py:34
  316.7 7.0 convert_reduce_fusion
  325.9 16.0 %fusion.8 = f32[1024,2048]{1,0:T(8,128)} fusion(bf16[1024,2326]{0,1:T(8,128)(2,1)S(1)} %get-tuple-element.87, bf16[2048,2326]{0,1:T(8,128)(2,1)} %all-gather.14.cloned.1.call-done), kind=kOutput, calls=%fused_computation.64 | convolution fusion | flops 9755951104 | bytes 22679552 | tf_op jit(solution)/shard_map/dot_general | solution.py:44
  342.0 69.6 %reduce-scatter.5.cloned.1.call-done = f32[1024,512]{1,0:T(8,128)} async-done(((f32[1024,2048]{1,0:T(8,128)}), f32[1024,512]{1,0:T(8,128)}) %reduce-scatter.5.cloned.1.call-update) | async-done | bytes 2097168 | tf_op jit(solution)/shard_map/reduce_scatter | solution.py:60
  436.4 19.4 %abs_reduce_fusion = (f32[2326]{0:T(1024)S(1)}, f32[2048,2326]{0,1:T(8,128)}) fusion(bf16[1,2048,2326]{1,2,0:T(8,128)(2,1)} %param.31, bf16[1024,2048]{1,0:T(8,128)(2,1)} %all-gather.12.cloned.1.call-done, bf16[1024,2326]{0,1:T(8,128)(2,1)} %copy-done.1), kind=kOutput, calls=%fused_computation.3 | convolution fusion | flops 9775003648 | bytes 37549144 | tf_op jit(solution)/shard_map/dot_general | solution.py:38
  455.8 36.4 %reduce-scatter.7.cloned.1.call-done = f32[1024,512]{1,0:T(8,128)} async-done(((f32[1024,2048]{1,0:T(8,128)}), f32[1024,512]{1,0:T(8,128)}) %reduce-scatter.7.cloned.1.call-update) | async-done | bytes 2097168 | tf_op jit(solution)/shard_map/reduce_scatter | solution.py:60
  497.6 20.7 %subtract_bitcast_fusion = (f32[1,2048,2326]{1,2,0:T(8,128)}, f32[2048,2326]{0,1:T(8,128)}) fusion(f32[2048,2326]{0,1:T(8,128)} %get-tuple-element.109, f32[2326]{0:T(1024)S(1)} %multiply_add_fusion.3), kind=kLoop, calls=%fused_computation.1 | loop fusion | flops 19054592 | bytes 57173080 | tf_op jit(solution)/shard_map/broadcast_in_dim | solution.py:670
  519.0 65.9 %reduce-scatter.9.cloned.1.call-done = f32[256,512]{0,1:T(8,128)} async-done(((f32[2048,512]{0,1:T(8,128)}), f32[256,512]{0,1:T(8,128)}) %reduce-scatter.9.cloned.1.call-update) | async-done | bytes 524304 | tf_op jit(solution)/shard_map/reduce_scatter | solution.py:615
  586.7 37.3 %all-reduce.2 = (f32[]{:T(128)}, f32[3350]{0:T(1024)S(1)}) all-reduce(f32[]{:T(128)} %select_reduce_fusion.1, f32[3350]{0:T(1024)S(1)} %pad_maximum_fusion), channel_id=1, replica_groups=mesh['blk'=8,'col'=4] {'blk'}, use_global_device_ids=true, to_apply=%region_7.8 | all-reduce | flops 3351 | bytes 26808 | tf_op jit(solution)/shard_map/psum | solution.py:618
  624.6 41.2 %all-reduce.6.cloned.1.call-done = f32[440,512]{1,0:T(8,128)} async-done(((f32[440,512]{1,0:T(8,128)}), f32[440,512]{1,0:T(8,128)}) %all-reduce.6.cloned.1.call-update) | async-done | bytes 901136 | tf_op jit(solution)/shard_map/psum | solution.py:618
  669.8 314.6 %reduce-scatter.11.cloned.1.call-done = f32[256,2326]{0,1:T(8,128)} async-done(((f32[2048,2326]{0,1:T(8,128)}), f32[256,2326]{0,1:T(8,128)}) %reduce-scatter.11.cloned.1.call-update) | async-done | bytes 2381840 | tf_op jit(solution)/shard_map/reduce_scatter | solution.py:616
  990.0 39.3 %psum.61 = f32[]{:T(128)} all-reduce(f32[]{:T(128)S(6)} %add.182), channel_id=1, replica_groups=mesh['blk'=8,'col'=4] {'blk','col'}, use_global_device_ids=true, to_apply=%region_24.25 | all-reduce | flops 1 | bytes 8 | tf_op jit(solution)/shard_map/psum | solution.py:625
  1035.5 40.2 %all-reduce.1 = (f32[]{:T(128)}, f32[]{:T(128)}) all-reduce(f32[]{:T(128)} %get-tuple-element.80, f32[]{:T(128)S(6)} %mul.254), channel_id=1, replica_groups=mesh['blk'=8,'col'=4] {'blk','col'}, use_global_device_ids=true, to_apply=%region_26.27 | all-reduce | flops 2 | bytes 16 | tf_op jit(solution)/shard_map/psum | solution.py:629
  1080.5 34.9 %copy.52 = f32[1,2048,2326]{1,0,2:T(1,128)} copy(f32[1,2048,2326]{1,2,0:T(8,128)} %get-tuple-element.88) | data formatting | bytes 38109184
  1122.5 8.4 multiply_subtract_fusion
  1131.0 21.7 %all-gather.16.cloned.1.call-done = f32[2048,512]{0,1:T(8,128)} async-done(((f32[256,512]{0,1:T(8,128)}), f32[2048,512]{0,1:T(8,128)}) %all-gather.16.cloned.1.call-update) | async-done | bytes 4194320 | tf_op jit(solution)/shard_map/all_gather | solution.py:64
  1155.0 32.0 %all-gather.18.cloned.1.call-done.xin_ref = f32[512,2048]{1,0:T(8,128)} async-done(((f32[512,512]{1,0:T(8,128)}), f32[512,2048]{1,0:T(8,128)}) %all-gather.18.cloned.1.call-update) | async-done | bytes 4194320 | tf_op jit(solution)/shard_map/all_gather | solution.py:56
  1187.0 303.9 %shard_map.271 = (f32[4,128,256]{2,1,0:T(8,128)}, f32[512,512]{1,0:T(8,128)}) custom-call(f32[128,2048]{1,0:T(8,128)} %dynamic-slice_bitcast_fusion.xt_ref, f32[512,2048]{1,0:T(8,128)} %all-gather.18.cloned.1.call-done.xin_ref), custom_call_target="tpu_custom_call" | custom-call | tf_op jit(solution)/shard_map/pallas_call | solution.py:363
  (96 shorter events, 96.4 us)
Async XLA Ops:
  7.2 55.6 %all-gather.10.cloned.1.call-start = ((), (), s32[]{:S(2)}) async-start(), calls=%async_computation.5 | async-start | bytes 2359296 | tf_op jit(solution)/shard_map/all_gather | solution.py:64
  9.0 88.8 %all-gather.8.cloned.1.call-start = ((), (), s32[]{:S(2)}) async-start(), calls=%async_computation.4 | async-start | bytes 5242880 | tf_op jit(solution)/shard_map/all_gather | solution.py:56
  21.5 4.2 copy-start.4
  25.7 114.1 %all-gather.12.cloned.1.call-start = ((), (), s32[]{:S(2)}) async-start(), calls=%async_computation.6 | async-start | bytes 5242880 | tf_op jit(solution)/shard_map/all_gather | solution.py:56
  97.9 7.4 copy-start
  105.2 1.3 copy-start.11
  105.2 6.5 copy-start.7
  105.2 176.5 %all-gather.14.cloned.1.call-start = ((), (), s32[]{:S(2)}) async-start(), calls=%async_computation.7 | async-start | bytes 10727424 | tf_op jit(solution)/shard_map/all_gather | solution.py:64
  106.4 305.2 %reduce-scatter.5.cloned.1.call-start = ((), (), s32[]{:S(2)}) async-start(), calls=%async_computation.8 | async-start | bytes 10485760 | tf_op jit(solution)/shard_map/reduce_scatter | solution.py:60
  323.7 2.2 copy-start.1
  342.0 150.3 %reduce-scatter.7.cloned.1.call-start = ((), (), s32[]{:S(2)}) async-start(), calls=%async_computation.9 | async-start | bytes 10485760 | tf_op jit(solution)/shard_map/reduce_scatter | solution.py:60
  411.6 3.0 copy-start.12
  420.4 164.6 %reduce-scatter.9.cloned.1.call-start = ((), (), s32[]{:S(2)}) async-start(), calls=%async_computation.11 | async-start | bytes 4718592 | tf_op jit(solution)/shard_map/reduce_scatter | solution.py:615
  436.3 229.4 %all-reduce.6.cloned.1.call-start = ((), (), s32[]{:S(2)}) async-start(), calls=%async_computation.10 | async-start | bytes 1802240 | tf_op jit(solution)/shard_map/psum | solution.py:618
  455.8 39.3 %copy-start.5 = (bf16[1024,440]{1,0:T(8,128)(2,1)S(1)}, bf16[1024,440]{1,0:T(8,128)(2,1)}, u32[]{:S(2)}) copy-start(bf16[1024,440]{1,0:T(8,128)(2,1)} %copy-done.4) | copy-start | bytes 2703364
  492.2 2.9 copy-start.13
  497.3 487.1 %reduce-scatter.11.cloned.1.call-start = ((), (), s32[]{:S(2)}) async-start(), calls=%async_computation.12 | async-start | bytes 21454848 | tf_op jit(solution)/shard_map/reduce_scatter | solution.py:616
  518.3 634.3 %all-gather.16.cloned.1.call-start = ((), (), s32[]{:S(2)}) async-start(), calls=%async_computation.13 | async-start | bytes 4718592 | tf_op jit(solution)/shard_map/all_gather | solution.py:64
  665.8 364.3 %copy-start.2 = (f32[440,512]{1,0:T(8,128)S(1)}, f32[440,512]{1,0:T(8,128)}, u32[]{:S(2)}) copy-start(f32[440,512]{1,0:T(8,128)} %all-reduce.6.cloned.1.call-done) | copy-start | bytes 2703364
  1077.3 109.7 %all-gather.18.cloned.1.call-start = ((), (), s32[]{:S(2)}) async-start(), calls=%async_computation.14 | async-start | bytes 5242880 | tf_op jit(solution)/shard_map/all_gather | solution.py:56
  1115.4 6.4 copy-start.8
  1115.4 6.4 copy-start.9
  1131.0 359.9 %copy-start.6 = (f32[440,512]{1,0:T(8,128)S(1)}, f32[440,512]{1,0:T(8,128)}, u32[]{:S(2)}) copy-start(f32[440,512]{1,0:T(8,128)} %param.19) | copy-start | bytes 2703364
  1155.0 339.5 %copy-start.3 = (f32[256,512]{1,0:T(8,128)S(1)}, f32[256,512]{1,0:T(8,128)}, u32[]{:S(2)}) copy-start(f32[256,512]{1,0:T(8,128)} %param.20) | copy-start | bytes 1572868
  (1 other events, 1.3 us)
Sparse Core Ops, SparseCore 0:
  10.7 51.9 all-gather.9
  64.9 32.9 all-gather.7
  105.3 34.4 all-gather.11
  142.3 139.3 all-gather.13
  342.1 69.4 reduce-scatter.4
  420.5 71.6 reduce-scatter.6
  496.4 88.4 reduce-scatter.8
  589.4 76.3 all-reduce.5
  670.2 314.2 reduce-scatter.10
  1077.4 75.1 all-gather.15
  1154.3 32.6 all-gather.17

commit v2 on v1

--- a/solution.py
+++ b/solution.py
@@ -392,6 +392,540 @@
             collective_id=0, has_side_effects=True, vmem_limit_bytes=60 * 1024 * 1024
         ),
     )(xt, xin)
+
+
+RING = 8
+STEPS = RING - 1
+OUT_ROWS = 592
+OUT_GROUPS = 4
+BLOCKS = (304, 288)
+HID_ROWS = 512
+SCALE_ROWS = 16
+
+
+def ring_place(blk):
+    odd = blk % 2
+    return (blk // 2) * (1 - odd) + (7 - blk // 2) * odd
+
+
+def ring_blk(place):
+    back = place // 4
+    return 2 * place * (1 - back) + (15 - 2 * place) * back
+
+
+def scale_code(size):
+    return jnp.ceil(jnp.log(jnp.maximum(size, 1e-30)) * (LEVELS / LN2))
+
+
+def code_scale(code):
+    return jnp.exp(code * (LN2 / LEVELS))
+
+
+def to_codes(values):
+    return jnp.round(values).astype(jnp.int32).astype(I16)
+
+
+def from_codes(codes):
+    return codes.astype(jnp.int32).astype(F32)
+
+
+def reduce_kernel(
+    deep,
+    dl_ref,
+    h_two_ref,
+    res_out_ref,
+    dz_two_ref,
+    h_one_ref,
+    res_hid_ref,
+    dz_one_ref,
+    x_ref,
+    res_in_ref,
+    vec_ref,
+    next_out_ref,
+    next_hid_ref,
+    next_in_ref,
+    red_out_ref,
+    red_hid_ref,
+    red_in_ref,
+    vec_sum_ref,
+    stats_ref,
+    grad,
+    stage,
+    res_buf,
+    marks,
+    own_out,
+    got_out,
+    size_out,
+    own_hid,
+    got_hid,
+    size_hid,
+    own_in,
+    got_in,
+    size_in,
+    share_in,
+    vecs,
+    res_sems,
+    stage_sems,
+    out_send,
+    out_recv,
+    hid_send,
+    hid_recv,
+    in_send,
+    in_recv,
+    share_send,
+    share_recv,
+    vec_send,
+    vec_recv,
+):
+    blk = lax.axis_index("blk")
+    here = ring_place(blk)
+    total_rows = next_out_ref.shape[0]
+    barrier = pltpu.get_barrier_semaphore()
+    for away in range(1, RING):
+        pl.semaphore_signal(
+            barrier, inc=1, device_id={"blk": (blk + away) % RING}, device_id_type=MESH
+        )
+
+    starts = [sum(BLOCKS[:part]) for part in range(len(BLOCKS))]
+
+    def res_copy(group, part):
+        rows = BLOCKS[part]
+        return pltpu.make_async_copy(
+            res_out_ref.at[pl.ds(group * OUT_ROWS + starts[part], rows), :],
+            res_buf.at[part, pl.ds(0, rows), :],
+            res_sems.at[part],
+        )
+
+    def stage_copy(group, part, rows):
+        return pltpu.make_async_copy(
+            stage.at[pl.ds(0, rows)],
+            next_out_ref.at[pl.ds(group * OUT_ROWS + starts[part], rows)],
+            stage_sems.at[0],
+        )
+
+    last_rows = total_rows - (OUT_GROUPS - 1) * OUT_ROWS - starts[-1]
+
+    def stage_start(group, part):
+        if part < len(BLOCKS) - 1:
+            stage_copy(group, part, BLOCKS[part]).start()
+        else:
+
+            @pl.when(group < OUT_GROUPS - 1)
+            def _():
+                stage_copy(group, part, BLOCKS[part]).start()
+
+            @pl.when(group == OUT_GROUPS - 1)
+            def _():
+                stage_copy(group, part, last_rows).start()
+
+    res_copy(0, 0).start()
+    res_copy(0, 1).start()
+    marks[...] = jnp.zeros_like(marks)
+    stats_ref[...] = jnp.zeros_like(stats_ref)
+    pl.semaphore_wait(barrier, RING - 1)
+
+    vec_copies = []
+    for away in range(1, RING):
+        copy = pltpu.make_async_remote_copy(
+            src_ref=vec_ref,
+            dst_ref=vecs.at[blk],
+            send_sem=vec_send.at[away - 1],
+            recv_sem=vec_recv.at[away - 1],
+            device_id={"blk": (blk + away) % RING},
+            device_id_type=MESH,
+        )
+        copy.start()
+        vec_copies.append(copy)
+
+    def row_scale(value, count):
+        size = jnp.sum(jnp.abs(value), axis=1, keepdims=True) * (1.0 / count) + 1e-12
+        code = scale_code(size)
+        return size, code, size * (TOP_CODE / code_scale(code))
+
+    def lane_codes(first):
+        return jnp.transpose(marks[first : first + 128, :])[0:1, :]
+
+    def set_sizes(rows, own, sizes):
+        parts = [lane_codes(first) for first in range(0, rows, 128)]
+        parts.append(jnp.zeros((SCALE_ROWS - len(parts), 128), F32))
+        codes = jnp.concatenate(parts, axis=0)
+        sizes[...] = code_scale(codes[0:8, :])
+        for number in range(2 * RING):
+            own[number, rows : rows + SCALE_ROWS, :] = codes.astype(jnp.int32).astype(I16)
+
+    def squash_rows(first, count, own, first_own, read_res, write_next):
+        def some(number, carry):
+            row = pl.multiple_of(number * 16, 16)
+            value = grad[pl.ds(row, 16), :] + read_res(row)
+            size, code, factor = row_scale(value, value.shape[1])
+            grad[pl.ds(row, 16), :] = value
+            marks[pl.ds(first_own + row, 16), :] = jnp.broadcast_to(code, (16, 128))
+            steep = 2.0 / size
+            for lane in range(0, value.shape[1], 128):
+                piece = grad[pl.ds(row, 16), lane : lane + 128]
+                curve = jnp.tanh(piece * steep)
+                number_of = lane // 256
+                chunk = number_of // 2 if number_of % 2 == 0 else 7 - number_of // 2
+                own[2 * chunk + lane // 128 % 2, pl.ds(first_own + row, 16), :] = to_codes(
+                    curve * factor
+                )
+                write_next(row, lane, piece - size * curve)
+            return carry
+
+        lax.fori_loop(0, count // 16, some, 0)
+
+    def out_group(group):
+        for part, rows in enumerate(BLOCKS):
+            base = pl.multiple_of(group * OUT_ROWS + starts[part], 16)
+            for lane in range(0, grad.shape[1], 512):
+                grad[0:rows, lane : lane + 512] = dot_nn(
+                    dl_ref[pl.ds(base, rows), :], h_two_ref[:, lane : lane + 512]
+                )
+            res_copy(group, part).wait()
+            if part == 0:
+
+                @pl.when(group > 0)
+                def _():
+                    stage_copy(group - 1, len(BLOCKS) - 1, BLOCKS[-1]).wait()
+
+            else:
+                stage_copy(group, part - 1, BLOCKS[part - 1]).wait()
+
+            def write_next(row, lane, values):
+                stage[pl.ds(row, 16), 0, lane : lane + 128] = values
+
+            squash_rows(
+                0,
+                rows,
+                own_out.at[group],
+                starts[part],
+                lambda row, part=part: res_buf[part, pl.ds(row, 16), :].astype(F32),
+                write_next,
+            )
+            stage_start(group, part)
+
+            @pl.when(group < OUT_GROUPS - 1)
+            def _(part=part):
+                res_copy(group + 1, part).start()
+
+        set_sizes(OUT_ROWS, own_out.at[group], size_out.at[group])
+
+    def hid_group():
+        for first in range(0, HID_ROWS, 256):
+            for lane in range(0, grad.shape[1], 512):
+                grad[0:256, lane : lane + 512] = dot_nn(
+                    dz_two_ref[first : first + 256, :], h_one_ref[:, lane : lane + 512]
+                )
+
+            def write_next(row, lane, values, first=first):
+                next_hid_ref[pl.ds(first + row, 16), lane : lane + 128] = values
+
+            squash_rows(
+                0,
+                256,
+                own_hid,
+                first,
+                lambda row, first=first: res_hid_ref[pl.ds(first + row, 16), :].astype(F32),
+                write_next,
+            )
+        set_sizes(HID_ROWS, own_hid, size_hid)
+
+    def in_group():
+        wide = x_ref.shape[1]
+        for first in range(0, HID_ROWS, 256):
+            grad[0:256, 0:wide] = dot_nn(dz_one_ref[first : first + 256, :], x_ref[...])
+
+            def some(number, carry, first=first):
+                row = pl.multiple_of(number * 16, 16)
+                place = pl.multiple_of(first + row, 16)
+                value = grad[pl.ds(row, 16), 0:wide] + res_in_ref[pl.ds(place, 16), :].astype(F32)
+                size, code, factor = row_scale(value, deep)
+                curve = jnp.tanh(value * (2.0 / size))
+                next_in_ref[pl.ds(place, 16), :] = value - size * curve
+                marks[pl.ds(place, 16), :] = jnp.broadcast_to(code, (16, 128))
+                chunk = first // 64 + number // 4
+                inside = pl.multiple_of(number % 4 * 16, 16)
+                codes = to_codes(curve * factor)
+                for way in range(2):
+                    own_in[2 * chunk + way, pl.ds(inside, 16), :] = codes[
+                        :, way * 256 : (way + 1) * 256
+                    ]
+                return carry
+
+            lax.fori_loop(0, 16, some, 0)
+        for chunk in range(RING):
+            codes = jnp.concatenate(
+                [lane_codes(64 * chunk), jnp.zeros((SCALE_ROWS - 1, 128), F32)], axis=0
+            )
+            size_in[chunk] = code_scale(codes[0:8, :])
+            for way in range(2):
+                own_in[2 * chunk + way, 64 : 64 + SCALE_ROWS, 0:128] = codes.astype(
+                    jnp.int32
+                ).astype(I16)
+                own_in[2 * chunk + way, 64 : 64 + SCALE_ROWS, 128:256] = jnp.zeros(
+                    (SCALE_ROWS, 128), I16
+                )
+
+    def towards(way):
+        return {"blk": ring_blk((here + 1 - 2 * way + RING) % RING)}
+
+    def move(src, got, step, way, send_sem, recv_sem):
+        return pltpu.make_async_remote_copy(
+            src_ref=src,
+            dst_ref=got.at[way, step],
+            send_sem=send_sem.at[way, step],
+            recv_sem=recv_sem.at[way, step],
+            device_id=towards(way),
+            device_id_type=MESH,
+        )
+
+    def first_moves(own, got, send_sem, recv_sem):
+        for way in range(2):
+            chunk = (here - 1 + 2 * way + RING) % RING
+            move(own.at[2 * chunk + way], got, 0, way, send_sem, recv_sem).start()
+
+    def hop(rows, own, got, own_sizes, step, way, send_sem, recv_sem, keep):
+        message = got.at[way, step]
+        move(message, got, step, way, send_sem, recv_sem).wait_recv()
+        ahead = here - 2 - step + way * (4 + 2 * step) + 2 * RING
+        chunk = ahead % RING
+        mine = own.at[2 * chunk + way]
+        size = own_sizes(chunk)
+        came = code_scale(from_codes(message[rows : rows + SCALE_ROWS, 0:128])[0:8, :])
+        code = scale_code(came + size)
+        whole = code_scale(code)
+        blank = jnp.zeros((112, 128), F32)
+        wide = message.shape[1]
+
+        @pl.when(step < STEPS - 1)
+        def _():
+            shares = jnp.transpose(jnp.concatenate([came / whole, size / whole, blank], axis=0))
+            for number, first in enumerate(range(0, rows, 128)):
+                count = min(128, rows - first)
+                there = slice(first, first + count)
+                message[there, :] = to_codes(
+                    from_codes(message[there, :]) * shares[0:count, number : number + 1]
+                    + from_codes(mine[there, :]) * shares[0:count, 8 + number : 9 + number]
+                )
+            codes = jnp.concatenate([code, jnp.zeros((SCALE_ROWS - 8, 128), F32)], axis=0)
+            message[rows : rows + SCALE_ROWS, 0:128] = codes.astype(jnp.int32).astype(I16)
+            move(message, got, step + 1, way, send_sem, recv_sem).start()
+
+        @pl.when(step == STEPS - 1)
+        def _():
+            shares = jnp.transpose(
+                jnp.concatenate([came * (1.0 / TOP_CODE), size * (1.0 / TOP_CODE), blank], axis=0)
+            )
+            square = jnp.zeros((1, wide), F32)
+            for number, first in enumerate(range(0, rows, 128)):
+                count = min(128, rows - first)
+                there = slice(first, first + count)
+                value = (
+                    from_codes(message[there, :]) * shares[0:count, number : number + 1]
+                    + from_codes(mine[there, :]) * shares[0:count, 8 + number : 9 + number]
+                )
+                keep(first, count, value)
+                square = square + jnp.sum(value * value, axis=0, keepdims=True)
+            for lane in range(0, wide, 128):
+                stats_ref[0:1, :] += square[:, lane : lane + 128]
+
+    def out_hop(group, step, way):
+        def keep(first, count, value):
+            row = pl.multiple_of(group * OUT_ROWS + first, 16)
+
+            @pl.when(way == 0)
+            def _():
+                red_out_ref[pl.ds(row, count), 0:128] = value
+
+            @pl.when(way == 1)
+            def _():
+                red_out_ref[pl.ds(row, count), 128:256] = value
+
+        hop(
+            OUT_ROWS,
+            own_out.at[group],
+            got_out.at[group],
+            lambda chunk: size_out[group],
+            step,
+            way,
+            out_send.at[group],
+            out_recv.at[group],
+            keep,
+        )
+
+    def hid_hop(step, way):
+        def keep(first, count, value):
+            @pl.when(way == 0)
+            def _():
+                red_hid_ref[first : first + count, 0:128] = value
+
+            @pl.when(way == 1)
+            def _():
+                red_hid_ref[first : first + count, 128:256] = value
+
+        hop(
+            HID_ROWS, own_hid, got_hid, lambda chunk: size_hid[...], step, way, hid_send, hid_recv, keep
+        )
+
+    def share_move(step, way):
+        place = (here - step + 2 * step * way + 2 * RING) % RING
+        return pltpu.make_async_remote_copy(
+            src_ref=share_in.at[way, place],
+            dst_ref=share_in.at[way, place],
+            send_sem=share_send.at[way, step],
+            recv_sem=share_recv.at[way, step],
+            device_id=towards(way),
+            device_id_type=MESH,
+        )
+
+    def in_hop(step, way):
+        def keep(first, count, value):
+            share_in[way, here] = value
+
+        hop(64, own_in, got_in, lambda chunk: size_in[chunk], step, way, in_send, in_recv, keep)
+
+        @pl.when(step == STEPS - 1)
+        def _():
+            share_move(0, way).start()
+
+    def share_hop(step, way):
+        share_move(step, way).wait_recv()
+
+        @pl.when(step < STEPS - 1)
+        def _():
+            share_move(step + 1, way).start()
+
+    def wave(number, carry):
+        @pl.when(number == 0)
+        def _():
+            in_group()
+            first_moves(own_in, got_in, in_send, in_recv)
+            hid_group()
+            first_moves(own_hid, got_hid, hid_send, hid_recv)
+
+        @pl.when(number < OUT_GROUPS)
+        def _():
+            out_group(number)
+            first_moves(own_out.at[number], got_out.at[number], out_send.at[number], out_recv.at[number])
+
+        def both(way, carry):
+            @pl.when((number >= 1) & (number <= STEPS))
+            def _():
+                in_hop(number - 1, way)
+                hid_hop(number - 1, way)
+
+            @pl.when(number > STEPS)
+            def _():
+                share_hop(2 * (number - STEPS - 1), way)
+
+                @pl.when(number < STEPS + 4)
+                def _():
+                    share_hop(2 * (number - STEPS - 1) + 1, way)
+
+            def outs(group, carry):
+                step = number - 1 - group
+
+                @pl.when((step >= 0) & (step < STEPS))
+                def _():
+                    out_hop(group, step, way)
+
+                return carry
+
+            lax.fori_loop(0, OUT_GROUPS, outs, 0)
+            return carry
+
+        lax.fori_loop(0, 2, both, 0)
+        return carry
+
+    lax.fori_loop(0, STEPS + OUT_GROUPS + 1, wave, 0)
+
+    for place in range(RING):
+        for way in range(2):
+            red_in_ref[place * 64 : (place + 1) * 64, way * 256 : (way + 1) * 256] = share_in[
+                way, place
+            ]
+    for copy in vec_copies:
+        copy.wait_recv()
+    vecs[blk] = vec_ref[...]
+    total = vecs[0]
+    for number in range(1, RING):
+        total = total + vecs[number]
+    vec_sum_ref[...] = total
+    for copy in vec_copies:
+        copy.wait_send()
+    stage_copy(OUT_GROUPS - 1, len(BLOCKS) - 1, last_rows).wait()
+    for way in range(2):
+        for step in range(STEPS):
+            for group in range(OUT_GROUPS):
+                move(
+                    got_out.at[group, way, step],
+                    got_out.at[group],
+                    step,
+                    way,
+                    out_send.at[group],
+                    out_recv.at[group],
+                ).wait_send()
+            move(got_hid.at[way, step], got_hid, step, way, hid_send, hid_recv).wait_send()
+            move(got_in.at[way, step], got_in, step, way, in_send, in_recv).wait_send()
+            share_move(step, way).wait_send()
+
+
+def reduce_grads(dl, h_two, res_out, dz_two, h_one, res_hid, dz_one, x, res_in, vec, senones, deep):
+    wide = h_two.shape[1]
+    in_wide = x.shape[1]
+    vmem = pl.BlockSpec(memory_space=pltpu.VMEM)
+    hbm = pl.BlockSpec(memory_space=pl.ANY)
+    message = OUT_ROWS + SCALE_ROWS
+    hid_message = HID_ROWS + SCALE_ROWS
+    in_message = 64 + SCALE_ROWS
+    sem = pltpu.SemaphoreType.DMA
+    return pl.pallas_call(
+        functools.partial(reduce_kernel, deep),
+        out_shape=(
+            jax.ShapeDtypeStruct((senones, 1, wide), F32),
+            jax.ShapeDtypeStruct((HID_ROWS, wide), F32),
+            jax.ShapeDtypeStruct((HID_ROWS, in_wide), F32),
+            jax.ShapeDtypeStruct((OUT_GROUPS * OUT_ROWS, 256), F32),
+            jax.ShapeDtypeStruct((HID_ROWS, 256), F32),
+            jax.ShapeDtypeStruct((HID_ROWS, in_wide), F32),
+            jax.ShapeDtypeStruct(vec.shape, F32),
+            jax.ShapeDtypeStruct((8, 128), F32),
+        ),
+        in_specs=[vmem, vmem, hbm] + [vmem] * 7,
+        out_specs=(hbm,) + (vmem,) * 7,
+        scratch_shapes=[
+            pltpu.VMEM((BLOCKS[0], wide), F32),
+            pltpu.VMEM((BLOCKS[0], 1, wide), F32),
+            pltpu.VMEM((2, BLOCKS[0], wide), BF16),
+            pltpu.VMEM((640, 128), F32),
+            pltpu.VMEM((OUT_GROUPS, 2 * RING, message, 128), I16),
+            pltpu.VMEM((OUT_GROUPS, 2, STEPS, message, 128), I16),
+            pltpu.VMEM((OUT_GROUPS, 8, 128), F32),
+            pltpu.VMEM((2 * RING, hid_message, 128), I16),
+            pltpu.VMEM((2, STEPS, hid_message, 128), I16),
+            pltpu.VMEM((8, 128), F32),
+            pltpu.VMEM((2 * RING, in_message, 256), I16),
+            pltpu.VMEM((2, STEPS, in_message, 256), I16),
+            pltpu.VMEM((RING, 8, 128), F32),
+            pltpu.VMEM((2, RING, 64, 256), F32),
+            pltpu.VMEM((RING,) + vec.shape, F32),
+            sem((2,)),
+            sem((1,)),
+            sem((OUT_GROUPS, 2, STEPS)),
+            sem((OUT_GROUPS, 2, STEPS)),
+            sem((2, STEPS)),
+            sem((2, STEPS)),
+            sem((2, STEPS)),
+            sem((2, STEPS)),
+            sem((2, STEPS)),
+            sem((2, STEPS)),
+            sem((STEPS,)),
+            sem((STEPS,)),
+        ],
+        compiler_params=pltpu.CompilerParams(
+            collective_id=1, has_side_effects=True, vmem_limit_bytes=62 * 1024 * 1024
+        ),
+    )(dl, h_two, res_out, dz_two, h_one, res_hid, dz_one, x, res_in, vec)
 
 
 def plain_body(
@@ -594,13 +1128,10 @@
     d_logits = (
         jnp.where(live_rows[:, None], probs - target_hit.astype(jnp.float32), 0.0) / slot_count
     ).astype(jnp.bfloat16)
-    grad_output = inner_rows(h_two, d_logits)
     d_h_two = reduce_cols(outer_cols(d_logits, low_output))
     d_z_two = (d_h_two * sig_two * (1.0 - sig_two)).astype(jnp.bfloat16)
-    grad_hidden = inner_rows(h_one, d_z_two)
     d_h_one = reduce_cols(outer_cols(d_z_two, low_hidden))
     d_z_one = (d_h_one * sig_one * (1.0 - sig_one)).astype(jnp.bfloat16)
-    grad_input = inner_rows(inputs, d_z_one)
     grad_bias = jnp.concatenate(
         [
             jnp.sum(d_z_one.astype(jnp.float32), axis=0),
@@ -608,20 +1139,36 @@
             jnp.sum(d_logits.astype(jnp.float32), axis=0),
         ]
     )
-    q_input, next_res_input = squash(grad_input, res_input[0])
-    q_hidden, next_res_hidden = squash(grad_hidden, res_hidden[0])
-    q_output, next_res_output = squash(grad_output, res_output[0])
-    red_hidden, red_output = (
-        lax.psum_scatter(q_hidden, "blk", scatter_dimension=0, tiled=True),
-        lax.psum_scatter(q_output, "blk", scatter_dimension=0, tiled=True),
-    )
-    red_input, red_bias, loss_sum = lax.psum((q_input, grad_bias, loss_local), "blk")
+    deep = w_input.shape[0]
+    padded = 512
+    rows_out = OUT_GROUPS * OUT_ROWS
+    vec = jnp.concatenate([grad_bias, loss_local[None]])
+    vec = jnp.pad(vec, (0, 4096 - vec.shape[0])).reshape(32, 128)
+    next_out, next_hid, next_in, red_out, red_hid, red_in, vec_sum, stats = reduce_grads(
+        jnp.pad(d_logits, ((0, 0), (0, rows_out - scol))).T,
+        h_two,
+        jnp.pad(res_output[0], ((0, 0), (0, rows_out - scol))).T,
+        d_z_two.T,
+        h_one,
+        res_hidden[0].T,
+        d_z_one.T,
+        jnp.pad(inputs, ((0, 0), (0, padded - deep))),
+        jnp.pad(res_input[0], ((0, padded - deep), (0, 0))).T,
+        vec,
+        scol,
+        deep,
+    )
+    next_res_output = next_out.transpose(1, 2, 0)
+    next_res_hidden = next_hid.T
+    next_res_input = next_in[:, :deep].T
+    red_output = red_out[:scol].T
+    red_hidden = red_hid.T
+    red_input = red_in[:, :deep].T
+    vec_sum = vec_sum.reshape(-1)
+    red_bias = vec_sum[: bias_row.shape[0]]
+    loss_sum = vec_sum[bias_row.shape[0]]
     share_blk = 1.0 / nblk
-    grad_square = (
-        share_blk * (jnp.sum(red_input * red_input) + jnp.sum(red_bias * red_bias))
-        + jnp.sum(red_hidden * red_hidden)
-        + jnp.sum(red_output * red_output)
-    )
+    grad_square = share_blk * jnp.sum(red_bias * red_bias) + jnp.sum(stats)
     clip_norm = jnp.sqrt(lax.psum(grad_square, ("blk", "col")))
     factor = jnp.minimum(1.0, CLIP / clip_norm)
     next_mom_input = 0.5 * mom_input + factor * red_input
@@ -638,8 +1185,6 @@
     tall = collect_rows(iter_hidden)
     piece = hcol // 4
     mine = lax.dynamic_slice_in_dim(tall, (blk_index % 4) * piece, piece, axis=1).T
-    deep = w_input.shape[0]
-    padded = 512
     whole_input = spread_cols(jnp.pad(iter_input, ((0, padded - deep), (0, 0))))
     done_hidden, done_input = muon(mine, whole_input, w_hidden.shape[0], hcol)
     done_hidden = done_hidden.reshape(hcol, w_hidden.shape[0]).T
@@ -667,7 +1212,7 @@
         next_bias_second,
         next_res_input[None],
         next_res_hidden[None],
-        next_res_output[None],
+        next_res_output,
     )
 
 

time: 1510 us -> 1230 us (0.81)
  waiting for transfers between devices: 824 us -> 434 us
  Pallas kernels: 304 us -> 491 us
  blocking collectives: 146 us -> 109 us
  other arithmetic: 77.3 us -> 40.5 us
  matrix products: 76.3 us -> 49.6 us
  local copies, waits for them, and re-layouts: 54 us -> 72.2 us
    reduce_scatter x2 -> x0, waiting for transfers between devices: 381 us -> none  [the longest x1 315 us: fast_body(): lax.psum_scatter(q_output, 'blk', scatter_dimension=0, tiled=True)]
    pallas_call x0 -> x1, Pallas kernels: none -> 187 us  [reduce_grads(): pl.pallas_call(functools.partial(reduce_kernel, deep), out_shape=(jax.Sha...]
    psum x1 -> x0, waiting for transfers between devices: 41.2 us -> none  [fast_body(): lax.psum((q_input, grad_bias, loss_local), 'blk')]
    psum x1 -> x0, blocking collectives: 37.3 us -> none  [fast_body(): lax.psum((q_input, grad_bias, loss_local), 'blk')]
    all_gather x3, waiting for transfers between devices: 201 us -> 233 us  [collect_rows(): return lax.all_gather(values, 'blk', axis=0, tiled=True)]
    broadcast_in_dim x3 -> x0, other arithmetic: 27.4 us -> none  [the longest x1 20.7 us: fast_body(): next_res_output[None]]
    dot_general x3 -> x0, matrix products: 26.7 us -> none  [inner_rows(): lax.dot_general(left_side, right_side, (((0,), (0,)), ((), ())), preferre...]
    unnamed x34 -> x50, local copies, waits for them, and re-layouts: 49.6 us -> 31.2 us
  transfers between devices with their start and end apart: 11 -> 8, of which waited for: 11 -> 8; matrix products, arithmetic and copies ran while one was open for 8% -> 5% of each run, Pallas kernels for 0% -> 0%
where the time goes in v2:
time: 1230 us; the launch traced here: 1220 us
  Pallas kernels  491 us (40%)
  waiting for transfers between devices  434 us (35%)
  blocking collectives  109 us (9%)
  local copies, waits for them, and re-layouts  72.2 us (6%)
  matrix products  49.6 us (4%)
  other arithmetic  40.5 us (3%)
  between operations  20.1 us (2%)
    pallas_call x1, Pallas kernels, muon(): pl.pallas_call(muon_kernel, out_shape=(jax.ShapeDtypeStruct((4, rows, hei...  304 us
    all_gather x3, waiting for transfers between devices, collect_rows(): return lax.all_gather(values, 'blk', axis=0, tiled=True)  233 us
    pallas_call x1, Pallas kernels, reduce_grads(): pl.pallas_call(functools.partial(reduce_kernel, deep), out_shape=(jax.Sha...  187 us
    reduce_scatter x2, waiting for transfers between devices, reduce_cols(): return lax.psum_scatter(values, 'col', scatter_dimension=1, tiled=True)  105 us
    all_gather x3, waiting for transfers between devices, spread_cols(): return lax.all_gather(values, 'col', axis=1, tiled=True)  95.2 us
    psum x1, blocking collectives, fast_body(): lax.psum((share_blk * jnp.sum(next_mom_input * next_mom_input), jnp.sum(n...  40.2 us
    psum x1, blocking collectives, fast_body(): clip_norm = jnp.sqrt(lax.psum(grad_square, ('blk', 'col')))  38.7 us
    unnamed x50, local copies, waits for them, and re-layouts  31.2 us
  transfers between devices with their start and end apart: 8, of which 8 were waited for; matrix products, arithmetic and copies ran while one was open for 5% of the time, Pallas kernels for 0%

profile of v2, /device:TPU:0, one launch (start us, length us, event | category | flops | bytes accessed | tf_op | source)
XLA Modules:
  0.0 1216.6 jit_solution(13295330364931782148)
XLA Ops:
  9.8 11.7 all_gather.25
  25.8 36.9 %all-gather.10.cloned.1.call-done = bf16[2048,512]{1,0:T(8,128)(2,1)} async-done(((bf16[256,512]{1,0:T(8,128)(2,1)}), bf16[2048,512]{1,0:T(8,128)(2,1)}) %all-gather.10.cloned.1.call-update) | async-done | bytes 2097168 | tf_op jit(solution)/shard_map/all_gather | solution.py:64
  62.7 35.1 %all-gather.8.cloned.1.call-done = bf16[1024,2048]{0,1:T(8,128)(2,1)} async-done(((bf16[1024,512]{0,1:T(8,128)(2,1)}), bf16[1024,2048]{0,1:T(8,128)(2,1)}) %all-gather.8.cloned.1.call-update) | async-done | bytes 4194320 | tf_op jit(solution)/shard_map/all_gather | solution.py:56
  97.9 7.3 fusion.9
  111.8 28.1 %all-gather.12.cloned.1.call-done = bf16[1024,2048]{0,1:T(8,128)(2,1)} async-done(((bf16[1024,512]{0,1:T(8,128)(2,1)}), bf16[1024,2048]{0,1:T(8,128)(2,1)}) %all-gather.12.cloned.1.call-update) | async-done | bytes 4194320 | tf_op jit(solution)/shard_map/all_gather | solution.py:56
  139.9 141.9 %all-gather.14.cloned.1.call-done = bf16[2048,2326]{0,1:T(8,128)(2,1)} async-done(((bf16[256,2326]{0,1:T(8,128)(2,1)}), bf16[2048,2326]{0,1:T(8,128)(2,1)}) %all-gather.14.cloned.1.call-update) | async-done | bytes 9527312 | tf_op jit(solution)/shard_map/all_gather | solution.py:64
  281.7 16.3 %add_reduce_fusion = (f32[1024]{0:T(1024)S(1)}, f32[1024,2326]{0,1:T(8,128)}) fusion(f32[2326]{0:T(1024)S(1)} %slice_reduce_fusion, bf16[1024,2048]{0,1:T(8,128)(2,1)} %all-gather.12.cloned.1.call-done, bf16[2048,2326]{0,1:T(8,128)(2,1)} %all-gather.14.cloned.1.call-done), kind=kOutput, calls=%fused_computation.7 | convolution fusion | flops 9760713728 | bytes 23262296 | tf_op jit(solution)/shard_map/dot_general | solution.py:34
  298.0 6.1 pmax.7
  309.9 6.7 all-reduce.7
  316.6 7.0 convert_reduce_fusion
  325.8 16.0 %fusion.10 = f32[1024,2048]{0,1:T(8,128)} fusion(bf16[1024,2326]{0,1:T(8,128)(2,1)S(1)} %get-tuple-element.97, bf16[2048,2326]{0,1:T(8,128)(2,1)} %all-gather.14.cloned.1.call-done), kind=kOutput, calls=%fused_computation.52 | convolution fusion | flops 9755951104 | bytes 22679552 | tf_op jit(solution)/shard_map/dot_general | solution.py:44
  342.0 69.6 %reduce-scatter.3.cloned.1.call-done = f32[1024,512]{0,1:T(8,128)} async-done(((f32[1024,2048]{0,1:T(8,128)}), f32[1024,512]{0,1:T(8,128)}) %reduce-scatter.3.cloned.1.call-update) | async-done | bytes 2097168 | tf_op jit(solution)/shard_map/reduce_scatter | solution.py:60
  425.9 11.1 pad_bitcast_fusion.res_out_ref
  437.1 6.5 copy.67.h_one_ref
  443.6 6.6 copy.66.h_two_ref
  456.2 35.8 %reduce-scatter.5.cloned.1.call-done = f32[1024,512]{0,1:T(8,128)} async-done(((f32[1024,2048]{0,1:T(8,128)}), f32[1024,512]{0,1:T(8,128)}) %reduce-scatter.5.cloned.1.call-update) | async-done | bytes 2097168 | tf_op jit(solution)/shard_map/reduce_scatter | solution.py:60
  496.2 187.4 %shard_map.271 = (f32[2326,1,2048]{2,1,0:T(1,128)}, f32[512,2048]{1,0:T(8,128)}, f32[512,512]{1,0:T(8,128)}, f32[2368,256]{1,0:T(8,128)}, f32[512,256]{1,0:T(8,1...) custom-call(bf16[2368,1024]{1,0:T(8,128)(2,1)} %pad_bitcast_fusion.1.dl_ref, ...), custom_call_target="tpu_custom_call" | custom-call | tf_op jit(solution)/shard_map/pallas_call | solution.py:882
  688.8 38.7 %psum.37 = f32[]{:T(128)} all-reduce(f32[]{:T(128)S(6)} %add.131), channel_id=1, replica_groups=mesh['blk'=8,'col'=4] {'blk','col'}, use_global_device_ids=true, to_apply=%region_14.15 | all-reduce | flops 1 | bytes 8 | tf_op jit(solution)/shard_map/psum | solution.py:1172
  733.2 40.2 %all-reduce.6 = (f32[]{:T(128)}, f32[]{:T(128)}) all-reduce(f32[]{:T(128)} %get-tuple-element.94, f32[]{:T(128)S(6)} %mul.199), channel_id=1, replica_groups=mesh['blk'=8,'col'=4] {'blk','col'}, use_global_device_ids=true, to_apply=%region_16.17 | all-reduce | flops 2 | bytes 16 | tf_op jit(solution)/shard_map/psum | solution.py:1176
  787.4 8.4 multiply_subtract_fusion
  795.8 54.4 %all-gather.16.cloned.1.call-done = f32[2048,512]{0,1:T(8,128)} async-done(((f32[256,512]{0,1:T(8,128)}), f32[2048,512]{0,1:T(8,128)}) %all-gather.16.cloned.1.call-update) | async-done | bytes 4194320 | tf_op jit(solution)/shard_map/all_gather | solution.py:64
  852.5 32.0 %all-gather.18.cloned.1.call-done.xin_ref = f32[512,2048]{1,0:T(8,128)} async-done(((f32[512,512]{1,0:T(8,128)}), f32[512,2048]{1,0:T(8,128)}) %all-gather.18.cloned.1.call-update) | async-done | bytes 4194320 | tf_op jit(solution)/shard_map/all_gather | solution.py:56
  884.5 303.9 %shard_map.272 = (f32[4,128,256]{2,1,0:T(8,128)}, f32[512,512]{1,0:T(8,128)}) custom-call(f32[128,2048]{1,0:T(8,128)} %dynamic-slice_bitcast_fusion.xt_ref, f32[512,2048]{1,0:T(8,128)} %all-gather.18.cloned.1.call-done.xin_ref), custom_call_target="tpu_custom_call" | custom-call | tf_op jit(solution)/shard_map/pallas_call | solution.py:363
  1191.8 16.3 %copy.79 = f32[1,2048,2326]{1,0,2:T(1,128)} copy(f32[1,2048,2326]{1,0,2:T(1,128)} %bitcast.60) | data formatting | bytes 38109184
  (102 shorter events, 72.4 us)
Async XLA Ops:
  7.2 55.6 %all-gather.10.cloned.1.call-start = ((), (), s32[]{:S(2)}) async-start(), calls=%async_computation.3 | async-start | bytes 2359296 | tf_op jit(solution)/shard_map/all_gather | solution.py:64
  9.0 88.8 %all-gather.8.cloned.1.call-start = ((), (), s32[]{:S(2)}) async-start(), calls=%async_computation.2 | async-start | bytes 5242880 | tf_op jit(solution)/shard_map/all_gather | solution.py:56
  21.5 4.3 copy-start.4
  25.8 114.1 %all-gather.12.cloned.1.call-start = ((), (), s32[]{:S(2)}) async-start(), calls=%async_computation.4 | async-start | bytes 5242880 | tf_op jit(solution)/shard_map/all_gather | solution.py:56
  97.9 7.4 copy-start.1
  105.2 6.5 copy-start.15
  105.2 176.5 %all-gather.14.cloned.1.call-start = ((), (), s32[]{:S(2)}) async-start(), calls=%async_computation.5 | async-start | bytes 10727424 | tf_op jit(solution)/shard_map/all_gather | solution.py:64
  106.5 305.1 %reduce-scatter.3.cloned.1.call-start = ((), (), s32[]{:S(2)}) async-start(), calls=%async_computation.6 | async-start | bytes 10485760 | tf_op jit(solution)/shard_map/reduce_scatter | solution.py:60
  341.9 150.1 %reduce-scatter.5.cloned.1.call-start = ((), (), s32[]{:S(2)}) async-start(), calls=%async_computation.7 | async-start | bytes 10485760 | tf_op jit(solution)/shard_map/reduce_scatter | solution.py:60
  411.6 2.9 copy-start.20
  414.3 5.8 copy-start.3
  420.1 2.3 copy-start.9
  420.2 430.1 %all-gather.16.cloned.1.call-start = ((), (), s32[]{:S(2)}) async-start(), calls=%async_computation.8 | async-start | bytes 4718592 | tf_op jit(solution)/shard_map/all_gather | solution.py:64
  422.5 2.4 copy-start.13
  450.8 41.2 %copy-start.7 = (f32[1024,512]{0,1:T(8,128)S(1)}, f32[1024,512]{0,1:T(8,128)}, u32[]{:S(2)}) copy-start(f32[1024,512]{0,1:T(8,128)} %get-tuple-element.107) | copy-start | bytes 6291460
  683.6 46.2 %copy-start.10 = (f32[440,512]{1,0:T(8,128)S(1)}, f32[440,512]{1,0:T(8,128)}, u32[]{:S(2)}) copy-start(f32[440,512]{1,0:T(8,128)} %param.23) | copy-start | bytes 2703364
  730.7 45.1 %copy-start.6 = (f32[440,512]{1,0:T(8,128)}, f32[440,512]{1,0:T(8,128)S(1)}, u32[]{:S(2)}) copy-start(f32[440,512]{1,0:T(8,128)S(1)} %get-tuple-element.133) | copy-start | bytes 2703364
  775.0 109.5 %all-gather.18.cloned.1.call-start = ((), (), s32[]{:S(2)}) async-start(), calls=%async_computation.9 | async-start | bytes 5242880 | tf_op jit(solution)/shard_map/all_gather | solution.py:56
  784.0 2.7 copy-start.16
  784.0 2.7 copy-start.17
  784.0 3.4 copy-start.2
  852.5 337.3 %copy-start.8 = (f32[256,512]{1,0:T(8,128)S(1)}, f32[256,512]{1,0:T(8,128)}, u32[]{:S(2)}) copy-start(f32[256,512]{1,0:T(8,128)} %param.20) | copy-start | bytes 1572868
  1188.4 2.4 copy-start.11
  1188.4 2.3 copy-start.12
  (5 other events, 8.2 us)
Sparse Core Ops, SparseCore 0:
  10.7 51.9 all-gather.9
  64.9 32.9 all-gather.7
  105.3 34.4 all-gather.11
  142.3 139.3 all-gather.13
  342.0 69.4 reduce-scatter.2
  420.3 71.6 reduce-scatter.4
  775.1 75.0 all-gather.15
  851.8 32.6 all-gather.17

commit v3 on v2

--- a/solution.py
+++ b/solution.py
@@ -93,305 +93,6 @@
     return lax.dot_general(
         left_side, right_side, (((1,), (1,)), ((), ())), preferred_element_type=F32
     )
-
-
-DIM_BITS = (2, 4, 8)
-ORDERS = ((0, 1, 2), (1, 2, 0), (2, 0, 1))
-PIECE = 48
-
-
-def span_of(dims):
-    slots = [0]
-    for dim in dims:
-        slots = slots + [slot | DIM_BITS[dim] for slot in slots]
-    return slots
-
-
-def stage_sends(stage):
-    moves = []
-    for piece, order in enumerate(ORDERS):
-        for slot in span_of(order[:stage]):
-            moves.append((piece, slot, order[stage]))
-    return sorted(moves, key=lambda move: (move[1] | DIM_BITS[move[2]], move[0]))
-
-
-def muon_kernel(
-    xt_ref,
-    xin_ref,
-    hid_ref,
-    inp_ref,
-    codes,
-    tops,
-    lows,
-    scales,
-    xs,
-    us,
-    vs,
-    lhs,
-    xin,
-    xin_top,
-    xin_low,
-    gram,
-    back,
-    send_sems,
-    core_sems,
-    recv_sems,
-    back_send,
-    back_recv,
-):
-    blk = lax.axis_index("blk")
-    col = lax.axis_index("col")
-    rows, wide = xs.shape
-    other_core = {"col": col + 1 - 2 * (col % 2)}
-    dims = (
-        {"blk": blk + 1 - 2 * (blk % 2)},
-        {"col": (col + 2) % 4},
-        {"blk": blk + 2 - 4 * ((blk // 2) % 2)},
-    )
-    diagonal = {"blk": 4 * (blk // 4) + 3 - blk % 4}
-    barrier = pltpu.get_barrier_semaphore()
-    for target in (other_core, *dims, diagonal):
-        pl.semaphore_signal(barrier, inc=1, device_id=target, device_id_type=MESH)
-
-    xs[...] = xt_ref[...]
-    xin[...] = xin_ref[...]
-    for turn in range(2):
-        codes[turn, 0, rows:, :] = jnp.zeros((codes.shape[2] - rows, wide), I16)
-    eye = lax.broadcasted_iota(jnp.int32, (rows, rows), 0) == lax.broadcasted_iota(
-        jnp.int32, (rows, rows), 1
-    )
-    pl.semaphore_wait(barrier, 5)
-
-    stages = [stage_sends(stage) for stage in range(3)]
-    numbers = {move: number for number, move in enumerate(sum(stages, []))}
-
-    def part(turn, slot, piece):
-        return codes.at[turn, slot, pl.ds(piece * PIECE, PIECE), :]
-
-    def send(turn, move):
-        piece, slot, dim = move
-        return pltpu.make_async_remote_copy(
-            src_ref=part(turn, slot, piece),
-            dst_ref=part(turn, slot | DIM_BITS[dim], piece),
-            send_sem=send_sems.at[numbers[move]],
-            recv_sem=recv_sems.at[turn, slot | DIM_BITS[dim], piece],
-            device_id=dims[dim],
-            device_id_type=MESH,
-        )
-
-    def to_core(turn, slot, piece):
-        return pltpu.make_async_remote_copy(
-            src_ref=part(turn, slot, piece),
-            dst_ref=part(turn, slot + 1, piece),
-            send_sem=core_sems.at[slot // 2, piece],
-            recv_sem=recv_sems.at[turn, slot + 1, piece],
-            device_id=other_core,
-            device_id_type=MESH,
-        )
-
-    def arrived(turn, slot, piece):
-        pltpu.make_async_remote_copy(
-            src_ref=part(turn, slot, piece),
-            dst_ref=part(turn, slot, piece),
-            send_sem=core_sems.at[0, 0],
-            recv_sem=recv_sems.at[turn, slot, piece],
-            device_id=other_core,
-            device_id_type=MESH,
-        ).wait_recv()
-
-    def forward(turn, slot, piece):
-        arrived(turn, slot, piece)
-        to_core(turn, slot, piece).start()
-
-    def landed(stage):
-        return [(slot | DIM_BITS[dim], piece) for piece, slot, dim in stages[stage]]
-
-    def unpack(turn, pair):
-        for core in range(2):
-            whole = codes[turn, 2 * pair + core, 0:rows, :].astype(jnp.int32).astype(F32)
-            top, low = halves(whole)
-            tops[pair, core * rows : (core + 1) * rows, :] = top
-            lows[pair, core * rows : (core + 1) * rows, :] = low
-            step = codes[turn, 2 * pair + core, rows : rows + 16, 0:rows].astype(jnp.int32)
-            size = jnp.exp(step.astype(F32)[0:8, :] * (LN2 / LEVELS)) * (1.0 / TOP_CODE)
-            scales[pair, :, core * rows : (core + 1) * rows] = size * size
-
-    def apply_pair(pair, out):
-        both = dot_nt(lhs[...], tops[pair])
-        inner = both[:rows] + both[rows:] + dot_nt(lhs[0:rows, :], lows[pair])
-        inner = inner * scales[pair, 0:1, :]
-        top, low = halves(inner)
-        stack = jnp.concatenate([top, low], axis=0)
-        cut = 512
-        for start in range(0, wide, cut):
-            lanes = slice(start, start + cut)
-            both = dot_nn(stack, tops[pair, :, lanes])
-            out[:, lanes] += both[:rows] + both[rows:] + dot_nn(top, lows[pair, :, lanes])
-
-    def set_lhs(values):
-        top, low = halves(values)
-        lhs[0:rows, :] = top
-        lhs[rows:, :] = low
-
-    def input_gram():
-        top, low = halves(xin[...])
-        xin_top[...] = top
-        xin_low[...] = low
-        gram[...] = (
-            dot_nt(xin_top[...], xin_top[...])
-            + dot_nt(xin_low[...], xin_top[...])
-            + dot_nt(xin_top[...], xin_low[...])
-        )
-
-    def input_step():
-        size = gram.shape[0]
-        top, low = halves(gram[...])
-        square = dot_nn(top, top) + dot_nn(low, top) + dot_nn(top, low)
-        same = lax.broadcasted_iota(jnp.int32, (size, size), 0) == lax.broadcasted_iota(
-            jnp.int32, (size, size), 1
-        )
-        poly = NS_B * gram[...] + NS_C * square + jnp.where(same, NS_A, 0.0)
-        top, low = halves(poly)
-        cut = 512
-        for start in range(0, wide, cut):
-            lanes = slice(start, start + cut)
-            xin[:, lanes] = (
-                dot_nn(top, xin_top[:, lanes])
-                + dot_nn(low, xin_top[:, lanes])
-                + dot_nn(top, xin_low[:, lanes])
-            )
-
-    def iteration(number, carry):
-        turn = number % 2
-        values = xs[...]
-        largest = jnp.maximum(jnp.max(jnp.abs(values), axis=1, keepdims=True), 1e-30)
-        step = jnp.ceil(jnp.log(largest) * (LEVELS / LN2))
-        codes[turn, 0, 0:rows, :] = (
-            jnp.round(values * (TOP_CODE / jnp.exp(step * (LN2 / LEVELS))))
-            .astype(jnp.int32)
-            .astype(I16)
-        )
-        lane_step = jnp.sum(jnp.where(eye, step, 0.0), axis=0, keepdims=True)
-        codes[turn, 0, rows : rows + 16, 0:rows] = jnp.broadcast_to(
-            lane_step.astype(jnp.int32), (16, rows)
-        ).astype(I16)
-        for move in stages[0]:
-            send(turn, move).start()
-        for piece in range(3):
-            to_core(turn, 0, piece).start()
-        set_lhs(values)
-        us[...] = jnp.zeros_like(us)
-        vs[...] = jnp.zeros_like(vs)
-
-        def first_pass(pair, carry):
-            @pl.when(pair == 1)
-            def _():
-                for slot, piece in landed(0):
-                    forward(turn, slot, piece)
-                for move in stages[1]:
-                    send(turn, move).start()
-                input_gram()
-                for slot, piece in landed(1):
-                    forward(turn, slot, piece)
-                for move in stages[2]:
-                    send(turn, move).start()
-                input_step()
-
-            for slot_pair in range(1, 8):
-                mine = [(slot, piece) for slot, piece in landed(2) if slot == 2 * slot_pair]
-
-                @pl.when(pair == max(slot_pair - 1, 1))
-                def _(mine=mine):
-                    for slot, piece in mine:
-                        forward(turn, slot, piece)
-
-            for piece in range(3):
-                arrived(turn, 2 * pair + 1, piece)
-            unpack(turn, pair)
-            apply_pair(pair, us)
-            return carry
-
-        lax.fori_loop(0, 8, first_pass, 0)
-        set_lhs(us[...])
-
-        def second_pass(pair, carry):
-            apply_pair(pair, vs)
-            return carry
-
-        lax.fori_loop(0, 8, second_pass, 0)
-        xs[...] = NS_A * xs[...] + NS_B * us[...] + NS_C * vs[...]
-        for stage in stages:
-            for move in stage:
-                send(turn, move).wait_send()
-        for pair in range(8):
-            for piece in range(3):
-                to_core(turn, 2 * pair, piece).wait_send()
-        return carry
-
-    lax.fori_loop(0, NS, iteration, 0)
-
-    place = blk % 4
-    height = back.shape[2]
-    copies = []
-    for rel, target in ((1, dims[0]), (2, dims[2]), (3, diagonal)):
-        copies.append(
-            pltpu.make_async_remote_copy(
-                src_ref=xs.at[:, pl.ds(pl.multiple_of(target["blk"] * height, height), height)],
-                dst_ref=back.at[place],
-                send_sem=back_send.at[rel - 1],
-                recv_sem=back_recv.at[rel - 1],
-                device_id=target,
-                device_id_type=MESH,
-            )
-        )
-        copies[-1].start()
-    hid_ref[place] = xs[:, pl.ds(pl.multiple_of(blk * height, height), height)]
-    part_wide = inp_ref.shape[1]
-    inp_ref[...] = xin[:, pl.ds(pl.multiple_of(col * part_wide, part_wide), part_wide)]
-    for copy in copies:
-        copy.wait_recv()
-    for target in (dims[0], dims[2], diagonal):
-        other = target["blk"] % 4
-        hid_ref[other] = back[other]
-    for copy in copies:
-        copy.wait_send()
-
-
-def muon(xt, xin, height, part_wide):
-    rows, wide = xt.shape
-    deep = xin.shape[0]
-    return pl.pallas_call(
-        muon_kernel,
-        out_shape=(
-            jax.ShapeDtypeStruct((4, rows, height), F32),
-            jax.ShapeDtypeStruct((deep, part_wide), F32),
-        ),
-        in_specs=[pl.BlockSpec(memory_space=pltpu.VMEM)] * 2,
-        out_specs=(pl.BlockSpec(memory_space=pltpu.VMEM), pl.BlockSpec(memory_space=pltpu.VMEM)),
-        scratch_shapes=[
-            pltpu.VMEM((2, 16, 3 * PIECE, wide), I16),
-            pltpu.VMEM((8, 2 * rows, wide), BF16),
-            pltpu.VMEM((8, 2 * rows, wide), BF16),
-            pltpu.VMEM((8, 8, 2 * rows), F32),
-            pltpu.VMEM((rows, wide), F32),
-            pltpu.VMEM((rows, wide), F32),
-            pltpu.VMEM((rows, wide), F32),
-            pltpu.VMEM((2 * rows, wide), BF16),
-            pltpu.VMEM((deep, wide), F32),
-            pltpu.VMEM((deep, wide), BF16),
-            pltpu.VMEM((deep, wide), BF16),
-            pltpu.VMEM((deep, deep), F32),
-            pltpu.VMEM((4, rows, height), F32),
-            pltpu.SemaphoreType.DMA((21,)),
-            pltpu.SemaphoreType.DMA((8, 3)),
-            pltpu.SemaphoreType.DMA((2, 16, 3)),
-            pltpu.SemaphoreType.DMA((3,)),
-            pltpu.SemaphoreType.DMA((3,)),
-        ],
-        compiler_params=pltpu.CompilerParams(
-            collective_id=0, has_side_effects=True, vmem_limit_bytes=60 * 1024 * 1024
-        ),
-    )(xt, xin)
 
 
 RING = 8
@@ -928,6 +629,468 @@
     )(dl, h_two, res_out, dz_two, h_one, res_hid, dz_one, x, res_in, vec)
 
 
+DIM_BITS = (2, 4, 8)
+ORDERS = ((0, 1, 2), (1, 2, 0), (2, 0, 1))
+PIECE = 48
+LIGHT_HID = 3
+LIGHT_IN = 2
+
+
+def stage_sends(stage, sources):
+    moves = []
+    for piece, order in enumerate(ORDERS):
+        slot = sum(DIM_BITS[order[index]] for index in sources)
+        moves.append((piece, slot, order[stage]))
+    return moves
+
+
+def landed(moves):
+    return [(slot | DIM_BITS[dim], piece) for piece, slot, dim in moves]
+
+
+FIRST = stage_sends(0, ())
+SECOND = stage_sends(1, ())
+SECOND_ON = stage_sends(1, (0,))
+THIRD = stage_sends(2, ())
+THIRD_A = stage_sends(2, (0,))
+THIRD_B = stage_sends(2, (1,))
+THIRD_C = stage_sends(2, (0, 1))
+MOVES = FIRST + SECOND + SECOND_ON + THIRD + THIRD_A + THIRD_B + THIRD_C
+
+
+def muon_kernel(
+    stats_ref,
+    red_hid_ref,
+    mom_hid_ref,
+    red_in_ref,
+    mom_in_ref,
+    hid_ref,
+    inp_ref,
+    next_hid_ref,
+    next_in_ref,
+    norm_ref,
+    codes,
+    tops,
+    lows,
+    scales,
+    xs,
+    us,
+    vs,
+    lhs,
+    xin,
+    xin_top,
+    xin_low,
+    gram,
+    gram_got,
+    back,
+    sums,
+    sums_got,
+    send_sems,
+    core_sems,
+    recv_sems,
+    back_send,
+    back_recv,
+    sums_send,
+    sums_recv,
+    spread_send,
+    spread_recv,
+    pair_send,
+    pair_recv,
+):
+    blk = lax.axis_index("blk")
+    col = lax.axis_index("col")
+    rows, wide = xs.shape
+    height = back.shape[2]
+    part_wide = inp_ref.shape[1]
+    other_core = {"col": col + 1 - 2 * (col % 2)}
+    dims = (
+        {"blk": blk + 1 - 2 * (blk % 2)},
+        {"col": (col + 2) % 4},
+        {"blk": blk + 2 - 4 * ((blk // 2) % 2)},
+    )
+    far = {"blk": (blk + 4) % 8}
+    diagonal = {"blk": 4 * (blk // 4) + 3 - blk % 4}
+    barrier = pltpu.get_barrier_semaphore()
+    for target in (other_core, dims[1], *({"blk": (blk + away) % 8} for away in range(1, 8))):
+        pl.semaphore_signal(barrier, inc=1, device_id=target, device_id_type=MESH)
+
+    def fold(values):
+        line = jnp.sum(values, axis=0, keepdims=True)
+        return sum(line[:, lane : lane + 128] for lane in range(0, line.shape[1], 128))
+
+    share = 0.125
+    sums[0, 0:1, :] = fold(stats_ref[...])
+    sums[0, 1:2, :] = fold(mom_hid_ref[...] * mom_hid_ref[...])
+    sums[0, 2:3, :] = fold(mom_hid_ref[...] * red_hid_ref[...])
+    sums[0, 3:4, :] = fold(red_hid_ref[...] * red_hid_ref[...])
+    sums[0, 4:5, :] = fold(mom_in_ref[...] * mom_in_ref[...]) * share
+    sums[0, 5:6, :] = fold(mom_in_ref[...] * red_in_ref[...]) * share
+    sums[0, 6:7, :] = fold(red_in_ref[...] * red_in_ref[...]) * share
+    sums[0, 7:8, :] = jnp.zeros((1, 128), F32)
+    for turn in range(2):
+        codes[turn, 0, rows:, :] = jnp.zeros((codes.shape[2] - rows, wide), I16)
+    eye = lax.broadcasted_iota(jnp.int32, (rows, rows), 0) == lax.broadcasted_iota(
+        jnp.int32, (rows, rows), 1
+    )
+    pl.semaphore_wait(barrier, 9)
+
+    for number, target in enumerate((other_core, *dims, far)):
+        copy = pltpu.make_async_remote_copy(
+            src_ref=sums.at[number],
+            dst_ref=sums_got.at[number],
+            send_sem=sums_send.at[number],
+            recv_sem=sums_recv.at[number],
+            device_id=target,
+            device_id_type=MESH,
+        )
+        copy.start()
+        copy.wait()
+        sums[number + 1] = sums[number] + sums_got[number]
+    whole = jnp.sum(sums[5], axis=1, keepdims=True)
+    clip = jnp.sqrt(whole[0:1])
+    factor = jnp.minimum(1.0, CLIP / clip)
+
+    def norm_of(first):
+        square = (
+            0.25 * whole[first : first + 1]
+            + factor * whole[first + 1 : first + 2]
+            + factor * factor * whole[first + 2 : first + 3]
+        )
+        return 1.0 / (jnp.sqrt(jnp.maximum(square, 0.0)) + 1e-07)
+
+    norm_ref[0:4, :] = jnp.broadcast_to(clip, (4, 128))
+    norm_ref[4:8, :] = jnp.broadcast_to(factor, (4, 128))
+    next_hid_ref[...] = 0.5 * mom_hid_ref[...] + factor * red_hid_ref[...]
+    next_in_ref[...] = 0.5 * mom_in_ref[...] + factor * red_in_ref[...]
+
+    my_lanes = pl.ds(pl.multiple_of(blk * height, height), height)
+    spread = []
+    for away in range(1, 8):
+        target = (blk + away) % 8
+        spread.append(
+            pltpu.make_async_remote_copy(
+                src_ref=next_hid_ref.at[
+                    pl.ds(pl.multiple_of(target % 4 * rows, rows), rows), :
+                ],
+                dst_ref=xs.at[:, my_lanes],
+                send_sem=spread_send.at[away - 1],
+                recv_sem=spread_recv.at[away - 1],
+                device_id={"blk": target},
+                device_id_type=MESH,
+            )
+        )
+        spread[-1].start()
+    high = col // 2
+    my_half = pl.ds(pl.multiple_of(high * part_wide, part_wide), part_wide)
+    half_copy = pltpu.make_async_remote_copy(
+        src_ref=next_in_ref,
+        dst_ref=xin.at[:, my_half],
+        send_sem=pair_send.at[0],
+        recv_sem=pair_recv.at[0],
+        device_id=dims[1],
+        device_id_type=MESH,
+    )
+    half_copy.start()
+    xs[:, my_lanes] = next_hid_ref[pl.ds(pl.multiple_of(blk % 4 * rows, rows), rows), :]
+    xin[:, my_half] = next_in_ref[...]
+    for copy in spread:
+        copy.wait_recv()
+    xs[...] = xs[...] * norm_of(1)
+    in_scale = norm_of(4)
+
+    numbers = {move: number for number, move in enumerate(MOVES)}
+
+    def part(turn, slot, piece):
+        return codes.at[turn, slot, pl.ds(piece * PIECE, PIECE), :]
+
+    def send(turn, move):
+        piece, slot, dim = move
+        return pltpu.make_async_remote_copy(
+            src_ref=part(turn, slot, piece),
+            dst_ref=part(turn, slot | DIM_BITS[dim], piece),
+            send_sem=send_sems.at[numbers[move]],
+            recv_sem=recv_sems.at[turn, slot | DIM_BITS[dim], piece],
+            device_id=dims[dim],
+            device_id_type=MESH,
+        )
+
+    def send_all(turn, moves):
+        for move in moves:
+            send(turn, move).start()
+
+    def to_core(turn, slot, piece):
+        return pltpu.make_async_remote_copy(
+            src_ref=part(turn, slot, piece),
+            dst_ref=part(turn, slot + 1, piece),
+            send_sem=core_sems.at[slot // 2, piece],
+            recv_sem=recv_sems.at[turn, slot + 1, piece],
+            device_id=other_core,
+            device_id_type=MESH,
+        )
+
+    def arrived(turn, slot, piece):
+        pltpu.make_async_remote_copy(
+            src_ref=part(turn, slot, piece),
+            dst_ref=part(turn, slot, piece),
+            send_sem=core_sems.at[0, 0],
+            recv_sem=recv_sems.at[turn, slot, piece],
+            device_id=other_core,
+            device_id_type=MESH,
+        ).wait_recv()
+
+    def forward(turn, moves, on=()):
+        for number, (slot, piece) in enumerate(landed(moves)):
+            arrived(turn, slot, piece)
+            to_core(turn, slot, piece).start()
+            if on:
+                send(turn, on[number]).start()
+
+    def gram_copy():
+        return pltpu.make_async_remote_copy(
+            src_ref=gram,
+            dst_ref=gram_got,
+            send_sem=pair_send.at[1],
+            recv_sem=pair_recv.at[1],
+            device_id=other_core,
+            device_id_type=MESH,
+        )
+
+    def unpack(turn, pair, light):
+        for core in range(2):
+            here = slice(core * rows, (core + 1) * rows)
+            whole = from_codes(codes[turn, 2 * pair + core, 0:rows, :])
+            if light:
+                tops[pair, here, :] = whole.astype(BF16)
+            else:
+                top, low = halves(whole)
+                tops[pair, here, :] = top
+                lows[pair, here, :] = low
+            step = from_codes(codes[turn, 2 * pair + core, rows : rows + 16, 0:rows])
+            size = code_scale(step[0:8, :]) * (1.0 / TOP_CODE)
+            scales[pair, :, here] = size * size
+
+    def apply_pair(pair, out, light):
+        cut = 512
+        if light:
+            inner = (dot_nt(lhs[0:rows, :], tops[pair]) * scales[pair, 0:1, :]).astype(BF16)
+            for start in range(0, wide, cut):
+                lanes = slice(start, start + cut)
+                out[:, lanes] += dot_nn(inner, tops[pair, :, lanes])
+            return
+        both = dot_nt(lhs[...], tops[pair])
+        inner = both[:rows] + both[rows:] + dot_nt(lhs[0:rows, :], lows[pair])
+        inner = inner * scales[pair, 0:1, :]
+        top, low = halves(inner)
+        stack = jnp.concatenate([top, low], axis=0)
+        for start in range(0, wide, cut):
+            lanes = slice(start, start + cut)
+            both = dot_nn(stack, tops[pair, :, lanes])
+            out[:, lanes] += both[:rows] + both[rows:] + dot_nn(top, lows[pair, :, lanes])
+
+    def set_lhs(values):
+        top, low = halves(values)
+        lhs[0:rows, :] = top
+        lhs[rows:, :] = low
+
+    def input_gram(light):
+        top, low = halves(xin[...])
+        xin_top[...] = top
+        if light:
+            gram[...] = dot_nt(xin_top[...], xin_top[...])
+        else:
+            xin_low[...] = low
+            cross = dot_nt(xin_top[...], xin_low[...])
+            gram[...] = dot_nt(xin_top[...], xin_top[...]) + (cross + jnp.transpose(cross))
+        gram_copy().start()
+
+    def input_step(light):
+        gram_copy().wait()
+        square_of = gram[...] + gram_got[...]
+        top, low = halves(square_of)
+        if light:
+            poly = NS_B * square_of + NS_C * dot_nn(top, top)
+        else:
+            cross = dot_nn(top, low)
+            poly = NS_B * square_of + NS_C * (dot_nn(top, top) + (cross + jnp.transpose(cross)))
+        top, low = halves(poly)
+        cut = 512
+        for start in range(0, xin.shape[1], cut):
+            lanes = slice(start, start + cut)
+            change = dot_nn(top, xin_top[:, lanes])
+            if not light:
+                change = change + dot_nn(low, xin_top[:, lanes]) + dot_nn(top, xin_low[:, lanes])
+            xin[:, lanes] = NS_A * xin[:, lanes] + change
+
+    def by_weight(number, limit, work):
+        @pl.when(number < limit)
+        def _():
+            work(True)
+
+        @pl.when(number >= limit)
+        def _():
+            work(False)
+
+    def iteration(number, carry):
+        turn = number % 2
+        values = xs[...]
+        largest = jnp.max(jnp.abs(values), axis=1, keepdims=True)
+        step = scale_code(largest)
+        codes[turn, 0, 0:rows, :] = to_codes(values * (TOP_CODE / code_scale(step)))
+        lane_step = jnp.sum(jnp.where(eye, step, 0.0), axis=0, keepdims=True)
+        codes[turn, 0, rows : rows + 16, 0:rows] = jnp.broadcast_to(
+            lane_step.astype(jnp.int32), (16, rows)
+        ).astype(I16)
+        send_all(turn, FIRST)
+        for piece in range(3):
+            to_core(turn, 0, piece).start()
+        send_all(turn, SECOND)
+        set_lhs(values)
+        us[...] = jnp.zeros_like(us)
+        vs[...] = jnp.zeros_like(vs)
+
+        def first_pass(index, carry):
+            pair = index + (index // 3) * (1 - index // 4) - (index // 4) * (1 - index // 5)
+
+            @pl.when(index == 1)
+            def _():
+                forward(turn, FIRST, SECOND_ON)
+                send_all(turn, THIRD)
+                send_all(turn, THIRD_A)
+
+                @pl.when(number > 0)
+                def _():
+                    by_weight(number, LIGHT_IN, input_gram)
+
+                forward(turn, SECOND, THIRD_B)
+                forward(turn, SECOND_ON, THIRD_C)
+
+                @pl.when(number > 0)
+                def _():
+                    by_weight(number, LIGHT_IN, input_step)
+
+                forward(turn, THIRD)
+
+            @pl.when(index == 4)
+            def _():
+                forward(turn, THIRD_A)
+                forward(turn, THIRD_B)
+
+            @pl.when((index == 6) & (number == 0))
+            def _():
+                half_copy.wait()
+                xin[...] = xin[...] * in_scale
+                input_gram(True)
+                input_step(True)
+
+            @pl.when(index == 7)
+            def _():
+                forward(turn, THIRD_C)
+
+            for piece in range(3):
+                arrived(turn, 2 * pair + 1, piece)
+
+            def work(light):
+                unpack(turn, pair, light)
+                apply_pair(pair, us, light)
+
+            by_weight(number, LIGHT_HID, work)
+            return carry
+
+        lax.fori_loop(0, 8, first_pass, 0)
+        set_lhs(us[...])
+
+        def second_pass(pair, carry):
+            by_weight(number, LIGHT_HID, lambda light: apply_pair(pair, vs, light))
+            return carry
+
+        lax.fori_loop(0, 8, second_pass, 0)
+        xs[...] = NS_A * xs[...] + NS_B * us[...] + NS_C * vs[...]
+        for move in MOVES:
+            send(turn, move).wait_send()
+        for pair in range(8):
+            for piece in range(3):
+                to_core(turn, 2 * pair, piece).wait_send()
+        return carry
+
+    lax.fori_loop(0, NS, iteration, 0)
+
+    place = blk % 4
+    copies = []
+    for rel, target in ((1, dims[0]), (2, dims[2]), (3, diagonal)):
+        copies.append(
+            pltpu.make_async_remote_copy(
+                src_ref=xs.at[:, pl.ds(pl.multiple_of(target["blk"] * height, height), height)],
+                dst_ref=back.at[place],
+                send_sem=back_send.at[rel - 1],
+                recv_sem=back_recv.at[rel - 1],
+                device_id=target,
+                device_id_type=MESH,
+            )
+        )
+        copies[-1].start()
+    hid_ref[place] = xs[:, my_lanes]
+    inp_ref[...] = xin[:, my_half]
+    for copy in copies:
+        copy.wait_recv()
+    for target in (dims[0], dims[2], diagonal):
+        other = target["blk"] % 4
+        hid_ref[other] = back[other]
+    for copy in copies + spread:
+        copy.wait_send()
+
+
+def muon(stats, red_hid, mom_hid, red_in, mom_in, wide):
+    rows = red_hid.shape[0] // 4
+    height = red_hid.shape[1]
+    deep, part_wide = red_in.shape
+    vmem = pl.BlockSpec(memory_space=pltpu.VMEM)
+    sem = pltpu.SemaphoreType.DMA
+    return pl.pallas_call(
+        muon_kernel,
+        out_shape=(
+            jax.ShapeDtypeStruct((4, rows, height), F32),
+            jax.ShapeDtypeStruct((deep, part_wide), F32),
+            jax.ShapeDtypeStruct(red_hid.shape, F32),
+            jax.ShapeDtypeStruct(red_in.shape, F32),
+            jax.ShapeDtypeStruct((8, 128), F32),
+        ),
+        in_specs=[vmem] * 5,
+        out_specs=(vmem,) * 5,
+        scratch_shapes=[
+            pltpu.VMEM((2, 16, 3 * PIECE, wide), I16),
+            pltpu.VMEM((8, 2 * rows, wide), BF16),
+            pltpu.VMEM((8, 2 * rows, wide), BF16),
+            pltpu.VMEM((8, 8, 2 * rows), F32),
+            pltpu.VMEM((rows, wide), F32),
+            pltpu.VMEM((rows, wide), F32),
+            pltpu.VMEM((rows, wide), F32),
+            pltpu.VMEM((2 * rows, wide), BF16),
+            pltpu.VMEM((deep, 2 * part_wide), F32),
+            pltpu.VMEM((deep, 2 * part_wide), BF16),
+            pltpu.VMEM((deep, 2 * part_wide), BF16),
+            pltpu.VMEM((deep, deep), F32),
+            pltpu.VMEM((deep, deep), F32),
+            pltpu.VMEM((4, rows, height), F32),
+            pltpu.VMEM((6, 8, 128), F32),
+            pltpu.VMEM((5, 8, 128), F32),
+            sem((len(MOVES),)),
+            sem((8, 3)),
+            sem((2, 16, 3)),
+            sem((3,)),
+            sem((3,)),
+            sem((5,)),
+            sem((5,)),
+            sem((7,)),
+            sem((7,)),
+            sem((2,)),
+            sem((2,)),
+        ],
+        compiler_params=pltpu.CompilerParams(
+            collective_id=0, has_side_effects=True, vmem_limit_bytes=60 * 1024 * 1024
+        ),
+    )(stats, red_hid, mom_hid, red_in, mom_in)
+
+
 def plain_body(
     frames,
     labels,
@@ -1162,31 +1325,22 @@
     next_res_hidden = next_hid.T
     next_res_input = next_in[:, :deep].T
     red_output = red_out[:scol].T
-    red_hidden = red_hid.T
-    red_input = red_in[:, :deep].T
     vec_sum = vec_sum.reshape(-1)
     red_bias = vec_sum[: bias_row.shape[0]]
     loss_sum = vec_sum[bias_row.shape[0]]
-    share_blk = 1.0 / nblk
-    grad_square = share_blk * jnp.sum(red_bias * red_bias) + jnp.sum(stats)
-    clip_norm = jnp.sqrt(lax.psum(grad_square, ("blk", "col")))
-    factor = jnp.minimum(1.0, CLIP / clip_norm)
-    next_mom_input = 0.5 * mom_input + factor * red_input
-    next_mom_hidden = 0.5 * mom_hidden + factor * red_hidden
-    square_input, square_hidden = lax.psum(
-        (
-            share_blk * jnp.sum(next_mom_input * next_mom_input),
-            jnp.sum(next_mom_hidden * next_mom_hidden),
-        ),
-        ("blk", "col"),
-    )
-    iter_input = next_mom_input / (jnp.sqrt(square_input) + 1e-07)
-    iter_hidden = next_mom_hidden / (jnp.sqrt(square_hidden) + 1e-07)
-    tall = collect_rows(iter_hidden)
-    piece = hcol // 4
-    mine = lax.dynamic_slice_in_dim(tall, (blk_index % 4) * piece, piece, axis=1).T
-    whole_input = spread_cols(jnp.pad(iter_input, ((0, padded - deep), (0, 0))))
-    done_hidden, done_input = muon(mine, whole_input, w_hidden.shape[0], hcol)
+    stats = stats.at[1, 0].set(jnp.sum(red_bias * red_bias) / nblk)
+    done_hidden, done_input, mom_hid_next, mom_in_next, norms = muon(
+        stats,
+        red_hid,
+        mom_hidden.T,
+        red_in.T,
+        jnp.pad(mom_input, ((0, padded - deep), (0, 0))),
+        hcol * ncol,
+    )
+    clip_norm = norms[0, 0]
+    factor = norms[4, 0]
+    next_mom_hidden = mom_hid_next.T
+    next_mom_input = mom_in_next[:deep]
     done_hidden = done_hidden.reshape(hcol, w_hidden.shape[0]).T
     muon_scale = LR_MUON * 0.2 * math.sqrt(hcol * ncol)
     new_input = w_input * (1.0 - LR_MUON * WD_MUON) - muon_scale * done_input[:deep]

time: 1230 us -> 1050 us (0.85)
  waiting for transfers between devices: 434 us -> 343 us
  blocking collectives: 109 us -> 29.6 us
    psum x2 -> x0, blocking collectives: 78.9 us -> none  [the longest x1 40.2 us: fast_body(): lax.psum((share_blk * jnp.sum(next_mom_input * next_mom_input), jnp.sum(n...]
    all_gather x3 -> x2, waiting for transfers between devices: 233 us -> 179 us  [collect_rows(): return lax.all_gather(values, 'blk', axis=0, tiled=True)]
    all_gather x3 -> x2, waiting for transfers between devices: 95.2 us -> 63.2 us  [spread_cols(): return lax.all_gather(values, 'col', axis=1, tiled=True)]
    unnamed x50 -> x52, local copies, waits for them, and re-layouts: 31.2 us -> 34.3 us
  transfers between devices with their start and end apart: 8 -> 6, of which waited for: 8 -> 6; matrix products, arithmetic and copies ran while one was open for 5% -> 4% of each run, Pallas kernels for 0% -> 0%
where the time goes in v3:
time: 1050 us; the launch traced here: 1040 us
  Pallas kernels  486 us (46%)
  waiting for transfers between devices  343 us (33%)
  local copies, waits for them, and re-layouts  77.8 us (7%)
  matrix products  49.6 us (5%)
  other arithmetic  36.8 us (4%)
  blocking collectives  29.6 us (3%)
  between operations  15.5 us (1%)
    pallas_call x1, Pallas kernels, muon(): pl.pallas_call(muon_kernel, out_shape=(jax.ShapeDtypeStruct((4, rows, hei...  298 us
    pallas_call x1, Pallas kernels, reduce_grads(): pl.pallas_call(functools.partial(reduce_kernel, deep), out_shape=(jax.Sha...  187 us
    all_gather x2, waiting for transfers between devices, collect_rows(): return lax.all_gather(values, 'blk', axis=0, tiled=True)  179 us
    reduce_scatter x2, waiting for transfers between devices, reduce_cols(): return lax.psum_scatter(values, 'col', scatter_dimension=1, tiled=True)  101 us
    all_gather x2, waiting for transfers between devices, spread_cols(): return lax.all_gather(values, 'col', axis=1, tiled=True)  63.2 us
    unnamed x52, local copies, waits for them, and re-layouts  34.3 us
    dot_general x3, matrix products, matmul(): return jnp.dot(left_side, right_side, preferred_element_type=jnp.float32)  27.9 us
    dot_general x2, matrix products, outer_cols(): lax.dot_general(left_side, right_side, (((1,), (1,)), ((), ())), preferre...  21.7 us
  transfers between devices with their start and end apart: 6, of which 6 were waited for; matrix products, arithmetic and copies ran while one was open for 4% of the time, Pallas kernels for 0%

profile of v3, /device:TPU:0, one launch (start us, length us, event | category | flops | bytes accessed | tf_op | source)
XLA Modules:
  0.0 1037.8 jit_solution(12242534947712786887)
XLA Ops:
  9.8 11.7 %all_gather.19 = bf16[1024,440]{1,0:T(8,128)(2,1)S(1)} all-gather(bf16[256,440]{1,0:T(8,128)(2,1)} %bitcast.67), channel_id=1, replica_groups=mesh['blk'=8,'col'=4] {'col'}, dimensions={0}, use_global_device_ids=true | all-gather | bytes 1126400 | tf_op jit(solution)/shard_map/all_gather | solution.py:1273
  25.8 36.9 %all-gather.8.cloned.1.call-done = bf16[2048,512]{1,0:T(8,128)(2,1)} async-done(((bf16[256,512]{1,0:T(8,128)(2,1)}), bf16[2048,512]{1,0:T(8,128)(2,1)}) %all-gather.8.cloned.1.call-update) | async-done | bytes 2097168 | tf_op jit(solution)/shard_map/all_gather | solution.py:64
  62.7 35.1 %all-gather.6.cloned.1.call-done = bf16[1024,2048]{0,1:T(8,128)(2,1)} async-done(((bf16[1024,512]{0,1:T(8,128)(2,1)}), bf16[1024,2048]{0,1:T(8,128)(2,1)}) %all-gather.6.cloned.1.call-update) | async-done | bytes 4194320 | tf_op jit(solution)/shard_map/all_gather | solution.py:56
  97.9 7.3 fusion.7
  111.8 28.1 %all-gather.10.cloned.1.call-done = bf16[1024,2048]{0,1:T(8,128)(2,1)} async-done(((bf16[1024,512]{0,1:T(8,128)(2,1)}), bf16[1024,2048]{0,1:T(8,128)(2,1)}) %all-gather.10.cloned.1.call-update) | async-done | bytes 4194320 | tf_op jit(solution)/shard_map/all_gather | solution.py:56
  139.9 141.9 %all-gather.12.cloned.1.call-done = bf16[2048,2326]{0,1:T(8,128)(2,1)} async-done(((bf16[256,2326]{0,1:T(8,128)(2,1)}), bf16[2048,2326]{0,1:T(8,128)(2,1)}) %all-gather.12.cloned.1.call-update) | async-done | bytes 9527312 | tf_op jit(solution)/shard_map/all_gather | solution.py:64
  281.7 16.3 %add_reduce_fusion = (f32[1024]{0:T(1024)S(1)}, f32[1024,2326]{0,1:T(8,128)}) fusion(f32[2326]{0:T(1024)S(1)} %slice_reduce_fusion, bf16[1024,2048]{0,1:T(8,128)(2,1)} %all-gather.10.cloned.1.call-done, bf16[2048,2326]{0,1:T(8,128)(2,1)} %all-gather.12.cloned.1.call-done), kind=kOutput, calls=%fused_computation.7 | convolution fusion | flops 9760713728 | bytes 23262296 | tf_op jit(solution)/shard_map/dot_general | solution.py:34
  298.0 6.1 pmax.7
  304.2 5.8 select_reduce_fusion
  309.9 6.7 all-reduce.6
  316.6 7.0 convert_reduce_fusion
  325.9 16.0 %fusion.8 = f32[1024,2048]{0,1:T(8,128)} fusion(bf16[1024,2326]{0,1:T(8,128)(2,1)S(1)} %get-tuple-element.109, bf16[2048,2326]{0,1:T(8,128)(2,1)} %all-gather.12.cloned.1.call-done), kind=kOutput, calls=%fused_computation.44 | convolution fusion | flops 9755951104 | bytes 22679552 | tf_op jit(solution)/shard_map/dot_general | solution.py:44
  342.0 69.6 %reduce-scatter.3.cloned.1.call-done = f32[1024,512]{0,1:T(8,128)} async-done(((f32[1024,2048]{0,1:T(8,128)}), f32[1024,512]{0,1:T(8,128)}) %reduce-scatter.3.cloned.1.call-update) | async-done | bytes 2097168 | tf_op jit(solution)/shard_map/reduce_scatter | solution.py:60
  414.4 5.7 fusion.9
  431.2 11.0 %pad_bitcast_fusion.res_out_ref = bf16[2368,2048]{1,0:T(8,128)(2,1)} fusion(bf16[2048,2326]{0,1:T(8,128)(2,1)} %bitcast.57), kind=kLoop, calls=%fused_computation | loop fusion | bytes 19226624 | tf_op jit(solution)/shard_map/transpose | solution.py:1313
  442.2 6.5 copy.67.h_one_ref
  448.7 6.4 copy.66.h_two_ref
  455.8 5.3 pad_bitcast_fusion.1.dl_ref
  461.1 31.0 %reduce-scatter.5.cloned.1.call-done = f32[1024,512]{0,1:T(8,128)} async-done(((f32[1024,2048]{0,1:T(8,128)}), f32[1024,512]{0,1:T(8,128)}) %reduce-scatter.5.cloned.1.call-update) | async-done | bytes 2097168 | tf_op jit(solution)/shard_map/reduce_scatter | solution.py:60
  496.2 187.3 %shard_map.271 = (f32[2326,1,2048]{2,1,0:T(1,128)}, f32[512,2048]{1,0:T(8,128)}, f32[512,512]{1,0:T(8,128)}, f32[2368,256]{1,0:T(8,128)}, f32[512,256]{1,0:T(8,1...) custom-call(bf16[2368,1024]{1,0:T(8,128)(2,1)} %pad_bitcast_fusion.1.dl_ref, ...), custom_call_target="tpu_custom_call" | custom-call | tf_op jit(solution)/shard_map/pallas_call | solution.py:583
  690.7 298.4 %shard_map.272 = (f32[4,128,256]{2,1,0:T(8,128)}, f32[512,512]{1,0:T(8,128)}, f32[512,256]{1,0:T(8,128)}, f32[512,512]{1,0:T(8,128)}, f32[8,128]{1,0:T(8,128)}) custom-call(f32[8,128]{1,0:T(8,128)} %scatter.4.stats_ref, f32[512,256]{1,0:T(8,128)} %get-tuple-element.42.red_hid_ref, f32[512,256]{1,0:T(8,128)} %bitcast.65, f32[512,512]{1,0:T(8,128)} %bitcast.62, ...), custom_call_target="tpu_custom_call" | custom-call | tf_op jit(solution)/shard_map/pallas_call | solution.py:1048
  996.4 5.3 copy.73
  1004.4 9.1 multiply_subtract_fusion
  1014.2 16.3 %copy.80 = f32[1,2048,2326]{1,0,2:T(1,128)} copy(f32[1,2048,2326]{1,0,2:T(1,128)} %bitcast.56) | data formatting | bytes 38109184
  (93 shorter events, 51.5 us)
Async XLA Ops:
  7.2 55.6 %all-gather.8.cloned.1.call-start = ((), (), s32[]{:S(2)}) async-start(), calls=%async_computation.3 | async-start | bytes 2359296 | tf_op jit(solution)/shard_map/all_gather | solution.py:64
  9.0 88.8 %all-gather.6.cloned.1.call-start = ((), (), s32[]{:S(2)}) async-start(), calls=%async_computation.2 | async-start | bytes 5242880 | tf_op jit(solution)/shard_map/all_gather | solution.py:56
  21.5 4.3 copy-start.4
  25.8 114.1 %all-gather.10.cloned.1.call-start = ((), (), s32[]{:S(2)}) async-start(), calls=%async_computation.4 | async-start | bytes 5242880 | tf_op jit(solution)/shard_map/all_gather | solution.py:56
  97.9 7.4 copy-start.1
  105.2 6.5 copy-start.15
  105.2 176.5 %all-gather.12.cloned.1.call-start = ((), (), s32[]{:S(2)}) async-start(), calls=%async_computation.5 | async-start | bytes 10727424 | tf_op jit(solution)/shard_map/all_gather | solution.py:64
  106.5 305.1 %reduce-scatter.3.cloned.1.call-start = ((), (), s32[]{:S(2)}) async-start(), calls=%async_computation.6 | async-start | bytes 10485760 | tf_op jit(solution)/shard_map/reduce_scatter | solution.py:60
  323.6 2.2 copy-start
  341.9 150.1 %reduce-scatter.5.cloned.1.call-start = ((), (), s32[]{:S(2)}) async-start(), calls=%async_computation.7 | async-start | bytes 10485760 | tf_op jit(solution)/shard_map/reduce_scatter | solution.py:60
  411.6 2.9 copy-start.21
  414.3 5.8 copy-start.3
  425.9 3.4 copy-start.9
  455.8 36.2 %copy-start.6 = (f32[1024,512]{0,1:T(8,128)S(1)}, f32[1024,512]{0,1:T(8,128)}, u32[]{:S(2)}) copy-start(f32[1024,512]{0,1:T(8,128)} %get-tuple-element.121) | copy-start | bytes 6291460
  686.1 304.3 %copy-start.14 = (f32[32,128]{1,0:T(8,128)S(1)}, f32[32,128]{1,0:T(8,128)}, u32[]{:S(2)}) copy-start(f32[32,128]{1,0:T(8,128)} %get-tuple-element.40) | copy-start | bytes 49156
  690.7 301.7 %copy-start.7 = (f32[256,512]{1,0:T(8,128)S(1)}, f32[256,512]{1,0:T(8,128)}, u32[]{:S(2)}) copy-start(f32[256,512]{1,0:T(8,128)} %param.22) | copy-start | bytes 1572868
  989.1 4.2 copy-start.10
  989.1 4.2 copy-start.12
  992.4 2.0 copy-start.11
  993.3 2.1 copy-start.13
  1001.7 2.7 copy-start.2
  1004.4 9.1 copy-start.16
  1004.4 9.1 copy-start.17
  1004.4 9.1 copy-start.18
  (4 other events, 5.8 us)
Sparse Core Ops, SparseCore 0:
  10.7 51.9 all-gather.7
  64.9 32.9 all-gather.5
  105.3 34.4 all-gather.9
  142.3 139.3 all-gather.11
  342.1 69.4 reduce-scatter.2
  420.3 71.6 reduce-scatter.4

commit v4 on v3

--- a/solution.py
+++ b/solution.py
@@ -629,6 +629,383 @@
     )(dl, h_two, res_out, dz_two, h_one, res_hid, dz_one, x, res_in, vec)
 
 
+RING_STARTS = (0, 2, 5, 7, 9)
+LAYER_TWO_WAVE = 7
+LOGIT_WAVES = (11, 12, 14, 16)
+
+
+def forward_kernel(
+    slot_count,
+    x_ref,
+    tags_ref,
+    w_in_ref,
+    w_hid_ref,
+    w_out_ref,
+    bias_ref,
+    bias_out_ref,
+    x_out,
+    h_one_out,
+    h_two_out,
+    slope_one_out,
+    slope_two_out,
+    w_hid_out,
+    w_out_out,
+    dl_ref,
+    bias_sum_ref,
+    loss_ref,
+    x_all,
+    h_one,
+    h_two,
+    slope_one,
+    slope_two,
+    w_in,
+    w_hid,
+    w_out,
+    curve,
+    bias_col,
+    tags,
+    sums,
+    ring_send,
+    ring_recv,
+    x_send,
+    x_recv,
+    h_send,
+    h_recv,
+    tag_send,
+    tag_recv,
+    sum_send,
+    sum_recv,
+    out_sems,
+):
+    blk = lax.axis_index("blk")
+    col = lax.axis_index("col")
+    here = ring_place(blk)
+    senones, depth = w_out_ref.shape
+    own_rows, deep = x_ref.shape
+    units = w_hid_ref.shape[1]
+    frames = x_all.shape[0]
+    cores = {"col": col + 1 - 2 * (col % 2)}
+    across = {"col": (col + 2) % 4}
+    corner = {"col": (col + 2) % 4 + 1 - 2 * (col % 2)}
+    others = (cores, across, corner)
+
+    barrier = pltpu.get_barrier_semaphore()
+    for target in others + tuple({"blk": ring_blk((here + way) % RING)} for way in (1, 7)):
+        pl.semaphore_signal(barrier, inc=1, device_id=target, device_id_type=MESH)
+
+    w_hid[pl.ds(pl.multiple_of(blk * depth, depth), depth), :] = w_hid_ref[...].astype(BF16)
+    own_lanes = pl.ds(pl.multiple_of(blk * depth, depth), depth)
+    w_out[senones // 16 * 16 :, own_lanes] = jnp.zeros(
+        (w_out.shape[0] - senones // 16 * 16, depth), BF16
+    )
+    w_out[0:senones, own_lanes] = w_out_ref[...].astype(BF16)
+    own_frames = pl.ds(pl.multiple_of(col * own_rows, own_rows), own_rows)
+    x_all[own_frames, :] = jnp.zeros((own_rows, x_all.shape[1]), BF16)
+    x_all[own_frames, 0:deep] = x_ref[...]
+    tags[col] = tags_ref[...]
+    sums[...] = jnp.zeros_like(sums)
+    pl.semaphore_wait(barrier, 5)
+
+    def ring_part(group, origin, way):
+        start = pl.multiple_of(origin * depth + way * 128, 128)
+        if group == 0:
+            return w_hid.at[pl.ds(start, 128), :]
+        return w_out.at[pl.ds((group - 1) * OUT_ROWS, OUT_ROWS), pl.ds(start, 128)]
+
+    def ring_move(group, step, way):
+        origin = ring_blk((here - step + 2 * step * way + RING) % RING)
+        part = ring_part(group, origin, way)
+        return pltpu.make_async_remote_copy(
+            src_ref=part,
+            dst_ref=part,
+            send_sem=ring_send.at[group, way, step],
+            recv_sem=ring_recv.at[group, way, step],
+            device_id={"blk": ring_blk((here + 1 - 2 * way + RING) % RING)},
+            device_id_type=MESH,
+        )
+
+    def ring_wave(wave):
+        for group, start in enumerate(RING_STARTS):
+            step = wave - 1 - start
+            for way in range(2):
+                if step == -1:
+                    ring_move(group, 0, way).start()
+                if 0 <= step < STEPS:
+                    ring_move(group, step, way).wait_recv()
+                    if step < STEPS - 1:
+                        ring_move(group, step + 1, way).start()
+
+    def copy_to(target, src, send_sem, recv_sem):
+        return pltpu.make_async_remote_copy(
+            src_ref=src,
+            dst_ref=src,
+            send_sem=send_sem,
+            recv_sem=recv_sem,
+            device_id=target,
+            device_id_type=MESH,
+        )
+
+    def rows_of(owner):
+        return pl.ds(pl.multiple_of(owner * own_rows, own_rows), own_rows)
+
+    def lanes_of(owner):
+        return pl.ds(pl.multiple_of(owner * units, units), units)
+
+    def x_move(number):
+        owner = across["col"] if number == 2 else col
+        target = across if number == 1 else cores
+        return copy_to(target, x_all.at[rows_of(owner), :], x_send.at[number], x_recv.at[number])
+
+    def h_move(layer, number, block):
+        owner = across["col"] if number == 2 else col
+        target = across if number == 1 else cores
+        whole = (h_one, h_two)[layer]
+        part = whole.at[pl.ds(block * own_rows, own_rows), lanes_of(owner)]
+        return copy_to(
+            target, part, h_send.at[layer, number, block], h_recv.at[layer, number, block]
+        )
+
+    def h_start(layer, block):
+        h_move(layer, 0, block).start()
+        h_move(layer, 1, block).start()
+
+    def h_forward(layer, block):
+        h_move(layer, 1, block).wait_recv()
+        h_move(layer, 2, block).start()
+
+    def h_ready(layer, block):
+        h_move(layer, 0, block).wait_recv()
+        h_move(layer, 2, block).wait_recv()
+
+    ring_wave(0)
+    x_move(0).start()
+    x_move(1).start()
+    tag_copies = [
+        copy_to(target, tags.at[col], tag_send.at[number], tag_recv.at[number])
+        for number, target in enumerate(others)
+    ]
+    for copy in tag_copies:
+        copy.start()
+    w_in[...] = jnp.zeros_like(w_in)
+    w_in[0:deep, :] = w_in_ref[...].astype(BF16)
+    for number in range(bias_out_ref.shape[0]):
+        line = jnp.broadcast_to(bias_out_ref[number : number + 1, :], (128, 128))
+        bias_col[number * 128 : (number + 1) * 128, :] = jnp.transpose(line)
+    ring_wave(1)
+    x_move(1).wait_recv()
+    x_move(2).start()
+    x_move(0).wait_recv()
+    x_move(2).wait_recv()
+
+    def layer(number, block, inputs, weights, whole, slopes):
+        there = slice(block * own_rows, (block + 1) * own_rows)
+        value = jax.nn.sigmoid(
+            dot_nn(inputs[there, :], weights[...]) + bias_ref[number : number + 1, :]
+        )
+        slopes[there, :] = value * (1.0 - value)
+        whole[there, lanes_of(col)] = value.astype(BF16)
+        h_start(number, block)
+
+    outs = []
+
+    def put(src, dst):
+        copy = pltpu.make_async_copy(src, dst, out_sems.at[len(outs)])
+        copy.start()
+        outs.append(copy)
+
+    for block in range(4):
+        layer(0, block, x_all, w_in, h_one, slope_one)
+    put(x_all, x_out)
+    put(slope_one, slope_one_out)
+
+    def all_tags():
+        return jnp.concatenate([tags[owner, 0:1, :] for owner in range(4)], axis=1)
+
+    def own_row(line):
+        line = line - col * senones
+        return jnp.where(line < senones, line, -1)
+
+    def logits(group):
+        first = group * OUT_ROWS
+        half = frames // 2
+        for part in range(2):
+            curve[first : first + OUT_ROWS, part * half : (part + 1) * half] = dot_nt(
+                w_out[first : first + OUT_ROWS, :], h_two[part * half : (part + 1) * half, :]
+            )
+        base = lax.broadcasted_iota(jnp.int32, (16, frames), 0)
+
+        def largest(number, top):
+            row = pl.multiple_of(first + number * 16, 16)
+            value = curve[pl.ds(row, 16), :] + bias_col[pl.ds(row, 16), 0:1]
+            if group == OUT_GROUPS - 1:
+                value = jnp.where(base + row < senones, value, -1e30)
+            curve[pl.ds(row, 16), :] = value
+            return jnp.maximum(top, value)
+
+        top = lax.fori_loop(0, OUT_ROWS // 16, largest, jnp.full((16, frames), -1e30, F32))
+        top = jnp.max(top, axis=0, keepdims=True)
+        line = jnp.broadcast_to(own_row(all_tags()), (16, frames))
+
+        def exponents(number, carry):
+            total, picked = carry
+            row = pl.multiple_of(first + number * 16, 16)
+            value = curve[pl.ds(row, 16), :]
+            power = jnp.exp(value - top)
+            curve[pl.ds(row, 16), :] = power
+            return total + power, picked + jnp.where(base + row == line, value, 0.0)
+
+        blank = jnp.zeros((16, frames), F32)
+        total, picked = lax.fori_loop(0, OUT_ROWS // 16, exponents, (blank, blank))
+        sums[col, group : group + 1, :] = top
+        sums[col, 4 + group : 5 + group, :] = jnp.sum(total, axis=0, keepdims=True)
+        sums[col, 8 + group : 9 + group, :] = jnp.sum(picked, axis=0, keepdims=True)
+
+    last_wave = RING_STARTS[-1] + STEPS
+    for wave in range(2, last_wave + 1):
+        ring_wave(wave)
+        if 2 <= wave < 6:
+            h_forward(0, wave - 2)
+        if wave == LAYER_TWO_WAVE:
+            for block in range(4):
+                h_ready(0, block)
+                layer(1, block, h_one, w_hid, h_two, slope_two)
+            put(h_one, h_one_out)
+            put(slope_two, slope_two_out)
+            put(w_hid, w_hid_out)
+        if LAYER_TWO_WAVE < wave <= LAYER_TWO_WAVE + 4:
+            h_forward(1, wave - LAYER_TWO_WAVE - 1)
+        for group, when in enumerate(LOGIT_WAVES):
+            if wave == when:
+                if group == 0:
+                    for block in range(4):
+                        h_ready(1, block)
+                    put(h_two, h_two_out)
+                    for copy in tag_copies:
+                        copy.wait_recv()
+                rows = pl.ds(group * OUT_ROWS, OUT_ROWS)
+                put(w_out.at[rows, :], w_out_out.at[rows, :])
+                logits(group)
+
+    sum_copies = [
+        copy_to(target, sums.at[col], sum_send.at[number], sum_recv.at[number])
+        for number, target in enumerate(others)
+    ]
+    for copy in sum_copies:
+        copy.start()
+    for copy in sum_copies:
+        copy.wait_recv()
+
+    def lines(first):
+        return [sums[owner, first + group : first + group + 1, :] for owner in range(4) for group in range(4)]
+
+    tops = lines(0)
+    top = functools.reduce(jnp.maximum, tops)
+    total = functools.reduce(
+        jnp.add, [size * jnp.exp(own - top) for own, size in zip(tops, lines(4), strict=True)]
+    )
+    picked = functools.reduce(jnp.add, lines(8))
+    line = all_tags()
+    live = line >= 0
+    loss = jnp.where(live, top + jnp.log(total) - picked, 0.0)
+    loss_ref[...] = jnp.zeros_like(loss_ref)
+    loss_ref[0:1, :] = functools.reduce(
+        jnp.add, [loss[:, lane : lane + 128] for lane in range(0, frames, 128)]
+    )
+    weight = jnp.where(live, 1.0 / slot_count, 0.0)
+    line = jnp.broadcast_to(own_row(line), (16, frames))
+    hit_weight = jnp.broadcast_to(weight, (16, frames))
+    base = lax.broadcasted_iota(jnp.int32, (16, frames), 0)
+    bias_col[...] = jnp.zeros_like(bias_col)
+    for group in range(OUT_GROUPS):
+        share = jnp.exp(sums[col, group : group + 1, :] - top) / total * weight
+
+        def gradient(number, carry, first=group * OUT_ROWS, share=share):
+            row = pl.multiple_of(first + number * 16, 16)
+            value = curve[pl.ds(row, 16), :] * share - jnp.where(base + row == line, hit_weight, 0.0)
+            value = value.astype(BF16)
+            dl_ref[pl.ds(row, 16), :] = value
+            bias_col[pl.ds(row, 16), :] = jnp.broadcast_to(
+                jnp.sum(value.astype(F32), axis=1, keepdims=True), (16, 128)
+            )
+            return carry
+
+        lax.fori_loop(0, OUT_ROWS // 16, gradient, 0)
+    bias_sum_ref[...] = jnp.zeros_like(bias_sum_ref)
+    for number in range(bias_out_ref.shape[0]):
+        block = jnp.transpose(bias_col[number * 128 : (number + 1) * 128, :])
+        bias_sum_ref[number : number + 1, :] = block[0:1, :]
+
+    for group in range(len(RING_STARTS)):
+        for way in range(2):
+            for step in range(STEPS):
+                ring_move(group, step, way).wait_send()
+    for number in range(3):
+        x_move(number).wait_send()
+        for block in range(4):
+            h_move(0, number, block).wait_send()
+            h_move(1, number, block).wait_send()
+    for copy in tag_copies + sum_copies:
+        copy.wait_send()
+    for copy in outs:
+        copy.wait()
+
+
+def forward_pass(x, tags, w_in, w_hid, w_out, bias, bias_out, slot_count):
+    own_rows = x.shape[0]
+    units = w_hid.shape[1]
+    frames = 4 * own_rows
+    wide = 4 * units
+    rows = OUT_GROUPS * OUT_ROWS
+    blocks = bias_out.shape[0]
+    vmem = pl.BlockSpec(memory_space=pltpu.VMEM)
+    hbm = pl.BlockSpec(memory_space=pl.ANY)
+    sem = pltpu.SemaphoreType.DMA
+    kept = (
+        ((frames, 512), BF16),
+        ((frames, wide), BF16),
+        ((frames, wide), BF16),
+        ((frames, units), F32),
+        ((frames, units), F32),
+        ((wide, units), BF16),
+        ((rows, wide), BF16),
+    )
+    return pl.pallas_call(
+        functools.partial(forward_kernel, slot_count),
+        out_shape=tuple(jax.ShapeDtypeStruct(shape, kind) for shape, kind in kept)
+        + (
+            jax.ShapeDtypeStruct((rows, frames), BF16),
+            jax.ShapeDtypeStruct((24, 128), F32),
+            jax.ShapeDtypeStruct((8, 128), F32),
+        ),
+        in_specs=[vmem] * 7,
+        out_specs=(hbm,) * 7 + (vmem,) * 3,
+        scratch_shapes=[pltpu.VMEM(shape, kind) for shape, kind in kept[:5]]
+        + [
+            pltpu.VMEM((512, units), BF16),
+            pltpu.VMEM((wide, units), BF16),
+            pltpu.VMEM((rows, wide), BF16),
+            pltpu.VMEM((rows, frames), F32),
+            pltpu.VMEM((blocks * 128, 128), F32),
+            pltpu.VMEM((4,) + tags.shape, jnp.int32),
+            pltpu.VMEM((4, 16, frames), F32),
+            sem((5, 2, STEPS)),
+            sem((5, 2, STEPS)),
+            sem((3,)),
+            sem((3,)),
+            sem((2, 3, 4)),
+            sem((2, 3, 4)),
+            sem((3,)),
+            sem((3,)),
+            sem((3,)),
+            sem((3,)),
+            sem((16,)),
+        ],
+        compiler_params=pltpu.CompilerParams(
+            collective_id=2, has_side_effects=True, vmem_limit_bytes=60 * 1024 * 1024
+        ),
+    )(x, tags, w_in, w_hid, w_out, bias, bias_out)
+
+
 DIM_BITS = (2, 4, 8)
 ORDERS = ((0, 1, 2), (1, 2, 0), (2, 0, 1))
 PIECE = 48
@@ -1264,58 +1641,48 @@
     micro = frames.shape[0]
     slot_count = frames.shape[1] * micro * nblk * ncol
     bias_row = biases[0]
-    b_one = bias_row[:hcol]
-    b_two = bias_row[hcol : 2 * hcol]
-    b_out = bias_row[2 * hcol :]
-    low_input = w_input.astype(jnp.bfloat16)
-    own_tags = jnp.where(mask > 0, labels, -1).reshape(-1)
-    own_inputs = frames.reshape(-1, frames.shape[2])
-    inputs = lax.all_gather(own_inputs, "col", axis=0, tiled=True)
-    tags_group = lax.all_gather(own_tags, "col", axis=0, tiled=True)
-    low_hidden = collect_rows(w_hidden.astype(jnp.bfloat16))
-    low_output = collect_rows(w_output.astype(jnp.bfloat16))
-    sig_one = jax.nn.sigmoid(matmul(inputs, low_input) + b_one)
-    h_one = spread_cols(sig_one.astype(jnp.bfloat16))
-    sig_two = jax.nn.sigmoid(matmul(h_one, low_hidden) + b_two)
-    h_two = spread_cols(sig_two.astype(jnp.bfloat16))
-    logits = matmul(h_two, low_output) + b_out
-    row_top = lax.pmax(jnp.max(logits, axis=1), "col")
-    exponent = jnp.exp(logits - row_top[:, None])
-    target_hit = jnp.arange(scol)[None, :] == (tags_group - col_index * scol)[:, None]
-    row_total, picked = lax.psum(
-        (jnp.sum(exponent, axis=1), jnp.sum(jnp.where(target_hit, logits, 0.0), axis=1)), "col"
-    )
-    live_rows = tags_group >= 0
-    loss_local = jnp.sum(jnp.where(live_rows, row_top + jnp.log(row_total) - picked, 0.0))
-    probs = exponent / row_total[:, None]
-    d_logits = (
-        jnp.where(live_rows[:, None], probs - target_hit.astype(jnp.float32), 0.0) / slot_count
-    ).astype(jnp.bfloat16)
-    d_h_two = reduce_cols(outer_cols(d_logits, low_output))
-    d_z_two = (d_h_two * sig_two * (1.0 - sig_two)).astype(jnp.bfloat16)
+    deep = w_input.shape[0]
+    padded = 512
+    rows_out = OUT_GROUPS * OUT_ROWS
+    own_tags = jnp.where(mask > 0, labels, -1).reshape(1, -1)
+    layer_biases = jnp.pad(bias_row[: 2 * hcol].reshape(2, hcol), ((0, 6), (0, 0)))
+    blocks = -(-rows_out // 128)
+    out_biases = jnp.pad(bias_row[2 * hcol :], (0, blocks * 128 - scol)).reshape(blocks, 128)
+    inputs, h_one, h_two, slope_one, slope_two, low_hidden, low_output, d_logits, bias_sums, losses = (
+        forward_pass(
+            frames.reshape(-1, deep),
+            jnp.broadcast_to(own_tags, (8, own_tags.shape[1])),
+            w_input,
+            w_hidden,
+            w_output.T,
+            layer_biases,
+            out_biases,
+            slot_count,
+        )
+    )
+    loss_local = jnp.sum(losses)
+    d_h_two = reduce_cols(inner_rows(d_logits, low_output))
+    d_z_two = (d_h_two * slope_two).astype(jnp.bfloat16)
     d_h_one = reduce_cols(outer_cols(d_z_two, low_hidden))
-    d_z_one = (d_h_one * sig_one * (1.0 - sig_one)).astype(jnp.bfloat16)
+    d_z_one = (d_h_one * slope_one).astype(jnp.bfloat16)
     grad_bias = jnp.concatenate(
         [
             jnp.sum(d_z_one.astype(jnp.float32), axis=0),
             jnp.sum(d_z_two.astype(jnp.float32), axis=0),
-            jnp.sum(d_logits.astype(jnp.float32), axis=0),
+            bias_sums.reshape(-1)[:scol],
         ]
     )
-    deep = w_input.shape[0]
-    padded = 512
-    rows_out = OUT_GROUPS * OUT_ROWS
     vec = jnp.concatenate([grad_bias, loss_local[None]])
     vec = jnp.pad(vec, (0, 4096 - vec.shape[0])).reshape(32, 128)
     next_out, next_hid, next_in, red_out, red_hid, red_in, vec_sum, stats = reduce_grads(
-        jnp.pad(d_logits, ((0, 0), (0, rows_out - scol))).T,
+        d_logits,
         h_two,
         jnp.pad(res_output[0], ((0, 0), (0, rows_out - scol))).T,
         d_z_two.T,
         h_one,
         res_hidden[0].T,
         d_z_one.T,
-        jnp.pad(inputs, ((0, 0), (0, padded - deep))),
+        inputs,
         jnp.pad(res_input[0], ((0, padded - deep), (0, 0))).T,
         vec,
         scol,

time: 1050 us -> 892 us (0.85)
  waiting for transfers between devices: 343 us -> 119 us
  Pallas kernels: 486 us -> 645 us
  blocking collectives: 29.6 us -> 0 us
  matrix products: 49.6 us -> 23.2 us
  other arithmetic: 36.8 us -> 20.9 us
  local copies, waits for them, and re-layouts: 77.8 us -> 62.4 us
    all_gather x4 -> x0, waiting for transfers between devices: 242 us -> none  [the longest x2 179 us: collect_rows(): return lax.all_gather(values, 'blk', axis=0, tiled=True)]
    pallas_call x0 -> x1, Pallas kernels: none -> 160 us  [forward_pass(): pl.pallas_call(functools.partial(forward_kernel, slot_count), out_shape=t...]
    reduce_scatter x2, waiting for transfers between devices: 101 us -> 119 us  [reduce_cols(): return lax.psum_scatter(values, 'col', scatter_dimension=1, tiled=True)]
    all_gather x2 -> x0, blocking collectives: 16.8 us -> none  [the longest x1 11.7 us: fast_body(): inputs = lax.all_gather(own_inputs, 'col', axis=0, tiled=True)]
    dot_general x2 -> x1, matrix products: 21.7 us -> 5.69 us  [outer_cols(): lax.dot_general(left_side, right_side, (((1,), (1,)), ((), ())), preferre...]
    all_gather x2 -> x0, local copies, waits for them, and re-layouts: 13 us -> none  [spread_cols(): return lax.all_gather(values, 'col', axis=1, tiled=True)]
    reduce_sum x3 -> x1, other arithmetic: 13.4 us -> 0.6 us  [fast_body(): loss_local = jnp.sum(losses)]
    dot_general x3 -> x1, matrix products: 27.9 us -> 17.5 us  [inner_rows(): lax.dot_general(left_side, right_side, (((0,), (0,)), ((), ())), preferre...]
  transfers between devices with their start and end apart: 6 -> 2, of which waited for: 6 -> 2; matrix products, arithmetic and copies ran while one was open for 4% -> 3% of each run, Pallas kernels for 0% -> 0%
where the time goes in v4:
time: 892 us; the launch traced here: 886 us
  Pallas kernels  645 us (72%)
  waiting for transfers between devices  119 us (13%)
  local copies, waits for them, and re-layouts  62.4 us (7%)
  matrix products  23.2 us (3%)
  other arithmetic  20.9 us (2%)
  between operations  15.1 us (2%)
    pallas_call x1, Pallas kernels, muon(): pl.pallas_call(muon_kernel, out_shape=(jax.ShapeDtypeStruct((4, rows, hei...  298 us
    pallas_call x1, Pallas kernels, reduce_grads(): pl.pallas_call(functools.partial(reduce_kernel, deep), out_shape=(jax.Sha...  187 us
    pallas_call x1, Pallas kernels, forward_pass(): pl.pallas_call(functools.partial(forward_kernel, slot_count), out_shape=t...  160 us
    reduce_scatter x2, waiting for transfers between devices, reduce_cols(): return lax.psum_scatter(values, 'col', scatter_dimension=1, tiled=True)  119 us
    unnamed x37, local copies, waits for them, and re-layouts  31.6 us
  transfers between devices with their start and end apart: 2, of which 2 were waited for; matrix products, arithmetic and copies ran while one was open for 3% of the time, Pallas kernels for 0%

profile of v4, /device:TPU:0, one launch (start us, length us, event | category | flops | bytes accessed | tf_op | source)
XLA Modules:
  0.0 885.9 jit_solution(16179152925183333883)
XLA Ops:
  11.3 159.9 %shard_map.271 = (bf16[1024,512]{1,0:T(8,128)(2,1)}, bf16[1024,2048]{1,0:T(8,128)(2,1)}, bf16[1024,2048]{1,0:T(8,128)(2,1)}, f32[1024,512]{1,0:T(8,128)}, f32[10...) custom-call(bf16[256,440]{1,0:T(8,128)(2,1)} %bitcast.63, ...), custom_call_target="tpu_custom_call" | custom-call | tf_op jit(solution)/shard_map/pallas_call | solution.py:972
  171.2 17.5 %fusion.3 = f32[1024,2048]{0,1:T(8,128)} fusion(bf16[2368,1024]{1,0:T(8,128)(2,1)} %get-tuple-element.50.dl_ref, bf16[2368,2048]{1,0:T(8,128)(2,1)} %get-tuple-element.52), kind=kOutput, calls=%fused_computation.29 | convolution fusion | flops 9932111872 | bytes 22937600 | tf_op jit(solution)/shard_map/dot_general | solution.py:38
  188.8 2.5 copy.32
  191.2 69.6 %reduce-scatter.3.cloned.1.call-done = f32[1024,512]{0,1:T(8,128)} async-done(((f32[1024,2048]{0,1:T(8,128)}), f32[1024,512]{0,1:T(8,128)}) %reduce-scatter.3.cloned.1.call-update) | async-done | bytes 2097168 | tf_op jit(solution)/shard_map/reduce_scatter | solution.py:60
  260.9 2.0 convert_reduce_fusion
  263.1 5.7 fusion.4
  268.8 1.9 copy.35
  271.4 4.0 copy.33
  277.7 2.2 copy.37
  280.7 10.8 %pad_bitcast_fusion.res_out_ref = bf16[2368,2048]{1,0:T(8,128)(2,1)} fusion(bf16[2048,2326]{0,1:T(8,128)(2,1)} %bitcast.52), kind=kLoop, calls=%fused_computation | loop fusion | bytes 19226624 | tf_op jit(solution)/shard_map/transpose | solution.py:1680
  291.5 49.1 %reduce-scatter.5.cloned.1.call-done = f32[1024,512]{0,1:T(8,128)} async-done(((f32[1024,2048]{0,1:T(8,128)}), f32[1024,512]{0,1:T(8,128)}) %reduce-scatter.5.cloned.1.call-update) | async-done | bytes 2097168 | tf_op jit(solution)/shard_map/reduce_scatter | solution.py:60
  340.7 2.7 convert_reduce_fusion.1
  344.7 187.5 %shard_map.272 = (f32[2326,1,2048]{2,1,0:T(1,128)}, f32[512,2048]{1,0:T(8,128)}, f32[512,512]{1,0:T(8,128)}, f32[2368,256]{1,0:T(8,128)}, f32[512,256]{1,0:T(8,1...) custom-call(bf16[2368,1024]{1,0:T(8,128)(2,1)} %get-tuple-element.50.dl_ref, ...), custom_call_target="tpu_custom_call" | custom-call | tf_op jit(solution)/shard_map/pallas_call | solution.py:583
  532.2 1.3 multiply_reduce_fusion
  533.5 1.3 slice.69
  534.8 2.5 copy.38
  538.0 1.3 scatter.4.stats_ref
  539.3 298.0 %shard_map.273 = (f32[4,128,256]{2,1,0:T(8,128)}, f32[512,512]{1,0:T(8,128)}, f32[512,256]{1,0:T(8,128)}, f32[512,512]{1,0:T(8,128)}, f32[8,128]{1,0:T(8,128)}) custom-call(f32[8,128]{1,0:T(8,128)} %scatter.4.stats_ref, f32[512,256]{1,0:T(8,128)} %get-tuple-element.62.red_hid_ref, f32[512,256]{1,0:T(8,128)} %bitcast.61, f32[512,512]{1,0:T(8,128)} %bitcast.58, ...), custom_call_target="tpu_custom_call" | custom-call | tf_op jit(solution)/shard_map/pallas_call | solution.py:1425
  837.3 1.3 fusion.2
  844.7 5.3 copy.42
  850.0 1.4 slice_bitcast_fusion
  851.5 1.2 copy.41
  852.7 9.1 %multiply_subtract_fusion = (f32[256,2326]{0,1:T(8,128)}, f32[256,2326]{0,1:T(8,128)}, f32[256,2326]{0,1:T(8,128)}) fusion(f32[256,2326]{0,1:T(8,128)S(1)} %copy-done, f32[256,2326]{0,1:T(8,128)} %param.27, f32[2368,256]{1,0:T(8,128)} %get-tuple-element.67, f32[]{:T(128)} %bitcast.22, f32[256,2326]{0,1:T(8,128)} %param.28), kind=kLoop, calls=%fused_computation.4 | loop fusion | flops 8931840 | bytes 16672772 | tf_op jit(solution)/shard_map/sub | solution.py:78
  862.5 16.3 %copy.47 = f32[1,2048,2326]{1,0,2:T(1,128)} copy(f32[1,2048,2326]{1,0,2:T(1,128)} %bitcast.51) | data formatting | bytes 38109184
  (56 shorter events, 16.1 us)
Async XLA Ops:
  7.2 253.7 %reduce-scatter.3.cloned.1.call-start = ((), (), s32[]{:S(2)}) async-start(), calls=%async_computation.2 | async-start | bytes 10485760 | tf_op jit(solution)/shard_map/reduce_scatter | solution.py:60
  188.7 151.9 %reduce-scatter.5.cloned.1.call-start = ((), (), s32[]{:S(2)}) async-start(), calls=%async_computation.3 | async-start | bytes 10485760 | tf_op jit(solution)/shard_map/reduce_scatter | solution.py:60
  260.9 2.2 copy-start.14
  262.9 5.9 copy-start.1
  268.8 1.9 copy-start.13
  271.4 5.2 copy-start.4
  291.5 51.9 %copy-start.12 = (f32[24,128]{1,0:T(8,128)S(1)}, f32[24,128]{1,0:T(8,128)}, u32[]{:S(2)}) copy-start(f32[24,128]{1,0:T(8,128)} %get-tuple-element.58) | copy-start | bytes 36868
  534.8 303.9 %copy-start.8 = (f32[32,128]{1,0:T(8,128)S(1)}, f32[32,128]{1,0:T(8,128)}, u32[]{:S(2)}) copy-start(f32[32,128]{1,0:T(8,128)} %get-tuple-element.60) | copy-start | bytes 49156
  539.3 301.4 %copy-start.3 = (f32[256,512]{1,0:T(8,128)S(1)}, f32[256,512]{1,0:T(8,128)}, u32[]{:S(2)}) copy-start(f32[256,512]{1,0:T(8,128)} %w_hid_ref.1) | copy-start | bytes 1572868
  837.3 4.2 copy-start.2
  837.3 4.2 copy-start.6
  840.7 2.0 copy-start.5
  841.6 2.1 copy-start.7
  850.0 2.7 copy-start
  852.7 9.1 %copy-start.9 = (f32[1,3350]{1,0:T(1,128)S(1)}, f32[1,3350]{1,0:T(1,128)}, u32[]{:S(2)}) copy-start(f32[1,3350]{1,0:T(1,128)} %param.24) | copy-start | bytes 40204
  852.7 9.1 %copy-start.10 = (f32[1,3350]{1,0:T(1,128)S(1)}, f32[1,3350]{1,0:T(1,128)}, u32[]{:S(2)}) copy-start(f32[1,3350]{1,0:T(1,128)} %param.29) | copy-start | bytes 40204
  852.7 9.1 %copy-start.11 = (f32[1,3350]{1,0:T(1,128)S(1)}, f32[1,3350]{1,0:T(1,128)}, u32[]{:S(2)}) copy-start(f32[1,3350]{1,0:T(1,128)} %param.30) | copy-start | bytes 40204
Sparse Core Ops, SparseCore 0:
  188.8 71.9 reduce-scatter.2
  268.9 71.6 reduce-scatter.4

commit v5 on v4

--- a/solution.py
+++ b/solution.py
@@ -102,6 +102,8 @@
 BLOCKS = (304, 288)
 HID_ROWS = 512
 SCALE_ROWS = 16
+HID_WAVE = 4
+IN_WAVE = 6
 
 
 def ring_place(blk):
@@ -134,12 +136,14 @@
     deep,
     dl_ref,
     h_two_ref,
+    h_one_ref,
+    x_ref,
+    part_ref,
+    slope_two_ref,
+    slope_one_ref,
+    w_hid_ref,
     res_out_ref,
-    dz_two_ref,
-    h_one_ref,
     res_hid_ref,
-    dz_one_ref,
-    x_ref,
     res_in_ref,
     vec_ref,
     next_out_ref,
@@ -153,7 +157,18 @@
     grad,
     stage,
     res_buf,
+    dl_buf,
+    h_buf,
+    slope_buf,
     marks,
+    keep_sums,
+    dz,
+    dz_two,
+    dz_one,
+    core_out,
+    core_got,
+    far_out,
+    far_got,
     own_out,
     got_out,
     size_out,
@@ -164,9 +179,17 @@
     got_in,
     size_in,
     share_in,
+    vec,
     vecs,
     res_sems,
+    dl_sems,
+    load_sems,
     stage_sems,
+    slope_sems,
+    core_send,
+    core_recv,
+    far_send,
+    far_recv,
     out_send,
     out_recv,
     hid_send,
@@ -179,13 +202,15 @@
     vec_recv,
 ):
     blk = lax.axis_index("blk")
+    col = lax.axis_index("col")
     here = ring_place(blk)
     total_rows = next_out_ref.shape[0]
+    core, high = col % 2, col // 2
+    cores = {"col": col + 1 - 2 * core}
+    across = {"col": (col + 2) % 4}
     barrier = pltpu.get_barrier_semaphore()
-    for away in range(1, RING):
-        pl.semaphore_signal(
-            barrier, inc=1, device_id={"blk": (blk + away) % RING}, device_id_type=MESH
-        )
+    for target in (cores, across, *({"blk": (blk + away) % RING} for away in range(1, RING))):
+        pl.semaphore_signal(barrier, inc=1, device_id=target, device_id_type=MESH)
 
     starts = [sum(BLOCKS[:part]) for part in range(len(BLOCKS))]
 
@@ -197,6 +222,29 @@
             res_sems.at[part],
         )
 
+    def dl_copy(group, part):
+        rows = BLOCKS[part]
+        return pltpu.make_async_copy(
+            dl_ref.at[pl.ds(group * OUT_ROWS + starts[part], rows), :],
+            dl_buf.at[part, pl.ds(0, rows), :],
+            dl_sems.at[part],
+        )
+
+    def hid_res_copy(part):
+        return pltpu.make_async_copy(
+            res_hid_ref.at[pl.ds(part * 256, 256), :],
+            res_buf.at[part, pl.ds(0, 256), :],
+            res_sems.at[part],
+        )
+
+    def hid_next_copy(part):
+        return pltpu.make_async_copy(
+            grad.at[pl.ds(0, 256), :], next_hid_ref.at[pl.ds(part * 256, 256), :], load_sems.at[1]
+        )
+
+    def load(src, dst):
+        return pltpu.make_async_copy(src, dst, load_sems.at[0])
+
     def stage_copy(group, part, rows):
         return pltpu.make_async_copy(
             stage.at[pl.ds(0, rows)],
@@ -219,32 +267,204 @@
             def _():
                 stage_copy(group, part, last_rows).start()
 
-    res_copy(0, 0).start()
-    res_copy(0, 1).start()
+    for part in range(2):
+        res_copy(0, part).start()
+        dl_copy(0, part).start()
+    load(h_two_ref, h_buf).start()
     marks[...] = jnp.zeros_like(marks)
     stats_ref[...] = jnp.zeros_like(stats_ref)
-    pl.semaphore_wait(barrier, RING - 1)
-
-    vec_copies = []
-    for away in range(1, RING):
-        copy = pltpu.make_async_remote_copy(
-            src_ref=vec_ref,
+    vec[...] = vec_ref[...]
+    pl.semaphore_wait(barrier, RING + 1)
+
+    CHUNK = 256
+    units = slope_buf.shape[2]
+
+    def slope_copy(layer, block):
+        rows = pl.ds(pl.multiple_of(block * CHUNK, CHUNK), CHUNK)
+        src = (slope_two_ref, slope_one_ref)[layer]
+        return pltpu.make_async_copy(src.at[rows, :], slope_buf.at[block % 2], slope_sems.at[block % 2])
+
+    def core_move(layer, block):
+        return pltpu.make_async_remote_copy(
+            src_ref=core_out.at[block % 2],
+            dst_ref=core_got.at[layer, block],
+            send_sem=core_send.at[block % 2],
+            recv_sem=core_recv.at[layer, block],
+            device_id=cores,
+            device_id_type=MESH,
+        )
+
+    def far_move(layer, block):
+        return pltpu.make_async_remote_copy(
+            src_ref=far_out.at[block % 2],
+            dst_ref=far_got.at[layer, block],
+            send_sem=far_send.at[block % 2],
+            recv_sem=far_recv.at[layer, block],
+            device_id=across,
+            device_id_type=MESH,
+        )
+
+    def lanes_of(number):
+        return pl.ds(pl.multiple_of(number * units, units), units)
+
+    def rows_at(number):
+        return pl.ds(pl.multiple_of(number * 16, 16), 16)
+
+    def free(copy, layer, block):
+        @pl.when((layer > 0) | (block >= 2))
+        def _():
+            copy.wait_send()
+
+    def lane_codes(first):
+        return jnp.transpose(marks[first : first + 128, :])[0:1, :]
+
+    def row_codes(values, rows):
+        top = functools.reduce(
+            jnp.maximum, [jnp.max(jnp.abs(value), axis=1, keepdims=True) for value in values]
+        )
+        code = scale_code(top)
+        marks[rows, :] = jnp.broadcast_to(code, (16, 128))
+        factor = TOP_CODE / code_scale(code)
+        return [to_codes(value * factor) for value in values]
+
+    def put_scale(out):
+        codes = jnp.concatenate(
+            [lane_codes(0), lane_codes(128), jnp.zeros((14, 128), F32)], axis=0
+        )
+        out[CHUNK : CHUNK + 16, 0:128] = codes.astype(jnp.int32).astype(I16)
+
+    def read_scale(got):
+        step = code_scale(from_codes(got[CHUNK : CHUNK + 16, 0:128])) * (1.0 / TOP_CODE)
+        step = jnp.transpose(jnp.concatenate([step, jnp.zeros((112, 128), F32)], axis=0))
+        for up in range(2):
+            marks[CHUNK + up * 128 : CHUNK + (up + 1) * 128, :] = jnp.broadcast_to(
+                step[:, up : up + 1], (128, 128)
+            )
+
+    def step_at(number):
+        return marks[pl.ds(pl.multiple_of(CHUNK + number * 16, 16), 16), 0:1]
+
+    def split(layer, block):
+        free(core_move(layer, block), layer, block)
+
+        def write(number, carry):
+            rows = rows_at(number)
+            parts = row_codes(
+                [grad[rows, lanes_of(2 * half + 1 - core)] for half in range(2)], rows
+            )
+            for half in range(2):
+                there = slice(half * units, (half + 1) * units)
+                core_out[block % 2, rows, there] = parts[half]
+                keep_sums[block, rows, there] = grad[rows, lanes_of(2 * half + core)]
+            return carry
+
+        lax.fori_loop(0, CHUNK // 16, write, 0)
+        put_scale(core_out.at[block % 2])
+        core_move(layer, block).start()
+
+    def cross(layer, block):
+        core_move(layer, block).wait_recv()
+        free(far_move(layer, block), layer, block)
+        got = core_got.at[layer, block]
+        read_scale(got)
+
+        def add(number, carry):
+            rows = rows_at(number)
+            near, away = lanes_of(high), lanes_of(1 - high)
+            step = step_at(number)
+            keep_sums[block, rows, near] += from_codes(got[rows, near]) * step
+            value = keep_sums[block, rows, away] + from_codes(got[rows, away]) * step
+            far_out[block % 2, rows, :] = row_codes([value], rows)[0]
+            return carry
+
+        lax.fori_loop(0, CHUNK // 16, add, 0)
+        put_scale(far_out.at[block % 2])
+        far_move(layer, block).start()
+
+    def finish(layer, block):
+        far_move(layer, block).wait_recv()
+        slope_copy(layer, block).wait()
+        got = far_got.at[layer, block]
+        read_scale(got)
+
+        def one(number, total):
+            rows = rows_at(number)
+            value = keep_sums[block, rows, lanes_of(high)] + from_codes(got[rows, :]) * step_at(number)
+            value = (value * slope_buf[block % 2, rows, :]).astype(BF16)
+            dz[rows, :] = value
+            return total + value.astype(F32)
+
+        total = lax.fori_loop(0, CHUNK // 16, one, jnp.zeros((16, units), F32))
+        if layer == 0:
+
+            @pl.when(block < 2)
+            def _():
+                slope_copy(0, block + 2).start()
+
+            @pl.when(block >= 2)
+            def _():
+                slope_copy(1, block - 2).start()
+
+        else:
+
+            @pl.when(block < 2)
+            def _():
+                slope_copy(1, block + 2).start()
+
+        total = jnp.sum(total, axis=0, keepdims=True)
+        for number in range(units // 128):
+            row = 4 * (1 - layer) + number
+            vec[row : row + 1, :] += total[:, number * 128 : (number + 1) * 128]
+        flipped = (dz_two, dz_one)[layer]
+        for up in range(CHUNK // 128):
+            there = pl.ds(pl.multiple_of(block * CHUNK + up * 128, 128), 128)
+            for number in range(units // 128):
+                tile = dz[up * 128 : (up + 1) * 128, number * 128 : (number + 1) * 128]
+                flipped[number * 128 : (number + 1) * 128, there] = jnp.transpose(
+                    tile.astype(F32)
+                ).astype(BF16)
+
+    def blocks(first, last, work):
+        def one(block, carry):
+            work(block)
+            return carry
+
+        lax.fori_loop(first, last, one, 0)
+
+    def start_block(block):
+        rows = pl.ds(pl.multiple_of(block * CHUNK, CHUNK), CHUNK)
+        copy = pltpu.make_async_copy(part_ref.at[rows, :], grad.at[pl.ds(0, CHUNK), :], load_sems.at[1])
+        copy.start()
+        copy.wait()
+        split(0, block)
+
+    def turn_block(block):
+        finish(0, block)
+        for lane in range(0, grad.shape[1], 512):
+            grad[0:CHUNK, lane : lane + 512] = dot_nt(dz[...], w_hid_ref[lane : lane + 512, :])
+        split(1, block)
+
+    core_out[:, CHUNK:, :] = jnp.zeros((2, 16, 2 * units), I16)
+    far_out[:, CHUNK:, :] = jnp.zeros((2, 16, units), I16)
+    slope_copy(0, 0).start()
+    slope_copy(0, 1).start()
+    blocks(0, 4, start_block)
+    blocks(0, 4, lambda block: cross(0, block))
+
+    def vec_copy(away):
+        return pltpu.make_async_remote_copy(
+            src_ref=vec,
             dst_ref=vecs.at[blk],
             send_sem=vec_send.at[away - 1],
             recv_sem=vec_recv.at[away - 1],
             device_id={"blk": (blk + away) % RING},
             device_id_type=MESH,
         )
-        copy.start()
-        vec_copies.append(copy)
 
     def row_scale(value, count):
         size = jnp.sum(jnp.abs(value), axis=1, keepdims=True) * (1.0 / count) + 1e-12
         code = scale_code(size)
         return size, code, size * (TOP_CODE / code_scale(code))
-
-    def lane_codes(first):
-        return jnp.transpose(marks[first : first + 128, :])[0:1, :]
 
     def set_sizes(rows, own, sizes):
         parts = [lane_codes(first) for first in range(0, rows, 128)]
@@ -277,10 +497,16 @@
 
     def out_group(group):
         for part, rows in enumerate(BLOCKS):
-            base = pl.multiple_of(group * OUT_ROWS + starts[part], 16)
+            dl_copy(group, part).wait()
+            if part == 0:
+
+                @pl.when(group == 0)
+                def _():
+                    load(h_two_ref, h_buf).wait()
+
             for lane in range(0, grad.shape[1], 512):
                 grad[0:rows, lane : lane + 512] = dot_nn(
-                    dl_ref[pl.ds(base, rows), :], h_two_ref[:, lane : lane + 512]
+                    dl_buf[part, 0:rows, :], h_buf[:, lane : lane + 512]
                 )
             res_copy(group, part).wait()
             if part == 0:
@@ -308,33 +534,49 @@
             @pl.when(group < OUT_GROUPS - 1)
             def _(part=part):
                 res_copy(group + 1, part).start()
+                dl_copy(group + 1, part).start()
+
+            @pl.when(group == OUT_GROUPS - 1)
+            def _(part=part):
+                hid_res_copy(part).start()
+                if part == len(BLOCKS) - 1:
+                    load(h_one_ref, h_buf).start()
 
         set_sizes(OUT_ROWS, own_out.at[group], size_out.at[group])
 
     def hid_group():
-        for first in range(0, HID_ROWS, 256):
+        load(h_one_ref, h_buf).wait()
+        for part in range(2):
+            first = part * 256
+            if part:
+                hid_next_copy(part - 1).wait()
             for lane in range(0, grad.shape[1], 512):
                 grad[0:256, lane : lane + 512] = dot_nn(
-                    dz_two_ref[first : first + 256, :], h_one_ref[:, lane : lane + 512]
+                    dz_two[first : first + 256, :], h_buf[:, lane : lane + 512]
                 )
-
-            def write_next(row, lane, values, first=first):
-                next_hid_ref[pl.ds(first + row, 16), lane : lane + 128] = values
+            hid_res_copy(part).wait()
+
+            def write_next(row, lane, values):
+                grad[pl.ds(row, 16), lane : lane + 128] = values
 
             squash_rows(
                 0,
                 256,
                 own_hid,
                 first,
-                lambda row, first=first: res_hid_ref[pl.ds(first + row, 16), :].astype(F32),
+                lambda row, part=part: res_buf[part, pl.ds(row, 16), :].astype(F32),
                 write_next,
             )
+            hid_next_copy(part).start()
+        load(x_ref, h_buf.at[:, pl.ds(0, x_ref.shape[1])]).start()
         set_sizes(HID_ROWS, own_hid, size_hid)
+        hid_next_copy(1).wait()
 
     def in_group():
         wide = x_ref.shape[1]
+        load(x_ref, h_buf.at[:, pl.ds(0, wide)]).wait()
         for first in range(0, HID_ROWS, 256):
-            grad[0:256, 0:wide] = dot_nn(dz_one_ref[first : first + 256, :], x_ref[...])
+            grad[0:256, 0:wide] = dot_nn(dz_one[first : first + 256, :], h_buf[:, 0:wide])
 
             def some(number, carry, first=first):
                 row = pl.multiple_of(number * 16, 16)
@@ -496,32 +738,40 @@
         def _():
             share_move(step + 1, way).start()
 
+    def in_step(index, way):
+        @pl.when((index >= 0) & (index < STEPS))
+        def _():
+            in_hop(index, way)
+
+        @pl.when((index >= STEPS) & (index < 2 * STEPS))
+        def _():
+            share_hop(index - STEPS, way)
+
+    def ways(work):
+        def one(way, carry):
+            work(way)
+            return carry
+
+        lax.fori_loop(0, 2, one, 0)
+
     def wave(number, carry):
-        @pl.when(number == 0)
-        def _():
-            in_group()
-            first_moves(own_in, got_in, in_send, in_recv)
-            hid_group()
-            first_moves(own_hid, got_hid, hid_send, hid_recv)
-
         @pl.when(number < OUT_GROUPS)
         def _():
             out_group(number)
             first_moves(own_out.at[number], got_out.at[number], out_send.at[number], out_recv.at[number])
 
-        def both(way, carry):
-            @pl.when((number >= 1) & (number <= STEPS))
+        @pl.when(number == HID_WAVE)
+        def _():
+            hid_group()
+            first_moves(own_hid, got_hid, hid_send, hid_recv)
+
+        index = 2 * (number - IN_WAVE - 1)
+        ways(lambda way: in_step(index, way))
+
+        def both(way):
+            @pl.when((number > HID_WAVE) & (number <= HID_WAVE + STEPS))
             def _():
-                in_hop(number - 1, way)
-                hid_hop(number - 1, way)
-
-            @pl.when(number > STEPS)
-            def _():
-                share_hop(2 * (number - STEPS - 1), way)
-
-                @pl.when(number < STEPS + 4)
-                def _():
-                    share_hop(2 * (number - STEPS - 1) + 1, way)
+                hid_hop(number - HID_WAVE - 1, way)
 
             def outs(group, carry):
                 step = number - 1 - group
@@ -533,27 +783,47 @@
                 return carry
 
             lax.fori_loop(0, OUT_GROUPS, outs, 0)
-            return carry
-
-        lax.fori_loop(0, 2, both, 0)
+
+        ways(both)
+
+        @pl.when((number == 1) | (number == 2))
+        def _():
+            blocks(2 * number - 2, 2 * number, turn_block)
+
+        @pl.when(number == 3)
+        def _():
+            blocks(0, 4, lambda block: cross(1, block))
+
+        @pl.when(number == IN_WAVE)
+        def _():
+            blocks(0, 4, lambda block: finish(1, block))
+            in_group()
+            first_moves(own_in, got_in, in_send, in_recv)
+            for away in range(1, RING):
+                vec_copy(away).start()
+
+        ways(lambda way: in_step(index + 1, way))
         return carry
 
-    lax.fori_loop(0, STEPS + OUT_GROUPS + 1, wave, 0)
+    lax.fori_loop(0, IN_WAVE + 1 + STEPS, wave, 0)
 
     for place in range(RING):
         for way in range(2):
             red_in_ref[place * 64 : (place + 1) * 64, way * 256 : (way + 1) * 256] = share_in[
                 way, place
             ]
-    for copy in vec_copies:
-        copy.wait_recv()
-    vecs[blk] = vec_ref[...]
+    for away in range(1, RING):
+        vec_copy(away).wait_recv()
+    vecs[blk] = vec[...]
     total = vecs[0]
     for number in range(1, RING):
         total = total + vecs[number]
     vec_sum_ref[...] = total
-    for copy in vec_copies:
-        copy.wait_send()
+    for away in range(1, RING):
+        vec_copy(away).wait_send()
+    for slot in range(2):
+        core_move(1, 2 + slot).wait_send()
+        far_move(1, 2 + slot).wait_send()
     stage_copy(OUT_GROUPS - 1, len(BLOCKS) - 1, last_rows).wait()
     for way in range(2):
         for step in range(STEPS):
@@ -571,9 +841,12 @@
             share_move(step, way).wait_send()
 
 
-def reduce_grads(dl, h_two, res_out, dz_two, h_one, res_hid, dz_one, x, res_in, vec, senones, deep):
-    wide = h_two.shape[1]
+def reduce_grads(
+    dl, h_two, h_one, x, part, slope_two, slope_one, w_hid, res_out, res_hid, res_in, vec, senones, deep
+):
+    frames, wide = h_two.shape
     in_wide = x.shape[1]
+    units = w_hid.shape[1]
     vmem = pl.BlockSpec(memory_space=pltpu.VMEM)
     hbm = pl.BlockSpec(memory_space=pl.ANY)
     message = OUT_ROWS + SCALE_ROWS
@@ -592,13 +865,24 @@
             jax.ShapeDtypeStruct(vec.shape, F32),
             jax.ShapeDtypeStruct((8, 128), F32),
         ),
-        in_specs=[vmem, vmem, hbm] + [vmem] * 7,
-        out_specs=(hbm,) + (vmem,) * 7,
+        in_specs=[hbm] * 7 + [vmem] + [hbm] * 2 + [vmem] * 2,
+        out_specs=(hbm, hbm) + (vmem,) * 6,
         scratch_shapes=[
             pltpu.VMEM((BLOCKS[0], wide), F32),
             pltpu.VMEM((BLOCKS[0], 1, wide), F32),
             pltpu.VMEM((2, BLOCKS[0], wide), BF16),
+            pltpu.VMEM((2, BLOCKS[0], frames), BF16),
+            pltpu.VMEM((frames, wide), BF16),
+            pltpu.VMEM((2, 256, units), F32),
             pltpu.VMEM((640, 128), F32),
+            pltpu.VMEM((4, 256, 2 * units), F32),
+            pltpu.VMEM((256, units), BF16),
+            pltpu.VMEM((units, frames), BF16),
+            pltpu.VMEM((units, frames), BF16),
+            pltpu.VMEM((2, 272, 2 * units), I16),
+            pltpu.VMEM((2, 4, 272, 2 * units), I16),
+            pltpu.VMEM((2, 272, units), I16),
+            pltpu.VMEM((2, 4, 272, units), I16),
             pltpu.VMEM((OUT_GROUPS, 2 * RING, message, 128), I16),
             pltpu.VMEM((OUT_GROUPS, 2, STEPS, message, 128), I16),
             pltpu.VMEM((OUT_GROUPS, 8, 128), F32),
@@ -609,9 +893,17 @@
             pltpu.VMEM((2, STEPS, in_message, 256), I16),
             pltpu.VMEM((RING, 8, 128), F32),
             pltpu.VMEM((2, RING, 64, 256), F32),
+            pltpu.VMEM(vec.shape, F32),
             pltpu.VMEM((RING,) + vec.shape, F32),
             sem((2,)),
+            sem((2,)),
+            sem((2,)),
             sem((1,)),
+            sem((2,)),
+            sem((2,)),
+            sem((2, 4)),
+            sem((2,)),
+            sem((2, 4)),
             sem((OUT_GROUPS, 2, STEPS)),
             sem((OUT_GROUPS, 2, STEPS)),
             sem((2, STEPS)),
@@ -624,9 +916,9 @@
             sem((STEPS,)),
         ],
         compiler_params=pltpu.CompilerParams(
-            collective_id=1, has_side_effects=True, vmem_limit_bytes=62 * 1024 * 1024
+            collective_id=1, has_side_effects=True, vmem_limit_bytes=63 * 1024 * 1024
         ),
-    )(dl, h_two, res_out, dz_two, h_one, res_hid, dz_one, x, res_in, vec)
+    )(dl, h_two, h_one, x, part, slope_two, slope_one, w_hid, res_out, res_hid, res_in, vec)
 
 
 RING_STARTS = (0, 2, 5, 7, 9)
@@ -1661,28 +1953,20 @@
         )
     )
     loss_local = jnp.sum(losses)
-    d_h_two = reduce_cols(inner_rows(d_logits, low_output))
-    d_z_two = (d_h_two * slope_two).astype(jnp.bfloat16)
-    d_h_one = reduce_cols(outer_cols(d_z_two, low_hidden))
-    d_z_one = (d_h_one * slope_one).astype(jnp.bfloat16)
-    grad_bias = jnp.concatenate(
-        [
-            jnp.sum(d_z_one.astype(jnp.float32), axis=0),
-            jnp.sum(d_z_two.astype(jnp.float32), axis=0),
-            bias_sums.reshape(-1)[:scol],
-        ]
-    )
-    vec = jnp.concatenate([grad_bias, loss_local[None]])
+    partial = inner_rows(d_logits, low_output)
+    vec = jnp.concatenate([jnp.zeros((2 * hcol,), F32), bias_sums.reshape(-1)[:scol], loss_local[None]])
     vec = jnp.pad(vec, (0, 4096 - vec.shape[0])).reshape(32, 128)
     next_out, next_hid, next_in, red_out, red_hid, red_in, vec_sum, stats = reduce_grads(
         d_logits,
         h_two,
+        h_one,
+        inputs,
+        partial,
+        slope_two,
+        slope_one,
+        low_hidden,
         jnp.pad(res_output[0], ((0, 0), (0, rows_out - scol))).T,
-        d_z_two.T,
-        h_one,
         res_hidden[0].T,
-        d_z_one.T,
-        inputs,
         jnp.pad(res_input[0], ((0, padded - deep), (0, 0))).T,
         vec,
         scol,

time: 892 us -> 807 us (0.905)
  waiting for transfers between devices: 119 us -> 0 us
  Pallas kernels: 645 us -> 715 us
  between operations: 15.1 us -> 1.7 us
  local copies, waits for them, and re-layouts: 62.4 us -> 51.6 us
    reduce_scatter x2 -> x0, waiting for transfers between devices: 119 us -> none  [reduce_cols(): return lax.psum_scatter(values, 'col', scatter_dimension=1, tiled=True)]
    pallas_call x1, Pallas kernels: 187 us -> 256 us  [reduce_grads(): pl.pallas_call(functools.partial(reduce_kernel, deep), out_shape=(jax.Sha...]
    unnamed x37 -> x43, local copies, waits for them, and re-layouts: 31.6 us -> 28.4 us
  transfers between devices with their start and end apart: 2 -> 0, of which waited for: 2 -> 0; matrix products, arithmetic and copies ran while one was open for 3% -> 0% of each run, Pallas kernels for 0% -> 0%
where the time goes in v5:
time: 807 us; the launch traced here: 801 us
  Pallas kernels  715 us (89%)
  local copies, waits for them, and re-layouts  51.6 us (6%)
  matrix products  17.5 us (2%)
  other arithmetic  15.2 us (2%)
    pallas_call x1, Pallas kernels, muon(): pl.pallas_call(muon_kernel, out_shape=(jax.ShapeDtypeStruct((4, rows, hei...  299 us
    pallas_call x1, Pallas kernels, reduce_grads(): pl.pallas_call(functools.partial(reduce_kernel, deep), out_shape=(jax.Sha...  256 us
    pallas_call x1, Pallas kernels, forward_pass(): pl.pallas_call(functools.partial(forward_kernel, slot_count), out_shape=t...  160 us
    unnamed x43, local copies, waits for them, and re-layouts  28.4 us
    dot_general x1, matrix products, inner_rows(): lax.dot_general(left_side, right_side, (((0,), (0,)), ((), ())), preferre...  17.5 us

profile of v5, /device:TPU:0, one launch (start us, length us, event | category | flops | bytes accessed | tf_op | source)
XLA Modules:
  0.0 801.3 jit_solution(7768483853486372365)
XLA Ops:
  2.0 0.7 slice_reduce_fusion
  4.7 159.9 %shard_map.271 = (bf16[1024,512]{1,0:T(8,128)(2,1)}, bf16[1024,2048]{1,0:T(8,128)(2,1)}, bf16[1024,2048]{1,0:T(8,128)(2,1)}, f32[1024,512]{1,0:T(8,128)}, f32[10...) custom-call(bf16[256,440]{1,0:T(8,128)(2,1)} %bitcast.57, ...), custom_call_target="tpu_custom_call" | custom-call | tf_op jit(solution)/shard_map/pallas_call | solution.py:1264
  164.7 17.5 %fusion.3.part_ref = f32[1024,2048]{1,0:T(8,128)} fusion(bf16[2368,1024]{1,0:T(8,128)(2,1)} %get-tuple-element.50.dl_ref, bf16[2368,2048]{1,0:T(8,128)(2,1)} %get-tuple-element.54), kind=kOutput, calls=%fused_computation.25 | convolution fusion | flops 9932111872 | bytes 22937600 | tf_op jit(solution)/shard_map/dot_general | solution.py:38
  182.8 0.7 concatenate.5
  184.1 9.7 %pad_bitcast_fusion.res_out_ref = bf16[2368,2048]{1,0:T(8,128)(2,1)} fusion(bf16[2048,2326]{0,1:T(8,128)(2,1)} %bitcast.48), kind=kLoop, calls=%fused_computation | loop fusion | bytes 19226624 | tf_op jit(solution)/shard_map/transpose | solution.py:1968
  193.8 2.4 copy.31
  196.4 0.8 pad_bitcast_fusion.1.res_in_ref
  197.2 256.0 %shard_map.272 = (f32[2326,1,2048]{2,1,0:T(1,128)}, f32[512,2048]{1,0:T(8,128)}, f32[512,512]{1,0:T(8,128)}, f32[2368,256]{1,0:T(8,128)}, f32[512,256]{1,0:T(8,1...) custom-call(bf16[2368,1024]{1,0:T(8,128)(2,1)} %get-tuple-element.50.dl_ref, ...), custom_call_target="tpu_custom_call" | custom-call | tf_op jit(solution)/shard_map/pallas_call | solution.py:856
  453.3 1.4 multiply_reduce_fusion
  455.3 1.3 scatter.4.stats_ref
  456.6 2.5 copy.34
  459.2 1.1 pad.33.mom_in_ref
  460.3 1.0 copy.33
  461.3 299.3 %shard_map.273 = (f32[4,128,256]{2,1,0:T(8,128)}, f32[512,512]{1,0:T(8,128)}, f32[512,256]{1,0:T(8,128)}, f32[512,512]{1,0:T(8,128)}, f32[8,128]{1,0:T(8,128)}) custom-call(f32[8,128]{1,0:T(8,128)} %scatter.4.stats_ref, f32[512,256]{1,0:T(8,128)} %get-tuple-element.62.red_hid_ref, f32[512,256]{1,0:T(8,128)} %bitcast.55, f32[512,512]{1,0:T(8,128)} %bitcast.52, ...), custom_call_target="tpu_custom_call" | custom-call | tf_op jit(solution)/shard_map/pallas_call | solution.py:1717
  760.6 1.3 fusion.2
  763.3 9.1 %multiply_subtract_fusion = (f32[256,2326]{0,1:T(8,128)}, f32[256,2326]{0,1:T(8,128)}, f32[256,2326]{0,1:T(8,128)}) fusion(f32[256,2326]{0,1:T(8,128)S(1)} %copy-done, f32[256,2326]{0,1:T(8,128)} %param.27, f32[2368,256]{1,0:T(8,128)} %get-tuple-element.67, f32[]{:T(128)} %bitcast.20, f32[256,2326]{0,1:T(8,128)} %param.28), kind=kLoop, calls=%fused_computation.4 | loop fusion | flops 8931840 | bytes 16672772 | tf_op jit(solution)/shard_map/sub | solution.py:78
  772.7 0.8 copy-done.2
  773.4 0.9 bitcast_subtract_fusion
  774.3 1.1 multiply_subtract_fusion.1
  775.4 1.0 slice.66
  776.4 1.0 copy.36
  778.0 5.4 copy.38
  783.5 1.2 copy.37
  784.7 16.3 %copy.41 = f32[1,2048,2326]{1,0,2:T(1,128)} copy(f32[1,2048,2326]{1,0,2:T(1,128)} %bitcast.47) | data formatting | bytes 38109184
  (52 shorter events, 7.0 us)
Async XLA Ops:
  164.6 17.5 %copy-start.17 = (f32[8,128]{1,0:T(8,128)S(1)}, f32[8,128]{1,0:T(8,128)}, u32[]{:S(2)}) copy-start(f32[8,128]{1,0:T(8,128)} %get-tuple-element.59) | copy-start | bytes 12292
  164.7 18.1 %copy-start.16 = (f32[24,128]{1,0:T(8,128)S(1)}, f32[24,128]{1,0:T(8,128)}, u32[]{:S(2)}) copy-start(f32[24,128]{1,0:T(8,128)} %get-tuple-element.58) | copy-start | bytes 36868
  184.1 9.7 %copy-start.3 = (bf16[1,2048,512]{2,1,0:T(8,128)(2,1)S(1)}, bf16[1,2048,512]{2,1,0:T(8,128)(2,1)}, u32[]{:S(2)}) copy-start(bf16[1,2048,512]{2,1,0:T(8,128)(2,1)} %param.32) | copy-start | bytes 6291460
  193.8 2.4 copy-start.11
  453.2 5.9 copy-start.5
  453.2 7.0 copy-start.8
  460.3 301.6 %copy-start.12 = (f32[32,128]{1,0:T(8,128)S(1)}, f32[32,128]{1,0:T(8,128)}, u32[]{:S(2)}) copy-start(f32[32,128]{1,0:T(8,128)} %get-tuple-element.60) | copy-start | bytes 49156
  460.3 302.3 %copy-start.13 = (f32[1,3350]{1,0:T(1,128)S(1)}, f32[1,3350]{1,0:T(1,128)}, u32[]{:S(2)}) copy-start(f32[1,3350]{1,0:T(1,128)} %param.24) | copy-start | bytes 40204
  460.3 302.3 %copy-start.14 = (f32[1,3350]{1,0:T(1,128)S(1)}, f32[1,3350]{1,0:T(1,128)}, u32[]{:S(2)}) copy-start(f32[1,3350]{1,0:T(1,128)} %param.29) | copy-start | bytes 40204
  460.3 302.3 %copy-start.15 = (f32[1,3350]{1,0:T(1,128)S(1)}, f32[1,3350]{1,0:T(1,128)}, u32[]{:S(2)}) copy-start(f32[1,3350]{1,0:T(1,128)} %param.30) | copy-start | bytes 40204
  460.3 303.0 %copy-start = (f32[256,2326]{0,1:T(8,128)S(1)}, f32[256,2326]{0,1:T(8,128)}, u32[]{:S(2)}) copy-start(f32[256,2326]{0,1:T(8,128)} %param.23) | copy-start | bytes 7145476
  763.3 9.1 %copy-start.10 = (f32[4,128,256]{2,1,0:T(8,128)S(1)}, f32[4,128,256]{2,1,0:T(8,128)}, u32[]{:S(2)}) copy-start(f32[4,128,256]{2,1,0:T(8,128)} %get-tuple-element.66) | copy-start | bytes 1572868
  772.4 1.0 copy-start.2
  772.4 1.9 copy-start.1
  772.4 1.9 copy-start.7
  773.4 2.0 copy-start.6
  774.3 2.1 copy-start.9
  778.0 5.4 copy-start.4

commit v6 on v5

--- a/solution.py
+++ b/solution.py
@@ -101,7 +101,8 @@
 OUT_GROUPS = 4
 BLOCKS = (304, 288)
 HID_ROWS = 512
-SCALE_ROWS = 16
+HID_GROUP = 4
+IN_GROUP = 5
 HID_WAVE = 4
 IN_WAVE = 6
 
@@ -145,6 +146,7 @@
     res_out_ref,
     res_hid_ref,
     res_in_ref,
+    res_tail_ref,
     vec_ref,
     next_out_ref,
     next_hid_ref,
@@ -161,6 +163,7 @@
     h_buf,
     slope_buf,
     marks,
+    cols,
     keep_sums,
     dz,
     dz_two,
@@ -171,14 +174,13 @@
     far_got,
     own_out,
     got_out,
-    size_out,
     own_hid,
     got_hid,
-    size_hid,
     own_in,
     got_in,
-    size_in,
     share_in,
+    sizes,
+    shares,
     vec,
     vecs,
     res_sems,
@@ -200,6 +202,8 @@
     share_recv,
     vec_send,
     vec_recv,
+    size_send,
+    size_recv,
 ):
     blk = lax.axis_index("blk")
     col = lax.axis_index("col")
@@ -214,8 +218,8 @@
 
     starts = [sum(BLOCKS[:part]) for part in range(len(BLOCKS))]
 
-    def res_copy(group, part):
-        rows = BLOCKS[part]
+    def res_copy(group, part, rows=None):
+        rows = rows or BLOCKS[part]
         return pltpu.make_async_copy(
             res_out_ref.at[pl.ds(group * OUT_ROWS + starts[part], rows), :],
             res_buf.at[part, pl.ds(0, rows), :],
@@ -253,6 +257,7 @@
         )
 
     last_rows = total_rows - (OUT_GROUPS - 1) * OUT_ROWS - starts[-1]
+    whole_rows = last_rows // 16 * 16
 
     def stage_start(group, part):
         if part < len(BLOCKS) - 1:
@@ -318,14 +323,26 @@
     def lane_codes(first):
         return jnp.transpose(marks[first : first + 128, :])[0:1, :]
 
-    def row_codes(values, rows):
-        top = functools.reduce(
-            jnp.maximum, [jnp.max(jnp.abs(value), axis=1, keepdims=True) for value in values]
-        )
+    def set_factors():
+        top = jnp.max(cols[0, 0:CHUNK, :], axis=1, keepdims=True)
         code = scale_code(top)
-        marks[rows, :] = jnp.broadcast_to(code, (16, 128))
-        factor = TOP_CODE / code_scale(code)
-        return [to_codes(value * factor) for value in values]
+        marks[0:CHUNK, :] = jnp.broadcast_to(code, (CHUNK, 128))
+        cols[1, 0:CHUNK, :] = jnp.broadcast_to(TOP_CODE / code_scale(code), (CHUNK, 128))
+
+    def largest(values):
+        return functools.reduce(
+            jnp.maximum,
+            [
+                jnp.abs(value[:, lane : lane + 128])
+                for value in values
+                for lane in range(0, value.shape[1], 128)
+            ],
+        )
+
+    def scaled(values, factor):
+        return jnp.concatenate(
+            [values[:, lane : lane + 128] * factor for lane in range(0, values.shape[1], 128)], axis=1
+        )
 
     def put_scale(out):
         codes = jnp.concatenate(
@@ -342,19 +359,29 @@
             )
 
     def step_at(number):
-        return marks[pl.ds(pl.multiple_of(CHUNK + number * 16, 16), 16), 0:1]
+        return marks[pl.ds(pl.multiple_of(CHUNK + number * 16, 16), 16), :]
 
     def split(layer, block):
         free(core_move(layer, block), layer, block)
 
+        def measure(number, carry):
+            rows = rows_at(number)
+            cols[0, rows, :] = largest(
+                [grad[rows, lanes_of(2 * half + 1 - core)] for half in range(2)]
+            )
+            return carry
+
+        lax.fori_loop(0, CHUNK // 16, measure, 0)
+        set_factors()
+
         def write(number, carry):
             rows = rows_at(number)
-            parts = row_codes(
-                [grad[rows, lanes_of(2 * half + 1 - core)] for half in range(2)], rows
-            )
+            factor = cols[1, rows, :]
             for half in range(2):
                 there = slice(half * units, (half + 1) * units)
-                core_out[block % 2, rows, there] = parts[half]
+                core_out[block % 2, rows, there] = to_codes(
+                    scaled(grad[rows, lanes_of(2 * half + 1 - core)], factor)
+                )
                 keep_sums[block, rows, there] = grad[rows, lanes_of(2 * half + core)]
             return carry
 
@@ -372,12 +399,23 @@
             rows = rows_at(number)
             near, away = lanes_of(high), lanes_of(1 - high)
             step = step_at(number)
-            keep_sums[block, rows, near] += from_codes(got[rows, near]) * step
-            value = keep_sums[block, rows, away] + from_codes(got[rows, away]) * step
-            far_out[block % 2, rows, :] = row_codes([value], rows)[0]
+            keep_sums[block, rows, near] += scaled(from_codes(got[rows, near]), step)
+            value = keep_sums[block, rows, away] + scaled(from_codes(got[rows, away]), step)
+            keep_sums[block, rows, away] = value
+            cols[0, rows, :] = largest([value])
             return carry
 
         lax.fori_loop(0, CHUNK // 16, add, 0)
+        set_factors()
+
+        def write(number, carry):
+            rows = rows_at(number)
+            far_out[block % 2, rows, :] = to_codes(
+                scaled(keep_sums[block, rows, lanes_of(1 - high)], cols[1, rows, :])
+            )
+            return carry
+
+        lax.fori_loop(0, CHUNK // 16, write, 0)
         put_scale(far_out.at[block % 2])
         far_move(layer, block).start()
 
@@ -389,7 +427,9 @@
 
         def one(number, total):
             rows = rows_at(number)
-            value = keep_sums[block, rows, lanes_of(high)] + from_codes(got[rows, :]) * step_at(number)
+            value = keep_sums[block, rows, lanes_of(high)] + scaled(
+                from_codes(got[rows, :]), step_at(number)
+            )
             value = (value * slope_buf[block % 2, rows, :]).astype(BF16)
             dz[rows, :] = value
             return total + value.astype(F32)
@@ -461,34 +501,81 @@
             device_id_type=MESH,
         )
 
-    def row_scale(value, count):
-        size = jnp.sum(jnp.abs(value), axis=1, keepdims=True) * (1.0 / count) + 1e-12
-        code = scale_code(size)
-        return size, code, size * (TOP_CODE / code_scale(code))
-
-    def set_sizes(rows, own, sizes):
+    def set_rows(count, first_own, size):
+        size = jnp.broadcast_to(size, (count, 128))
+        marks[first_own : first_own + count, :] = size
+        cols[0, 0:count, :] = size
+        cols[1, 0:count, :] = 2.0 / size
+
+    def tell_sizes(group):
+        for away in range(1, RING):
+            size_copy(group, away).start()
+
+    def size_copy(group, away):
+        return pltpu.make_async_remote_copy(
+            src_ref=sizes.at[group, here],
+            dst_ref=sizes.at[group, here],
+            send_sem=size_send.at[group, away - 1],
+            recv_sem=size_recv.at[group, away - 1],
+            device_id={"blk": ring_blk((here + away) % RING)},
+            device_id_type=MESH,
+        )
+
+    def set_sizes(rows, group):
         parts = [lane_codes(first) for first in range(0, rows, 128)]
-        parts.append(jnp.zeros((SCALE_ROWS - len(parts), 128), F32))
-        codes = jnp.concatenate(parts, axis=0)
-        sizes[...] = code_scale(codes[0:8, :])
-        for number in range(2 * RING):
-            own[number, rows : rows + SCALE_ROWS, :] = codes.astype(jnp.int32).astype(I16)
-
-    def squash_rows(first, count, own, first_own, read_res, write_next):
+        parts.append(jnp.zeros((8 - len(parts), 128), F32))
+        sizes[group, here] = jnp.concatenate(parts, axis=0)
+        tell_sizes(group)
+
+    def make_shares(group, row_of):
+        for away in range(1, RING):
+            size_copy(group, away).wait_recv()
+        for way in range(2):
+            tiles = []
+            for step in range(STEPS):
+                mine = row_of(here, step, way)
+                came = mine * 0.0
+                for back in range(step + 1):
+                    came = came + row_of((here - 1 - back + (2 + 2 * back) * way + RING) % RING, step, way)
+                if step < STEPS - 1:
+                    whole = 1.0 / jnp.maximum(came + mine, 1e-30)
+                else:
+                    whole = 1.0 / TOP_CODE
+                tiles += [came * whole, mine * whole]
+            tiles.append(jnp.zeros((16, 128), F32))
+            shares[group, way] = jnp.transpose(jnp.concatenate(tiles, axis=0))
+
+    def squash_rows(count, own, first_own, read_res, write_next):
+        wide = grad.shape[1]
+
+        def add(number, carry):
+            row = pl.multiple_of(number * 16, 16)
+            value = grad[pl.ds(row, 16), :] + read_res(row)
+            grad[pl.ds(row, 16), :] = value
+            value = jnp.abs(value)
+            cols[0, pl.ds(row, 16), :] = functools.reduce(
+                jnp.add, [value[:, lane : lane + 128] for lane in range(0, wide, 128)]
+            )
+            return carry
+
+        lax.fori_loop(0, count // 16, add, 0)
+        set_rows(
+            count,
+            first_own,
+            jnp.sum(cols[0, 0:count, :], axis=1, keepdims=True) * (1.0 / wide) + 1e-12,
+        )
+
         def some(number, carry):
             row = pl.multiple_of(number * 16, 16)
-            value = grad[pl.ds(row, 16), :] + read_res(row)
-            size, code, factor = row_scale(value, value.shape[1])
-            grad[pl.ds(row, 16), :] = value
-            marks[pl.ds(first_own + row, 16), :] = jnp.broadcast_to(code, (16, 128))
-            steep = 2.0 / size
-            for lane in range(0, value.shape[1], 128):
+            size = cols[0, pl.ds(row, 16), :]
+            steep = cols[1, pl.ds(row, 16), :]
+            for lane in range(0, wide, 128):
                 piece = grad[pl.ds(row, 16), lane : lane + 128]
                 curve = jnp.tanh(piece * steep)
                 number_of = lane // 256
                 chunk = number_of // 2 if number_of % 2 == 0 else 7 - number_of // 2
                 own[2 * chunk + lane // 128 % 2, pl.ds(first_own + row, 16), :] = to_codes(
-                    curve * factor
+                    curve * TOP_CODE
                 )
                 write_next(row, lane, piece - size * curve)
             return carry
@@ -508,7 +595,22 @@
                 grad[0:rows, lane : lane + 512] = dot_nn(
                     dl_buf[part, 0:rows, :], h_buf[:, lane : lane + 512]
                 )
-            res_copy(group, part).wait()
+            if part == 0:
+                res_copy(group, part).wait()
+            else:
+
+                @pl.when(group < OUT_GROUPS - 1)
+                def _():
+                    res_copy(group, 1).wait()
+
+                @pl.when(group == OUT_GROUPS - 1)
+                def _():
+                    res_copy(group, 1, whole_rows).wait()
+                    res_buf[1, whole_rows : whole_rows + 16, :] = res_tail_ref[...]
+                    res_buf[1, whole_rows + 16 : BLOCKS[1], :] = jnp.zeros(
+                        (BLOCKS[1] - whole_rows - 16, res_buf.shape[2]), BF16
+                    )
+
             if part == 0:
 
                 @pl.when(group > 0)
@@ -522,7 +624,6 @@
                 stage[pl.ds(row, 16), 0, lane : lane + 128] = values
 
             squash_rows(
-                0,
                 rows,
                 own_out.at[group],
                 starts[part],
@@ -533,7 +634,18 @@
 
             @pl.when(group < OUT_GROUPS - 1)
             def _(part=part):
-                res_copy(group + 1, part).start()
+                if part == 0:
+                    res_copy(group + 1, 0).start()
+                else:
+
+                    @pl.when(group < OUT_GROUPS - 2)
+                    def _():
+                        res_copy(group + 1, 1).start()
+
+                    @pl.when(group == OUT_GROUPS - 2)
+                    def _():
+                        res_copy(group + 1, 1, whole_rows).start()
+
                 dl_copy(group + 1, part).start()
 
             @pl.when(group == OUT_GROUPS - 1)
@@ -542,7 +654,7 @@
                 if part == len(BLOCKS) - 1:
                     load(h_one_ref, h_buf).start()
 
-        set_sizes(OUT_ROWS, own_out.at[group], size_out.at[group])
+        set_sizes(OUT_ROWS, group)
 
     def hid_group():
         load(h_one_ref, h_buf).wait()
@@ -560,7 +672,6 @@
                 grad[pl.ds(row, 16), lane : lane + 128] = values
 
             squash_rows(
-                0,
                 256,
                 own_hid,
                 first,
@@ -569,7 +680,7 @@
             )
             hid_next_copy(part).start()
         load(x_ref, h_buf.at[:, pl.ds(0, x_ref.shape[1])]).start()
-        set_sizes(HID_ROWS, own_hid, size_hid)
+        set_sizes(HID_ROWS, HID_GROUP)
         hid_next_copy(1).wait()
 
     def in_group():
@@ -578,36 +689,45 @@
         for first in range(0, HID_ROWS, 256):
             grad[0:256, 0:wide] = dot_nn(dz_one[first : first + 256, :], h_buf[:, 0:wide])
 
+            def add(number, carry, first=first):
+                row = pl.multiple_of(number * 16, 16)
+                place = pl.multiple_of(first + row, 16)
+                value = grad[pl.ds(row, 16), 0:wide] + res_in_ref[pl.ds(place, 16), :].astype(F32)
+                grad[pl.ds(row, 16), 0:wide] = value
+                value = jnp.abs(value)
+                cols[0, pl.ds(row, 16), :] = functools.reduce(
+                    jnp.add, [value[:, lane : lane + 128] for lane in range(0, wide, 128)]
+                )
+                return carry
+
+            lax.fori_loop(0, 16, add, 0)
+            set_rows(
+                256,
+                first,
+                jnp.sum(cols[0, 0:256, :], axis=1, keepdims=True) * (1.0 / deep) + 1e-12,
+            )
+
             def some(number, carry, first=first):
                 row = pl.multiple_of(number * 16, 16)
                 place = pl.multiple_of(first + row, 16)
-                value = grad[pl.ds(row, 16), 0:wide] + res_in_ref[pl.ds(place, 16), :].astype(F32)
-                size, code, factor = row_scale(value, deep)
-                curve = jnp.tanh(value * (2.0 / size))
-                next_in_ref[pl.ds(place, 16), :] = value - size * curve
-                marks[pl.ds(place, 16), :] = jnp.broadcast_to(code, (16, 128))
+                size = cols[0, pl.ds(row, 16), :]
+                steep = cols[1, pl.ds(row, 16), :]
                 chunk = first // 64 + number // 4
                 inside = pl.multiple_of(number % 4 * 16, 16)
-                codes = to_codes(curve * factor)
-                for way in range(2):
-                    own_in[2 * chunk + way, pl.ds(inside, 16), :] = codes[
-                        :, way * 256 : (way + 1) * 256
-                    ]
+                for lane in range(0, wide, 128):
+                    piece = grad[pl.ds(row, 16), lane : lane + 128]
+                    curve = jnp.tanh(piece * steep)
+                    next_in_ref[pl.ds(place, 16), lane : lane + 128] = piece - size * curve
+                    own_in[
+                        2 * chunk + lane // 256, pl.ds(inside, 16), lane % 256 : lane % 256 + 128
+                    ] = to_codes(curve * TOP_CODE)
                 return carry
 
             lax.fori_loop(0, 16, some, 0)
-        for chunk in range(RING):
-            codes = jnp.concatenate(
-                [lane_codes(64 * chunk), jnp.zeros((SCALE_ROWS - 1, 128), F32)], axis=0
-            )
-            size_in[chunk] = code_scale(codes[0:8, :])
-            for way in range(2):
-                own_in[2 * chunk + way, 64 : 64 + SCALE_ROWS, 0:128] = codes.astype(
-                    jnp.int32
-                ).astype(I16)
-                own_in[2 * chunk + way, 64 : 64 + SCALE_ROWS, 128:256] = jnp.zeros(
-                    (SCALE_ROWS, 128), I16
-                )
+        sizes[IN_GROUP, here] = jnp.concatenate(
+            [lane_codes(64 * chunk) for chunk in range(RING)], axis=0
+        )
+        tell_sizes(IN_GROUP)
 
     def towards(way):
         return {"blk": ring_blk((here + 1 - 2 * way + RING) % RING)}
@@ -627,88 +747,69 @@
             chunk = (here - 1 + 2 * way + RING) % RING
             move(own.at[2 * chunk + way], got, 0, way, send_sem, recv_sem).start()
 
-    def hop(rows, own, got, own_sizes, step, way, send_sem, recv_sem, keep):
-        message = got.at[way, step]
-        move(message, got, step, way, send_sem, recv_sem).wait_recv()
-        ahead = here - 2 - step + way * (4 + 2 * step) + 2 * RING
-        chunk = ahead % RING
-        mine = own.at[2 * chunk + way]
-        size = own_sizes(chunk)
-        came = code_scale(from_codes(message[rows : rows + SCALE_ROWS, 0:128])[0:8, :])
-        code = scale_code(came + size)
-        whole = code_scale(code)
-        blank = jnp.zeros((112, 128), F32)
-        wide = message.shape[1]
-
-        @pl.when(step < STEPS - 1)
-        def _():
-            shares = jnp.transpose(jnp.concatenate([came / whole, size / whole, blank], axis=0))
+    def hop(rows, own, got, group, step, send_sem, recv_sem, keep):
+        for way in range(2):
+            move(got.at[way, step], got, step, way, send_sem, recv_sem).wait_recv()
+
+        def add(way, result):
+            message = got.at[way, step]
+            ahead = here - 2 - step + way * (4 + 2 * step) + 2 * RING
+            mine = own.at[2 * (ahead % RING) + way]
+            share = pltpu.roll(shares[group, way], (128 - 16 * step) % 128, 1)
             for number, first in enumerate(range(0, rows, 128)):
                 count = min(128, rows - first)
                 there = slice(first, first + count)
-                message[there, :] = to_codes(
-                    from_codes(message[there, :]) * shares[0:count, number : number + 1]
-                    + from_codes(mine[there, :]) * shares[0:count, 8 + number : 9 + number]
+                result(
+                    first,
+                    count,
+                    from_codes(message[there, :]) * share[0:count, number : number + 1]
+                    + from_codes(mine[there, :]) * share[0:count, 8 + number : 9 + number],
                 )
-            codes = jnp.concatenate([code, jnp.zeros((SCALE_ROWS - 8, 128), F32)], axis=0)
-            message[rows : rows + SCALE_ROWS, 0:128] = codes.astype(jnp.int32).astype(I16)
-            move(message, got, step + 1, way, send_sem, recv_sem).start()
+
+        @pl.when(step < STEPS - 1)
+        def _():
+            for way in range(2):
+
+                def write(first, count, value, way=way):
+                    got[way, step, first : first + count, :] = to_codes(value)
+
+                add(way, write)
+            for way in range(2):
+                move(got.at[way, step], got, step + 1, way, send_sem, recv_sem).start()
 
         @pl.when(step == STEPS - 1)
         def _():
-            shares = jnp.transpose(
-                jnp.concatenate([came * (1.0 / TOP_CODE), size * (1.0 / TOP_CODE), blank], axis=0)
-            )
-            square = jnp.zeros((1, wide), F32)
-            for number, first in enumerate(range(0, rows, 128)):
-                count = min(128, rows - first)
-                there = slice(first, first + count)
-                value = (
-                    from_codes(message[there, :]) * shares[0:count, number : number + 1]
-                    + from_codes(mine[there, :]) * shares[0:count, 8 + number : 9 + number]
-                )
-                keep(first, count, value)
-                square = square + jnp.sum(value * value, axis=0, keepdims=True)
-            for lane in range(0, wide, 128):
-                stats_ref[0:1, :] += square[:, lane : lane + 128]
-
-    def out_hop(group, step, way):
-        def keep(first, count, value):
+            for way in range(2):
+
+                def finish_rows(first, count, value, way=way):
+                    keep(way, first, count, value)
+                    square = jnp.sum(value * value, axis=0, keepdims=True)
+                    for lane in range(0, value.shape[1], 128):
+                        stats_ref[0:1, :] += square[:, lane : lane + 128]
+
+                add(way, finish_rows)
+
+    def out_hop(group, step):
+        def keep(way, first, count, value):
             row = pl.multiple_of(group * OUT_ROWS + first, 16)
-
-            @pl.when(way == 0)
-            def _():
-                red_out_ref[pl.ds(row, count), 0:128] = value
-
-            @pl.when(way == 1)
-            def _():
-                red_out_ref[pl.ds(row, count), 128:256] = value
+            red_out_ref[pl.ds(row, count), way * 128 : (way + 1) * 128] = value
 
         hop(
             OUT_ROWS,
             own_out.at[group],
             got_out.at[group],
-            lambda chunk: size_out[group],
+            group,
             step,
-            way,
             out_send.at[group],
             out_recv.at[group],
             keep,
         )
 
-    def hid_hop(step, way):
-        def keep(first, count, value):
-            @pl.when(way == 0)
-            def _():
-                red_hid_ref[first : first + count, 0:128] = value
-
-            @pl.when(way == 1)
-            def _():
-                red_hid_ref[first : first + count, 128:256] = value
-
-        hop(
-            HID_ROWS, own_hid, got_hid, lambda chunk: size_hid[...], step, way, hid_send, hid_recv, keep
-        )
+    def hid_hop(step):
+        def keep(way, first, count, value):
+            red_hid_ref[first : first + count, way * 128 : (way + 1) * 128] = value
+
+        hop(HID_ROWS, own_hid, got_hid, HID_GROUP, step, hid_send, hid_recv, keep)
 
     def share_move(step, way):
         place = (here - step + 2 * step * way + 2 * RING) % RING
@@ -721,38 +822,39 @@
             device_id_type=MESH,
         )
 
-    def in_hop(step, way):
-        def keep(first, count, value):
+    def in_hop(step):
+        def keep(way, first, count, value):
             share_in[way, here] = value
 
-        hop(64, own_in, got_in, lambda chunk: size_in[chunk], step, way, in_send, in_recv, keep)
+        hop(64, own_in, got_in, IN_GROUP, step, in_send, in_recv, keep)
 
         @pl.when(step == STEPS - 1)
         def _():
-            share_move(0, way).start()
-
-    def share_hop(step, way):
-        share_move(step, way).wait_recv()
+            for way in range(2):
+                share_move(0, way).start()
+
+    def share_hop(step):
+        for way in range(2):
+            share_move(step, way).wait_recv()
 
         @pl.when(step < STEPS - 1)
         def _():
-            share_move(step + 1, way).start()
-
-    def in_step(index, way):
+            for way in range(2):
+                share_move(step + 1, way).start()
+
+    def in_step(index):
         @pl.when((index >= 0) & (index < STEPS))
         def _():
-            in_hop(index, way)
+            in_hop(index)
 
         @pl.when((index >= STEPS) & (index < 2 * STEPS))
         def _():
-            share_hop(index - STEPS, way)
-
-    def ways(work):
-        def one(way, carry):
-            work(way)
-            return carry
-
-        lax.fori_loop(0, 2, one, 0)
+            share_hop(index - STEPS)
+
+    def chunk_row(place, step, way):
+        chunk = (here - 2 - step + way * (4 + 2 * step) + 2 * RING) % RING
+        line = sizes[IN_GROUP, place, pl.ds(chunk, 1), :]
+        return jnp.broadcast_to(line, (8, 128))
 
     def wave(number, carry):
         @pl.when(number < OUT_GROUPS)
@@ -765,26 +867,36 @@
             hid_group()
             first_moves(own_hid, got_hid, hid_send, hid_recv)
 
+        @pl.when((number >= 1) & (number <= OUT_GROUPS))
+        def _():
+            group = number - 1
+            make_shares(group, lambda place, step, way: sizes[group, place])
+
+        @pl.when(number == HID_WAVE + 1)
+        def _():
+            make_shares(HID_GROUP, lambda place, step, way: sizes[HID_GROUP, place])
+
+        @pl.when(number == IN_WAVE + 1)
+        def _():
+            make_shares(IN_GROUP, chunk_row)
+
         index = 2 * (number - IN_WAVE - 1)
-        ways(lambda way: in_step(index, way))
-
-        def both(way):
-            @pl.when((number > HID_WAVE) & (number <= HID_WAVE + STEPS))
+        in_step(index)
+
+        @pl.when((number > HID_WAVE) & (number <= HID_WAVE + STEPS))
+        def _():
+            hid_hop(number - HID_WAVE - 1)
+
+        def outs(group, carry):
+            step = number - 1 - group
+
+            @pl.when((step >= 0) & (step < STEPS))
             def _():
-                hid_hop(number - HID_WAVE - 1, way)
-
-            def outs(group, carry):
-                step = number - 1 - group
-
-                @pl.when((step >= 0) & (step < STEPS))
-                def _():
-                    out_hop(group, step, way)
-
-                return carry
-
-            lax.fori_loop(0, OUT_GROUPS, outs, 0)
-
-        ways(both)
+                out_hop(group, step)
+
+            return carry
+
+        lax.fori_loop(0, OUT_GROUPS, outs, 0)
 
         @pl.when((number == 1) | (number == 2))
         def _():
@@ -802,7 +914,7 @@
             for away in range(1, RING):
                 vec_copy(away).start()
 
-        ways(lambda way: in_step(index + 1, way))
+        in_step(index + 1)
         return carry
 
     lax.fori_loop(0, IN_WAVE + 1 + STEPS, wave, 0)
@@ -821,6 +933,8 @@
     vec_sum_ref[...] = total
     for away in range(1, RING):
         vec_copy(away).wait_send()
+        for group in range(OUT_GROUPS + 2):
+            size_copy(group, away).wait_send()
     for slot in range(2):
         core_move(1, 2 + slot).wait_send()
         far_move(1, 2 + slot).wait_send()
@@ -842,16 +956,16 @@
 
 
 def reduce_grads(
-    dl, h_two, h_one, x, part, slope_two, slope_one, w_hid, res_out, res_hid, res_in, vec, senones, deep
+    dl, h_two, h_one, x, part, slope_two, slope_one, w_hid, res_out, res_hid, res_in, res_tail, vec, senones, deep
 ):
     frames, wide = h_two.shape
     in_wide = x.shape[1]
     units = w_hid.shape[1]
     vmem = pl.BlockSpec(memory_space=pltpu.VMEM)
     hbm = pl.BlockSpec(memory_space=pl.ANY)
-    message = OUT_ROWS + SCALE_ROWS
-    hid_message = HID_ROWS + SCALE_ROWS
-    in_message = 64 + SCALE_ROWS
+    message = OUT_ROWS
+    hid_message = HID_ROWS
+    in_message = 64
     sem = pltpu.SemaphoreType.DMA
     return pl.pallas_call(
         functools.partial(reduce_kernel, deep),
@@ -865,7 +979,7 @@
             jax.ShapeDtypeStruct(vec.shape, F32),
             jax.ShapeDtypeStruct((8, 128), F32),
         ),
-        in_specs=[hbm] * 7 + [vmem] + [hbm] * 2 + [vmem] * 2,
+        in_specs=[hbm] * 7 + [vmem] + [hbm] * 2 + [vmem] * 3,
         out_specs=(hbm, hbm) + (vmem,) * 6,
         scratch_shapes=[
             pltpu.VMEM((BLOCKS[0], wide), F32),
@@ -875,6 +989,7 @@
             pltpu.VMEM((frames, wide), BF16),
             pltpu.VMEM((2, 256, units), F32),
             pltpu.VMEM((640, 128), F32),
+            pltpu.VMEM((2, BLOCKS[0], 128), F32),
             pltpu.VMEM((4, 256, 2 * units), F32),
             pltpu.VMEM((256, units), BF16),
             pltpu.VMEM((units, frames), BF16),
@@ -885,14 +1000,13 @@
             pltpu.VMEM((2, 4, 272, units), I16),
             pltpu.VMEM((OUT_GROUPS, 2 * RING, message, 128), I16),
             pltpu.VMEM((OUT_GROUPS, 2, STEPS, message, 128), I16),
-            pltpu.VMEM((OUT_GROUPS, 8, 128), F32),
             pltpu.VMEM((2 * RING, hid_message, 128), I16),
             pltpu.VMEM((2, STEPS, hid_message, 128), I16),
-            pltpu.VMEM((8, 128), F32),
             pltpu.VMEM((2 * RING, in_message, 256), I16),
             pltpu.VMEM((2, STEPS, in_message, 256), I16),
-            pltpu.VMEM((RING, 8, 128), F32),
             pltpu.VMEM((2, RING, 64, 256), F32),
+            pltpu.VMEM((OUT_GROUPS + 2, RING, 8, 128), F32),
+            pltpu.VMEM((OUT_GROUPS + 2, 2, 128, 128), F32),
             pltpu.VMEM(vec.shape, F32),
             pltpu.VMEM((RING,) + vec.shape, F32),
             sem((2,)),
@@ -914,11 +1028,13 @@
             sem((2, STEPS)),
             sem((STEPS,)),
             sem((STEPS,)),
+            sem((OUT_GROUPS + 2, STEPS)),
+            sem((OUT_GROUPS + 2, STEPS)),
         ],
         compiler_params=pltpu.CompilerParams(
             collective_id=1, has_side_effects=True, vmem_limit_bytes=63 * 1024 * 1024
         ),
-    )(dl, h_two, h_one, x, part, slope_two, slope_one, w_hid, res_out, res_hid, res_in, vec)
+    )(dl, h_two, h_one, x, part, slope_two, slope_one, w_hid, res_out, res_hid, res_in, res_tail, vec)
 
 
 RING_STARTS = (0, 2, 5, 7, 9)
@@ -1300,7 +1416,8 @@
 
 DIM_BITS = (2, 4, 8)
 ORDERS = ((0, 1, 2), (1, 2, 0), (2, 0, 1))
-PIECE = 48
+PIECES = ((0, 48), (48, 48), (96, 32))
+SIZE_PIECE = 2
 LIGHT_HID = 3
 LIGHT_IN = 2
 
@@ -1339,9 +1456,11 @@
     next_in_ref,
     norm_ref,
     codes,
+    sizes,
     tops,
     lows,
     scales,
+    weights,
     xs,
     us,
     vs,
@@ -1365,6 +1484,8 @@
     spread_recv,
     pair_send,
     pair_recv,
+    size_send,
+    size_recv,
 ):
     blk = lax.axis_index("blk")
     col = lax.axis_index("col")
@@ -1396,8 +1517,6 @@
     sums[0, 5:6, :] = fold(mom_in_ref[...] * red_in_ref[...]) * share
     sums[0, 6:7, :] = fold(red_in_ref[...] * red_in_ref[...]) * share
     sums[0, 7:8, :] = jnp.zeros((1, 128), F32)
-    for turn in range(2):
-        codes[turn, 0, rows:, :] = jnp.zeros((codes.shape[2] - rows, wide), I16)
     eye = lax.broadcasted_iota(jnp.int32, (rows, rows), 0) == lax.broadcasted_iota(
         jnp.int32, (rows, rows), 1
     )
@@ -1470,49 +1589,86 @@
     numbers = {move: number for number, move in enumerate(MOVES)}
 
     def part(turn, slot, piece):
-        return codes.at[turn, slot, pl.ds(piece * PIECE, PIECE), :]
+        first, count = PIECES[piece]
+        return codes.at[turn, slot, pl.ds(first, count), :]
 
     def send(turn, move):
         piece, slot, dim = move
-        return pltpu.make_async_remote_copy(
-            src_ref=part(turn, slot, piece),
-            dst_ref=part(turn, slot | DIM_BITS[dim], piece),
-            send_sem=send_sems.at[numbers[move]],
-            recv_sem=recv_sems.at[turn, slot | DIM_BITS[dim], piece],
-            device_id=dims[dim],
-            device_id_type=MESH,
-        )
+        there = slot | DIM_BITS[dim]
+        copies = [
+            pltpu.make_async_remote_copy(
+                src_ref=part(turn, slot, piece),
+                dst_ref=part(turn, there, piece),
+                send_sem=send_sems.at[numbers[move]],
+                recv_sem=recv_sems.at[turn, there, piece],
+                device_id=dims[dim],
+                device_id_type=MESH,
+            )
+        ]
+        if piece == SIZE_PIECE:
+            copies.append(
+                pltpu.make_async_remote_copy(
+                    src_ref=sizes.at[turn, slot],
+                    dst_ref=sizes.at[turn, there],
+                    send_sem=size_send.at[numbers[move]],
+                    recv_sem=size_recv.at[turn, there],
+                    device_id=dims[dim],
+                    device_id_type=MESH,
+                )
+            )
+        return copies
 
     def send_all(turn, moves):
         for move in moves:
-            send(turn, move).start()
+            for copy in send(turn, move):
+                copy.start()
 
     def to_core(turn, slot, piece):
-        return pltpu.make_async_remote_copy(
-            src_ref=part(turn, slot, piece),
-            dst_ref=part(turn, slot + 1, piece),
-            send_sem=core_sems.at[slot // 2, piece],
-            recv_sem=recv_sems.at[turn, slot + 1, piece],
-            device_id=other_core,
-            device_id_type=MESH,
-        )
+        copies = [
+            pltpu.make_async_remote_copy(
+                src_ref=part(turn, slot, piece),
+                dst_ref=part(turn, slot + 1, piece),
+                send_sem=core_sems.at[slot // 2, piece],
+                recv_sem=recv_sems.at[turn, slot + 1, piece],
+                device_id=other_core,
+                device_id_type=MESH,
+            )
+        ]
+        if piece == SIZE_PIECE:
+            copies.append(
+                pltpu.make_async_remote_copy(
+                    src_ref=sizes.at[turn, slot],
+                    dst_ref=sizes.at[turn, slot + 1],
+                    send_sem=core_sems.at[slot // 2, 3],
+                    recv_sem=size_recv.at[turn, slot + 1],
+                    device_id=other_core,
+                    device_id_type=MESH,
+                )
+            )
+        return copies
 
     def arrived(turn, slot, piece):
-        pltpu.make_async_remote_copy(
-            src_ref=part(turn, slot, piece),
-            dst_ref=part(turn, slot, piece),
-            send_sem=core_sems.at[0, 0],
-            recv_sem=recv_sems.at[turn, slot, piece],
-            device_id=other_core,
-            device_id_type=MESH,
-        ).wait_recv()
+        def wait(ref, sem):
+            pltpu.make_async_remote_copy(
+                src_ref=ref,
+                dst_ref=ref,
+                send_sem=core_sems.at[0, 0],
+                recv_sem=sem,
+                device_id=other_core,
+                device_id_type=MESH,
+            ).wait_recv()
+
+        wait(part(turn, slot, piece), recv_sems.at[turn, slot, piece])
+        if piece == SIZE_PIECE:
+            wait(sizes.at[turn, slot], size_recv.at[turn, slot])
 
     def forward(turn, moves, on=()):
         for number, (slot, piece) in enumerate(landed(moves)):
             arrived(turn, slot, piece)
-            to_core(turn, slot, piece).start()
+            for copy in to_core(turn, slot, piece):
+                copy.start()
             if on:
-                send(turn, on[number]).start()
+                send_all(turn, on[number : number + 1])
 
     def gram_copy():
         return pltpu.make_async_remote_copy(
@@ -1524,37 +1680,44 @@
             device_id_type=MESH,
         )
 
-    def unpack(turn, pair, light):
+    def unpack(turn, index, pair, light):
         for core in range(2):
-            here = slice(core * rows, (core + 1) * rows)
-            whole = from_codes(codes[turn, 2 * pair + core, 0:rows, :])
+            here = pl.ds(pl.multiple_of(index * 2 * rows + core * rows, rows), rows)
+            slot = 2 * pair + core
             if light:
-                tops[pair, here, :] = whole.astype(BF16)
+                tops[here, :] = from_codes(codes[turn, slot]).astype(BF16)
             else:
-                top, low = halves(whole)
-                tops[pair, here, :] = top
-                lows[pair, here, :] = low
-            step = from_codes(codes[turn, 2 * pair + core, rows : rows + 16, 0:rows])
-            size = code_scale(step[0:8, :]) * (1.0 / TOP_CODE)
-            scales[pair, :, here] = size * size
-
-    def apply_pair(pair, out, light):
+                top, low = halves(from_codes(codes[turn, slot]))
+                tops[here, :] = top
+                lows[here, :] = low
+            size = sizes[turn, slot]
+            scales[:, here] = size * size
+
+    def inner(first, count, light):
+        here = pl.ds(first, count)
+        if light:
+            values = dot_nt(lhs[0:rows, :], tops[here, :])
+            weights[0:rows, here] = (values * scales[0:1, here]).astype(BF16)
+        else:
+            both = dot_nt(lhs[...], tops[here, :])
+            values = both[:rows] + both[rows:] + dot_nt(lhs[0:rows, :], lows[here, :])
+            top, low = halves(values * scales[0:1, here])
+            weights[0:rows, here] = top
+            weights[rows:, here] = low
+
+    def outer(first, count, out, add, light):
         cut = 512
-        if light:
-            inner = (dot_nt(lhs[0:rows, :], tops[pair]) * scales[pair, 0:1, :]).astype(BF16)
-            for start in range(0, wide, cut):
-                lanes = slice(start, start + cut)
-                out[:, lanes] += dot_nn(inner, tops[pair, :, lanes])
-            return
-        both = dot_nt(lhs[...], tops[pair])
-        inner = both[:rows] + both[rows:] + dot_nt(lhs[0:rows, :], lows[pair])
-        inner = inner * scales[pair, 0:1, :]
-        top, low = halves(inner)
-        stack = jnp.concatenate([top, low], axis=0)
+        here = slice(first, first + count)
         for start in range(0, wide, cut):
             lanes = slice(start, start + cut)
-            both = dot_nn(stack, tops[pair, :, lanes])
-            out[:, lanes] += both[:rows] + both[rows:] + dot_nn(top, lows[pair, :, lanes])
+            if light:
+                value = dot_nn(weights[0:rows, here], tops[here, lanes])
+            else:
+                both = dot_nn(weights[:, here], tops[here, lanes])
+                value = both[:rows] + both[rows:] + dot_nn(weights[0:rows, here], lows[here, lanes])
+            if add:
+                value = value + out[:, lanes]
+            out[:, lanes] = value
 
     def set_lhs(values):
         top, low = halves(values)
@@ -1602,20 +1765,16 @@
     def iteration(number, carry):
         turn = number % 2
         values = xs[...]
-        largest = jnp.max(jnp.abs(values), axis=1, keepdims=True)
-        step = scale_code(largest)
-        codes[turn, 0, 0:rows, :] = to_codes(values * (TOP_CODE / code_scale(step)))
-        lane_step = jnp.sum(jnp.where(eye, step, 0.0), axis=0, keepdims=True)
-        codes[turn, 0, rows : rows + 16, 0:rows] = jnp.broadcast_to(
-            lane_step.astype(jnp.int32), (16, rows)
-        ).astype(I16)
+        largest = jnp.maximum(jnp.max(jnp.abs(values), axis=1, keepdims=True), 1e-30)
+        codes[turn, 0] = to_codes(values * (TOP_CODE / largest))
+        lane_size = jnp.sum(jnp.where(eye, largest, 0.0), axis=0, keepdims=True)
+        sizes[turn, 0] = jnp.broadcast_to(lane_size * (1.0 / TOP_CODE), (8, rows))
         send_all(turn, FIRST)
         for piece in range(3):
-            to_core(turn, 0, piece).start()
+            for copy in to_core(turn, 0, piece):
+                copy.start()
         send_all(turn, SECOND)
         set_lhs(values)
-        us[...] = jnp.zeros_like(us)
-        vs[...] = jnp.zeros_like(vs)
 
         def first_pass(index, carry):
             pair = index + (index // 3) * (1 - index // 4) - (index // 4) * (1 - index // 5)
@@ -1659,26 +1818,35 @@
                 arrived(turn, 2 * pair + 1, piece)
 
             def work(light):
-                unpack(turn, pair, light)
-                apply_pair(pair, us, light)
+                unpack(turn, index, pair, light)
+                inner(pl.multiple_of(index * 2 * rows, 2 * rows), 2 * rows, light)
 
             by_weight(number, LIGHT_HID, work)
+
+            @pl.when(index == 3)
+            def _():
+                by_weight(number, LIGHT_HID, lambda light: outer(0, wide // 2, us, False, light))
+
             return carry
 
         lax.fori_loop(0, 8, first_pass, 0)
-        set_lhs(us[...])
-
-        def second_pass(pair, carry):
-            by_weight(number, LIGHT_HID, lambda light: apply_pair(pair, vs, light))
-            return carry
-
-        lax.fori_loop(0, 8, second_pass, 0)
+
+        def second_pass(light):
+            outer(wide // 2, wide // 2, us, True, light)
+            set_lhs(us[...])
+            for first in range(0, wide, 512):
+                inner(first, 512, light)
+            outer(0, wide, vs, False, light)
+
+        by_weight(number, LIGHT_HID, second_pass)
         xs[...] = NS_A * xs[...] + NS_B * us[...] + NS_C * vs[...]
         for move in MOVES:
-            send(turn, move).wait_send()
+            for copy in send(turn, move):
+                copy.wait_send()
         for pair in range(8):
             for piece in range(3):
-                to_core(turn, 2 * pair, piece).wait_send()
+                for copy in to_core(turn, 2 * pair, piece):
+                    copy.wait_send()
         return carry
 
     lax.fori_loop(0, NS, iteration, 0)
@@ -1726,10 +1894,12 @@
         in_specs=[vmem] * 5,
         out_specs=(vmem,) * 5,
         scratch_shapes=[
-            pltpu.VMEM((2, 16, 3 * PIECE, wide), I16),
-            pltpu.VMEM((8, 2 * rows, wide), BF16),
-            pltpu.VMEM((8, 2 * rows, wide), BF16),
-            pltpu.VMEM((8, 8, 2 * rows), F32),
+            pltpu.VMEM((2, 16, rows, wide), I16),
+            pltpu.VMEM((2, 16, 8, rows), F32),
+            pltpu.VMEM((wide, wide), BF16),
+            pltpu.VMEM((wide, wide), BF16),
+            pltpu.VMEM((8, wide), F32),
+            pltpu.VMEM((2 * rows, wide), BF16),
             pltpu.VMEM((rows, wide), F32),
             pltpu.VMEM((rows, wide), F32),
             pltpu.VMEM((rows, wide), F32),
@@ -1743,7 +1913,7 @@
             pltpu.VMEM((6, 8, 128), F32),
             pltpu.VMEM((5, 8, 128), F32),
             sem((len(MOVES),)),
-            sem((8, 3)),
+            sem((8, 4)),
             sem((2, 16, 3)),
             sem((3,)),
             sem((3,)),
@@ -1753,6 +1923,8 @@
             sem((7,)),
             sem((2,)),
             sem((2,)),
+            sem((len(MOVES),)),
+            sem((2, 16)),
         ],
         compiler_params=pltpu.CompilerParams(
             collective_id=0, has_side_effects=True, vmem_limit_bytes=60 * 1024 * 1024
@@ -1965,9 +2137,10 @@
         slope_two,
         slope_one,
         low_hidden,
-        jnp.pad(res_output[0], ((0, 0), (0, rows_out - scol))).T,
+        res_output[0].T,
         res_hidden[0].T,
         jnp.pad(res_input[0], ((0, padded - deep), (0, 0))).T,
+        jnp.pad(res_output[0, :, scol // 16 * 16 :], ((0, 0), (0, 16 - scol % 16))).T,
         vec,
         scol,
         deep,

time: 807 us -> 720 us (0.89)
  Pallas kernels: 715 us -> 637 us
  local copies, waits for them, and re-layouts: 51.6 us -> 43.3 us
    pallas_call x1, Pallas kernels: 256 us -> 215 us  [reduce_grads(): pl.pallas_call(functools.partial(reduce_kernel, deep), out_shape=(jax.Sha...]
    pallas_call x1, Pallas kernels: 299 us -> 262 us  [muon(): pl.pallas_call(muon_kernel, out_shape=(jax.ShapeDtypeStruct((4, rows, hei...]
    transpose x1, local copies, waits for them, and re-layouts: 9.65 us -> 0.64 us  [fast_body(): jnp.pad(res_output[0, :, scol // 16 * 16:], ((0, 0), (0, 16 - scol % 16)))]
where the time goes in v6:
time: 720 us; the launch traced here: 714 us
  Pallas kernels  637 us (88%)
  local copies, waits for them, and re-layouts  43.3 us (6%)
  matrix products  17.5 us (2%)
  other arithmetic  15.2 us (2%)
    pallas_call x1, Pallas kernels, muon(): pl.pallas_call(muon_kernel, out_shape=(jax.ShapeDtypeStruct((4, rows, hei...  262 us
    pallas_call x1, Pallas kernels, reduce_grads(): pl.pallas_call(functools.partial(reduce_kernel, deep), out_shape=(jax.Sha...  215 us
    pallas_call x1, Pallas kernels, forward_pass(): pl.pallas_call(functools.partial(forward_kernel, slot_count), out_shape=t...  160 us
    unnamed x43, local copies, waits for them, and re-layouts  28.4 us
    dot_general x1, matrix products, inner_rows(): lax.dot_general(left_side, right_side, (((0,), (0,)), ((), ())), preferre...  17.5 us

profile of v6, /device:TPU:0, one launch (start us, length us, event | category | flops | bytes accessed | tf_op | source)
XLA Modules:
  0.0 714.4 jit_solution(3048404685138774270)
XLA Ops:
  2.0 0.7 slice_reduce_fusion
  4.7 159.9 %shard_map.271 = (bf16[1024,512]{1,0:T(8,128)(2,1)}, bf16[1024,2048]{1,0:T(8,128)(2,1)}, bf16[1024,2048]{1,0:T(8,128)(2,1)}, f32[1024,512]{1,0:T(8,128)}, f32[10...) custom-call(bf16[256,440]{1,0:T(8,128)(2,1)} %bitcast.61, ...), custom_call_target="tpu_custom_call" | custom-call | tf_op jit(solution)/shard_map/pallas_call | solution.py:1380
  164.7 17.5 %fusion.3.part_ref = f32[1024,2048]{1,0:T(8,128)} fusion(bf16[2368,1024]{1,0:T(8,128)(2,1)} %get-tuple-element.50.dl_ref, bf16[2368,2048]{1,0:T(8,128)(2,1)} %get-tuple-element.54), kind=kOutput, calls=%fused_computation.26 | convolution fusion | flops 9932111872 | bytes 22937600 | tf_op jit(solution)/shard_map/dot_general | solution.py:38
  182.8 0.7 concatenate.5
  184.1 2.4 copy.31
  186.7 0.8 pad_bitcast_fusion.res_in_ref
  187.6 0.8 slice_bitcast_fusion.1
  188.9 215.2 %shard_map.272 = (f32[2326,1,2048]{2,1,0:T(1,128)}, f32[512,2048]{1,0:T(8,128)}, f32[512,512]{1,0:T(8,128)}, f32[2368,256]{1,0:T(8,128)}, f32[512,256]{1,0:T(8,1...) custom-call(bf16[2368,1024]{1,0:T(8,128)(2,1)} %get-tuple-element.50.dl_ref, ...), custom_call_target="tpu_custom_call" | custom-call | tf_op jit(solution)/shard_map/pallas_call | solution.py:970
  404.1 1.4 multiply_reduce_fusion
  406.2 1.3 scatter.4.stats_ref
  407.5 2.5 copy.34
  410.0 1.1 pad.33.mom_in_ref
  411.2 1.0 copy.33
  412.2 261.6 %shard_map.273 = (f32[4,128,256]{2,1,0:T(8,128)}, f32[512,512]{1,0:T(8,128)}, f32[512,256]{1,0:T(8,128)}, f32[512,512]{1,0:T(8,128)}, f32[8,128]{1,0:T(8,128)}) custom-call(f32[8,128]{1,0:T(8,128)} %scatter.4.stats_ref, f32[512,256]{1,0:T(8,128)} %get-tuple-element.62.red_hid_ref, f32[512,256]{1,0:T(8,128)} %bitcast.59, f32[512,512]{1,0:T(8,128)} %bitcast.56, ...), custom_call_target="tpu_custom_call" | custom-call | tf_op jit(solution)/shard_map/pallas_call | solution.py:1885
  673.7 1.3 fusion.2
  676.4 9.1 %multiply_subtract_fusion = (f32[256,2326]{0,1:T(8,128)}, f32[256,2326]{0,1:T(8,128)}, f32[256,2326]{0,1:T(8,128)}) fusion(f32[256,2326]{0,1:T(8,128)S(1)} %copy-done, f32[256,2326]{0,1:T(8,128)} %param.27, f32[2368,256]{1,0:T(8,128)} %get-tuple-element.67, f32[]{:T(128)} %bitcast.22, f32[256,2326]{0,1:T(8,128)} %param.28), kind=kLoop, calls=%fused_computation.3 | loop fusion | flops 8931840 | bytes 16672772 | tf_op jit(solution)/shard_map/sub | solution.py:78
  685.8 0.8 copy-done.2
  686.5 0.9 bitcast_subtract_fusion
  687.4 1.1 multiply_subtract_fusion.1
  688.6 1.0 slice.70
  689.5 1.0 copy.36
  691.1 5.4 copy.38
  696.6 1.2 copy.37
  697.9 16.3 %copy.41 = f32[1,2048,2326]{1,0,2:T(1,128)} copy(f32[1,2048,2326]{1,0,2:T(1,128)} %bitcast.51) | data formatting | bytes 38109184
  (53 shorter events, 7.7 us)
Async XLA Ops:
  164.6 17.6 %copy-start.17 = (f32[8,128]{1,0:T(8,128)S(1)}, f32[8,128]{1,0:T(8,128)}, u32[]{:S(2)}) copy-start(f32[8,128]{1,0:T(8,128)} %get-tuple-element.59) | copy-start | bytes 12292
  164.6 18.2 %copy-start.16 = (f32[24,128]{1,0:T(8,128)S(1)}, f32[24,128]{1,0:T(8,128)}, u32[]{:S(2)}) copy-start(f32[24,128]{1,0:T(8,128)} %get-tuple-element.58) | copy-start | bytes 36868
  164.6 19.5 %copy-start.3 = (bf16[1,2048,512]{2,1,0:T(8,128)(2,1)S(1)}, bf16[1,2048,512]{2,1,0:T(8,128)(2,1)}, u32[]{:S(2)}) copy-start(bf16[1,2048,512]{2,1,0:T(8,128)(2,1)} %param.32) | copy-start | bytes 6291460
  182.2 4.3 copy-start.11
  404.1 5.9 copy-start.5
  404.1 7.0 copy-start.8
  411.1 263.9 %copy-start.12 = (f32[32,128]{1,0:T(8,128)S(1)}, f32[32,128]{1,0:T(8,128)}, u32[]{:S(2)}) copy-start(f32[32,128]{1,0:T(8,128)} %get-tuple-element.60) | copy-start | bytes 49156
  411.1 264.6 %copy-start.13 = (f32[1,3350]{1,0:T(1,128)S(1)}, f32[1,3350]{1,0:T(1,128)}, u32[]{:S(2)}) copy-start(f32[1,3350]{1,0:T(1,128)} %param.24) | copy-start | bytes 40204
  411.1 264.6 %copy-start.14 = (f32[1,3350]{1,0:T(1,128)S(1)}, f32[1,3350]{1,0:T(1,128)}, u32[]{:S(2)}) copy-start(f32[1,3350]{1,0:T(1,128)} %param.29) | copy-start | bytes 40204
  411.1 264.6 %copy-start.15 = (f32[1,3350]{1,0:T(1,128)S(1)}, f32[1,3350]{1,0:T(1,128)}, u32[]{:S(2)}) copy-start(f32[1,3350]{1,0:T(1,128)} %param.30) | copy-start | bytes 40204
  411.1 265.3 %copy-start = (f32[256,2326]{0,1:T(8,128)S(1)}, f32[256,2326]{0,1:T(8,128)}, u32[]{:S(2)}) copy-start(f32[256,2326]{0,1:T(8,128)} %param.23) | copy-start | bytes 7145476
  676.4 9.1 %copy-start.10 = (f32[4,128,256]{2,1,0:T(8,128)S(1)}, f32[4,128,256]{2,1,0:T(8,128)}, u32[]{:S(2)}) copy-start(f32[4,128,256]{2,1,0:T(8,128)} %get-tuple-element.66) | copy-start | bytes 1572868
  685.5 1.0 copy-start.2
  685.5 1.9 copy-start.1
  685.5 1.9 copy-start.7
  686.5 2.0 copy-start.6
  687.4 2.1 copy-start.9
  691.1 5.4 copy-start.4

commit v7 on v6

--- a/solution.py
+++ b/solution.py
@@ -103,7 +103,7 @@
 HID_ROWS = 512
 HID_GROUP = 4
 IN_GROUP = 5
-HID_WAVE = 4
+HID_WAVE = 6
 IN_WAVE = 6
 
 
@@ -154,6 +154,7 @@
     red_out_ref,
     red_hid_ref,
     red_in_ref,
+    red_far_ref,
     vec_sum_ref,
     stats_ref,
     grad,
@@ -179,6 +180,7 @@
     own_in,
     got_in,
     share_in,
+    share_far,
     sizes,
     shares,
     vec,
@@ -204,6 +206,8 @@
     vec_recv,
     size_send,
     size_recv,
+    share_far_send,
+    share_far_recv,
 ):
     blk = lax.axis_index("blk")
     col = lax.axis_index("col")
@@ -488,9 +492,6 @@
     far_out[:, CHUNK:, :] = jnp.zeros((2, 16, units), I16)
     slope_copy(0, 0).start()
     slope_copy(0, 1).start()
-    blocks(0, 4, start_block)
-    blocks(0, 4, lambda block: cross(0, block))
-
     def vec_copy(away):
         return pltpu.make_async_remote_copy(
             src_ref=vec,
@@ -822,6 +823,16 @@
             device_id_type=MESH,
         )
 
+    def share_across(way, place):
+        return pltpu.make_async_remote_copy(
+            src_ref=share_in.at[way, place],
+            dst_ref=share_far.at[way, place],
+            send_sem=share_far_send.at[way, place],
+            recv_sem=share_far_recv.at[way, place],
+            device_id=across,
+            device_id_type=MESH,
+        )
+
     def in_hop(step):
         def keep(way, first, count, value):
             share_in[way, here] = value
@@ -832,10 +843,12 @@
         def _():
             for way in range(2):
                 share_move(0, way).start()
+                share_across(way, here).start()
 
     def share_hop(step):
         for way in range(2):
             share_move(step, way).wait_recv()
+            share_across(way, (here - 1 - step + (2 + 2 * step) * way + RING) % RING).start()
 
         @pl.when(step < STEPS - 1)
         def _():
@@ -898,11 +911,19 @@
 
         lax.fori_loop(0, OUT_GROUPS, outs, 0)
 
-        @pl.when((number == 1) | (number == 2))
+        @pl.when(number == 1)
         def _():
-            blocks(2 * number - 2, 2 * number, turn_block)
-
-        @pl.when(number == 3)
+            blocks(0, 4, start_block)
+
+        @pl.when(number == 2)
+        def _():
+            blocks(0, 4, lambda block: cross(0, block))
+
+        @pl.when((number == 3) | (number == 4))
+        def _():
+            blocks(2 * number - 6, 2 * number - 4, turn_block)
+
+        @pl.when(number == 4)
         def _():
             blocks(0, 4, lambda block: cross(1, block))
 
@@ -919,11 +940,22 @@
 
     lax.fori_loop(0, IN_WAVE + 1 + STEPS, wave, 0)
 
+    def unfold(shares_of, out):
+        for place in range(0, RING, 2):
+            for way in range(2):
+                for lane in range(0, 256, 128):
+                    tile = jnp.concatenate(
+                        [shares_of[way, place + more, :, lane : lane + 128] for more in range(2)],
+                        axis=0,
+                    )
+                    first = way * 256 + lane
+                    out[first : first + 128, place * 64 : place * 64 + 128] = jnp.transpose(tile)
+
+    unfold(share_in, red_in_ref)
     for place in range(RING):
         for way in range(2):
-            red_in_ref[place * 64 : (place + 1) * 64, way * 256 : (way + 1) * 256] = share_in[
-                way, place
-            ]
+            share_across(way, place).wait_recv()
+    unfold(share_far, red_far_ref)
     for away in range(1, RING):
         vec_copy(away).wait_recv()
     vecs[blk] = vec[...]
@@ -931,6 +963,11 @@
     for number in range(1, RING):
         total = total + vecs[number]
     vec_sum_ref[...] = total
+    flat = 128 * lax.broadcasted_iota(jnp.int32, total.shape, 0) + lax.broadcasted_iota(
+        jnp.int32, total.shape, 1
+    )
+    total = jnp.where(flat < 2 * units + total_rows, total, 0.0)
+    stats_ref[1:2, :] = jnp.sum(total * total, axis=0, keepdims=True) * (1.0 / RING)
     for away in range(1, RING):
         vec_copy(away).wait_send()
         for group in range(OUT_GROUPS + 2):
@@ -953,6 +990,8 @@
             move(got_hid.at[way, step], got_hid, step, way, hid_send, hid_recv).wait_send()
             move(got_in.at[way, step], got_in, step, way, in_send, in_recv).wait_send()
             share_move(step, way).wait_send()
+        for place in range(RING):
+            share_across(way, place).wait_send()
 
 
 def reduce_grads(
@@ -975,12 +1014,13 @@
             jax.ShapeDtypeStruct((HID_ROWS, in_wide), F32),
             jax.ShapeDtypeStruct((OUT_GROUPS * OUT_ROWS, 256), F32),
             jax.ShapeDtypeStruct((HID_ROWS, 256), F32),
-            jax.ShapeDtypeStruct((HID_ROWS, in_wide), F32),
+            jax.ShapeDtypeStruct((in_wide, HID_ROWS), F32),
+            jax.ShapeDtypeStruct((in_wide, HID_ROWS), F32),
             jax.ShapeDtypeStruct(vec.shape, F32),
             jax.ShapeDtypeStruct((8, 128), F32),
         ),
         in_specs=[hbm] * 7 + [vmem] + [hbm] * 2 + [vmem] * 3,
-        out_specs=(hbm, hbm) + (vmem,) * 6,
+        out_specs=(hbm, hbm) + (vmem,) * 7,
         scratch_shapes=[
             pltpu.VMEM((BLOCKS[0], wide), F32),
             pltpu.VMEM((BLOCKS[0], 1, wide), F32),
@@ -1004,6 +1044,7 @@
             pltpu.VMEM((2, STEPS, hid_message, 128), I16),
             pltpu.VMEM((2 * RING, in_message, 256), I16),
             pltpu.VMEM((2, STEPS, in_message, 256), I16),
+            pltpu.VMEM((2, RING, 64, 256), F32),
             pltpu.VMEM((2, RING, 64, 256), F32),
             pltpu.VMEM((OUT_GROUPS + 2, RING, 8, 128), F32),
             pltpu.VMEM((OUT_GROUPS + 2, 2, 128, 128), F32),
@@ -1030,6 +1071,8 @@
             sem((STEPS,)),
             sem((OUT_GROUPS + 2, STEPS)),
             sem((OUT_GROUPS + 2, STEPS)),
+            sem((2, RING)),
+            sem((2, RING)),
         ],
         compiler_params=pltpu.CompilerParams(
             collective_id=1, has_side_effects=True, vmem_limit_bytes=63 * 1024 * 1024
@@ -1051,6 +1094,7 @@
     w_out_ref,
     bias_ref,
     bias_out_ref,
+    mom_ref,
     x_out,
     h_one_out,
     h_two_out,
@@ -1058,6 +1102,7 @@
     slope_two_out,
     w_hid_out,
     w_out_out,
+    mom_far_ref,
     dl_ref,
     bias_sum_ref,
     loss_ref,
@@ -1084,6 +1129,7 @@
     sum_send,
     sum_recv,
     out_sems,
+    mom_sems,
 ):
     blk = lax.axis_index("blk")
     col = lax.axis_index("col")
@@ -1268,6 +1314,14 @@
         sums[col, 4 + group : 5 + group, :] = jnp.sum(total, axis=0, keepdims=True)
         sums[col, 8 + group : 9 + group, :] = jnp.sum(picked, axis=0, keepdims=True)
 
+    mom_copy = pltpu.make_async_remote_copy(
+        src_ref=mom_ref,
+        dst_ref=mom_far_ref,
+        send_sem=mom_sems.at[0],
+        recv_sem=mom_sems.at[1],
+        device_id=across,
+        device_id_type=MESH,
+    )
     last_wave = RING_STARTS[-1] + STEPS
     for wave in range(2, last_wave + 1):
         ring_wave(wave)
@@ -1288,6 +1342,7 @@
                     for block in range(4):
                         h_ready(1, block)
                     put(h_two, h_two_out)
+                    mom_copy.start()
                     for copy in tag_copies:
                         copy.wait_recv()
                 rows = pl.ds(group * OUT_ROWS, OUT_ROWS)
@@ -1332,8 +1387,9 @@
             value = curve[pl.ds(row, 16), :] * share - jnp.where(base + row == line, hit_weight, 0.0)
             value = value.astype(BF16)
             dl_ref[pl.ds(row, 16), :] = value
-            bias_col[pl.ds(row, 16), :] = jnp.broadcast_to(
-                jnp.sum(value.astype(F32), axis=1, keepdims=True), (16, 128)
+            value = value.astype(F32)
+            bias_col[pl.ds(row, 16), :] = functools.reduce(
+                jnp.add, [value[:, lane : lane + 128] for lane in range(0, frames, 128)]
             )
             return carry
 
@@ -1341,7 +1397,7 @@
     bias_sum_ref[...] = jnp.zeros_like(bias_sum_ref)
     for number in range(bias_out_ref.shape[0]):
         block = jnp.transpose(bias_col[number * 128 : (number + 1) * 128, :])
-        bias_sum_ref[number : number + 1, :] = block[0:1, :]
+        bias_sum_ref[number : number + 1, :] = jnp.sum(block, axis=0, keepdims=True)
 
     for group in range(len(RING_STARTS)):
         for way in range(2):
@@ -1354,11 +1410,12 @@
             h_move(1, number, block).wait_send()
     for copy in tag_copies + sum_copies:
         copy.wait_send()
+    mom_copy.wait()
     for copy in outs:
         copy.wait()
 
 
-def forward_pass(x, tags, w_in, w_hid, w_out, bias, bias_out, slot_count):
+def forward_pass(x, tags, w_in, w_hid, w_out, bias, bias_out, mom, slot_count):
     own_rows = x.shape[0]
     units = w_hid.shape[1]
     frames = 4 * own_rows
@@ -1381,12 +1438,13 @@
         functools.partial(forward_kernel, slot_count),
         out_shape=tuple(jax.ShapeDtypeStruct(shape, kind) for shape, kind in kept)
         + (
+            jax.ShapeDtypeStruct(mom.shape, F32),
             jax.ShapeDtypeStruct((rows, frames), BF16),
             jax.ShapeDtypeStruct((24, 128), F32),
             jax.ShapeDtypeStruct((8, 128), F32),
         ),
-        in_specs=[vmem] * 7,
-        out_specs=(hbm,) * 7 + (vmem,) * 3,
+        in_specs=[vmem] * 7 + [hbm],
+        out_specs=(hbm,) * 8 + (vmem,) * 3,
         scratch_shapes=[pltpu.VMEM(shape, kind) for shape, kind in kept[:5]]
         + [
             pltpu.VMEM((512, units), BF16),
@@ -1407,11 +1465,12 @@
             sem((3,)),
             sem((3,)),
             sem((16,)),
+            sem((2,)),
         ],
         compiler_params=pltpu.CompilerParams(
             collective_id=2, has_side_effects=True, vmem_limit_bytes=60 * 1024 * 1024
         ),
-    )(x, tags, w_in, w_hid, w_out, bias, bias_out)
+    )(x, tags, w_in, w_hid, w_out, bias, bias_out, mom)
 
 
 DIM_BITS = (2, 4, 8)
@@ -1450,6 +1509,8 @@
     mom_hid_ref,
     red_in_ref,
     mom_in_ref,
+    red_far_ref,
+    mom_far_ref,
     hid_ref,
     inp_ref,
     next_hid_ref,
@@ -1473,6 +1534,10 @@
     back,
     sums,
     sums_got,
+    spread_out,
+    spread_got,
+    spread_size_out,
+    spread_size_got,
     send_sems,
     core_sems,
     recv_sems,
@@ -1498,10 +1563,11 @@
         {"col": (col + 2) % 4},
         {"blk": blk + 2 - 4 * ((blk // 2) % 2)},
     )
-    far = {"blk": (blk + 4) % 8}
     diagonal = {"blk": 4 * (blk // 4) + 3 - blk % 4}
     barrier = pltpu.get_barrier_semaphore()
-    for target in (other_core, dims[1], *({"blk": (blk + away) % 8} for away in range(1, 8))):
+    corner = {"col": (col + 2) % 4 + 1 - 2 * (col % 2)}
+    cols = (other_core, dims[1], corner)
+    for target in (*cols, *({"blk": (blk + away) % 8} for away in range(1, 8))):
         pl.semaphore_signal(barrier, inc=1, device_id=target, device_id_type=MESH)
 
     def fold(values):
@@ -1509,32 +1575,42 @@
         return sum(line[:, lane : lane + 128] for lane in range(0, line.shape[1], 128))
 
     share = 0.125
-    sums[0, 0:1, :] = fold(stats_ref[...])
-    sums[0, 1:2, :] = fold(mom_hid_ref[...] * mom_hid_ref[...])
-    sums[0, 2:3, :] = fold(mom_hid_ref[...] * red_hid_ref[...])
-    sums[0, 3:4, :] = fold(red_hid_ref[...] * red_hid_ref[...])
-    sums[0, 4:5, :] = fold(mom_in_ref[...] * mom_in_ref[...]) * share
-    sums[0, 5:6, :] = fold(mom_in_ref[...] * red_in_ref[...]) * share
-    sums[0, 6:7, :] = fold(red_in_ref[...] * red_in_ref[...]) * share
-    sums[0, 7:8, :] = jnp.zeros((1, 128), F32)
+    sums[blk, 0:1, :] = fold(stats_ref[...])
+    sums[blk, 1:2, :] = fold(mom_hid_ref[...] * mom_hid_ref[...])
+    sums[blk, 2:3, :] = fold(mom_hid_ref[...] * red_hid_ref[...])
+    sums[blk, 3:4, :] = fold(red_hid_ref[...] * red_hid_ref[...])
+    sums[blk, 4:5, :] = fold(mom_in_ref[...] * mom_in_ref[...]) * share
+    sums[blk, 5:6, :] = fold(mom_in_ref[...] * red_in_ref[...]) * share
+    sums[blk, 6:7, :] = fold(red_in_ref[...] * red_in_ref[...]) * share
+    sums[blk, 7:8, :] = jnp.zeros((1, 128), F32)
     eye = lax.broadcasted_iota(jnp.int32, (rows, rows), 0) == lax.broadcasted_iota(
         jnp.int32, (rows, rows), 1
     )
-    pl.semaphore_wait(barrier, 9)
-
-    for number, target in enumerate((other_core, *dims, far)):
-        copy = pltpu.make_async_remote_copy(
-            src_ref=sums.at[number],
-            dst_ref=sums_got.at[number],
-            send_sem=sums_send.at[number],
-            recv_sem=sums_recv.at[number],
-            device_id=target,
-            device_id_type=MESH,
-        )
-        copy.start()
-        copy.wait()
-        sums[number + 1] = sums[number] + sums_got[number]
-    whole = jnp.sum(sums[5], axis=1, keepdims=True)
+    pl.semaphore_wait(barrier, 10)
+
+    def tell(own, targets, first):
+        copies = []
+        for number, target in enumerate(targets, start=first):
+            copies.append(
+                pltpu.make_async_remote_copy(
+                    src_ref=own,
+                    dst_ref=own,
+                    send_sem=sums_send.at[number],
+                    recv_sem=sums_recv.at[number],
+                    device_id=target,
+                    device_id_type=MESH,
+                )
+            )
+            copies[-1].start()
+        for copy in copies:
+            copy.wait_recv()
+        return copies
+
+    told = tell(sums.at[blk], [{"blk": (blk + away) % 8} for away in range(1, 8)], 0)
+    sums_got[col] = functools.reduce(jnp.add, [sums[number] for number in range(8)])
+    told += tell(sums_got.at[col], cols, 7)
+    whole = functools.reduce(jnp.add, [sums_got[number] for number in range(4)])
+    whole = jnp.sum(whole, axis=1, keepdims=True)
     clip = jnp.sqrt(whole[0:1])
     factor = jnp.minimum(1.0, CLIP / clip)
 
@@ -1552,39 +1628,48 @@
     next_in_ref[...] = 0.5 * mom_in_ref[...] + factor * red_in_ref[...]
 
     my_lanes = pl.ds(pl.multiple_of(blk * height, height), height)
+    for number in range(4):
+        there = slice(number * rows, (number + 1) * rows)
+        value = next_hid_ref[there, :]
+        largest = jnp.maximum(jnp.max(jnp.abs(value), axis=1, keepdims=True), 1e-30)
+        spread_out[number] = to_codes(value * (TOP_CODE / largest))
+        line = jnp.sum(jnp.where(eye, largest, 0.0), axis=0, keepdims=True)
+        spread_size_out[number] = jnp.broadcast_to(line * (1.0 / TOP_CODE), (8, rows))
     spread = []
     for away in range(1, 8):
         target = (blk + away) % 8
-        spread.append(
-            pltpu.make_async_remote_copy(
-                src_ref=next_hid_ref.at[
-                    pl.ds(pl.multiple_of(target % 4 * rows, rows), rows), :
-                ],
-                dst_ref=xs.at[:, my_lanes],
-                send_sem=spread_send.at[away - 1],
-                recv_sem=spread_recv.at[away - 1],
-                device_id={"blk": target},
-                device_id_type=MESH,
+        for kind, (src, dst) in enumerate(
+            ((spread_out, spread_got), (spread_size_out, spread_size_got))
+        ):
+            spread.append(
+                pltpu.make_async_remote_copy(
+                    src_ref=src.at[target % 4],
+                    dst_ref=dst.at[blk],
+                    send_sem=spread_send.at[kind, away - 1],
+                    recv_sem=spread_recv.at[kind, away - 1],
+                    device_id={"blk": target},
+                    device_id_type=MESH,
+                )
             )
-        )
-        spread[-1].start()
+            spread[-1].start()
     high = col // 2
     my_half = pl.ds(pl.multiple_of(high * part_wide, part_wide), part_wide)
-    half_copy = pltpu.make_async_remote_copy(
-        src_ref=next_in_ref,
-        dst_ref=xin.at[:, my_half],
-        send_sem=pair_send.at[0],
-        recv_sem=pair_recv.at[0],
-        device_id=dims[1],
-        device_id_type=MESH,
-    )
-    half_copy.start()
-    xs[:, my_lanes] = next_hid_ref[pl.ds(pl.multiple_of(blk % 4 * rows, rows), rows), :]
-    xin[:, my_half] = next_in_ref[...]
+    far_half = pl.ds(pl.multiple_of((1 - high) * part_wide, part_wide), part_wide)
+    in_scale = norm_of(4)
+    xin[:, my_half] = next_in_ref[...] * in_scale
+    xin[:, far_half] = (0.5 * mom_far_ref[...] + factor * red_far_ref[...]) * in_scale
+    spread_got[blk] = spread_out[blk % 4]
+    spread_size_got[blk] = spread_size_out[blk % 4]
     for copy in spread:
         copy.wait_recv()
-    xs[...] = xs[...] * norm_of(1)
-    in_scale = norm_of(4)
+    hid_scale = norm_of(1)
+    for number in range(8):
+        size = jnp.broadcast_to(spread_size_got[number, 0:1, :], (rows, rows))
+        size = jnp.transpose(size) * hid_scale
+        for lane in range(0, height, 128):
+            xs[:, number * height + lane : number * height + lane + 128] = (
+                from_codes(spread_got[number, :, lane : lane + 128]) * size
+            )
 
     numbers = {move: number for number, move in enumerate(MOVES)}
 
@@ -1785,16 +1870,12 @@
                 send_all(turn, THIRD)
                 send_all(turn, THIRD_A)
 
-                @pl.when(number > 0)
-                def _():
-                    by_weight(number, LIGHT_IN, input_gram)
+                by_weight(number, LIGHT_IN, input_gram)
 
                 forward(turn, SECOND, THIRD_B)
                 forward(turn, SECOND_ON, THIRD_C)
 
-                @pl.when(number > 0)
-                def _():
-                    by_weight(number, LIGHT_IN, input_step)
+                by_weight(number, LIGHT_IN, input_step)
 
                 forward(turn, THIRD)
 
@@ -1802,13 +1883,6 @@
             def _():
                 forward(turn, THIRD_A)
                 forward(turn, THIRD_B)
-
-            @pl.when((index == 6) & (number == 0))
-            def _():
-                half_copy.wait()
-                xin[...] = xin[...] * in_scale
-                input_gram(True)
-                input_step(True)
 
             @pl.when(index == 7)
             def _():
@@ -1872,11 +1946,11 @@
     for target in (dims[0], dims[2], diagonal):
         other = target["blk"] % 4
         hid_ref[other] = back[other]
-    for copy in copies + spread:
+    for copy in copies + spread + told:
         copy.wait_send()
 
 
-def muon(stats, red_hid, mom_hid, red_in, mom_in, wide):
+def muon(stats, red_hid, mom_hid, red_in, mom_in, red_far, mom_far, wide):
     rows = red_hid.shape[0] // 4
     height = red_hid.shape[1]
     deep, part_wide = red_in.shape
@@ -1891,7 +1965,7 @@
             jax.ShapeDtypeStruct(red_in.shape, F32),
             jax.ShapeDtypeStruct((8, 128), F32),
         ),
-        in_specs=[vmem] * 5,
+        in_specs=[vmem] * 7,
         out_specs=(vmem,) * 5,
         scratch_shapes=[
             pltpu.VMEM((2, 16, rows, wide), I16),
@@ -1910,17 +1984,21 @@
             pltpu.VMEM((deep, deep), F32),
             pltpu.VMEM((deep, deep), F32),
             pltpu.VMEM((4, rows, height), F32),
-            pltpu.VMEM((6, 8, 128), F32),
-            pltpu.VMEM((5, 8, 128), F32),
+            pltpu.VMEM((8, 8, 128), F32),
+            pltpu.VMEM((4, 8, 128), F32),
+            pltpu.VMEM((4, rows, height), I16),
+            pltpu.VMEM((8, rows, height), I16),
+            pltpu.VMEM((4, 8, rows), F32),
+            pltpu.VMEM((8, 8, rows), F32),
             sem((len(MOVES),)),
             sem((8, 4)),
             sem((2, 16, 3)),
             sem((3,)),
             sem((3,)),
-            sem((5,)),
-            sem((5,)),
-            sem((7,)),
-            sem((7,)),
+            sem((10,)),
+            sem((10,)),
+            sem((2, 7)),
+            sem((2, 7)),
             sem((2,)),
             sem((2,)),
             sem((len(MOVES),)),
@@ -1929,7 +2007,7 @@
         compiler_params=pltpu.CompilerParams(
             collective_id=0, has_side_effects=True, vmem_limit_bytes=60 * 1024 * 1024
         ),
-    )(stats, red_hid, mom_hid, red_in, mom_in)
+    )(stats, red_hid, mom_hid, red_in, mom_in, red_far, mom_far)
 
 
 def plain_body(
@@ -2108,11 +2186,12 @@
     deep = w_input.shape[0]
     padded = 512
     rows_out = OUT_GROUPS * OUT_ROWS
+    mom_in_padded = jnp.pad(mom_input, ((0, padded - deep), (0, 0)))
     own_tags = jnp.where(mask > 0, labels, -1).reshape(1, -1)
     layer_biases = jnp.pad(bias_row[: 2 * hcol].reshape(2, hcol), ((0, 6), (0, 0)))
     blocks = -(-rows_out // 128)
     out_biases = jnp.pad(bias_row[2 * hcol :], (0, blocks * 128 - scol)).reshape(blocks, 128)
-    inputs, h_one, h_two, slope_one, slope_two, low_hidden, low_output, d_logits, bias_sums, losses = (
+    inputs, h_one, h_two, slope_one, slope_two, low_hidden, low_output, mom_far, d_logits, bias_sums, losses = (
         forward_pass(
             frames.reshape(-1, deep),
             jnp.broadcast_to(own_tags, (8, own_tags.shape[1])),
@@ -2121,6 +2200,7 @@
             w_output.T,
             layer_biases,
             out_biases,
+            mom_in_padded,
             slot_count,
         )
     )
@@ -2128,7 +2208,7 @@
     partial = inner_rows(d_logits, low_output)
     vec = jnp.concatenate([jnp.zeros((2 * hcol,), F32), bias_sums.reshape(-1)[:scol], loss_local[None]])
     vec = jnp.pad(vec, (0, 4096 - vec.shape[0])).reshape(32, 128)
-    next_out, next_hid, next_in, red_out, red_hid, red_in, vec_sum, stats = reduce_grads(
+    next_out, next_hid, next_in, red_out, red_hid, red_in, red_far, vec_sum, stats = reduce_grads(
         d_logits,
         h_two,
         h_one,
@@ -2152,13 +2232,14 @@
     vec_sum = vec_sum.reshape(-1)
     red_bias = vec_sum[: bias_row.shape[0]]
     loss_sum = vec_sum[bias_row.shape[0]]
-    stats = stats.at[1, 0].set(jnp.sum(red_bias * red_bias) / nblk)
     done_hidden, done_input, mom_hid_next, mom_in_next, norms = muon(
         stats,
         red_hid,
         mom_hidden.T,
-        red_in.T,
-        jnp.pad(mom_input, ((0, padded - deep), (0, 0))),
+        red_in,
+        mom_in_padded,
+        red_far,
+        mom_far,
         hcol * ncol,
     )
     clip_norm = norms[0, 0]

time: 720 us -> 680 us (0.944)
  Pallas kernels: 637 us -> 602 us
    pallas_call x1, Pallas kernels: 262 us -> 246 us  [muon(): pl.pallas_call(muon_kernel, out_shape=(jax.ShapeDtypeStruct((4, rows, hei...]
    pallas_call x1, Pallas kernels: 160 us -> 149 us  [forward_pass(): pl.pallas_call(functools.partial(forward_kernel, slot_count), out_shape=t...]
    pallas_call x1, Pallas kernels: 215 us -> 208 us  [reduce_grads(): pl.pallas_call(functools.partial(reduce_kernel, deep), out_shape=(jax.Sha...]
    unnamed x43 -> x41, local copies, waits for them, and re-layouts: 28.4 us -> 28.4 us
where the time goes in v7:
time: 680 us; the launch traced here: 675 us
  Pallas kernels  602 us (89%)
  local copies, waits for them, and re-layouts  40.7 us (6%)
  matrix products  17.5 us (3%)
  other arithmetic  13.8 us (2%)
    pallas_call x1, Pallas kernels, muon(): pl.pallas_call(muon_kernel, out_shape=(jax.ShapeDtypeStruct((4, rows, hei...  246 us
    pallas_call x1, Pallas kernels, reduce_grads(): pl.pallas_call(functools.partial(reduce_kernel, deep), out_shape=(jax.Sha...  208 us
    pallas_call x1, Pallas kernels, forward_pass(): pl.pallas_call(functools.partial(forward_kernel, slot_count), out_shape=t...  149 us
    unnamed x41, local copies, waits for them, and re-layouts  28.4 us
    dot_general x1, matrix products, inner_rows(): lax.dot_general(left_side, right_side, (((0,), (0,)), ((), ())), preferre...  17.5 us

profile of v7, /device:TPU:0, one launch (start us, length us, event | category | flops | bytes accessed | tf_op | source)
XLA Modules:
  0.0 675.1 jit_solution(2530401246415372565)
XLA Ops:
  0.6 2.3 pad.26.mom_ref.mom_in_ref
  2.9 0.7 slice_reduce_fusion.1
  4.2 0.7 slice_reduce_fusion
  5.6 0.7 compare_select_fusion
  7.0 148.8 %shard_map.271 = (bf16[1024,512]{1,0:T(8,128)(2,1)}, bf16[1024,2048]{1,0:T(8,128)(2,1)}, bf16[1024,2048]{1,0:T(8,128)(2,1)}, f32[1024,512]{1,0:T(8,128)}, f32[10...) custom-call(bf16[256,440]{1,0:T(8,128)(2,1)} %bitcast.58, ...), custom_call_target="tpu_custom_call" | custom-call | tf_op jit(solution)/shard_map/pallas_call | solution.py:1437
  155.8 17.5 %fusion.3.part_ref = f32[1024,2048]{1,0:T(8,128)} fusion(bf16[2368,1024]{1,0:T(8,128)(2,1)} %get-tuple-element.40.dl_ref, bf16[2368,2048]{1,0:T(8,128)(2,1)} %get-tuple-element.44), kind=kOutput, calls=%fused_computation.25 | convolution fusion | flops 9932111872 | bytes 22937600 | tf_op jit(solution)/shard_map/dot_general | solution.py:38
  174.0 0.7 concatenate.3
  175.3 2.4 copy.31
  177.9 0.8 pad_bitcast_fusion.res_in_ref
  178.7 0.8 slice_bitcast_fusion.1
  180.1 207.6 %shard_map.272 = (f32[2326,1,2048]{2,1,0:T(1,128)}, f32[512,2048]{1,0:T(8,128)}, f32[512,512]{1,0:T(8,128)}, f32[2368,256]{1,0:T(8,128)}, f32[512,256]{1,0:T(8,1...) custom-call(bf16[2368,1024]{1,0:T(8,128)(2,1)} %get-tuple-element.40.dl_ref, ...), custom_call_target="tpu_custom_call" | custom-call | tf_op jit(solution)/shard_map/pallas_call | solution.py:1009
  387.8 1.0 copy.33
  388.8 245.6 %shard_map.273 = (f32[4,128,256]{2,1,0:T(8,128)}, f32[512,512]{1,0:T(8,128)}, f32[512,256]{1,0:T(8,128)}, f32[512,512]{1,0:T(8,128)}, f32[8,128]{1,0:T(8,128)}) custom-call(f32[8,128]{1,0:T(8,128)} %get-tuple-element.51.stats_ref, f32[512,256]{1,0:T(8,128)} %get-tuple-element.52.red_hid_ref, f32[512,256]{1,0:T(8,128)} %bitcast.54, ...), custom_call_target="tpu_custom_call" | custom-call | tf_op jit(solution)/shard_map/pallas_call | solution.py:1959
  634.4 1.3 fusion.2
  636.4 0.7 multiply_subtract_fusion.2
  637.1 9.1 %multiply_subtract_fusion = (f32[256,2326]{0,1:T(8,128)}, f32[256,2326]{0,1:T(8,128)}, f32[256,2326]{0,1:T(8,128)}) fusion(f32[256,2326]{0,1:T(8,128)S(1)} %copy-done, f32[256,2326]{0,1:T(8,128)} %param.25, f32[2368,256]{1,0:T(8,128)} %get-tuple-element.59, f32[]{:T(128)} %bitcast.20, f32[256,2326]{0,1:T(8,128)} %param.26), kind=kLoop, calls=%fused_computation.3 | loop fusion | flops 8931840 | bytes 16672772 | tf_op jit(solution)/shard_map/sub | solution.py:78
  646.4 0.8 copy-done.2
  647.2 0.9 bitcast_subtract_fusion
  648.1 1.1 multiply_subtract_fusion.1
  649.2 1.0 slice.51
  650.2 1.0 copy.35
  651.2 5.4 copy.37
  656.7 1.2 copy.36
  658.5 16.3 %copy.39 = f32[1,2048,2326]{1,0,2:T(1,128)} copy(f32[1,2048,2326]{1,0,2:T(1,128)} %bitcast.49) | data formatting | bytes 38109184
  (48 shorter events, 5.6 us)
Async XLA Ops:
  155.8 17.6 %copy-start.16 = (f32[8,128]{1,0:T(8,128)S(1)}, f32[8,128]{1,0:T(8,128)}, u32[]{:S(2)}) copy-start(f32[8,128]{1,0:T(8,128)} %get-tuple-element.49) | copy-start | bytes 12292
  155.8 18.2 %copy-start.15 = (f32[24,128]{1,0:T(8,128)S(1)}, f32[24,128]{1,0:T(8,128)}, u32[]{:S(2)}) copy-start(f32[24,128]{1,0:T(8,128)} %get-tuple-element.48) | copy-start | bytes 36868
  155.8 19.5 %copy-start.3 = (bf16[1,2048,512]{2,1,0:T(8,128)(2,1)S(1)}, bf16[1,2048,512]{2,1,0:T(8,128)(2,1)}, u32[]{:S(2)}) copy-start(bf16[1,2048,512]{2,1,0:T(8,128)(2,1)} %param.30) | copy-start | bytes 6291460
  173.4 4.3 copy-start.10
  180.1 207.6 %copy-start.7 = (f32[256,512]{1,0:T(8,128)S(1)}, f32[256,512]{1,0:T(8,128)}, u32[]{:S(2)}) copy-start(f32[256,512]{1,0:T(8,128)} %param.24) | copy-start | bytes 1572868
  388.8 246.9 %copy-start.12 = (f32[32,128]{1,0:T(8,128)S(1)}, f32[32,128]{1,0:T(8,128)}, u32[]{:S(2)}) copy-start(f32[32,128]{1,0:T(8,128)} %get-tuple-element.50) | copy-start | bytes 49156
  388.8 247.6 %copy-start.11 = (f32[1,3350]{1,0:T(1,128)S(1)}, f32[1,3350]{1,0:T(1,128)}, u32[]{:S(2)}) copy-start(f32[1,3350]{1,0:T(1,128)} %param.22) | copy-start | bytes 40204
  388.8 247.6 %copy-start.13 = (f32[1,3350]{1,0:T(1,128)S(1)}, f32[1,3350]{1,0:T(1,128)}, u32[]{:S(2)}) copy-start(f32[1,3350]{1,0:T(1,128)} %param.27) | copy-start | bytes 40204
  388.8 247.6 %copy-start.14 = (f32[1,3350]{1,0:T(1,128)S(1)}, f32[1,3350]{1,0:T(1,128)}, u32[]{:S(2)}) copy-start(f32[1,3350]{1,0:T(1,128)} %param.28) | copy-start | bytes 40204
  388.8 248.3 %copy-start = (f32[256,2326]{0,1:T(8,128)S(1)}, f32[256,2326]{0,1:T(8,128)}, u32[]{:S(2)}) copy-start(f32[256,2326]{0,1:T(8,128)} %param.21) | copy-start | bytes 7145476
  637.1 9.1 %copy-start.9 = (f32[4,128,256]{2,1,0:T(8,128)S(1)}, f32[4,128,256]{2,1,0:T(8,128)}, u32[]{:S(2)}) copy-start(f32[4,128,256]{2,1,0:T(8,128)} %get-tuple-element.58) | copy-start | bytes 1572868
  646.1 1.0 copy-start.2
  646.2 1.9 copy-start.1
  646.2 1.9 copy-start.6
  647.2 2.0 copy-start.5
  648.1 2.1 copy-start.8
  651.2 5.4 copy-start.4

commit v8 on v7

--- a/solution.py
+++ b/solution.py
@@ -99,12 +99,15 @@
 STEPS = RING - 1
 OUT_ROWS = 592
 OUT_GROUPS = 4
-BLOCKS = (304, 288)
 HID_ROWS = 512
 HID_GROUP = 4
 IN_GROUP = 5
-HID_WAVE = 6
-IN_WAVE = 6
+TURN_AT = 5
+CROSS_AT = 6
+HID_AT = 13
+FINISH_AT = 14
+IN_AT = 20
+HID_HOP = 3
 
 
 def ring_place(blk):
@@ -133,22 +136,97 @@
     return codes.astype(jnp.int32).astype(F32)
 
 
+def chunk_of(lane):
+    number = lane // 256
+    return number // 2 if number % 2 == 0 else 7 - number // 2
+
+
+def squash_kernel(senones, dl_ref, h_ref, res_ref, next_ref, codes_ref, size_ref, grad, cols, marks):
+    group = pl.program_id(0)
+    rows, wide = grad.shape
+    valid = senones - group * rows
+    for first, count in ((0, rows // 32 * 16), (rows // 32 * 16, rows - rows // 32 * 16)):
+        there = slice(first, first + count)
+        total = jnp.zeros((count, 128), F32)
+        for lane in range(0, wide, 512):
+            value = dot_nn(dl_ref[there, :], h_ref[:, lane : lane + 512])
+            value = value + res_ref[there, lane : lane + 512].astype(F32)
+            row = first + lax.broadcasted_iota(jnp.int32, value.shape, 0)
+            value = jnp.where(row < valid, value, 0.0)
+            grad[there, lane : lane + 512] = value
+            value = jnp.abs(value)
+            for part in range(0, 512, 128):
+                total = total + value[:, part : part + 128]
+        size = jnp.sum(total, axis=1, keepdims=True) * (1.0 / wide) + 1e-12
+        size = jnp.broadcast_to(size, (count, 128))
+        marks[there, :] = size
+        cols[0, there, :] = size
+        cols[1, there, :] = 2.0 / size
+
+    def some(number, carry):
+        row = pl.multiple_of(number * 16, 16)
+        size = cols[0, pl.ds(row, 16), :]
+        steep = cols[1, pl.ds(row, 16), :]
+        for lane in range(0, wide, 128):
+            piece = grad[pl.ds(row, 16), lane : lane + 128]
+            curve = jnp.tanh(piece * steep)
+            codes_ref[0, 2 * chunk_of(lane) + lane // 128 % 2, pl.ds(row, 16), :] = to_codes(
+                curve * TOP_CODE
+            )
+            next_ref[pl.ds(row, 16), 0, lane : lane + 128] = piece - size * curve
+        return carry
+
+    lax.fori_loop(0, rows // 16, some, 0)
+    marks[rows:, :] = jnp.zeros((marks.shape[0] - rows, 128), F32)
+    lines = [jnp.transpose(marks[first : first + 128, :])[0:1, :] for first in range(0, rows, 128)]
+    lines.append(jnp.zeros((8 - len(lines), 128), F32))
+    size_ref[0] = jnp.concatenate(lines, axis=0)
+
+
+def squash_out(dl, h_two, res_out):
+    senones, wide = res_out.shape
+    frames = dl.shape[1]
+    return pl.pallas_call(
+        functools.partial(squash_kernel, senones),
+        grid=(OUT_GROUPS,),
+        out_shape=(
+            jax.ShapeDtypeStruct((senones, 1, wide), F32),
+            jax.ShapeDtypeStruct((OUT_GROUPS, 2 * RING, OUT_ROWS, 128), I16),
+            jax.ShapeDtypeStruct((OUT_GROUPS, 8, 128), F32),
+        ),
+        in_specs=[
+            pl.BlockSpec((OUT_ROWS, frames), lambda group: (group, 0)),
+            pl.BlockSpec((frames, wide), lambda group: (0, 0)),
+            pl.BlockSpec((OUT_ROWS, wide), lambda group: (group, 0)),
+        ],
+        out_specs=(
+            pl.BlockSpec((OUT_ROWS, 1, wide), lambda group: (group, 0, 0)),
+            pl.BlockSpec((1, 2 * RING, OUT_ROWS, 128), lambda group: (group, 0, 0, 0)),
+            pl.BlockSpec((1, 8, 128), lambda group: (group, 0, 0)),
+        ),
+        scratch_shapes=[
+            pltpu.VMEM((OUT_ROWS, wide), F32),
+            pltpu.VMEM((2, OUT_ROWS, 128), F32),
+            pltpu.VMEM((640, 128), F32),
+        ],
+        compiler_params=pltpu.CompilerParams(vmem_limit_bytes=60 * 1024 * 1024),
+    )(dl, h_two, res_out)
+
+
 def reduce_kernel(
     deep,
-    dl_ref,
-    h_two_ref,
+    senones,
+    codes_ref,
+    sizes_ref,
     h_one_ref,
     x_ref,
     part_ref,
     slope_two_ref,
     slope_one_ref,
     w_hid_ref,
-    res_out_ref,
     res_hid_ref,
     res_in_ref,
-    res_tail_ref,
     vec_ref,
-    next_out_ref,
     next_hid_ref,
     next_in_ref,
     red_out_ref,
@@ -158,9 +236,7 @@
     vec_sum_ref,
     stats_ref,
     grad,
-    stage,
     res_buf,
-    dl_buf,
     h_buf,
     slope_buf,
     marks,
@@ -186,9 +262,8 @@
     vec,
     vecs,
     res_sems,
-    dl_sems,
     load_sems,
-    stage_sems,
+    code_sems,
     slope_sems,
     core_send,
     core_recv,
@@ -212,7 +287,6 @@
     blk = lax.axis_index("blk")
     col = lax.axis_index("col")
     here = ring_place(blk)
-    total_rows = next_out_ref.shape[0]
     core, high = col % 2, col // 2
     cores = {"col": col + 1 - 2 * core}
     across = {"col": (col + 2) % 4}
@@ -220,23 +294,8 @@
     for target in (cores, across, *({"blk": (blk + away) % RING} for away in range(1, RING))):
         pl.semaphore_signal(barrier, inc=1, device_id=target, device_id_type=MESH)
 
-    starts = [sum(BLOCKS[:part]) for part in range(len(BLOCKS))]
-
-    def res_copy(group, part, rows=None):
-        rows = rows or BLOCKS[part]
-        return pltpu.make_async_copy(
-            res_out_ref.at[pl.ds(group * OUT_ROWS + starts[part], rows), :],
-            res_buf.at[part, pl.ds(0, rows), :],
-            res_sems.at[part],
-        )
-
-    def dl_copy(group, part):
-        rows = BLOCKS[part]
-        return pltpu.make_async_copy(
-            dl_ref.at[pl.ds(group * OUT_ROWS + starts[part], rows), :],
-            dl_buf.at[part, pl.ds(0, rows), :],
-            dl_sems.at[part],
-        )
+    def code_copy(group):
+        return pltpu.make_async_copy(codes_ref.at[group], own_out.at[group], code_sems.at[group])
 
     def hid_res_copy(part):
         return pltpu.make_async_copy(
@@ -253,33 +312,11 @@
     def load(src, dst):
         return pltpu.make_async_copy(src, dst, load_sems.at[0])
 
-    def stage_copy(group, part, rows):
-        return pltpu.make_async_copy(
-            stage.at[pl.ds(0, rows)],
-            next_out_ref.at[pl.ds(group * OUT_ROWS + starts[part], rows)],
-            stage_sems.at[0],
-        )
-
-    last_rows = total_rows - (OUT_GROUPS - 1) * OUT_ROWS - starts[-1]
-    whole_rows = last_rows // 16 * 16
-
-    def stage_start(group, part):
-        if part < len(BLOCKS) - 1:
-            stage_copy(group, part, BLOCKS[part]).start()
-        else:
-
-            @pl.when(group < OUT_GROUPS - 1)
-            def _():
-                stage_copy(group, part, BLOCKS[part]).start()
-
-            @pl.when(group == OUT_GROUPS - 1)
-            def _():
-                stage_copy(group, part, last_rows).start()
-
+    for group in range(OUT_GROUPS):
+        code_copy(group).start()
     for part in range(2):
-        res_copy(0, part).start()
-        dl_copy(0, part).start()
-    load(h_two_ref, h_buf).start()
+        hid_res_copy(part).start()
+    load(h_one_ref, h_buf).start()
     marks[...] = jnp.zeros_like(marks)
     stats_ref[...] = jnp.zeros_like(stats_ref)
     vec[...] = vec_ref[...]
@@ -546,139 +583,40 @@
             tiles.append(jnp.zeros((16, 128), F32))
             shares[group, way] = jnp.transpose(jnp.concatenate(tiles, axis=0))
 
-    def squash_rows(count, own, first_own, read_res, write_next):
-        wide = grad.shape[1]
-
-        def add(number, carry):
-            row = pl.multiple_of(number * 16, 16)
-            value = grad[pl.ds(row, 16), :] + read_res(row)
-            grad[pl.ds(row, 16), :] = value
-            value = jnp.abs(value)
-            cols[0, pl.ds(row, 16), :] = functools.reduce(
-                jnp.add, [value[:, lane : lane + 128] for lane in range(0, wide, 128)]
-            )
-            return carry
-
-        lax.fori_loop(0, count // 16, add, 0)
-        set_rows(
-            count,
-            first_own,
-            jnp.sum(cols[0, 0:count, :], axis=1, keepdims=True) * (1.0 / wide) + 1e-12,
-        )
-
-        def some(number, carry):
-            row = pl.multiple_of(number * 16, 16)
-            size = cols[0, pl.ds(row, 16), :]
-            steep = cols[1, pl.ds(row, 16), :]
-            for lane in range(0, wide, 128):
-                piece = grad[pl.ds(row, 16), lane : lane + 128]
-                curve = jnp.tanh(piece * steep)
-                number_of = lane // 256
-                chunk = number_of // 2 if number_of % 2 == 0 else 7 - number_of // 2
-                own[2 * chunk + lane // 128 % 2, pl.ds(first_own + row, 16), :] = to_codes(
-                    curve * TOP_CODE
-                )
-                write_next(row, lane, piece - size * curve)
-            return carry
-
-        lax.fori_loop(0, count // 16, some, 0)
-
-    def out_group(group):
-        for part, rows in enumerate(BLOCKS):
-            dl_copy(group, part).wait()
-            if part == 0:
-
-                @pl.when(group == 0)
-                def _():
-                    load(h_two_ref, h_buf).wait()
-
-            for lane in range(0, grad.shape[1], 512):
-                grad[0:rows, lane : lane + 512] = dot_nn(
-                    dl_buf[part, 0:rows, :], h_buf[:, lane : lane + 512]
-                )
-            if part == 0:
-                res_copy(group, part).wait()
-            else:
-
-                @pl.when(group < OUT_GROUPS - 1)
-                def _():
-                    res_copy(group, 1).wait()
-
-                @pl.when(group == OUT_GROUPS - 1)
-                def _():
-                    res_copy(group, 1, whole_rows).wait()
-                    res_buf[1, whole_rows : whole_rows + 16, :] = res_tail_ref[...]
-                    res_buf[1, whole_rows + 16 : BLOCKS[1], :] = jnp.zeros(
-                        (BLOCKS[1] - whole_rows - 16, res_buf.shape[2]), BF16
-                    )
-
-            if part == 0:
-
-                @pl.when(group > 0)
-                def _():
-                    stage_copy(group - 1, len(BLOCKS) - 1, BLOCKS[-1]).wait()
-
-            else:
-                stage_copy(group, part - 1, BLOCKS[part - 1]).wait()
-
-            def write_next(row, lane, values):
-                stage[pl.ds(row, 16), 0, lane : lane + 128] = values
-
-            squash_rows(
-                rows,
-                own_out.at[group],
-                starts[part],
-                lambda row, part=part: res_buf[part, pl.ds(row, 16), :].astype(F32),
-                write_next,
-            )
-            stage_start(group, part)
-
-            @pl.when(group < OUT_GROUPS - 1)
-            def _(part=part):
-                if part == 0:
-                    res_copy(group + 1, 0).start()
-                else:
-
-                    @pl.when(group < OUT_GROUPS - 2)
-                    def _():
-                        res_copy(group + 1, 1).start()
-
-                    @pl.when(group == OUT_GROUPS - 2)
-                    def _():
-                        res_copy(group + 1, 1, whole_rows).start()
-
-                dl_copy(group + 1, part).start()
-
-            @pl.when(group == OUT_GROUPS - 1)
-            def _(part=part):
-                hid_res_copy(part).start()
-                if part == len(BLOCKS) - 1:
-                    load(h_one_ref, h_buf).start()
-
-        set_sizes(OUT_ROWS, group)
-
     def hid_group():
         load(h_one_ref, h_buf).wait()
+        wide = grad.shape[1]
         for part in range(2):
             first = part * 256
+            hid_res_copy(part).wait()
             if part:
                 hid_next_copy(part - 1).wait()
-            for lane in range(0, grad.shape[1], 512):
-                grad[0:256, lane : lane + 512] = dot_nn(
-                    dz_two[first : first + 256, :], h_buf[:, lane : lane + 512]
-                )
-            hid_res_copy(part).wait()
-
-            def write_next(row, lane, values):
-                grad[pl.ds(row, 16), lane : lane + 128] = values
-
-            squash_rows(
-                256,
-                own_hid,
-                first,
-                lambda row, part=part: res_buf[part, pl.ds(row, 16), :].astype(F32),
-                write_next,
+            total = jnp.zeros((256, 128), F32)
+            for lane in range(0, wide, 512):
+                value = dot_nn(dz_two[first : first + 256, :], h_buf[:, lane : lane + 512])
+                value = value + res_buf[part, :, lane : lane + 512].astype(F32)
+                grad[:, lane : lane + 512] = value
+                value = jnp.abs(value)
+                for more in range(0, 512, 128):
+                    total = total + value[:, more : more + 128]
+            set_rows(
+                256, first, jnp.sum(total, axis=1, keepdims=True) * (1.0 / wide) + 1e-12
             )
+
+            def some(number, carry, first=first):
+                row = pl.multiple_of(number * 16, 16)
+                size = cols[0, pl.ds(row, 16), :]
+                steep = cols[1, pl.ds(row, 16), :]
+                for lane in range(0, wide, 128):
+                    piece = grad[pl.ds(row, 16), lane : lane + 128]
+                    curve = jnp.tanh(piece * steep)
+                    own_hid[2 * chunk_of(lane) + lane // 128 % 2, pl.ds(first + row, 16), :] = (
+                        to_codes(curve * TOP_CODE)
+                    )
+                    grad[pl.ds(row, 16), lane : lane + 128] = piece - size * curve
+                return carry
+
+            lax.fori_loop(0, 16, some, 0)
             hid_next_copy(part).start()
         load(x_ref, h_buf.at[:, pl.ds(0, x_ref.shape[1])]).start()
         set_sizes(HID_ROWS, HID_GROUP)
@@ -869,76 +807,62 @@
         line = sizes[IN_GROUP, place, pl.ds(chunk, 1), :]
         return jnp.broadcast_to(line, (8, 128))
 
-    def wave(number, carry):
+    for group in range(OUT_GROUPS):
+        sizes[group, here] = sizes_ref[group]
+        tell_sizes(group)
+        code_copy(group).wait()
+        first_moves(own_out.at[group], got_out.at[group], out_send.at[group], out_recv.at[group])
+    blocks(0, 4, start_block)
+
+    def each(number, first, spacing, count, work):
+        after = number - first
+
+        @pl.when((after >= 0) & (after < spacing * count) & (after % spacing == 0))
+        def _():
+            work(after // spacing)
+
+    def turn(number, carry):
         @pl.when(number < OUT_GROUPS)
         def _():
-            out_group(number)
-            first_moves(own_out.at[number], got_out.at[number], out_send.at[number], out_recv.at[number])
-
-        @pl.when(number == HID_WAVE)
+            make_shares(number, lambda place, step, way: sizes[number, place])
+
+        @pl.when(number < OUT_GROUPS * STEPS)
+        def _():
+            out_hop(number % OUT_GROUPS, number // OUT_GROUPS)
+
+        @pl.when(number == HID_AT + HID_HOP)
+        def _():
+            make_shares(HID_GROUP, lambda place, step, way: sizes[HID_GROUP, place])
+
+        each(number, HID_AT + HID_HOP, HID_HOP, STEPS, hid_hop)
+
+        @pl.when(number == IN_AT + 1)
+        def _():
+            make_shares(IN_GROUP, chunk_row)
+
+        in_step(number - IN_AT - 1)
+        each(number, 0, 1, 4, lambda block: cross(0, block))
+        each(number, TURN_AT, 2, 4, turn_block)
+        each(number, CROSS_AT, 2, 4, lambda block: cross(1, block))
+
+        @pl.when(number == HID_AT)
         def _():
             hid_group()
             first_moves(own_hid, got_hid, hid_send, hid_recv)
 
-        @pl.when((number >= 1) & (number <= OUT_GROUPS))
+        each(number, FINISH_AT, 2, 4, lambda block: finish(1, block))
+
+        @pl.when(number == IN_AT)
         def _():
-            group = number - 1
-            make_shares(group, lambda place, step, way: sizes[group, place])
-
-        @pl.when(number == HID_WAVE + 1)
-        def _():
-            make_shares(HID_GROUP, lambda place, step, way: sizes[HID_GROUP, place])
-
-        @pl.when(number == IN_WAVE + 1)
-        def _():
-            make_shares(IN_GROUP, chunk_row)
-
-        index = 2 * (number - IN_WAVE - 1)
-        in_step(index)
-
-        @pl.when((number > HID_WAVE) & (number <= HID_WAVE + STEPS))
-        def _():
-            hid_hop(number - HID_WAVE - 1)
-
-        def outs(group, carry):
-            step = number - 1 - group
-
-            @pl.when((step >= 0) & (step < STEPS))
-            def _():
-                out_hop(group, step)
-
-            return carry
-
-        lax.fori_loop(0, OUT_GROUPS, outs, 0)
-
-        @pl.when(number == 1)
-        def _():
-            blocks(0, 4, start_block)
-
-        @pl.when(number == 2)
-        def _():
-            blocks(0, 4, lambda block: cross(0, block))
-
-        @pl.when((number == 3) | (number == 4))
-        def _():
-            blocks(2 * number - 6, 2 * number - 4, turn_block)
-
-        @pl.when(number == 4)
-        def _():
-            blocks(0, 4, lambda block: cross(1, block))
-
-        @pl.when(number == IN_WAVE)
-        def _():
-            blocks(0, 4, lambda block: finish(1, block))
             in_group()
             first_moves(own_in, got_in, in_send, in_recv)
             for away in range(1, RING):
                 vec_copy(away).start()
 
-        in_step(index + 1)
         return carry
 
-    lax.fori_loop(0, IN_WAVE + 1 + STEPS, wave, 0)
+    turns = max(IN_AT + 1 + 2 * STEPS, HID_AT + HID_HOP * STEPS + 1, OUT_GROUPS * STEPS)
+    lax.fori_loop(0, turns, turn, 0)
 
     def unfold(shares_of, out):
         for place in range(0, RING, 2):
@@ -966,7 +890,7 @@
     flat = 128 * lax.broadcasted_iota(jnp.int32, total.shape, 0) + lax.broadcasted_iota(
         jnp.int32, total.shape, 1
     )
-    total = jnp.where(flat < 2 * units + total_rows, total, 0.0)
+    total = jnp.where(flat < 2 * units + senones, total, 0.0)
     stats_ref[1:2, :] = jnp.sum(total * total, axis=0, keepdims=True) * (1.0 / RING)
     for away in range(1, RING):
         vec_copy(away).wait_send()
@@ -975,7 +899,6 @@
     for slot in range(2):
         core_move(1, 2 + slot).wait_send()
         far_move(1, 2 + slot).wait_send()
-    stage_copy(OUT_GROUPS - 1, len(BLOCKS) - 1, last_rows).wait()
     for way in range(2):
         for step in range(STEPS):
             for group in range(OUT_GROUPS):
@@ -995,9 +918,9 @@
 
 
 def reduce_grads(
-    dl, h_two, h_one, x, part, slope_two, slope_one, w_hid, res_out, res_hid, res_in, res_tail, vec, senones, deep
+    codes, sizes, h_one, x, part, slope_two, slope_one, w_hid, res_hid, res_in, vec, senones, deep
 ):
-    frames, wide = h_two.shape
+    frames, wide = h_one.shape
     in_wide = x.shape[1]
     units = w_hid.shape[1]
     vmem = pl.BlockSpec(memory_space=pltpu.VMEM)
@@ -1007,9 +930,8 @@
     in_message = 64
     sem = pltpu.SemaphoreType.DMA
     return pl.pallas_call(
-        functools.partial(reduce_kernel, deep),
+        functools.partial(reduce_kernel, deep, senones),
         out_shape=(
-            jax.ShapeDtypeStruct((senones, 1, wide), F32),
             jax.ShapeDtypeStruct((HID_ROWS, wide), F32),
             jax.ShapeDtypeStruct((HID_ROWS, in_wide), F32),
             jax.ShapeDtypeStruct((OUT_GROUPS * OUT_ROWS, 256), F32),
@@ -1019,17 +941,15 @@
             jax.ShapeDtypeStruct(vec.shape, F32),
             jax.ShapeDtypeStruct((8, 128), F32),
         ),
-        in_specs=[hbm] * 7 + [vmem] + [hbm] * 2 + [vmem] * 3,
-        out_specs=(hbm, hbm) + (vmem,) * 7,
+        in_specs=[hbm, vmem] + [hbm] * 5 + [vmem, hbm, vmem, vmem],
+        out_specs=(hbm,) + (vmem,) * 7,
         scratch_shapes=[
-            pltpu.VMEM((BLOCKS[0], wide), F32),
-            pltpu.VMEM((BLOCKS[0], 1, wide), F32),
-            pltpu.VMEM((2, BLOCKS[0], wide), BF16),
-            pltpu.VMEM((2, BLOCKS[0], frames), BF16),
+            pltpu.VMEM((256, wide), F32),
+            pltpu.VMEM((2, 256, wide), BF16),
             pltpu.VMEM((frames, wide), BF16),
             pltpu.VMEM((2, 256, units), F32),
             pltpu.VMEM((640, 128), F32),
-            pltpu.VMEM((2, BLOCKS[0], 128), F32),
+            pltpu.VMEM((2, 256, 128), F32),
             pltpu.VMEM((4, 256, 2 * units), F32),
             pltpu.VMEM((256, units), BF16),
             pltpu.VMEM((units, frames), BF16),
@@ -1052,8 +972,7 @@
             pltpu.VMEM((RING,) + vec.shape, F32),
             sem((2,)),
             sem((2,)),
-            sem((2,)),
-            sem((1,)),
+            sem((OUT_GROUPS,)),
             sem((2,)),
             sem((2,)),
             sem((2, 4)),
@@ -1077,7 +996,7 @@
         compiler_params=pltpu.CompilerParams(
             collective_id=1, has_side_effects=True, vmem_limit_bytes=63 * 1024 * 1024
         ),
-    )(dl, h_two, h_one, x, part, slope_two, slope_one, w_hid, res_out, res_hid, res_in, res_tail, vec)
+    )(codes, sizes, h_one, x, part, slope_two, slope_one, w_hid, res_hid, res_in, vec)
 
 
 RING_STARTS = (0, 2, 5, 7, 9)
@@ -2208,19 +2127,18 @@
     partial = inner_rows(d_logits, low_output)
     vec = jnp.concatenate([jnp.zeros((2 * hcol,), F32), bias_sums.reshape(-1)[:scol], loss_local[None]])
     vec = jnp.pad(vec, (0, 4096 - vec.shape[0])).reshape(32, 128)
-    next_out, next_hid, next_in, red_out, red_hid, red_in, red_far, vec_sum, stats = reduce_grads(
-        d_logits,
-        h_two,
+    next_out, codes, sizes = squash_out(d_logits, h_two, res_output[0].T)
+    next_hid, next_in, red_out, red_hid, red_in, red_far, vec_sum, stats = reduce_grads(
+        codes,
+        sizes,
         h_one,
         inputs,
         partial,
         slope_two,
         slope_one,
         low_hidden,
-        res_output[0].T,
         res_hidden[0].T,
         jnp.pad(res_input[0], ((0, padded - deep), (0, 0))).T,
-        jnp.pad(res_output[0, :, scol // 16 * 16 :], ((0, 0), (0, 16 - scol % 16))).T,
         vec,
         scol,
         deep,

time: 680 us -> 663 us (0.975)
  local copies, waits for them, and re-layouts: 40.7 us -> 24.7 us
  Pallas kernels: 602 us -> 594 us
    unnamed x41 -> x30, local copies, waits for them, and re-layouts: 28.4 us -> 13.5 us
    pallas_call x1 -> x2, Pallas kernels: 208 us -> 199 us  [the longest x1 165 us: reduce_grads(): pl.pallas_call(functools.partial(reduce_kernel, deep, senones), out_shape...]
where the time goes in v8:
time: 663 us; the launch traced here: 654 us
  Pallas kernels  594 us (90%)
  local copies, waits for them, and re-layouts  24.7 us (4%)
  matrix products  17.2 us (3%)
  other arithmetic  17 us (3%)
    pallas_call x1, Pallas kernels, muon(): pl.pallas_call(muon_kernel, out_shape=(jax.ShapeDtypeStruct((4, rows, hei...  246 us
    pallas_call x1, Pallas kernels, reduce_grads(): pl.pallas_call(functools.partial(reduce_kernel, deep, senones), out_shape...  165 us
    pallas_call x1, Pallas kernels, forward_pass(): pl.pallas_call(functools.partial(forward_kernel, slot_count), out_shape=t...  149 us
    pallas_call x1, Pallas kernels, squash_out(): pl.pallas_call(functools.partial(squash_kernel, senones), grid=(OUT_GROUP...  34.2 us
    dot_general x1, matrix products, inner_rows(): lax.dot_general(left_side, right_side, (((0,), (0,)), ((), ())), preferre...  17.2 us
    unnamed x30, local copies, waits for them, and re-layouts  13.5 us

profile of v8, /device:TPU:0, one launch (start us, length us, event | category | flops | bytes accessed | tf_op | source)
XLA Modules:
  0.0 654.2 jit_solution(17685974823200619872)
XLA Ops:
  0.7 0.8 compare_select_fusion
  3.4 0.7 slice_reduce_fusion
  4.8 2.2 copy.33
  7.0 1.2 copy.32
  8.2 0.8 pad_bitcast_fusion.res_in_ref
  9.0 1.1 pad.22.mom_ref.mom_in_ref
  10.1 2.4 copy.31
  12.5 149.1 %shard_map.271 = (bf16[1024,512]{1,0:T(8,128)(2,1)}, bf16[1024,2048]{1,0:T(8,128)(2,1)}, bf16[1024,2048]{1,0:T(8,128)(2,1)}, f32[1024,512]{1,0:T(8,128)}, f32[10...) custom-call(bf16[256,440]{1,0:T(8,128)(2,1)} %bitcast.53, ...), custom_call_target="tpu_custom_call" | custom-call | tf_op jit(solution)/shard_map/pallas_call | solution.py:1356
  161.6 1.3 reduce_sum.9
  162.9 1.4 concatenate.3
  164.9 17.2 %fusion.3.part_ref = f32[1024,2048]{1,0:T(8,128)} fusion(bf16[2368,1024]{1,0:T(8,128)(2,1)} %get-tuple-element.42.dl_ref, bf16[2368,2048]{1,0:T(8,128)(2,1)} %get-tuple-element.48), kind=kOutput, calls=%fused_computation.23 | convolution fusion | flops 9932111872 | bytes 22937600 | tf_op jit(solution)/shard_map/dot_general | solution.py:38
  182.1 34.2 %shard_map.272 = (f32[2326,1,2048]{2,1,0:T(1,128)}, s16[4,16,592,128]{3,2,1,0:T(8,128)(2,1)}, f32[4,8,128]{2,1,0:T(8,128)}) custom-call(bf16[2368,1024]{1,0:T(8,128)(2,1)} %get-tuple-element.42.dl_ref, bf16[1024,2048]{1,0:T(8,128)(2,1)} %get-tuple-element.43.h_ref, bf16[2326,2048]{1,0:T(8,128)(2,1)} %bitcast.45), custom_call_target="tpu_custom_call" | custom-call | tf_op jit(solution)/shard_map/pallas_call | solution.py:189
  216.3 164.9 %shard_map.273 = (f32[512,2048]{1,0:T(8,128)}, f32[512,512]{1,0:T(8,128)}, f32[2368,256]{1,0:T(8,128)}, f32[512,256]{1,0:T(8,128)}, f32[512,512]{1,0:T(8,128)}, ...) custom-call(s16[4,16,592,128]{3,2,1,0:T(8,128)(2,1)} %get-tuple-element.44.codes_ref, ...), custom_call_target="tpu_custom_call" | custom-call | tf_op jit(solution)/shard_map/pallas_call | solution.py:932
  381.2 1.3 slice.50
  382.5 245.9 %shard_map.274 = (f32[4,128,256]{2,1,0:T(8,128)}, f32[512,512]{1,0:T(8,128)}, f32[512,256]{1,0:T(8,128)}, f32[512,512]{1,0:T(8,128)}, f32[8,128]{1,0:T(8,128)}) custom-call(f32[8,128]{1,0:T(8,128)} %get-tuple-element.55.stats_ref, f32[512,256]{1,0:T(8,128)} %get-tuple-element.56.red_hid_ref, f32[512,256]{1,0:T(8,128)} %bitcast.49, ...), custom_call_target="tpu_custom_call" | custom-call | tf_op jit(solution)/shard_map/pallas_call | solution.py:1878
  628.5 1.4 fusion.2
  631.3 1.2 broadcast_multiply_fusion.1
  632.7 0.9 bitcast_subtract_fusion
  633.6 1.0 copy.35
  634.6 2.4 multiply_subtract_fusion.1
  637.0 1.0 slice.47
  638.0 1.2 copy.36
  639.2 5.5 copy.37
  644.7 9.1 %multiply_subtract_fusion = (f32[256,2326]{0,1:T(8,128)}, f32[256,2326]{0,1:T(8,128)}, f32[256,2326]{0,1:T(8,128)}) fusion(f32[256,2326]{0,1:T(8,128)S(1)} %copy-done, f32[256,2326]{0,1:T(8,128)} %param.25, f32[2368,256]{1,0:T(8,128)} %get-tuple-element.63, f32[]{:T(128)} %bitcast.18, f32[256,2326]{0,1:T(8,128)} %param.26), kind=kLoop, calls=%fused_computation.3 | loop fusion | flops 8931840 | bytes 16672772 | tf_op jit(solution)/shard_map/sub | solution.py:78
  (36 shorter events, 4.9 us)
Async XLA Ops:
  0.6 8.4 %copy-start.5 = (f32[440,512]{1,0:T(8,128)S(1)}, f32[440,512]{1,0:T(8,128)}, u32[]{:S(2)}) copy-start(f32[440,512]{1,0:T(8,128)} %param.23) | copy-start | bytes 2703364
  4.8 5.3 copy-start.3
  382.5 247.4 %copy-start.9 = (f32[32,128]{1,0:T(8,128)S(1)}, f32[32,128]{1,0:T(8,128)}, u32[]{:S(2)}) copy-start(f32[32,128]{1,0:T(8,128)} %get-tuple-element.54) | copy-start | bytes 49156
  382.5 248.1 %copy-start.8 = (f32[1,3350]{1,0:T(1,128)S(1)}, f32[1,3350]{1,0:T(1,128)}, u32[]{:S(2)}) copy-start(f32[1,3350]{1,0:T(1,128)} %param.22) | copy-start | bytes 40204
  382.5 248.1 %copy-start.10 = (f32[1,3350]{1,0:T(1,128)S(1)}, f32[1,3350]{1,0:T(1,128)}, u32[]{:S(2)}) copy-start(f32[1,3350]{1,0:T(1,128)} %param.27) | copy-start | bytes 40204
  382.5 248.1 %copy-start.11 = (f32[1,3350]{1,0:T(1,128)S(1)}, f32[1,3350]{1,0:T(1,128)}, u32[]{:S(2)}) copy-start(f32[1,3350]{1,0:T(1,128)} %param.28) | copy-start | bytes 40204
  628.5 4.2 copy-start.2
  628.5 5.1 copy-start.7
  631.3 3.3 copy-start.1
  632.7 4.3 copy-start.6
  634.6 3.4 copy-start.4
  639.2 5.5 copy-start

commit v9 on v8

--- a/solution.py
+++ b/solution.py
@@ -236,6 +236,7 @@
     vec_sum_ref,
     stats_ref,
     grad,
+    turned,
     res_buf,
     h_buf,
     slope_buf,
@@ -299,14 +300,14 @@
 
     def hid_res_copy(part):
         return pltpu.make_async_copy(
-            res_hid_ref.at[pl.ds(part * 256, 256), :],
-            res_buf.at[part, pl.ds(0, 256), :],
+            res_hid_ref.at[:, pl.ds(part * 256, 256)],
+            res_buf.at[part],
             res_sems.at[part],
         )
 
     def hid_next_copy(part):
         return pltpu.make_async_copy(
-            grad.at[pl.ds(0, 256), :], next_hid_ref.at[pl.ds(part * 256, 256), :], load_sems.at[1]
+            turned, next_hid_ref.at[:, pl.ds(part * 256, 256)], load_sems.at[1]
         )
 
     def load(src, dst):
@@ -589,12 +590,10 @@
         for part in range(2):
             first = part * 256
             hid_res_copy(part).wait()
-            if part:
-                hid_next_copy(part - 1).wait()
             total = jnp.zeros((256, 128), F32)
             for lane in range(0, wide, 512):
                 value = dot_nn(dz_two[first : first + 256, :], h_buf[:, lane : lane + 512])
-                value = value + res_buf[part, :, lane : lane + 512].astype(F32)
+                value = value + jnp.transpose(res_buf[part, lane : lane + 512, :].astype(F32))
                 grad[:, lane : lane + 512] = value
                 value = jnp.abs(value)
                 for more in range(0, 512, 128):
@@ -617,6 +616,10 @@
                 return carry
 
             lax.fori_loop(0, 16, some, 0)
+            if part:
+                hid_next_copy(part - 1).wait()
+            for lane in range(0, wide, 128):
+                turned[lane : lane + 128, :] = jnp.transpose(grad[:, lane : lane + 128])
             hid_next_copy(part).start()
         load(x_ref, h_buf.at[:, pl.ds(0, x_ref.shape[1])]).start()
         set_sizes(HID_ROWS, HID_GROUP)
@@ -932,7 +935,7 @@
     return pl.pallas_call(
         functools.partial(reduce_kernel, deep, senones),
         out_shape=(
-            jax.ShapeDtypeStruct((HID_ROWS, wide), F32),
+            jax.ShapeDtypeStruct((wide, HID_ROWS), F32),
             jax.ShapeDtypeStruct((HID_ROWS, in_wide), F32),
             jax.ShapeDtypeStruct((OUT_GROUPS * OUT_ROWS, 256), F32),
             jax.ShapeDtypeStruct((HID_ROWS, 256), F32),
@@ -945,7 +948,8 @@
         out_specs=(hbm,) + (vmem,) * 7,
         scratch_shapes=[
             pltpu.VMEM((256, wide), F32),
-            pltpu.VMEM((2, 256, wide), BF16),
+            pltpu.VMEM((wide, 256), F32),
+            pltpu.VMEM((2, wide, 256), BF16),
             pltpu.VMEM((frames, wide), BF16),
             pltpu.VMEM((2, 256, units), F32),
             pltpu.VMEM((640, 128), F32),
@@ -999,9 +1003,9 @@
     )(codes, sizes, h_one, x, part, slope_two, slope_one, w_hid, res_hid, res_in, vec)
 
 
-RING_STARTS = (0, 2, 5, 7, 9)
+RING_STARTS = (0, 0, 5, 6, 7)
 LAYER_TWO_WAVE = 7
-LOGIT_WAVES = (11, 12, 14, 16)
+LOGIT_WAVES = (11, 12, 13, 14)
 
 
 def forward_kernel(
@@ -1023,8 +1027,7 @@
     w_out_out,
     mom_far_ref,
     dl_ref,
-    bias_sum_ref,
-    loss_ref,
+    vec_ref,
     x_all,
     h_one,
     h_two,
@@ -1289,10 +1292,7 @@
     line = all_tags()
     live = line >= 0
     loss = jnp.where(live, top + jnp.log(total) - picked, 0.0)
-    loss_ref[...] = jnp.zeros_like(loss_ref)
-    loss_ref[0:1, :] = functools.reduce(
-        jnp.add, [loss[:, lane : lane + 128] for lane in range(0, frames, 128)]
-    )
+    loss = jnp.sum(loss, axis=1, keepdims=True)
     weight = jnp.where(live, 1.0 / slot_count, 0.0)
     line = jnp.broadcast_to(own_row(line), (16, frames))
     hit_weight = jnp.broadcast_to(weight, (16, frames))
@@ -1313,10 +1313,14 @@
             return carry
 
         lax.fori_loop(0, OUT_ROWS // 16, gradient, 0)
-    bias_sum_ref[...] = jnp.zeros_like(bias_sum_ref)
+    vec_ref[...] = jnp.zeros_like(vec_ref)
+    row = 2 * units // 128
     for number in range(bias_out_ref.shape[0]):
-        block = jnp.transpose(bias_col[number * 128 : (number + 1) * 128, :])
-        bias_sum_ref[number : number + 1, :] = jnp.sum(block, axis=0, keepdims=True)
+        line = jnp.transpose(bias_col[number * 128 : (number + 1) * 128, :])
+        line = jnp.sum(line, axis=0, keepdims=True)
+        place = 128 * number + lax.broadcasted_iota(jnp.int32, line.shape, 1)
+        line = jnp.where(place < senones, line, jnp.where(place == senones, loss, 0.0))
+        vec_ref[row + number : row + number + 1, :] = line
 
     for group in range(len(RING_STARTS)):
         for way in range(2):
@@ -1359,11 +1363,10 @@
         + (
             jax.ShapeDtypeStruct(mom.shape, F32),
             jax.ShapeDtypeStruct((rows, frames), BF16),
-            jax.ShapeDtypeStruct((24, 128), F32),
-            jax.ShapeDtypeStruct((8, 128), F32),
+            jax.ShapeDtypeStruct((32, 128), F32),
         ),
         in_specs=[vmem] * 7 + [hbm],
-        out_specs=(hbm,) * 8 + (vmem,) * 3,
+        out_specs=(hbm,) * 8 + (vmem,) * 2,
         scratch_shapes=[pltpu.VMEM(shape, kind) for shape, kind in kept[:5]]
         + [
             pltpu.VMEM((512, units), BF16),
@@ -1394,7 +1397,11 @@
 
 DIM_BITS = (2, 4, 8)
 ORDERS = ((0, 1, 2), (1, 2, 0), (2, 0, 1))
-PIECES = ((0, 48), (48, 48), (96, 32))
+PIECES = (
+    ((0, 48, 0, 1792),),
+    ((48, 96, 0, 1792),),
+    ((96, 128, 0, 2048), (0, 96, 1792, 2048)),
+)
 SIZE_PIECE = 2
 LIGHT_HID = 3
 LIGHT_IN = 2
@@ -1468,13 +1475,12 @@
     spread_recv,
     pair_send,
     pair_recv,
-    size_send,
-    size_recv,
 ):
     blk = lax.axis_index("blk")
     col = lax.axis_index("col")
     rows, wide = xs.shape
     height = back.shape[2]
+    deep = mom_in_ref.shape[0]
     part_wide = inp_ref.shape[1]
     other_core = {"col": col + 1 - 2 * (col % 2)}
     dims = (
@@ -1496,11 +1502,12 @@
     share = 0.125
     sums[blk, 0:1, :] = fold(stats_ref[...])
     sums[blk, 1:2, :] = fold(mom_hid_ref[...] * mom_hid_ref[...])
-    sums[blk, 2:3, :] = fold(mom_hid_ref[...] * red_hid_ref[...])
+    red_hid = jnp.transpose(red_hid_ref[...])
+    sums[blk, 2:3, :] = fold(mom_hid_ref[...] * red_hid)
     sums[blk, 3:4, :] = fold(red_hid_ref[...] * red_hid_ref[...])
     sums[blk, 4:5, :] = fold(mom_in_ref[...] * mom_in_ref[...]) * share
-    sums[blk, 5:6, :] = fold(mom_in_ref[...] * red_in_ref[...]) * share
-    sums[blk, 6:7, :] = fold(red_in_ref[...] * red_in_ref[...]) * share
+    sums[blk, 5:6, :] = fold(mom_in_ref[...] * red_in_ref[0:deep, :]) * share
+    sums[blk, 6:7, :] = fold(red_in_ref[0:deep, :] * red_in_ref[0:deep, :]) * share
     sums[blk, 7:8, :] = jnp.zeros((1, 128), F32)
     eye = lax.broadcasted_iota(jnp.int32, (rows, rows), 0) == lax.broadcasted_iota(
         jnp.int32, (rows, rows), 1
@@ -1543,13 +1550,13 @@
 
     norm_ref[0:4, :] = jnp.broadcast_to(clip, (4, 128))
     norm_ref[4:8, :] = jnp.broadcast_to(factor, (4, 128))
-    next_hid_ref[...] = 0.5 * mom_hid_ref[...] + factor * red_hid_ref[...]
-    next_in_ref[...] = 0.5 * mom_in_ref[...] + factor * red_in_ref[...]
+    next_hid_ref[...] = 0.5 * mom_hid_ref[...] + factor * jnp.transpose(red_hid_ref[...])
+    next_in_ref[...] = 0.5 * mom_in_ref[...] + factor * red_in_ref[0:deep, :]
 
     my_lanes = pl.ds(pl.multiple_of(blk * height, height), height)
     for number in range(4):
         there = slice(number * rows, (number + 1) * rows)
-        value = next_hid_ref[there, :]
+        value = jnp.transpose(next_hid_ref[:, there])
         largest = jnp.maximum(jnp.max(jnp.abs(value), axis=1, keepdims=True), 1e-30)
         spread_out[number] = to_codes(value * (TOP_CODE / largest))
         line = jnp.sum(jnp.where(eye, largest, 0.0), axis=0, keepdims=True)
@@ -1575,8 +1582,11 @@
     my_half = pl.ds(pl.multiple_of(high * part_wide, part_wide), part_wide)
     far_half = pl.ds(pl.multiple_of((1 - high) * part_wide, part_wide), part_wide)
     in_scale = norm_of(4)
-    xin[:, my_half] = next_in_ref[...] * in_scale
-    xin[:, far_half] = (0.5 * mom_far_ref[...] + factor * red_far_ref[...]) * in_scale
+    xin[deep:, :] = jnp.zeros((xin.shape[0] - deep, xin.shape[1]), F32)
+    xin[0:deep, my_half] = next_in_ref[...] * in_scale
+    xin[0:deep, far_half] = (
+        0.5 * mom_far_ref[...] + factor * red_far_ref[0:deep, :]
+    ) * in_scale
     spread_got[blk] = spread_out[blk % 4]
     spread_size_got[blk] = spread_size_out[blk % 4]
     for copy in spread:
@@ -1592,35 +1602,32 @@
 
     numbers = {move: number for number, move in enumerate(MOVES)}
 
-    def part(turn, slot, piece):
-        first, count = PIECES[piece]
-        return codes.at[turn, slot, pl.ds(first, count), :]
+    def parts(turn, slot, piece):
+        refs = [
+            codes.at[turn, slot, pl.ds(top, low - top), pl.ds(left, right - left)]
+            for top, low, left, right in PIECES[piece]
+        ]
+        numbered = [(piece, refs[0])]
+        if piece == SIZE_PIECE:
+            numbered += [(3, refs[1]), (4, sizes.at[turn, slot])]
+        return numbered
 
     def send(turn, move):
         piece, slot, dim = move
         there = slot | DIM_BITS[dim]
-        copies = [
+        return [
             pltpu.make_async_remote_copy(
-                src_ref=part(turn, slot, piece),
-                dst_ref=part(turn, there, piece),
-                send_sem=send_sems.at[numbers[move]],
-                recv_sem=recv_sems.at[turn, there, piece],
+                src_ref=src,
+                dst_ref=dst,
+                send_sem=send_sems.at[numbers[move], max(number - 2, 0)],
+                recv_sem=recv_sems.at[turn, there, number],
                 device_id=dims[dim],
                 device_id_type=MESH,
             )
+            for (number, src), (_, dst) in zip(
+                parts(turn, slot, piece), parts(turn, there, piece), strict=True
+            )
         ]
-        if piece == SIZE_PIECE:
-            copies.append(
-                pltpu.make_async_remote_copy(
-                    src_ref=sizes.at[turn, slot],
-                    dst_ref=sizes.at[turn, there],
-                    send_sem=size_send.at[numbers[move]],
-                    recv_sem=size_recv.at[turn, there],
-                    device_id=dims[dim],
-                    device_id_type=MESH,
-                )
-            )
-        return copies
 
     def send_all(turn, moves):
         for move in moves:
@@ -1628,43 +1635,30 @@
                 copy.start()
 
     def to_core(turn, slot, piece):
-        copies = [
+        return [
             pltpu.make_async_remote_copy(
-                src_ref=part(turn, slot, piece),
-                dst_ref=part(turn, slot + 1, piece),
-                send_sem=core_sems.at[slot // 2, piece],
-                recv_sem=recv_sems.at[turn, slot + 1, piece],
+                src_ref=src,
+                dst_ref=dst,
+                send_sem=core_sems.at[slot // 2, number],
+                recv_sem=recv_sems.at[turn, slot + 1, number],
                 device_id=other_core,
                 device_id_type=MESH,
             )
+            for (number, src), (_, dst) in zip(
+                parts(turn, slot, piece), parts(turn, slot + 1, piece), strict=True
+            )
         ]
-        if piece == SIZE_PIECE:
-            copies.append(
-                pltpu.make_async_remote_copy(
-                    src_ref=sizes.at[turn, slot],
-                    dst_ref=sizes.at[turn, slot + 1],
-                    send_sem=core_sems.at[slot // 2, 3],
-                    recv_sem=size_recv.at[turn, slot + 1],
-                    device_id=other_core,
-                    device_id_type=MESH,
-                )
-            )
-        return copies
 
     def arrived(turn, slot, piece):
-        def wait(ref, sem):
+        for number, ref in parts(turn, slot, piece):
             pltpu.make_async_remote_copy(
                 src_ref=ref,
                 dst_ref=ref,
                 send_sem=core_sems.at[0, 0],
-                recv_sem=sem,
+                recv_sem=recv_sems.at[turn, slot, number],
                 device_id=other_core,
                 device_id_type=MESH,
             ).wait_recv()
-
-        wait(part(turn, slot, piece), recv_sems.at[turn, slot, piece])
-        if piece == SIZE_PIECE:
-            wait(sizes.at[turn, slot], size_recv.at[turn, slot])
 
     def forward(turn, moves, on=()):
         for number, (slot, piece) in enumerate(landed(moves)):
@@ -1858,13 +1852,12 @@
             )
         )
         copies[-1].start()
-    hid_ref[place] = xs[:, my_lanes]
-    inp_ref[...] = xin[:, my_half]
+    back[place] = xs[:, my_lanes]
+    inp_ref[...] = xin[0:deep, my_half]
     for copy in copies:
         copy.wait_recv()
-    for target in (dims[0], dims[2], diagonal):
-        other = target["blk"] % 4
-        hid_ref[other] = back[other]
+    for number in range(4):
+        hid_ref[:, number * rows : (number + 1) * rows] = jnp.transpose(back[number])
     for copy in copies + spread + told:
         copy.wait_send()
 
@@ -1878,10 +1871,10 @@
     return pl.pallas_call(
         muon_kernel,
         out_shape=(
-            jax.ShapeDtypeStruct((4, rows, height), F32),
-            jax.ShapeDtypeStruct((deep, part_wide), F32),
-            jax.ShapeDtypeStruct(red_hid.shape, F32),
-            jax.ShapeDtypeStruct(red_in.shape, F32),
+            jax.ShapeDtypeStruct(mom_hid.shape, F32),
+            jax.ShapeDtypeStruct(mom_in.shape, F32),
+            jax.ShapeDtypeStruct(mom_hid.shape, F32),
+            jax.ShapeDtypeStruct(mom_in.shape, F32),
             jax.ShapeDtypeStruct((8, 128), F32),
         ),
         in_specs=[vmem] * 7,
@@ -1909,9 +1902,9 @@
             pltpu.VMEM((8, rows, height), I16),
             pltpu.VMEM((4, 8, rows), F32),
             pltpu.VMEM((8, 8, rows), F32),
-            sem((len(MOVES),)),
-            sem((8, 4)),
-            sem((2, 16, 3)),
+            sem((len(MOVES), 3)),
+            sem((8, 5)),
+            sem((2, 16, 5)),
             sem((3,)),
             sem((3,)),
             sem((10,)),
@@ -1920,8 +1913,6 @@
             sem((2, 7)),
             sem((2,)),
             sem((2,)),
-            sem((len(MOVES),)),
-            sem((2, 16)),
         ],
         compiler_params=pltpu.CompilerParams(
             collective_id=0, has_side_effects=True, vmem_limit_bytes=60 * 1024 * 1024
@@ -2105,12 +2096,11 @@
     deep = w_input.shape[0]
     padded = 512
     rows_out = OUT_GROUPS * OUT_ROWS
-    mom_in_padded = jnp.pad(mom_input, ((0, padded - deep), (0, 0)))
     own_tags = jnp.where(mask > 0, labels, -1).reshape(1, -1)
     layer_biases = jnp.pad(bias_row[: 2 * hcol].reshape(2, hcol), ((0, 6), (0, 0)))
     blocks = -(-rows_out // 128)
     out_biases = jnp.pad(bias_row[2 * hcol :], (0, blocks * 128 - scol)).reshape(blocks, 128)
-    inputs, h_one, h_two, slope_one, slope_two, low_hidden, low_output, mom_far, d_logits, bias_sums, losses = (
+    inputs, h_one, h_two, slope_one, slope_two, low_hidden, low_output, mom_far, d_logits, vec = (
         forward_pass(
             frames.reshape(-1, deep),
             jnp.broadcast_to(own_tags, (8, own_tags.shape[1])),
@@ -2119,14 +2109,11 @@
             w_output.T,
             layer_biases,
             out_biases,
-            mom_in_padded,
+            mom_input,
             slot_count,
         )
     )
-    loss_local = jnp.sum(losses)
     partial = inner_rows(d_logits, low_output)
-    vec = jnp.concatenate([jnp.zeros((2 * hcol,), F32), bias_sums.reshape(-1)[:scol], loss_local[None]])
-    vec = jnp.pad(vec, (0, 4096 - vec.shape[0])).reshape(32, 128)
     next_out, codes, sizes = squash_out(d_logits, h_two, res_output[0].T)
     next_hid, next_in, red_out, red_hid, red_in, red_far, vec_sum, stats = reduce_grads(
         codes,
@@ -2137,36 +2124,33 @@
         slope_two,
         slope_one,
         low_hidden,
-        res_hidden[0].T,
+        res_hidden[0],
         jnp.pad(res_input[0], ((0, padded - deep), (0, 0))).T,
         vec,
         scol,
         deep,
     )
     next_res_output = next_out.transpose(1, 2, 0)
-    next_res_hidden = next_hid.T
+    next_res_hidden = next_hid
     next_res_input = next_in[:, :deep].T
     red_output = red_out[:scol].T
     vec_sum = vec_sum.reshape(-1)
     red_bias = vec_sum[: bias_row.shape[0]]
     loss_sum = vec_sum[bias_row.shape[0]]
-    done_hidden, done_input, mom_hid_next, mom_in_next, norms = muon(
+    done_hidden, done_input, next_mom_hidden, next_mom_input, norms = muon(
         stats,
         red_hid,
-        mom_hidden.T,
+        mom_hidden,
         red_in,
-        mom_in_padded,
+        mom_input,
         red_far,
         mom_far,
         hcol * ncol,
     )
     clip_norm = norms[0, 0]
     factor = norms[4, 0]
-    next_mom_hidden = mom_hid_next.T
-    next_mom_input = mom_in_next[:deep]
-    done_hidden = done_hidden.reshape(hcol, w_hidden.shape[0]).T
     muon_scale = LR_MUON * 0.2 * math.sqrt(hcol * ncol)
-    new_input = w_input * (1.0 - LR_MUON * WD_MUON) - muon_scale * done_input[:deep]
+    new_input = w_input * (1.0 - LR_MUON * WD_MUON) - muon_scale * done_input
     new_hidden = w_hidden * (1.0 - LR_MUON * WD_MUON) - muon_scale * done_hidden
     new_output, next_out_first, next_out_second = adam_step(
         w_output, factor * red_output, out_first, out_second

time: 663 us -> 634 us (0.956)
  Pallas kernels: 594 us -> 581 us
  local copies, waits for them, and re-layouts: 24.7 us -> 14.3 us
    unnamed x30 -> x27, local copies, waits for them, and re-layouts: 13.5 us -> 6.23 us
where the time goes in v9:
time: 634 us; the launch traced here: 629 us
  Pallas kernels  581 us (92%)
  matrix products  17.4 us (3%)
  other arithmetic  15.1 us (2%)
  local copies, waits for them, and re-layouts  14.3 us (2%)
    pallas_call x1, Pallas kernels, muon(): pl.pallas_call(muon_kernel, out_shape=(jax.ShapeDtypeStruct(mom_hid.shape...  241 us
    pallas_call x1, Pallas kernels, reduce_grads(): pl.pallas_call(functools.partial(reduce_kernel, deep, senones), out_shape...  163 us
    pallas_call x1, Pallas kernels, forward_pass(): pl.pallas_call(functools.partial(forward_kernel, slot_count), out_shape=t...  143 us
    pallas_call x1, Pallas kernels, squash_out(): pl.pallas_call(functools.partial(squash_kernel, senones), grid=(OUT_GROUP...  34.1 us
    dot_general x1, matrix products, inner_rows(): lax.dot_general(left_side, right_side, (((0,), (0,)), ((), ())), preferre...  17.4 us

profile of v9, /device:TPU:0, one launch (start us, length us, event | category | flops | bytes accessed | tf_op | source)
XLA Modules:
  0.0 628.6 jit_solution(5162671986104247644)
XLA Ops:
  0.6 0.7 compare_select_fusion
  1.4 0.7 slice_reduce_fusion.1
  2.7 0.6 pad.12.bias_ref
  3.4 0.7 slice_reduce_fusion
  4.1 0.6 pad_bitcast_fusion.1.bias_out_ref
  4.7 1.2 copy.31
  5.9 0.8 pad_bitcast_fusion.res_in_ref
  6.8 142.6 %shard_map.271 = (bf16[1024,512]{1,0:T(8,128)(2,1)}, bf16[1024,2048]{1,0:T(8,128)(2,1)}, bf16[1024,2048]{1,0:T(8,128)(2,1)}, f32[1024,512]{1,0:T(8,128)}, f32[10...) custom-call(bf16[256,440]{1,0:T(8,128)(2,1)} %bitcast.36, ...), custom_call_target="tpu_custom_call" | custom-call | tf_op jit(solution)/shard_map/pallas_call | solution.py:1360
  149.4 17.4 %fusion.3.part_ref = f32[1024,2048]{1,0:T(8,128)} fusion(bf16[2368,1024]{1,0:T(8,128)(2,1)} %get-tuple-element.41.dl_ref, bf16[2368,2048]{1,0:T(8,128)(2,1)} %get-tuple-element.47), kind=kOutput, calls=%fused_computation.21 | convolution fusion | flops 9932111872 | bytes 22937600 | tf_op jit(solution)/shard_map/dot_general | solution.py:38
  166.8 34.1 %shard_map.272 = (f32[2326,1,2048]{2,1,0:T(1,128)}, s16[4,16,592,128]{3,2,1,0:T(8,128)(2,1)}, f32[4,8,128]{2,1,0:T(8,128)}) custom-call(bf16[2368,1024]{1,0:T(8,128)(2,1)} %get-tuple-element.41.dl_ref, bf16[1024,2048]{1,0:T(8,128)(2,1)} %get-tuple-element.42.h_ref, bf16[2326,2048]{1,0:T(8,128)(2,1)} %bitcast.31), custom_call_target="tpu_custom_call" | custom-call | tf_op jit(solution)/shard_map/pallas_call | solution.py:189
  200.9 162.9 %shard_map.273 = (f32[2048,512]{1,0:T(8,128)}, f32[512,512]{1,0:T(8,128)}, f32[2368,256]{1,0:T(8,128)}, f32[512,256]{1,0:T(8,128)}, f32[512,512]{1,0:T(8,128)}, ...) custom-call(s16[4,16,592,128]{3,2,1,0:T(8,128)(2,1)} %get-tuple-element.43.codes_ref, ...), custom_call_target="tpu_custom_call" | custom-call | tf_op jit(solution)/shard_map/pallas_call | solution.py:935
  363.8 1.3 slice.37
  365.1 1.3 slice_bitcast_fusion
  366.4 1.2 copy.32
  367.7 241.1 %shard_map.274 = (f32[256,512]{1,0:T(8,128)}, f32[440,512]{1,0:T(8,128)}, f32[256,512]{1,0:T(8,128)}, f32[440,512]{1,0:T(8,128)}, f32[8,128]{1,0:T(8,128)}) custom-call(f32[8,128]{1,0:T(8,128)} %get-tuple-element.53.stats_ref, f32[512,256]{1,0:T(8,128)} %get-tuple-element.54.red_hid_ref, f32[256,512]{1,0:T(8,128)} %mom_hid_ref.1, ...), custom_call_target="tpu_custom_call" | custom-call | tf_op jit(solution)/shard_map/pallas_call | solution.py:1871
  608.8 1.3 fusion.2
  610.1 0.7 multiply_multiply_fusion.1
  610.8 0.7 multiply_subtract_fusion.3
  611.5 1.9 multiply_subtract_fusion.2
  613.5 2.3 multiply_subtract_fusion.1
  615.8 8.8 %multiply_subtract_fusion = (f32[256,2326]{0,1:T(8,128)}, f32[256,2326]{0,1:T(8,128)}, f32[256,2326]{0,1:T(8,128)}) fusion(f32[256,2326]{0,1:T(8,128)S(1)} %copy-done, f32[256,2326]{0,1:T(8,128)S(1)} %copy-done.3, f32[2368,256]{1,0:T(8,128)} %get-tuple-element.61, f32[]{:T(128)} %bitcast.11, f32[256,2326]{0,1:T(8,128)} %param.26), kind=kLoop, calls=%fused_computation.3 | loop fusion | flops 8931840 | bytes 16672772 | tf_op jit(solution)/shard_map/sub | solution.py:78
  624.6 0.9 copy.36
  625.6 0.8 copy.37
  626.4 2.0 copy.38
  (25 shorter events, 0.7 us)
Async XLA Ops:
  367.6 242.5 %copy-start.8 = (f32[32,128]{1,0:T(8,128)S(1)}, f32[32,128]{1,0:T(8,128)}, u32[]{:S(2)}) copy-start(f32[32,128]{1,0:T(8,128)} %get-tuple-element.52) | copy-start | bytes 49156
  367.6 243.2 %copy-start.7 = (f32[1,3350]{1,0:T(1,128)S(1)}, f32[1,3350]{1,0:T(1,128)}, u32[]{:S(2)}) copy-start(f32[1,3350]{1,0:T(1,128)} %param.22) | copy-start | bytes 40204
  367.6 243.2 %copy-start.9 = (f32[1,3350]{1,0:T(1,128)S(1)}, f32[1,3350]{1,0:T(1,128)}, u32[]{:S(2)}) copy-start(f32[1,3350]{1,0:T(1,128)} %param.27) | copy-start | bytes 40204
  367.6 243.2 %copy-start.10 = (f32[1,3350]{1,0:T(1,128)S(1)}, f32[1,3350]{1,0:T(1,128)}, u32[]{:S(2)}) copy-start(f32[1,3350]{1,0:T(1,128)} %param.28) | copy-start | bytes 40204
  367.6 243.9 %copy-start.4 = (f32[256,512]{1,0:T(8,128)S(1)}, f32[256,512]{1,0:T(8,128)}, u32[]{:S(2)}) copy-start(f32[256,512]{1,0:T(8,128)} %w_hid_ref.1) | copy-start | bytes 1572868
  367.7 245.8 %copy-start.2 = (f32[440,512]{1,0:T(8,128)S(1)}, f32[440,512]{1,0:T(8,128)}, u32[]{:S(2)}) copy-start(f32[440,512]{1,0:T(8,128)} %w_in_ref.1) | copy-start | bytes 2703364
  367.7 248.1 %copy-start.3 = (f32[256,2326]{0,1:T(8,128)S(1)}, f32[256,2326]{0,1:T(8,128)}, u32[]{:S(2)}) copy-start(f32[256,2326]{0,1:T(8,128)} %param.25) | copy-start | bytes 7145476
  608.8 7.0 %copy-start = (f32[256,2326]{0,1:T(8,128)S(1)}, f32[256,2326]{0,1:T(8,128)}, u32[]{:S(2)}) copy-start(f32[256,2326]{0,1:T(8,128)} %param.21) | copy-start | bytes 7145476
  615.8 8.9 %copy-start.5 = (f32[440,512]{1,0:T(8,128)S(1)}, f32[440,512]{1,0:T(8,128)}, u32[]{:S(2)}) copy-start(f32[440,512]{1,0:T(8,128)} %get-tuple-element.113) | copy-start | bytes 2703364
  615.8 9.8 %copy-start.6 = (f32[256,512]{1,0:T(8,128)S(1)}, f32[256,512]{1,0:T(8,128)}, u32[]{:S(2)}) copy-start(f32[256,512]{1,0:T(8,128)} %get-tuple-element.114) | copy-start | bytes 1572868
  615.8 10.6 %copy-start.1 = (f32[2048,512]{1,0:T(8,128)S(1)}, f32[2048,512]{1,0:T(8,128)}, u32[]{:S(2)}) copy-start(f32[2048,512]{1,0:T(8,128)} %get-tuple-element.65) | copy-start | bytes 12582916

commit v10 on v9

--- a/solution.py
+++ b/solution.py
@@ -102,11 +102,11 @@
 HID_ROWS = 512
 HID_GROUP = 4
 IN_GROUP = 5
-TURN_AT = 5
-CROSS_AT = 6
-HID_AT = 13
-FINISH_AT = 14
-IN_AT = 20
+TURN_AT = 4
+CROSS_AT = 5
+HID_AT = 11
+FINISH_AT = 12
+IN_AT = 18
 HID_HOP = 3
 
 
@@ -141,7 +141,23 @@
     return number // 2 if number % 2 == 0 else 7 - number // 2
 
 
-def squash_kernel(senones, dl_ref, h_ref, res_ref, next_ref, codes_ref, size_ref, grad, cols, marks):
+def squash_kernel(
+    senones,
+    dl_ref,
+    h_ref,
+    res_ref,
+    w_ref,
+    next_ref,
+    codes_ref,
+    size_ref,
+    part_ref,
+    grad,
+    cols,
+    marks,
+    flipped,
+    total_part,
+    part_sem,
+):
     group = pl.program_id(0)
     rows, wide = grad.shape
     valid = senones - group * rows
@@ -163,7 +179,20 @@
         cols[0, there, :] = size
         cols[1, there, :] = 2.0 / size
 
-    def some(number, carry):
+    frames = dl_ref.shape[1]
+    for first in range(0, rows, 128):
+        count = min(128, rows - first)
+        for lane in range(0, frames, 128):
+            tile = dl_ref[first : first + count, lane : lane + 128].astype(F32)
+            if count < 128:
+                tile = jnp.concatenate([tile, jnp.zeros((128 - count, 128), F32)], axis=0)
+            flipped[lane : lane + 128, first : first + 128] = jnp.transpose(tile).astype(BF16)
+
+    @pl.when(group == 0)
+    def _():
+        total_part[...] = jnp.zeros_like(total_part)
+
+    def some(number):
         row = pl.multiple_of(number * 16, 16)
         size = cols[0, pl.ds(row, 16), :]
         steep = cols[1, pl.ds(row, 16), :]
@@ -174,16 +203,37 @@
                 curve * TOP_CODE
             )
             next_ref[pl.ds(row, 16), 0, lane : lane + 128] = piece - size * curve
+
+    parts = wide // 256
+    each = rows // 16 // parts
+
+    def beside(number, carry):
+        lanes = pl.ds(pl.multiple_of(number * 256, 256), 256)
+        total_part[:, lanes] += dot_nn(flipped[:, 0:rows], w_ref[:, lanes])
+        for more in range(each):
+            some(number * each + more)
         return carry
 
-    lax.fori_loop(0, rows // 16, some, 0)
+    lax.fori_loop(0, parts, beside, 0)
+    for number in range(parts * each, rows // 16):
+        some(number)
+    copy = pltpu.make_async_copy(total_part, part_ref, part_sem.at[0])
+
+    @pl.when(group == OUT_GROUPS - 1)
+    def _():
+        copy.start()
+
     marks[rows:, :] = jnp.zeros((marks.shape[0] - rows, 128), F32)
     lines = [jnp.transpose(marks[first : first + 128, :])[0:1, :] for first in range(0, rows, 128)]
     lines.append(jnp.zeros((8 - len(lines), 128), F32))
     size_ref[0] = jnp.concatenate(lines, axis=0)
 
-
-def squash_out(dl, h_two, res_out):
+    @pl.when(group == OUT_GROUPS - 1)
+    def _():
+        copy.wait()
+
+
+def squash_out(dl, h_two, res_out, w_out):
     senones, wide = res_out.shape
     frames = dl.shape[1]
     return pl.pallas_call(
@@ -193,24 +243,30 @@
             jax.ShapeDtypeStruct((senones, 1, wide), F32),
             jax.ShapeDtypeStruct((OUT_GROUPS, 2 * RING, OUT_ROWS, 128), I16),
             jax.ShapeDtypeStruct((OUT_GROUPS, 8, 128), F32),
+            jax.ShapeDtypeStruct((frames, wide), F32),
         ),
         in_specs=[
             pl.BlockSpec((OUT_ROWS, frames), lambda group: (group, 0)),
             pl.BlockSpec((frames, wide), lambda group: (0, 0)),
+            pl.BlockSpec((OUT_ROWS, wide), lambda group: (group, 0)),
             pl.BlockSpec((OUT_ROWS, wide), lambda group: (group, 0)),
         ],
         out_specs=(
             pl.BlockSpec((OUT_ROWS, 1, wide), lambda group: (group, 0, 0)),
             pl.BlockSpec((1, 2 * RING, OUT_ROWS, 128), lambda group: (group, 0, 0, 0)),
             pl.BlockSpec((1, 8, 128), lambda group: (group, 0, 0)),
+            pl.BlockSpec(memory_space=pl.ANY),
         ),
         scratch_shapes=[
             pltpu.VMEM((OUT_ROWS, wide), F32),
             pltpu.VMEM((2, OUT_ROWS, 128), F32),
             pltpu.VMEM((640, 128), F32),
+            pltpu.VMEM((frames, 640), BF16),
+            pltpu.VMEM((frames, wide), F32),
+            pltpu.SemaphoreType.DMA((1,)),
         ],
         compiler_params=pltpu.CompilerParams(vmem_limit_bytes=60 * 1024 * 1024),
-    )(dl, h_two, res_out)
+    )(dl, h_two, res_out, w_out)
 
 
 def reduce_kernel(
@@ -2113,8 +2169,7 @@
             slot_count,
         )
     )
-    partial = inner_rows(d_logits, low_output)
-    next_out, codes, sizes = squash_out(d_logits, h_two, res_output[0].T)
+    next_out, codes, sizes, partial = squash_out(d_logits, h_two, res_output[0].T, low_output)
     next_hid, next_in, red_out, red_hid, red_in, red_far, vec_sum, stats = reduce_grads(
         codes,
         sizes,

time: 634 us -> 637 us (level)
  Pallas kernels: 581 us -> 603 us
  matrix products: 17.4 us -> 0 us
    pallas_call x1, Pallas kernels: 34.1 us -> 55.6 us  [squash_out(): pl.pallas_call(functools.partial(squash_kernel, senones), grid=(OUT_GROUP...]
    dot_general x1 -> x0, matrix products: 17.4 us -> none  [inner_rows(): lax.dot_general(left_side, right_side, (((0,), (0,)), ((), ())), preferre...]
where the time goes in v10:
time: 637 us; the launch traced here: 631 us
  Pallas kernels  603 us (95%)
  local copies, waits for them, and re-layouts  14.2 us (2%)
  other arithmetic  13.2 us (2%)
    pallas_call x1, Pallas kernels, muon(): pl.pallas_call(muon_kernel, out_shape=(jax.ShapeDtypeStruct(mom_hid.shape...  241 us
    pallas_call x1, Pallas kernels, reduce_grads(): pl.pallas_call(functools.partial(reduce_kernel, deep, senones), out_shape...  164 us
    pallas_call x1, Pallas kernels, forward_pass(): pl.pallas_call(functools.partial(forward_kernel, slot_count), out_shape=t...  143 us
    pallas_call x1, Pallas kernels, squash_out(): pl.pallas_call(functools.partial(squash_kernel, senones), grid=(OUT_GROUP...  55.6 us

profile of v10, /device:TPU:0, one launch (start us, length us, event | category | flops | bytes accessed | tf_op | source)
XLA Modules:
  0.0 631.4 jit_solution(1546424225917636520)
XLA Ops:
  0.6 0.7 slice_reduce_fusion.1
  1.4 0.6 pad.12.bias_ref
  2.0 0.7 slice_reduce_fusion
  2.7 0.6 pad_bitcast_fusion.1.bias_out_ref
  3.3 0.7 compare_select_fusion
  4.1 0.6 broadcast_in_dim.20.tags_ref
  4.7 142.6 %shard_map.271 = (bf16[1024,512]{1,0:T(8,128)(2,1)}, bf16[1024,2048]{1,0:T(8,128)(2,1)}, bf16[1024,2048]{1,0:T(8,128)(2,1)}, f32[1024,512]{1,0:T(8,128)}, f32[10...) custom-call(bf16[256,440]{1,0:T(8,128)(2,1)} %bitcast.34, ...), custom_call_target="tpu_custom_call" | custom-call | tf_op jit(solution)/shard_map/pallas_call | solution.py:1416
  147.3 55.6 %shard_map.272 = (f32[2326,1,2048]{2,1,0:T(1,128)}, s16[4,16,592,128]{3,2,1,0:T(8,128)(2,1)}, f32[4,8,128]{2,1,0:T(8,128)}, f32[1024,2048]{1,0:T(8,128)}) custom-call(bf16[2368,1024]{1,0:T(8,128)(2,1)} %get-tuple-element.42.dl_ref, bf16[1024,2048]{1,0:T(8,128)(2,1)} %get-tuple-element.43.h_ref, bf16[2326,2048]{1,0:T(8,128)(2,1)} %bitcast.29, ...), custom_call_target="tpu_custom_call" | custom-call | tf_op jit(solution)/shard_map/pallas_call | solution.py:239
  202.9 0.2 copy.31
  203.2 0.8 pad_bitcast_fusion.res_in_ref
  204.0 163.6 %shard_map.273 = (f32[2048,512]{1,0:T(8,128)}, f32[512,512]{1,0:T(8,128)}, f32[2368,256]{1,0:T(8,128)}, f32[512,256]{1,0:T(8,128)}, f32[512,512]{1,0:T(8,128)}, ...) custom-call(s16[4,16,592,128]{3,2,1,0:T(8,128)(2,1)} %get-tuple-element.45.codes_ref, ...), custom_call_target="tpu_custom_call" | custom-call | tf_op jit(solution)/shard_map/pallas_call | solution.py:991
  367.6 241.2 %shard_map.274 = (f32[256,512]{1,0:T(8,128)}, f32[440,512]{1,0:T(8,128)}, f32[256,512]{1,0:T(8,128)}, f32[440,512]{1,0:T(8,128)}, f32[8,128]{1,0:T(8,128)}) custom-call(f32[8,128]{1,0:T(8,128)} %get-tuple-element.55.stats_ref, f32[512,256]{1,0:T(8,128)} %get-tuple-element.56.red_hid_ref, f32[256,512]{1,0:T(8,128)} %mom_hid_ref.1, ...), custom_call_target="tpu_custom_call" | custom-call | tf_op jit(solution)/shard_map/pallas_call | solution.py:1927
  608.8 1.3 fusion.2
  610.1 0.7 multiply_multiply_fusion.1
  610.8 0.7 multiply_subtract_fusion.3
  611.5 9.2 %multiply_subtract_fusion = (f32[256,2326]{0,1:T(8,128)}, f32[256,2326]{0,1:T(8,128)}, f32[256,2326]{0,1:T(8,128)}) fusion(f32[256,2326]{0,1:T(8,128)S(1)} %copy-done, f32[256,2326]{0,1:T(8,128)} %param.25, f32[2368,256]{1,0:T(8,128)} %get-tuple-element.63, f32[]{:T(128)} %bitcast.11, f32[256,2326]{0,1:T(8,128)} %param.26), kind=kLoop, calls=%fused_computation.3 | loop fusion | flops 8931840 | bytes 16672772 | tf_op jit(solution)/shard_map/sub | solution.py:78
  620.7 1.1 multiply_subtract_fusion.1
  621.8 0.2 copy-done.6
  622.0 0.9 multiply_subtract_fusion.2
  623.0 1.2 copy.32
  624.2 0.6 slice.37
  624.8 0.9 copy.36
  625.7 0.8 copy.37
  626.5 4.6 copy.38
  (28 shorter events, 0.2 us)
Async XLA Ops:
  147.3 55.6 %copy-start.8 = (bf16[1,440,512]{2,1,0:T(8,128)(2,1)S(1)}, bf16[1,440,512]{2,1,0:T(8,128)(2,1)}, u32[]{:S(2)}) copy-start(bf16[1,440,512]{2,1,0:T(8,128)(2,1)} %param.29) | copy-start | bytes 1351684
  367.6 242.5 %copy-start.10 = (f32[32,128]{1,0:T(8,128)S(1)}, f32[32,128]{1,0:T(8,128)}, u32[]{:S(2)}) copy-start(f32[32,128]{1,0:T(8,128)} %get-tuple-element.54) | copy-start | bytes 49156
  367.6 243.2 %copy-start.9 = (f32[1,3350]{1,0:T(1,128)S(1)}, f32[1,3350]{1,0:T(1,128)}, u32[]{:S(2)}) copy-start(f32[1,3350]{1,0:T(1,128)} %param.22) | copy-start | bytes 40204
  367.6 243.2 %copy-start.11 = (f32[1,3350]{1,0:T(1,128)S(1)}, f32[1,3350]{1,0:T(1,128)}, u32[]{:S(2)}) copy-start(f32[1,3350]{1,0:T(1,128)} %param.27) | copy-start | bytes 40204
  367.6 243.2 %copy-start.12 = (f32[1,3350]{1,0:T(1,128)S(1)}, f32[1,3350]{1,0:T(1,128)}, u32[]{:S(2)}) copy-start(f32[1,3350]{1,0:T(1,128)} %param.28) | copy-start | bytes 40204
  367.6 243.8 %copy-start = (f32[256,2326]{0,1:T(8,128)S(1)}, f32[256,2326]{0,1:T(8,128)}, u32[]{:S(2)}) copy-start(f32[256,2326]{0,1:T(8,128)} %param.21) | copy-start | bytes 7145476
  611.5 9.2 %copy-start.1 = (f32[440,512]{1,0:T(8,128)S(1)}, f32[440,512]{1,0:T(8,128)}, u32[]{:S(2)}) copy-start(f32[440,512]{1,0:T(8,128)} %w_in_ref.1) | copy-start | bytes 2703364
  611.5 9.2 %copy-start.5 = (f32[440,512]{1,0:T(8,128)S(1)}, f32[440,512]{1,0:T(8,128)}, u32[]{:S(2)}) copy-start(f32[440,512]{1,0:T(8,128)} %get-tuple-element.61) | copy-start | bytes 2703364
  620.6 1.1 copy-start.2
  620.6 1.4 copy-start.6
  620.7 2.3 copy-start.3
  622.9 1.9 copy-start.4
  623.0 2.7 copy-start.7

commit v11 on v9

--- a/solution.py
+++ b/solution.py
@@ -628,13 +628,23 @@
     def in_group():
         wide = x_ref.shape[1]
         load(x_ref, h_buf.at[:, pl.ds(0, wide)]).wait()
+        for top in range(0, wide, 128):
+            count = min(128, deep - top)
+            for left in range(0, HID_ROWS, 128):
+                tile = res_in_ref[top : top + count, left : left + 128].astype(F32)
+                if count < 128:
+                    tile = jnp.concatenate([tile, jnp.zeros((128 - count, 128), F32)], axis=0)
+                place, lane = top // 256 * HID_ROWS + left, top % 256
+                turned[place : place + 128, lane : lane + 128] = jnp.transpose(tile)
         for first in range(0, HID_ROWS, 256):
             grad[0:256, 0:wide] = dot_nn(dz_one[first : first + 256, :], h_buf[:, 0:wide])
 
             def add(number, carry, first=first):
                 row = pl.multiple_of(number * 16, 16)
                 place = pl.multiple_of(first + row, 16)
-                value = grad[pl.ds(row, 16), 0:wide] + res_in_ref[pl.ds(place, 16), :].astype(F32)
+                value = grad[pl.ds(row, 16), 0:wide] + jnp.concatenate(
+                    [turned[pl.ds(place, 16), :], turned[pl.ds(HID_ROWS + place, 16), :]], axis=1
+                )
                 grad[pl.ds(row, 16), 0:wide] = value
                 value = jnp.abs(value)
                 cols[0, pl.ds(row, 16), :] = functools.reduce(
@@ -659,13 +669,21 @@
                 for lane in range(0, wide, 128):
                     piece = grad[pl.ds(row, 16), lane : lane + 128]
                     curve = jnp.tanh(piece * steep)
-                    next_in_ref[pl.ds(place, 16), lane : lane + 128] = piece - size * curve
+                    turned[
+                        pl.ds(lane // 256 * HID_ROWS + place, 16), lane % 256 : lane % 256 + 128
+                    ] = piece - size * curve
                     own_in[
                         2 * chunk + lane // 256, pl.ds(inside, 16), lane % 256 : lane % 256 + 128
                     ] = to_codes(curve * TOP_CODE)
                 return carry
 
             lax.fori_loop(0, 16, some, 0)
+        for top in range(0, wide, 128):
+            count = min(128, deep - top)
+            for left in range(0, HID_ROWS, 128):
+                place, lane = top // 256 * HID_ROWS + left, top % 256
+                tile = jnp.transpose(turned[place : place + 128, lane : lane + 128])
+                next_in_ref[top : top + count, left : left + 128] = tile[0:count, :]
         sizes[IN_GROUP, here] = jnp.concatenate(
             [lane_codes(64 * chunk) for chunk in range(RING)], axis=0
         )
@@ -936,7 +954,7 @@
         functools.partial(reduce_kernel, deep, senones),
         out_shape=(
             jax.ShapeDtypeStruct((wide, HID_ROWS), F32),
-            jax.ShapeDtypeStruct((HID_ROWS, in_wide), F32),
+            jax.ShapeDtypeStruct(res_in.shape, F32),
             jax.ShapeDtypeStruct((OUT_GROUPS * OUT_ROWS, 256), F32),
             jax.ShapeDtypeStruct((HID_ROWS, 256), F32),
             jax.ShapeDtypeStruct((in_wide, HID_ROWS), F32),
@@ -1011,12 +1029,12 @@
 def forward_kernel(
     slot_count,
     x_ref,
-    tags_ref,
+    labels_ref,
+    mask_ref,
     w_in_ref,
     w_hid_ref,
     w_out_ref,
     bias_ref,
-    bias_out_ref,
     mom_ref,
     x_out,
     h_one_out,
@@ -1037,6 +1055,7 @@
     w_hid,
     w_out,
     curve,
+    bias_line,
     bias_col,
     tags,
     sums,
@@ -1078,7 +1097,11 @@
     own_frames = pl.ds(pl.multiple_of(col * own_rows, own_rows), own_rows)
     x_all[own_frames, :] = jnp.zeros((own_rows, x_all.shape[1]), BF16)
     x_all[own_frames, 0:deep] = x_ref[...]
-    tags[col] = tags_ref[...]
+    own_tags = jnp.where(mask_ref[...] > 0, labels_ref[...], -1)
+    own_tags = jnp.concatenate([own_tags[row : row + 1, :] for row in range(own_tags.shape[0])], axis=1)
+    tags[col] = jnp.broadcast_to(own_tags, (8, own_rows))
+    bias_line[...] = jnp.zeros_like(bias_line)
+    bias_line[:, 0 : bias_ref.shape[1]] = bias_ref[...]
     sums[...] = jnp.zeros_like(sums)
     pl.semaphore_wait(barrier, 5)
 
@@ -1164,8 +1187,9 @@
         copy.start()
     w_in[...] = jnp.zeros_like(w_in)
     w_in[0:deep, :] = w_in_ref[...].astype(BF16)
-    for number in range(bias_out_ref.shape[0]):
-        line = jnp.broadcast_to(bias_out_ref[number : number + 1, :], (128, 128))
+    for number in range(bias_col.shape[0] // 128):
+        first = 2 * units + number * 128
+        line = jnp.broadcast_to(bias_line[:, first : first + 128], (128, 128))
         bias_col[number * 128 : (number + 1) * 128, :] = jnp.transpose(line)
     ring_wave(1)
     x_move(1).wait_recv()
@@ -1176,7 +1200,8 @@
     def layer(number, block, inputs, weights, whole, slopes):
         there = slice(block * own_rows, (block + 1) * own_rows)
         value = jax.nn.sigmoid(
-            dot_nn(inputs[there, :], weights[...]) + bias_ref[number : number + 1, :]
+            dot_nn(inputs[there, :], weights[...])
+            + bias_line[:, number * units : (number + 1) * units]
         )
         slopes[there, :] = value * (1.0 - value)
         whole[there, lanes_of(col)] = value.astype(BF16)
@@ -1315,7 +1340,7 @@
         lax.fori_loop(0, OUT_ROWS // 16, gradient, 0)
     vec_ref[...] = jnp.zeros_like(vec_ref)
     row = 2 * units // 128
-    for number in range(bias_out_ref.shape[0]):
+    for number in range(bias_col.shape[0] // 128):
         line = jnp.transpose(bias_col[number * 128 : (number + 1) * 128, :])
         line = jnp.sum(line, axis=0, keepdims=True)
         place = 128 * number + lax.broadcasted_iota(jnp.int32, line.shape, 1)
@@ -1338,13 +1363,13 @@
         copy.wait()
 
 
-def forward_pass(x, tags, w_in, w_hid, w_out, bias, bias_out, mom, slot_count):
+def forward_pass(x, labels, mask, w_in, w_hid, w_out, bias, mom, slot_count):
     own_rows = x.shape[0]
     units = w_hid.shape[1]
     frames = 4 * own_rows
     wide = 4 * units
     rows = OUT_GROUPS * OUT_ROWS
-    blocks = bias_out.shape[0]
+    blocks = -(-rows // 128)
     vmem = pl.BlockSpec(memory_space=pltpu.VMEM)
     hbm = pl.BlockSpec(memory_space=pl.ANY)
     sem = pltpu.SemaphoreType.DMA
@@ -1373,8 +1398,9 @@
             pltpu.VMEM((wide, units), BF16),
             pltpu.VMEM((rows, wide), BF16),
             pltpu.VMEM((rows, frames), F32),
+            pltpu.VMEM((1, 2 * units + blocks * 128), F32),
             pltpu.VMEM((blocks * 128, 128), F32),
-            pltpu.VMEM((4,) + tags.shape, jnp.int32),
+            pltpu.VMEM((4, 8, own_rows), jnp.int32),
             pltpu.VMEM((4, 16, frames), F32),
             sem((5, 2, STEPS)),
             sem((5, 2, STEPS)),
@@ -1392,7 +1418,7 @@
         compiler_params=pltpu.CompilerParams(
             collective_id=2, has_side_effects=True, vmem_limit_bytes=60 * 1024 * 1024
         ),
-    )(x, tags, w_in, w_hid, w_out, bias, bias_out, mom)
+    )(x, labels, mask, w_in, w_hid, w_out, bias, mom)
 
 
 DIM_BITS = (2, 4, 8)
@@ -1920,6 +1946,84 @@
     )(stats, red_hid, mom_hid, red_in, mom_in, red_far, mom_far)
 
 
+def finish_kernel(
+    scale,
+    red_ref,
+    w_out_ref,
+    first_ref,
+    second_ref,
+    norm_ref,
+    hid_ref,
+    w_hid_ref,
+    inp_ref,
+    w_in_ref,
+    res_hid_ref,
+    res_in_ref,
+    mom_hid_ref,
+    mom_in_ref,
+    new_out_ref,
+    next_first_ref,
+    next_second_ref,
+    new_hid_ref,
+    new_in_ref,
+    next_res_hid_ref,
+    next_res_in_ref,
+    next_mom_hid_ref,
+    next_mom_in_ref,
+    sems,
+):
+    step = pl.program_id(0)
+    pairs = (
+        (res_hid_ref, next_res_hid_ref),
+        (res_in_ref, next_res_in_ref),
+        (mom_hid_ref, next_mom_hid_ref),
+        (mom_in_ref, next_mom_in_ref),
+    )
+    copies = [
+        pltpu.make_async_copy(src, dst, sems.at[number]) for number, (src, dst) in enumerate(pairs)
+    ]
+
+    @pl.when(step == 0)
+    def _():
+        for copy in copies:
+            copy.start()
+        new_hid_ref[...] = w_hid_ref[...] * (1.0 - LR_MUON * WD_MUON) - scale * hid_ref[...]
+        new_in_ref[...] = w_in_ref[...] * (1.0 - LR_MUON * WD_MUON) - scale * inp_ref[...]
+
+    new_out_ref[...], next_first_ref[...], next_second_ref[...] = adam_step(
+        w_out_ref[...], norm_ref[4:5, 0:1] * red_ref[...], first_ref[...], second_ref[...]
+    )
+
+    @pl.when(step == pl.num_programs(0) - 1)
+    def _():
+        for copy in copies:
+            copy.wait()
+
+
+def finish(red, w_out, first, second, norms, hid, w_hid, inp, w_in, kept, scale):
+    senones, depth = w_out.shape
+    rows = OUT_ROWS // 2
+    streamed = pl.BlockSpec((rows, depth), lambda step: (step, 0))
+    hbm = pl.BlockSpec(memory_space=pl.ANY)
+
+    def whole(array):
+        return pl.BlockSpec(array.shape, lambda step: (0, 0))
+
+    small = (norms, hid, w_hid, inp, w_in)
+    return pl.pallas_call(
+        functools.partial(finish_kernel, scale),
+        grid=(2 * OUT_GROUPS,),
+        out_shape=tuple(
+            jax.ShapeDtypeStruct(array.shape, F32)
+            for array in (w_out, w_out, w_out, w_hid, w_in, *kept)
+        ),
+        in_specs=[streamed] * 4 + [whole(array) for array in small] + [hbm] * 4,
+        out_specs=(streamed,) * 3 + (whole(w_hid), whole(w_in)) + (hbm,) * 4,
+        scratch_shapes=[pltpu.SemaphoreType.DMA((4,))],
+        compiler_params=pltpu.CompilerParams(vmem_limit_bytes=40 * 1024 * 1024),
+    )(red, w_out, first, second, *small, *kept)
+
+
 def plain_body(
     frames,
     labels,
@@ -2094,21 +2198,16 @@
     slot_count = frames.shape[1] * micro * nblk * ncol
     bias_row = biases[0]
     deep = w_input.shape[0]
-    padded = 512
     rows_out = OUT_GROUPS * OUT_ROWS
-    own_tags = jnp.where(mask > 0, labels, -1).reshape(1, -1)
-    layer_biases = jnp.pad(bias_row[: 2 * hcol].reshape(2, hcol), ((0, 6), (0, 0)))
-    blocks = -(-rows_out // 128)
-    out_biases = jnp.pad(bias_row[2 * hcol :], (0, blocks * 128 - scol)).reshape(blocks, 128)
     inputs, h_one, h_two, slope_one, slope_two, low_hidden, low_output, mom_far, d_logits, vec = (
         forward_pass(
             frames.reshape(-1, deep),
-            jnp.broadcast_to(own_tags, (8, own_tags.shape[1])),
+            labels,
+            mask,
             w_input,
             w_hidden,
             w_output.T,
-            layer_biases,
-            out_biases,
+            biases,
             mom_input,
             slot_count,
         )
@@ -2125,19 +2224,16 @@
         slope_one,
         low_hidden,
         res_hidden[0],
-        jnp.pad(res_input[0], ((0, padded - deep), (0, 0))).T,
+        res_input[0],
         vec,
         scol,
         deep,
     )
     next_res_output = next_out.transpose(1, 2, 0)
-    next_res_hidden = next_hid
-    next_res_input = next_in[:, :deep].T
-    red_output = red_out[:scol].T
     vec_sum = vec_sum.reshape(-1)
     red_bias = vec_sum[: bias_row.shape[0]]
     loss_sum = vec_sum[bias_row.shape[0]]
-    done_hidden, done_input, next_mom_hidden, next_mom_input, norms = muon(
+    done_hidden, done_input, mom_hid_next, mom_in_next, norms = muon(
         stats,
         red_hid,
         mom_hidden,
@@ -2150,10 +2246,28 @@
     clip_norm = norms[0, 0]
     factor = norms[4, 0]
     muon_scale = LR_MUON * 0.2 * math.sqrt(hcol * ncol)
-    new_input = w_input * (1.0 - LR_MUON * WD_MUON) - muon_scale * done_input
-    new_hidden = w_hidden * (1.0 - LR_MUON * WD_MUON) - muon_scale * done_hidden
-    new_output, next_out_first, next_out_second = adam_step(
-        w_output, factor * red_output, out_first, out_second
+    (
+        new_output,
+        next_out_first,
+        next_out_second,
+        new_hidden,
+        new_input,
+        next_res_hidden,
+        next_res_input,
+        next_mom_hidden,
+        next_mom_input,
+    ) = finish(
+        red_out,
+        w_output.T,
+        out_first.T,
+        out_second.T,
+        norms,
+        done_hidden,
+        w_hidden,
+        done_input,
+        w_input,
+        (next_hid, next_in, mom_hid_next, mom_in_next),
+        muon_scale,
     )
     new_biases, next_bias_first, next_bias_second = adam_step(
         biases, factor * red_bias[None, :], bias_first, bias_second
@@ -2163,12 +2277,12 @@
         clip_norm,
         new_input,
         new_hidden,
-        new_output,
+        new_output.T,
         new_biases,
         next_mom_input,
         next_mom_hidden,
-        next_out_first,
-        next_out_second,
+        next_out_first.T,
+        next_out_second.T,
         next_bias_first,
         next_bias_second,
         next_res_input[None],

time: 634 us -> 749 us (1.18)
  Pallas kernels: 581 us -> 711 us
  other arithmetic: 15.1 us -> 1.35 us
    pallas_call x0 -> x1, Pallas kernels: none -> 131 us  [finish(): pl.pallas_call(functools.partial(finish_kernel, scale), grid=(2 * OUT_GRO...]
    sub x2 -> x1, other arithmetic: 9.54 us -> 0.7 us  [adam_step(): return (weight - LR_ADAM * (update + WD_ADAM * weight), first, second)]
where the time goes in v11:
time: 749 us; the launch traced here: 743 us
  Pallas kernels  711 us (95%)
  matrix products  17.5 us (2%)
  local copies, waits for them, and re-layouts  12.4 us (2%)
    pallas_call x1, Pallas kernels, muon(): pl.pallas_call(muon_kernel, out_shape=(jax.ShapeDtypeStruct(mom_hid.shape...  241 us
    pallas_call x1, Pallas kernels, reduce_grads(): pl.pallas_call(functools.partial(reduce_kernel, deep, senones), out_shape...  163 us
    pallas_call x1, Pallas kernels, forward_pass(): pl.pallas_call(functools.partial(forward_kernel, slot_count), out_shape=t...  143 us
    pallas_call x1, Pallas kernels, finish(): pl.pallas_call(functools.partial(finish_kernel, scale), grid=(2 * OUT_GRO...  131 us
    pallas_call x1, Pallas kernels, squash_out(): pl.pallas_call(functools.partial(squash_kernel, senones), grid=(OUT_GROUP...  34.2 us
    dot_general x1, matrix products, inner_rows(): lax.dot_general(left_side, right_side, (((0,), (0,)), ((), ())), preferre...  17.5 us

profile of v11, /device:TPU:0, one launch (start us, length us, event | category | flops | bytes accessed | tf_op | source)
XLA Modules:
  0.0 743.1 jit_solution(10663379142605492499)
XLA Ops:
  0.6 142.8 %shard_map.271 = (bf16[1024,512]{1,0:T(8,128)(2,1)}, bf16[1024,2048]{1,0:T(8,128)(2,1)}, bf16[1024,2048]{1,0:T(8,128)(2,1)}, f32[1024,512]{1,0:T(8,128)}, f32[10...) custom-call(bf16[256,440]{1,0:T(8,128)(2,1)} %bitcast.28, ...), custom_call_target="tpu_custom_call" | custom-call | tf_op jit(solution)/shard_map/pallas_call | solution.py:1385
  143.4 17.5 %fusion.1.part_ref = f32[1024,2048]{1,0:T(8,128)} fusion(bf16[2368,1024]{1,0:T(8,128)(2,1)} %get-tuple-element.50.dl_ref, bf16[2368,2048]{1,0:T(8,128)(2,1)} %get-tuple-element.56), kind=kOutput, calls=%fused_computation.7 | convolution fusion | flops 9932111872 | bytes 22937600 | tf_op jit(solution)/shard_map/dot_general | solution.py:38
  160.9 34.2 %shard_map.272 = (f32[2326,1,2048]{2,1,0:T(1,128)}, s16[4,16,592,128]{3,2,1,0:T(8,128)(2,1)}, f32[4,8,128]{2,1,0:T(8,128)}) custom-call(bf16[2368,1024]{1,0:T(8,128)(2,1)} %get-tuple-element.50.dl_ref, bf16[1024,2048]{1,0:T(8,128)(2,1)} %get-tuple-element.51.h_ref, bf16[2326,2048]{1,0:T(8,128)(2,1)} %bitcast.25), custom_call_target="tpu_custom_call" | custom-call | tf_op jit(solution)/shard_map/pallas_call | solution.py:189
  195.1 162.9 %shard_map.273 = (f32[2048,512]{1,0:T(8,128)}, f32[440,512]{1,0:T(8,128)}, f32[2368,256]{1,0:T(8,128)}, f32[512,256]{1,0:T(8,128)}, f32[512,512]{1,0:T(8,128)}, ...) custom-call(s16[4,16,592,128]{3,2,1,0:T(8,128)(2,1)} %get-tuple-element.52.codes_ref, ...), custom_call_target="tpu_custom_call" | custom-call | tf_op jit(solution)/shard_map/pallas_call | solution.py:953
  358.0 0.0 copy-start.11
  358.0 0.0 copy-start.13
  358.0 0.0 copy-start.14
  358.1 0.0 copy-start
  358.1 0.0 copy-start.4
  358.1 1.4 slice.16
  359.5 240.5 %shard_map.274 = (f32[256,512]{1,0:T(8,128)}, f32[440,512]{1,0:T(8,128)}, f32[256,512]{1,0:T(8,128)}, f32[440,512]{1,0:T(8,128)}, f32[8,128]{1,0:T(8,128)}) custom-call(f32[8,128]{1,0:T(8,128)} %get-tuple-element.62.stats_ref, f32[512,256]{1,0:T(8,128)} %get-tuple-element.63.red_hid_ref, f32[256,512]{1,0:T(8,128)} %mom_hid_ref.1, ...), custom_call_target="tpu_custom_call" | custom-call | tf_op jit(solution)/shard_map/pallas_call | solution.py:1897
  600.0 1.3 fusion
  601.3 0.7 multiply_multiply_fusion
  602.0 0.7 multiply_subtract_fusion
  602.7 0.0 copy-start.2
  602.7 1.7 copy-done.2
  604.4 1.7 copy-done.3
  606.1 1.2 copy-done.5
  607.2 1.2 copy-done.6
  608.4 1.2 copy-done.7
  609.6 1.0 copy-done.8
  610.6 1.0 copy-done.9
  611.7 0.7 copy-done.10
  612.4 130.5 %shard_map.275 = (f32[2326,256]{1,0:T(8,128)}, f32[2326,256]{1,0:T(8,128)}, f32[2326,256]{1,0:T(8,128)}, f32[256,512]{1,0:T(8,128)}, f32[440,512]{1,0:T(8,128)},...) custom-call(f32[2368,256]{1,0:T(8,128)} %get-tuple-element.68.red_ref, ...), custom_call_target="tpu_custom_call" | custom-call | tf_op jit(solution)/shard_map/pallas_call | solution.py:2013
  (16 shorter events, 0.0 us)
Async XLA Ops:
  358.0 243.3 %copy-start.12 = (f32[32,128]{1,0:T(8,128)S(1)}, f32[32,128]{1,0:T(8,128)}, u32[]{:S(2)}) copy-start(f32[32,128]{1,0:T(8,128)} %get-tuple-element.61) | copy-start | bytes 49156
  358.0 244.0 %copy-start.11 = (f32[1,3350]{1,0:T(1,128)S(1)}, f32[1,3350]{1,0:T(1,128)}, u32[]{:S(2)}) copy-start(f32[1,3350]{1,0:T(1,128)} %bias_ref.1) | copy-start | bytes 40204
  358.0 244.0 %copy-start.13 = (f32[1,3350]{1,0:T(1,128)S(1)}, f32[1,3350]{1,0:T(1,128)}, u32[]{:S(2)}) copy-start(f32[1,3350]{1,0:T(1,128)} %param.27) | copy-start | bytes 40204
  358.0 244.0 %copy-start.14 = (f32[1,3350]{1,0:T(1,128)S(1)}, f32[1,3350]{1,0:T(1,128)}, u32[]{:S(2)}) copy-start(f32[1,3350]{1,0:T(1,128)} %param.28) | copy-start | bytes 40204
  358.1 244.7 %copy-start = (f32[256,2326]{0,1:T(8,128)S(1)}, f32[256,2326]{0,1:T(8,128)}, u32[]{:S(2)}) copy-start(f32[256,2326]{0,1:T(8,128)} %param.21) | copy-start | bytes 7145476
  358.1 244.6 %copy-start.1 = (f32[440,512]{1,0:T(8,128)S(1)}, f32[440,512]{1,0:T(8,128)}, u32[]{:S(2)}) copy-start(f32[440,512]{1,0:T(8,128)} %w_in_ref.3) | copy-start | bytes 2703364
  358.1 244.6 %copy-start.4 = (f32[256,512]{1,0:T(8,128)S(1)}, f32[256,512]{1,0:T(8,128)}, u32[]{:S(2)}) copy-start(f32[256,512]{1,0:T(8,128)} %w_hid_ref.3) | copy-start | bytes 1572868
  602.7 1.7 copy-start.2
  604.4 1.7 copy-start.3
  606.1 1.2 copy-start.5
  607.2 1.2 copy-start.6
  608.4 1.2 copy-start.7
  609.6 1.0 copy-start.8
  610.6 1.0 copy-start.9
  611.7 0.7 copy-start.10

commit v12 on v9

--- a/solution.py
+++ b/solution.py
@@ -628,13 +628,23 @@
     def in_group():
         wide = x_ref.shape[1]
         load(x_ref, h_buf.at[:, pl.ds(0, wide)]).wait()
+        for top in range(0, wide, 128):
+            count = min(128, deep - top)
+            for left in range(0, HID_ROWS, 128):
+                tile = res_in_ref[top : top + count, left : left + 128].astype(F32)
+                if count < 128:
+                    tile = jnp.concatenate([tile, jnp.zeros((128 - count, 128), F32)], axis=0)
+                place, lane = top // 256 * HID_ROWS + left, top % 256
+                turned[place : place + 128, lane : lane + 128] = jnp.transpose(tile)
         for first in range(0, HID_ROWS, 256):
             grad[0:256, 0:wide] = dot_nn(dz_one[first : first + 256, :], h_buf[:, 0:wide])
 
             def add(number, carry, first=first):
                 row = pl.multiple_of(number * 16, 16)
                 place = pl.multiple_of(first + row, 16)
-                value = grad[pl.ds(row, 16), 0:wide] + res_in_ref[pl.ds(place, 16), :].astype(F32)
+                value = grad[pl.ds(row, 16), 0:wide] + jnp.concatenate(
+                    [turned[pl.ds(place, 16), :], turned[pl.ds(HID_ROWS + place, 16), :]], axis=1
+                )
                 grad[pl.ds(row, 16), 0:wide] = value
                 value = jnp.abs(value)
                 cols[0, pl.ds(row, 16), :] = functools.reduce(
@@ -659,13 +669,21 @@
                 for lane in range(0, wide, 128):
                     piece = grad[pl.ds(row, 16), lane : lane + 128]
                     curve = jnp.tanh(piece * steep)
-                    next_in_ref[pl.ds(place, 16), lane : lane + 128] = piece - size * curve
+                    turned[
+                        pl.ds(lane // 256 * HID_ROWS + place, 16), lane % 256 : lane % 256 + 128
+                    ] = piece - size * curve
                     own_in[
                         2 * chunk + lane // 256, pl.ds(inside, 16), lane % 256 : lane % 256 + 128
                     ] = to_codes(curve * TOP_CODE)
                 return carry
 
             lax.fori_loop(0, 16, some, 0)
+        for top in range(0, wide, 128):
+            count = min(128, deep - top)
+            for left in range(0, HID_ROWS, 128):
+                place, lane = top // 256 * HID_ROWS + left, top % 256
+                tile = jnp.transpose(turned[place : place + 128, lane : lane + 128])
+                next_in_ref[top : top + count, left : left + 128] = tile[0:count, :]
         sizes[IN_GROUP, here] = jnp.concatenate(
             [lane_codes(64 * chunk) for chunk in range(RING)], axis=0
         )
@@ -936,7 +954,7 @@
         functools.partial(reduce_kernel, deep, senones),
         out_shape=(
             jax.ShapeDtypeStruct((wide, HID_ROWS), F32),
-            jax.ShapeDtypeStruct((HID_ROWS, in_wide), F32),
+            jax.ShapeDtypeStruct(res_in.shape, F32),
             jax.ShapeDtypeStruct((OUT_GROUPS * OUT_ROWS, 256), F32),
             jax.ShapeDtypeStruct((HID_ROWS, 256), F32),
             jax.ShapeDtypeStruct((in_wide, HID_ROWS), F32),
@@ -1011,12 +1029,12 @@
 def forward_kernel(
     slot_count,
     x_ref,
-    tags_ref,
+    labels_ref,
+    mask_ref,
     w_in_ref,
     w_hid_ref,
     w_out_ref,
     bias_ref,
-    bias_out_ref,
     mom_ref,
     x_out,
     h_one_out,
@@ -1037,6 +1055,7 @@
     w_hid,
     w_out,
     curve,
+    bias_line,
     bias_col,
     tags,
     sums,
@@ -1078,7 +1097,11 @@
     own_frames = pl.ds(pl.multiple_of(col * own_rows, own_rows), own_rows)
     x_all[own_frames, :] = jnp.zeros((own_rows, x_all.shape[1]), BF16)
     x_all[own_frames, 0:deep] = x_ref[...]
-    tags[col] = tags_ref[...]
+    own_tags = jnp.where(mask_ref[...] > 0, labels_ref[...], -1)
+    own_tags = jnp.concatenate([own_tags[row : row + 1, :] for row in range(own_tags.shape[0])], axis=1)
+    tags[col] = jnp.broadcast_to(own_tags, (8, own_rows))
+    bias_line[...] = jnp.zeros_like(bias_line)
+    bias_line[:, 0 : bias_ref.shape[1]] = bias_ref[...]
     sums[...] = jnp.zeros_like(sums)
     pl.semaphore_wait(barrier, 5)
 
@@ -1164,8 +1187,9 @@
         copy.start()
     w_in[...] = jnp.zeros_like(w_in)
     w_in[0:deep, :] = w_in_ref[...].astype(BF16)
-    for number in range(bias_out_ref.shape[0]):
-        line = jnp.broadcast_to(bias_out_ref[number : number + 1, :], (128, 128))
+    for number in range(bias_col.shape[0] // 128):
+        first = 2 * units + number * 128
+        line = jnp.broadcast_to(bias_line[:, first : first + 128], (128, 128))
         bias_col[number * 128 : (number + 1) * 128, :] = jnp.transpose(line)
     ring_wave(1)
     x_move(1).wait_recv()
@@ -1176,7 +1200,8 @@
     def layer(number, block, inputs, weights, whole, slopes):
         there = slice(block * own_rows, (block + 1) * own_rows)
         value = jax.nn.sigmoid(
-            dot_nn(inputs[there, :], weights[...]) + bias_ref[number : number + 1, :]
+            dot_nn(inputs[there, :], weights[...])
+            + bias_line[:, number * units : (number + 1) * units]
         )
         slopes[there, :] = value * (1.0 - value)
         whole[there, lanes_of(col)] = value.astype(BF16)
@@ -1315,7 +1340,7 @@
         lax.fori_loop(0, OUT_ROWS // 16, gradient, 0)
     vec_ref[...] = jnp.zeros_like(vec_ref)
     row = 2 * units // 128
-    for number in range(bias_out_ref.shape[0]):
+    for number in range(bias_col.shape[0] // 128):
         line = jnp.transpose(bias_col[number * 128 : (number + 1) * 128, :])
         line = jnp.sum(line, axis=0, keepdims=True)
         place = 128 * number + lax.broadcasted_iota(jnp.int32, line.shape, 1)
@@ -1338,13 +1363,13 @@
         copy.wait()
 
 
-def forward_pass(x, tags, w_in, w_hid, w_out, bias, bias_out, mom, slot_count):
+def forward_pass(x, labels, mask, w_in, w_hid, w_out, bias, mom, slot_count):
     own_rows = x.shape[0]
     units = w_hid.shape[1]
     frames = 4 * own_rows
     wide = 4 * units
     rows = OUT_GROUPS * OUT_ROWS
-    blocks = bias_out.shape[0]
+    blocks = -(-rows // 128)
     vmem = pl.BlockSpec(memory_space=pltpu.VMEM)
     hbm = pl.BlockSpec(memory_space=pl.ANY)
     sem = pltpu.SemaphoreType.DMA
@@ -1373,8 +1398,9 @@
             pltpu.VMEM((wide, units), BF16),
             pltpu.VMEM((rows, wide), BF16),
             pltpu.VMEM((rows, frames), F32),
+            pltpu.VMEM((1, 2 * units + blocks * 128), F32),
             pltpu.VMEM((blocks * 128, 128), F32),
-            pltpu.VMEM((4,) + tags.shape, jnp.int32),
+            pltpu.VMEM((4, 8, own_rows), jnp.int32),
             pltpu.VMEM((4, 16, frames), F32),
             sem((5, 2, STEPS)),
             sem((5, 2, STEPS)),
@@ -1392,7 +1418,7 @@
         compiler_params=pltpu.CompilerParams(
             collective_id=2, has_side_effects=True, vmem_limit_bytes=60 * 1024 * 1024
         ),
-    )(x, tags, w_in, w_hid, w_out, bias, bias_out, mom)
+    )(x, labels, mask, w_in, w_hid, w_out, bias, mom)
 
 
 DIM_BITS = (2, 4, 8)
@@ -2094,21 +2120,16 @@
     slot_count = frames.shape[1] * micro * nblk * ncol
     bias_row = biases[0]
     deep = w_input.shape[0]
-    padded = 512
     rows_out = OUT_GROUPS * OUT_ROWS
-    own_tags = jnp.where(mask > 0, labels, -1).reshape(1, -1)
-    layer_biases = jnp.pad(bias_row[: 2 * hcol].reshape(2, hcol), ((0, 6), (0, 0)))
-    blocks = -(-rows_out // 128)
-    out_biases = jnp.pad(bias_row[2 * hcol :], (0, blocks * 128 - scol)).reshape(blocks, 128)
     inputs, h_one, h_two, slope_one, slope_two, low_hidden, low_output, mom_far, d_logits, vec = (
         forward_pass(
             frames.reshape(-1, deep),
-            jnp.broadcast_to(own_tags, (8, own_tags.shape[1])),
+            labels,
+            mask,
             w_input,
             w_hidden,
             w_output.T,
-            layer_biases,
-            out_biases,
+            biases,
             mom_input,
             slot_count,
         )
@@ -2125,15 +2146,12 @@
         slope_one,
         low_hidden,
         res_hidden[0],
-        jnp.pad(res_input[0], ((0, padded - deep), (0, 0))).T,
+        res_input[0],
         vec,
         scol,
         deep,
     )
     next_res_output = next_out.transpose(1, 2, 0)
-    next_res_hidden = next_hid
-    next_res_input = next_in[:, :deep].T
-    red_output = red_out[:scol].T
     vec_sum = vec_sum.reshape(-1)
     red_bias = vec_sum[: bias_row.shape[0]]
     loss_sum = vec_sum[bias_row.shape[0]]
@@ -2153,7 +2171,7 @@
     new_input = w_input * (1.0 - LR_MUON * WD_MUON) - muon_scale * done_input
     new_hidden = w_hidden * (1.0 - LR_MUON * WD_MUON) - muon_scale * done_hidden
     new_output, next_out_first, next_out_second = adam_step(
-        w_output, factor * red_output, out_first, out_second
+        w_output, factor * red_out[:scol].T, out_first, out_second
     )
     new_biases, next_bias_first, next_bias_second = adam_step(
         biases, factor * red_bias[None, :], bias_first, bias_second
@@ -2171,8 +2189,8 @@
         next_out_second,
         next_bias_first,
         next_bias_second,
-        next_res_input[None],
-        next_res_hidden[None],
+        next_in[None],
+        next_hid[None],
         next_res_output,
     )
 

time: 634 us -> 626 us (0.987)
  local copies, waits for them, and re-layouts: 14.3 us -> 7.46 us
where the time goes in v12:
time: 626 us; the launch traced here: 621 us
  Pallas kernels  581 us (93%)
  matrix products  17.5 us (3%)
  other arithmetic  14 us (2%)
  local copies, waits for them, and re-layouts  7.46 us (1%)
    pallas_call x1, Pallas kernels, muon(): pl.pallas_call(muon_kernel, out_shape=(jax.ShapeDtypeStruct(mom_hid.shape...  241 us
    pallas_call x1, Pallas kernels, reduce_grads(): pl.pallas_call(functools.partial(reduce_kernel, deep, senones), out_shape...  163 us
    pallas_call x1, Pallas kernels, forward_pass(): pl.pallas_call(functools.partial(forward_kernel, slot_count), out_shape=t...  143 us
    pallas_call x1, Pallas kernels, squash_out(): pl.pallas_call(functools.partial(squash_kernel, senones), grid=(OUT_GROUP...  34.1 us
    dot_general x1, matrix products, inner_rows(): lax.dot_general(left_side, right_side, (((0,), (0,)), ((), ())), preferre...  17.5 us

profile of v12, /device:TPU:0, one launch (start us, length us, event | category | flops | bytes accessed | tf_op | source)
XLA Modules:
  0.0 620.8 jit_solution(12958463106492662370)
XLA Ops:
  0.6 142.8 %shard_map.271 = (bf16[1024,512]{1,0:T(8,128)(2,1)}, bf16[1024,2048]{1,0:T(8,128)(2,1)}, bf16[1024,2048]{1,0:T(8,128)(2,1)}, f32[1024,512]{1,0:T(8,128)}, f32[10...) custom-call(bf16[256,440]{1,0:T(8,128)(2,1)} %bitcast.30, ...), custom_call_target="tpu_custom_call" | custom-call | tf_op jit(solution)/shard_map/pallas_call | solution.py:1385
  143.4 17.5 %fusion.3.part_ref = f32[1024,2048]{1,0:T(8,128)} fusion(bf16[2368,1024]{1,0:T(8,128)(2,1)} %get-tuple-element.41.dl_ref, bf16[2368,2048]{1,0:T(8,128)(2,1)} %get-tuple-element.47), kind=kOutput, calls=%fused_computation.15 | convolution fusion | flops 9932111872 | bytes 22937600 | tf_op jit(solution)/shard_map/dot_general | solution.py:38
  160.9 34.1 %shard_map.272 = (f32[2326,1,2048]{2,1,0:T(1,128)}, s16[4,16,592,128]{3,2,1,0:T(8,128)(2,1)}, f32[4,8,128]{2,1,0:T(8,128)}) custom-call(bf16[2368,1024]{1,0:T(8,128)(2,1)} %get-tuple-element.41.dl_ref, bf16[1024,2048]{1,0:T(8,128)(2,1)} %get-tuple-element.42.h_ref, bf16[2326,2048]{1,0:T(8,128)(2,1)} %bitcast.24), custom_call_target="tpu_custom_call" | custom-call | tf_op jit(solution)/shard_map/pallas_call | solution.py:189
  195.0 163.1 %shard_map.273 = (f32[2048,512]{1,0:T(8,128)}, f32[440,512]{1,0:T(8,128)}, f32[2368,256]{1,0:T(8,128)}, f32[512,256]{1,0:T(8,128)}, f32[512,512]{1,0:T(8,128)}, ...) custom-call(s16[4,16,592,128]{3,2,1,0:T(8,128)(2,1)} %get-tuple-element.43.codes_ref, ...), custom_call_target="tpu_custom_call" | custom-call | tf_op jit(solution)/shard_map/pallas_call | solution.py:953
  358.1 1.3 slice.20
  359.4 0.0 copy-start.4
  359.4 0.0 copy-start.2
  359.4 0.0 copy-start.3
  359.4 240.9 %shard_map.274 = (f32[256,512]{1,0:T(8,128)}, f32[440,512]{1,0:T(8,128)}, f32[256,512]{1,0:T(8,128)}, f32[440,512]{1,0:T(8,128)}, f32[8,128]{1,0:T(8,128)}) custom-call(f32[8,128]{1,0:T(8,128)} %get-tuple-element.53.stats_ref, f32[512,256]{1,0:T(8,128)} %get-tuple-element.54.red_hid_ref, f32[256,512]{1,0:T(8,128)} %mom_hid_ref.1, ...), custom_call_target="tpu_custom_call" | custom-call | tf_op jit(solution)/shard_map/pallas_call | solution.py:1897
  600.3 0.0 copy-start
  600.3 1.4 fusion.2
  601.7 0.0 copy-done.9
  601.7 0.7 multiply_multiply_fusion.1
  602.3 0.0 copy-done.8
  602.3 0.0 copy-done.10
  602.4 0.7 multiply_subtract_fusion.3
  603.1 1.9 multiply_subtract_fusion.2
  605.0 2.3 multiply_subtract_fusion.1
  607.3 8.5 %multiply_subtract_fusion = (f32[256,2326]{0,1:T(8,128)}, f32[256,2326]{0,1:T(8,128)}, f32[256,2326]{0,1:T(8,128)}) fusion(f32[256,2326]{0,1:T(8,128)S(1)} %copy-done, f32[256,2326]{0,1:T(8,128)S(1)} %copy-done.3, f32[2368,256]{1,0:T(8,128)} %get-tuple-element.61, f32[]{:T(128)} %bitcast.9, f32[256,2326]{0,1:T(8,128)} %param.26), kind=kLoop, calls=%fused_computation.3 | loop fusion | flops 8931840 | bytes 16672772 | tf_op jit(solution)/shard_map/sub | solution.py:78
  615.8 0.9 copy.35
  616.7 0.8 copy.36
  617.5 0.9 copy.37
  618.4 0.2 copy-done.1
  618.6 2.0 copy.38
  (16 shorter events, 0.0 us)
Async XLA Ops:
  359.4 242.3 %copy-start.9 = (f32[32,128]{1,0:T(8,128)S(1)}, f32[32,128]{1,0:T(8,128)}, u32[]{:S(2)}) copy-start(f32[32,128]{1,0:T(8,128)} %get-tuple-element.52) | copy-start | bytes 49156
  359.4 242.9 %copy-start.8 = (f32[1,3350]{1,0:T(1,128)S(1)}, f32[1,3350]{1,0:T(1,128)}, u32[]{:S(2)}) copy-start(f32[1,3350]{1,0:T(1,128)} %bias_ref.1) | copy-start | bytes 40204
  359.4 243.0 %copy-start.10 = (f32[1,3350]{1,0:T(1,128)S(1)}, f32[1,3350]{1,0:T(1,128)}, u32[]{:S(2)}) copy-start(f32[1,3350]{1,0:T(1,128)} %param.27) | copy-start | bytes 40204
  359.4 243.0 %copy-start.11 = (f32[1,3350]{1,0:T(1,128)S(1)}, f32[1,3350]{1,0:T(1,128)}, u32[]{:S(2)}) copy-start(f32[1,3350]{1,0:T(1,128)} %param.28) | copy-start | bytes 40204
  359.4 243.7 %copy-start.4 = (f32[256,512]{1,0:T(8,128)S(1)}, f32[256,512]{1,0:T(8,128)}, u32[]{:S(2)}) copy-start(f32[256,512]{1,0:T(8,128)} %w_hid_ref.1) | copy-start | bytes 1572868
  359.4 245.6 %copy-start.2 = (f32[440,512]{1,0:T(8,128)S(1)}, f32[440,512]{1,0:T(8,128)}, u32[]{:S(2)}) copy-start(f32[440,512]{1,0:T(8,128)} %w_in_ref.1) | copy-start | bytes 2703364
  359.4 247.9 %copy-start.3 = (f32[256,2326]{0,1:T(8,128)S(1)}, f32[256,2326]{0,1:T(8,128)}, u32[]{:S(2)}) copy-start(f32[256,2326]{0,1:T(8,128)} %param.25) | copy-start | bytes 7145476
  600.3 7.0 %copy-start = (f32[256,2326]{0,1:T(8,128)S(1)}, f32[256,2326]{0,1:T(8,128)}, u32[]{:S(2)}) copy-start(f32[256,2326]{0,1:T(8,128)} %param.21) | copy-start | bytes 7145476
  607.3 8.5 %copy-start.6 = (f32[440,512]{1,0:T(8,128)S(1)}, f32[440,512]{1,0:T(8,128)}, u32[]{:S(2)}) copy-start(f32[440,512]{1,0:T(8,128)} %get-tuple-element.98) | copy-start | bytes 2703364
  607.3 9.4 %copy-start.7 = (f32[256,512]{1,0:T(8,128)S(1)}, f32[256,512]{1,0:T(8,128)}, u32[]{:S(2)}) copy-start(f32[256,512]{1,0:T(8,128)} %get-tuple-element.99) | copy-start | bytes 1572868
  607.3 10.2 %copy-start.5 = (f32[440,512]{1,0:T(8,128)S(1)}, f32[440,512]{1,0:T(8,128)}, u32[]{:S(2)}) copy-start(f32[440,512]{1,0:T(8,128)} %get-tuple-element.64) | copy-start | bytes 2703364
  615.8 2.8 copy-start.1

commit v13 on v12

--- a/solution.py
+++ b/solution.py
@@ -107,7 +107,7 @@
 HID_AT = 13
 FINISH_AT = 14
 IN_AT = 20
-HID_HOP = 3
+HID_HOP = 2
 
 
 def ring_place(blk):
@@ -861,7 +861,8 @@
         def _():
             make_shares(IN_GROUP, chunk_row)
 
-        in_step(number - IN_AT - 1)
+        index = 2 * (number - IN_AT - 1)
+        in_step(index)
         each(number, 0, 1, 4, lambda block: cross(0, block))
         each(number, TURN_AT, 2, 4, turn_block)
         each(number, CROSS_AT, 2, 4, lambda block: cross(1, block))
@@ -880,9 +881,10 @@
             for away in range(1, RING):
                 vec_copy(away).start()
 
+        in_step(index + 1)
         return carry
 
-    turns = max(IN_AT + 1 + 2 * STEPS, HID_AT + HID_HOP * STEPS + 1, OUT_GROUPS * STEPS)
+    turns = max(IN_AT + 1 + STEPS, HID_AT + HID_HOP * STEPS + 1, OUT_GROUPS * STEPS)
     lax.fori_loop(0, turns, turn, 0)
 
     def unfold(shares_of, out):

time: 626 us -> 629 us (level)
  no operation moved by 1% of the time
where the time goes in v13:
time: 629 us; the launch traced here: 624 us
  Pallas kernels  584 us (93%)
  matrix products  17.5 us (3%)
  other arithmetic  14 us (2%)
  local copies, waits for them, and re-layouts  7.46 us (1%)
    pallas_call x1, Pallas kernels, muon(): pl.pallas_call(muon_kernel, out_shape=(jax.ShapeDtypeStruct(mom_hid.shape...  240 us
    pallas_call x1, Pallas kernels, reduce_grads(): pl.pallas_call(functools.partial(reduce_kernel, deep, senones), out_shape...  167 us
    pallas_call x1, Pallas kernels, forward_pass(): pl.pallas_call(functools.partial(forward_kernel, slot_count), out_shape=t...  143 us
    pallas_call x1, Pallas kernels, squash_out(): pl.pallas_call(functools.partial(squash_kernel, senones), grid=(OUT_GROUP...  34.1 us
    dot_general x1, matrix products, inner_rows(): lax.dot_general(left_side, right_side, (((0,), (0,)), ((), ())), preferre...  17.5 us

profile of v13, /device:TPU:0, one launch (start us, length us, event | category | flops | bytes accessed | tf_op | source)
XLA Modules:
  0.0 623.6 jit_solution(15449979879596860518)
XLA Ops:
  0.6 142.8 %shard_map.271 = (bf16[1024,512]{1,0:T(8,128)(2,1)}, bf16[1024,2048]{1,0:T(8,128)(2,1)}, bf16[1024,2048]{1,0:T(8,128)(2,1)}, f32[1024,512]{1,0:T(8,128)}, f32[10...) custom-call(bf16[256,440]{1,0:T(8,128)(2,1)} %bitcast.30, ...), custom_call_target="tpu_custom_call" | custom-call | tf_op jit(solution)/shard_map/pallas_call | solution.py:1387
  143.4 17.5 %fusion.3.part_ref = f32[1024,2048]{1,0:T(8,128)} fusion(bf16[2368,1024]{1,0:T(8,128)(2,1)} %get-tuple-element.41.dl_ref, bf16[2368,2048]{1,0:T(8,128)(2,1)} %get-tuple-element.47), kind=kOutput, calls=%fused_computation.15 | convolution fusion | flops 9932111872 | bytes 22937600 | tf_op jit(solution)/shard_map/dot_general | solution.py:38
  160.9 34.1 %shard_map.272 = (f32[2326,1,2048]{2,1,0:T(1,128)}, s16[4,16,592,128]{3,2,1,0:T(8,128)(2,1)}, f32[4,8,128]{2,1,0:T(8,128)}) custom-call(bf16[2368,1024]{1,0:T(8,128)(2,1)} %get-tuple-element.41.dl_ref, bf16[1024,2048]{1,0:T(8,128)(2,1)} %get-tuple-element.42.h_ref, bf16[2326,2048]{1,0:T(8,128)(2,1)} %bitcast.24), custom_call_target="tpu_custom_call" | custom-call | tf_op jit(solution)/shard_map/pallas_call | solution.py:189
  195.0 166.6 %shard_map.273 = (f32[2048,512]{1,0:T(8,128)}, f32[440,512]{1,0:T(8,128)}, f32[2368,256]{1,0:T(8,128)}, f32[512,256]{1,0:T(8,128)}, f32[512,512]{1,0:T(8,128)}, ...) custom-call(s16[4,16,592,128]{3,2,1,0:T(8,128)(2,1)} %get-tuple-element.43.codes_ref, ...), custom_call_target="tpu_custom_call" | custom-call | tf_op jit(solution)/shard_map/pallas_call | solution.py:955
  361.7 1.3 slice.20
  363.0 0.0 copy-start.4
  363.0 0.0 copy-start.2
  363.0 0.0 copy-start.3
  363.0 240.1 %shard_map.274 = (f32[256,512]{1,0:T(8,128)}, f32[440,512]{1,0:T(8,128)}, f32[256,512]{1,0:T(8,128)}, f32[440,512]{1,0:T(8,128)}, f32[8,128]{1,0:T(8,128)}) custom-call(f32[8,128]{1,0:T(8,128)} %get-tuple-element.53.stats_ref, f32[512,256]{1,0:T(8,128)} %get-tuple-element.54.red_hid_ref, f32[256,512]{1,0:T(8,128)} %mom_hid_ref.1, ...), custom_call_target="tpu_custom_call" | custom-call | tf_op jit(solution)/shard_map/pallas_call | solution.py:1899
  603.1 0.0 copy-start
  603.1 1.4 fusion.2
  604.5 0.7 multiply_multiply_fusion.1
  605.2 0.0 copy-done.8
  605.2 0.0 copy-done.10
  605.2 0.0 copy-done.11
  605.2 0.7 multiply_subtract_fusion.3
  605.9 1.9 multiply_subtract_fusion.2
  607.8 2.3 multiply_subtract_fusion.1
  610.2 8.5 %multiply_subtract_fusion = (f32[256,2326]{0,1:T(8,128)}, f32[256,2326]{0,1:T(8,128)}, f32[256,2326]{0,1:T(8,128)}) fusion(f32[256,2326]{0,1:T(8,128)S(1)} %copy-done, f32[256,2326]{0,1:T(8,128)S(1)} %copy-done.3, f32[2368,256]{1,0:T(8,128)} %get-tuple-element.61, f32[]{:T(128)} %bitcast.9, f32[256,2326]{0,1:T(8,128)} %param.26), kind=kLoop, calls=%fused_computation.3 | loop fusion | flops 8931840 | bytes 16672772 | tf_op jit(solution)/shard_map/sub | solution.py:78
  618.6 0.9 copy.35
  619.5 0.8 copy.36
  620.3 0.9 copy.37
  621.2 0.2 copy-done.1
  621.4 2.0 copy.38
  (16 shorter events, 0.0 us)
Async XLA Ops:
  363.0 241.5 %copy-start.9 = (f32[32,128]{1,0:T(8,128)S(1)}, f32[32,128]{1,0:T(8,128)}, u32[]{:S(2)}) copy-start(f32[32,128]{1,0:T(8,128)} %get-tuple-element.52) | copy-start | bytes 49156
  363.0 242.2 %copy-start.8 = (f32[1,3350]{1,0:T(1,128)S(1)}, f32[1,3350]{1,0:T(1,128)}, u32[]{:S(2)}) copy-start(f32[1,3350]{1,0:T(1,128)} %bias_ref.1) | copy-start | bytes 40204
  363.0 242.2 %copy-start.10 = (f32[1,3350]{1,0:T(1,128)S(1)}, f32[1,3350]{1,0:T(1,128)}, u32[]{:S(2)}) copy-start(f32[1,3350]{1,0:T(1,128)} %param.27) | copy-start | bytes 40204
  363.0 242.2 %copy-start.11 = (f32[1,3350]{1,0:T(1,128)S(1)}, f32[1,3350]{1,0:T(1,128)}, u32[]{:S(2)}) copy-start(f32[1,3350]{1,0:T(1,128)} %param.28) | copy-start | bytes 40204
  363.0 242.9 %copy-start.4 = (f32[256,512]{1,0:T(8,128)S(1)}, f32[256,512]{1,0:T(8,128)}, u32[]{:S(2)}) copy-start(f32[256,512]{1,0:T(8,128)} %w_hid_ref.1) | copy-start | bytes 1572868
  363.0 244.9 %copy-start.2 = (f32[440,512]{1,0:T(8,128)S(1)}, f32[440,512]{1,0:T(8,128)}, u32[]{:S(2)}) copy-start(f32[440,512]{1,0:T(8,128)} %w_in_ref.1) | copy-start | bytes 2703364
  363.0 247.1 %copy-start.3 = (f32[256,2326]{0,1:T(8,128)S(1)}, f32[256,2326]{0,1:T(8,128)}, u32[]{:S(2)}) copy-start(f32[256,2326]{0,1:T(8,128)} %param.25) | copy-start | bytes 7145476
  603.1 7.0 %copy-start = (f32[256,2326]{0,1:T(8,128)S(1)}, f32[256,2326]{0,1:T(8,128)}, u32[]{:S(2)}) copy-start(f32[256,2326]{0,1:T(8,128)} %param.21) | copy-start | bytes 7145476
  610.1 8.5 %copy-start.6 = (f32[440,512]{1,0:T(8,128)S(1)}, f32[440,512]{1,0:T(8,128)}, u32[]{:S(2)}) copy-start(f32[440,512]{1,0:T(8,128)} %get-tuple-element.98) | copy-start | bytes 2703364
  610.1 9.4 %copy-start.7 = (f32[256,512]{1,0:T(8,128)S(1)}, f32[256,512]{1,0:T(8,128)}, u32[]{:S(2)}) copy-start(f32[256,512]{1,0:T(8,128)} %get-tuple-element.99) | copy-start | bytes 1572868
  610.1 10.2 %copy-start.5 = (f32[440,512]{1,0:T(8,128)S(1)}, f32[440,512]{1,0:T(8,128)}, u32[]{:S(2)}) copy-start(f32[440,512]{1,0:T(8,128)} %get-tuple-element.64) | copy-start | bytes 2703364
  618.6 2.8 copy-start.1
